TPU v7x, 32 devices: a whole 2x2x4 slice. The times are simulated.
32 devices in a mesh: grp: 2 (over y), ao: 4 (over z), aux: 2 (over x), orb: 2 (over core).
Axes of the slice: x: 2, y: 2, z: 4, core: 2. Of those that a mesh axis runs over, the one named last changes fastest.
Arguments:
- integrals: bfloat16 [8, 2048, 1280], P(('grp', 'aux'), 'ao'), parts along dimension 0, may hold values from -0.15625 to 0.15625
- coeffs: bfloat16 [4096, 1024], P(('grp', 'ao'), 'orb'), parts along dimension 0, may hold values from -6 to 6
- pair_blocks: int32 [128, 2], P('grp'), parts along dimension 0, may hold values from 0 to 7, as said below
- pair_count: int32 [8], P('grp'), parts along dimension 0, may hold values from 1 to 16, as said below
- orbital_count: int32 [16], P('grp'), parts along dimension 0, may hold values from 256 to 1024, as said below
Outputs:
- exchange_blocks: float32 [256, 128, 256], P(('aux', 'orb'), ('grp', 'ao')), parts along dimension 1
There are 2 independent parts, one for each index of `grp`. A program takes and returns all parts, laid end to end along the dimension named above; each array names one. Nothing has to cross between parts.
Inputs may be any that keep to these rules, and one draw needn't show every extreme that they name: `pair_blocks`: every row names blocks of two different block groups (a block group is the blocks b with equal b // 2), the first group the lower. Within the 16 rows of one owner, all blocks named from one block group are the same block; rows past the owner's count follow the same rule and are not used. `pair_count`: some owner has exactly 16 live slots and some owner exactly 1. Orbital i is significant on block b when i < orbital_count[b]; some block has all 1024, some exactly 256.
All inputs are finite; a program needn't handle non-finite values.
Results may differ from a plain program's by a relative error of at most 0.0039.
Values may be sent and summed in bfloat16 or wider, within the bound.
No kernel may reach another device: no remote copies, remote signals or barrier semaphores. Data moves between devices by JAX's collectives and lax.ppermute only.
A program may use at most 128 MiB of HBM per device.

v0:
```python
import math

import jax
import jax.numpy as jnp
from jax import lax
from jax.sharding import PartitionSpec as P

BLOCK = 256
AO_DEV = 2
WIN = 5
ORBS = 1024


def with_halo(cells, sides, width):
    for axis, dim in sides:
        count = lax.axis_size(axis)
        ends = count - 1
        head = lax.slice_in_dim(cells, 0, width, axis=dim)
        tail = lax.slice_in_dim(cells, cells.shape[dim] - width, cells.shape[dim], axis=dim)
        cells = jnp.concatenate(
            [
                lax.ppermute(tail, axis, [(i, (i + 1) % count) for i in range(ends)]),
                cells,
                lax.ppermute(head, axis, [((i + 1) % count, i) for i in range(ends)]),
            ],
            axis=dim,
        )
    return cells


def body(integrals, coeffs, pair_blocks, pair_count, orbital_count):
    orb_local = coeffs.shape[1]
    aux_devices = lax.axis_size("aux")
    total_aux = integrals.shape[0] * aux_devices
    rim = WIN // 2 * BLOCK
    extended = with_halo(coeffs, (("ao", 0),), rim)
    ao_here = lax.axis_index("ao")
    orbital_ids = lax.axis_index("orb") * orb_local + jnp.arange(orb_local, dtype=jnp.int32)
    pieces = []
    for offset in range(AO_DEV):
        slab = integrals[:, offset * BLOCK : (offset + 1) * BLOCK, :]
        slot_range = extended[offset * BLOCK : offset * BLOCK + WIN * BLOCK]
        values = jnp.einsum("pml,li->pmi", slab, slot_range, preferred_element_type=jnp.float32)
        limit = orbital_count[ao_here * AO_DEV + offset]
        values = jnp.where((orbital_ids < limit)[None, None, :], values, 0.0)
        pieces.append(values.astype(jnp.bfloat16))
    transformed = jnp.stack(pieces)
    owners = lax.axis_size("ao")
    table = pair_blocks.reshape(owners, -1, 2)
    slots = table.shape[1]
    live = jnp.arange(slots, dtype=jnp.int32)[None, :] < pair_count[:, None]
    touched = live[:, :, None] & (table // AO_DEV == ao_here)
    wanted = jnp.max(jnp.where(touched, table % AO_DEV, 0), axis=(1, 2))
    outgoing = transformed[wanted]
    received = lax.all_to_all(outgoing, "ao", split_axis=0, concat_axis=0, tiled=True)
    owned = table[ao_here]
    factor = 1.0 / math.sqrt(total_aux * ORBS)
    weights = jnp.where(live[ao_here], factor, 0.0).astype(jnp.float32)
    left_source = owned[:, 0] // AO_DEV
    right_source = owned[:, 1] // AO_DEV
    right_factors = received[right_source]
    lefts = received[left_source]
    term = jnp.einsum("spmi,spni->msn", lefts, right_factors, preferred_element_type=jnp.float32)
    return lax.psum_scatter(
        term * weights[None, :, None], ("aux", "orb"), scatter_dimension=0, tiled=True
    )


def solution(mesh):
    return jax.shard_map(
        body,
        mesh=mesh,
        in_specs=(
            P(("grp", "aux"), "ao", None),
            P(("grp", "ao"), "orb"),
            P("grp", None),
            P("grp"),
            P("grp"),
        ),
        out_specs=P(("aux", "orb"), ("grp", "ao"), None),
        check_vma=False,
    )
```

profile of v0, /device:TPU:8, one launch (start us, length us, event | category | flops | bytes accessed | tf_op | source)
XLA Modules:
  0.0 157.3 jit_solution(8940166735932786809)
XLA Ops:
  6.5 1.3 copy.12
  7.8 1.9 %collective-permute-start.1 = (bf16[512,512]{0,1:T(8,128)(2,1)S(1)}, bf16[512,512]{0,1:T(8,128)(2,1)S(1)}, u32[]{:S(2)}, u32[]{:S(2)}) collective-permute-start(bf16[512,512]{0,1:T(8,128)(2,1)S(1)} %copy.12), channel_id=1, source_target_pairs={{4,0},{8,4},{12,8},{5,1},{9,5},{13,9},{6,2},{10,6},{14,10},{7,3},{... | collective-permute-start | bytes 1572872 | tf_op jit(solution)/shard_map/ppermute | solution.py:24
  9.7 3.9 %collective-permute-start = (bf16[512,512]{0,1:T(8,128)(2,1)S(1)}, bf16[512,512]{0,1:T(8,128)(2,1)S(1)}, u32[]{:S(2)}, u32[]{:S(2)}) collective-permute-start(bf16[512,512]{0,1:T(8,128)(2,1)S(1)} %copy.12), channel_id=1, source_target_pairs={{0,4},{4,8},{8,12},{1,5},{5,9},{9,13},{2,6},{6,10},{10,14},{3,7},{... | collective-permute-start | bytes 1572872 | tf_op jit(solution)/shard_map/ppermute | solution.py:22
  13.7 0.7 iota_compare_fusion
  14.4 0.1 lt.83
  14.5 0.7 fusion.17
  15.2 0.1 reduce_max.15
  15.3 0.1 reduce_max.20
  15.4 1.4 fusion.22
  16.8 1.3 fusion.15
  18.1 5.2 %collective-permute-done.1 = bf16[512,512]{0,1:T(8,128)(2,1)S(1)} collective-permute-done((bf16[512,512]{0,1:T(8,128)(2,1)S(1)}, bf16[512,512]{0,1:T(8,128)(2,1)S(1)}, u32[]{:S(2)}, u32[]{:S(2)}) %collective-permute-start.1) | collective-permute-done | bytes 524320 | tf_op jit(solution)/shard_map/ppermute | solution.py:24
  23.3 1.9 %collective-permute-done = bf16[512,512]{0,1:T(8,128)(2,1)S(1)} collective-permute-done((bf16[512,512]{0,1:T(8,128)(2,1)S(1)}, bf16[512,512]{0,1:T(8,128)(2,1)S(1)}, u32[]{:S(2)}, u32[]{:S(2)}) %collective-permute-start) | collective-permute-done | bytes 524320 | tf_op jit(solution)/shard_map/ppermute | solution.py:22
  25.3 0.1 pad_maximum_fusion
  25.4 0.9 fusion.9
  26.3 0.9 fusion.12
  27.2 0.1 pad_maximum_fusion.1
  27.3 2.0 %gather_fusion = bf16[4,2,256,512]{2,3,1,0:T(8,128)(2,1)} fusion(bf16[2,2,256,512]{2,3,1,0:T(8,128)(2,1)S(1)} %pad_maximum_fusion.1, s32[1024]{0:T(1024)S(1)} %pad_clamp_fusion.2), kind=kCustom, calls=%fused_computation | custom fusion | bytes 4194320 | tf_op jit(solution)/shard_map/gather | solution.py:54
  29.3 5.6 %all-to-all-start = ((bf16[4,2,256,512]{2,3,1,0:T(8,128)(2,1)}), bf16[4,2,256,512]{2,3,1,0:T(8,128)(2,1)S(1)}, u32[]{:S(2)}, u32[]{:S(2)}) async-start(bf16[4,2,256,512]{2,3,1,0:T(8,128)(2,1)} %gather_fusion), calls=%async_computation | async-start | bytes 4194304 | tf_op jit(solution)/shard_map/all_to_all | solution.py:55
  35.0 43.6 %all-to-all-done = bf16[4,2,256,512]{2,3,1,0:T(8,128)(2,1)S(1)} async-done(((bf16[4,2,256,512]{2,3,1,0:T(8,128)(2,1)}), bf16[4,2,256,512]{2,3,1,0:T(8,128)(2,1)S(1)}, u32[]{:S(2)}, u32[]{:S(2)}) %all-to-all-start) | async-done | bytes 2097184 | tf_op jit(solution)/shard_map/all_to_all | solution.py:55
  78.6 4.7 %gather_fusion.2 = bf16[16,2,256,512]{2,3,1,0:T(8,128)(2,1)} fusion(bf16[4,2,256,512]{2,3,1,0:T(8,128)(2,1)S(1)} %all-to-all-done, s32[1024]{0:T(1024)S(1)} %get-tuple-element.11), kind=kCustom, calls=%fused_computation.2 | custom fusion | bytes 16777280 | tf_op jit(solution)/shard_map/gather | solution.py:62
  83.3 4.6 %gather_fusion.1 = bf16[16,2,256,512]{2,3,1,0:T(8,128)(2,1)} fusion(bf16[4,2,256,512]{2,3,1,0:T(8,128)(2,1)S(1)} %all-to-all-done, s32[1024]{0:T(1024)S(1)} %get-tuple-element.12), kind=kCustom, calls=%fused_computation.1 | custom fusion | bytes 16777280 | tf_op jit(solution)/shard_map/gather | solution.py:61
  87.9 10.4 %fusion = f32[256,16,256]{0,2,1:T(8,128)} fusion(bf16[16,2,256,512]{2,3,1,0:T(8,128)(2,1)} %gather_fusion.1, bf16[16,2,256,512]{2,3,1,0:T(8,128)(2,1)} %gather_fusion.2, f32[16]{0:T(128)S(1)} %fusion.18), kind=kOutput, calls=%fused_computation.4 | convolution fusion | flops 2148532224 | bytes 20971584 | tf_op jit(solution)/shard_map/spmi,spni->msn/dot_general | solution.py:63
  98.3 5.5 %copy.17 = f32[256,16,256]{2,1,0:T(8,128)} copy(f32[256,16,256]{0,2,1:T(8,128)} %fusion) | data formatting | bytes 8388608 | tf_op jit(solution)/shard_map/mul | solution.py:65
  103.8 46.6 %reduce-scatter.2.cloned.1.call-done = f32[64,16,256]{2,1,0:T(8,128)} async-done(((f32[256,16,256]{2,1,0:T(8,128)}), f32[64,16,256]{2,1,0:T(8,128)}) %reduce-scatter.2.cloned.1.call-update) | async-done | bytes 1048592 | tf_op jit(solution)/shard_map/reduce_scatter | solution.py:64
  (13 shorter events, 0.1 us)
Async XLA Ops:
  7.8 15.6 %collective-permute-start.1 = (bf16[512,512]{0,1:T(8,128)(2,1)S(1)}, bf16[512,512]{0,1:T(8,128)(2,1)S(1)}, u32[]{:S(2)}, u32[]{:S(2)}) collective-permute-start(bf16[512,512]{0,1:T(8,128)(2,1)S(1)} %copy.12), channel_id=1, source_target_pairs={{4,0},{8,4},{12,8},{5,1},{9,5},{13,9},{6,2},{10,6},{14,10},{7,3},{... | collective-permute-start | bytes 1572872 | tf_op jit(solution)/shard_map/ppermute | solution.py:24
  9.7 15.6 %collective-permute-start = (bf16[512,512]{0,1:T(8,128)(2,1)S(1)}, bf16[512,512]{0,1:T(8,128)(2,1)S(1)}, u32[]{:S(2)}, u32[]{:S(2)}) collective-permute-start(bf16[512,512]{0,1:T(8,128)(2,1)S(1)} %copy.12), channel_id=1, source_target_pairs={{0,4},{4,8},{8,12},{1,5},{5,9},{9,13},{2,6},{6,10},{10,14},{3,7},{... | collective-permute-start | bytes 1572872 | tf_op jit(solution)/shard_map/ppermute | solution.py:22
  15.4 10.0 %copy-start.1 = (bf16[2,512,1280]{2,1,0:T(8,128)(2,1)S(1)}, bf16[2,512,1280]{2,1,0:T(8,128)(2,1)}, u32[]{:S(2)}) copy-start(bf16[2,512,1280]{2,1,0:T(8,128)(2,1)} %param.5) | copy-start | bytes 7864324
  29.3 5.6 %copy-start = (s32[64,2]{0,1:T(2,128)S(1)}, s32[64,2]{0,1:T(2,128)}, u32[]{:S(2)}) copy-start(s32[64,2]{0,1:T(2,128)} %param.7) | copy-start | bytes 1540
  29.3 49.4 %all-to-all-start = ((bf16[4,2,256,512]{2,3,1,0:T(8,128)(2,1)}), bf16[4,2,256,512]{2,3,1,0:T(8,128)(2,1)S(1)}, u32[]{:S(2)}, u32[]{:S(2)}) async-start(bf16[4,2,256,512]{2,3,1,0:T(8,128)(2,1)} %gather_fusion), calls=%async_computation | async-start | bytes 4194304 | tf_op jit(solution)/shard_map/all_to_all | solution.py:55
  34.9 115.5 %reduce-scatter.2.cloned.1.call-start = ((), (), s32[]{:S(2)}) async-start(), calls=%async_computation.2 | async-start | bytes 5242880 | tf_op jit(solution)/shard_map/reduce_scatter | solution.py:64
Sparse Core Ops, SparseCore 0:
  103.9 46.4 reduce-scatter.1
where the time goes:
time: 159 us; the launch traced here: 157 us
  waiting for transfers between devices  97.4 us (61%)
  local copies, waits for them, and re-layouts  19.7 us (12%)
  between operations  13.5 us (8%)
  matrix products  12.2 us (8%)
  starting transfers between devices  11.5 us (7%)
  other arithmetic  3.06 us (2%)
    reduce_scatter x1, waiting for transfers between devices, body(): lax.psum_scatter(term * weights[None, :, None], ('aux', 'orb'), scatter_d...  46.6 us
    all_to_all x1, waiting for transfers between devices, body(): lax.all_to_all(outgoing, 'ao', split_axis=0, concat_axis=0, tiled=True)  43.6 us
    dot_general x1, matrix products, body(): jnp.einsum('spmi,spni->msn', lefts, right_factors, preferred_element_type...  10.4 us
    all_to_all x1, starting transfers between devices, body(): lax.all_to_all(outgoing, 'ao', split_axis=0, concat_axis=0, tiled=True)  5.63 us
    mul x1, local copies, waits for them, and re-layouts, body(): term * weights[None, :, None]  5.5 us
    ppermute x1, waiting for transfers between devices, with_halo(): lax.ppermute(head, axis, [((i + 1) % count, i) for i in range(ends)])  5.22 us
    gather x1, local copies, waits for them, and re-layouts, body(): lefts = received[left_source]  4.65 us
    gather x1, local copies, waits for them, and re-layouts, body(): right_factors = received[right_source]  4.58 us
  transfers between devices with their start and end apart: 4, of which 4 were waited for; matrix products, arithmetic and copies ran while one was open for 3% of the time, Pallas kernels for 0%

commit v1 on v0

--- a/solution.py
+++ b/solution.py
@@ -1,14 +1,19 @@
+import functools
 import math
 
 import jax
 import jax.numpy as jnp
 from jax import lax
+from jax.experimental import pallas as pl
+from jax.experimental.pallas import tpu as pltpu
 from jax.sharding import PartitionSpec as P
 
 BLOCK = 256
 AO_DEV = 2
 WIN = 5
 ORBS = 1024
+CHUNKS = 2
+VMEM_LIMIT = 40 * 1024 * 1024
 
 
 def with_halo(cells, sides, width):
@@ -28,7 +33,7 @@
     return cells
 
 
-def body(integrals, coeffs, pair_blocks, pair_count, orbital_count):
+def general_body(integrals, coeffs, pair_blocks, pair_count, orbital_count):
     orb_local = coeffs.shape[1]
     aux_devices = lax.axis_size("aux")
     total_aux = integrals.shape[0] * aux_devices
@@ -66,7 +71,205 @@
     )
 
 
+EARLY_PAIRS = ((0, 1), (0, 2), (1, 2))
+LATE_PAIRS = ((0, 3), (1, 3), (2, 3))
+ALL_PAIRS = EARLY_PAIRS + LATE_PAIRS
+
+
+def transform_kernel(meta, integrals, prev, own, following, out0, out1, out2, out3, half):
+    columns = own.shape[1]
+    ids = lax.broadcasted_iota(jnp.int32, (BLOCK, columns), 1)
+    mid = AO_DEV * BLOCK
+
+    def dot(a, b):
+        return jnp.dot(a, b, preferred_element_type=jnp.float32)
+
+    for offset in range(AO_DEV):
+        low = mid - offset * BLOCK
+        for p in range(integrals.shape[0]):
+            slab = integrals[p, offset * BLOCK : (offset + 1) * BLOCK, :]
+            values = dot(slab[:, low : low + mid], own[...])
+            values += dot(slab[:, :low], prev[offset * BLOCK :, :])
+            values += dot(slab[:, low + mid :], following[: (offset + 1) * BLOCK, :])
+            half[offset, p] = jnp.where(ids < meta[4 + offset], values, 0.0).astype(jnp.bfloat16)
+    for s, out in enumerate((out0, out1, out2, out3)):
+        out[...] = half[meta[s]]
+
+
+def transform(meta, integrals, prev, own, following):
+    shape = (integrals.shape[0], BLOCK, own.shape[1])
+    vmem = pl.BlockSpec(memory_space=pltpu.VMEM)
+    return pl.pallas_call(
+        transform_kernel,
+        out_shape=[jax.ShapeDtypeStruct(shape, jnp.bfloat16)] * 4,
+        in_specs=[pl.BlockSpec(memory_space=pltpu.SMEM)] + [vmem] * 4,
+        out_specs=[vmem] * 4,
+        scratch_shapes=[pltpu.VMEM((AO_DEV, *shape), jnp.bfloat16)],
+        compiler_params=pltpu.CompilerParams(vmem_limit_bytes=VMEM_LIMIT),
+        cost_estimate=pl.CostEstimate(
+            flops=2 * AO_DEV * math.prod(shape) * integrals.shape[2],
+            bytes_accessed=2 * (integrals.size + 3 * own.size + 4 * math.prod(shape)),
+            transcendentals=0,
+        ),
+        name="transform",
+    )(meta, integrals, prev, own, following)
+
+
+def pairs_kernel(pairs, used, meta, *refs):
+    blocks = {s: refs[i * CHUNKS : (i + 1) * CHUNKS] for i, s in enumerate(used)}
+    keep, give, grams = refs[len(used) * CHUNKS :]
+    here, aux, orb = meta[0], meta[1], meta[2]
+
+    def product(left, right):
+        total = None
+        for a, b in zip(blocks[left], blocks[right]):
+            for p in range(a.shape[0]):
+                part = lax.dot_general(
+                    a[p], b[p], (((1,), (1,)), ((), ())), preferred_element_type=jnp.float32
+                )
+                total = part if total is None else total + part
+        return total.reshape(grams.shape[1:])
+
+    for bit in (0, 1):
+        mine = [(k, a, b) for k, (a, b) in enumerate(pairs) if (a ^ b) >> 1 == bit]
+        upper = (here >> bit) & 1
+        for k, a, b in mine:
+
+            @pl.when(upper == 0)
+            def _(k=k, a=a, b=b):
+                grams[k] = product(a, b)
+
+            @pl.when(upper == 1)
+            def _(k=k, a=a, b=b):
+                grams[k] = product(b, a)
+
+    for k in range(len(pairs)):
+        for x in (0, 1):
+            row = 2 * (aux ^ x)
+            keep[x, k] = grams[k, row + orb]
+            give[x, k] = grams[k, row + 1 - orb]
+
+
+def pair_products(pairs, used, meta, blocks):
+    shape = jax.ShapeDtypeStruct((2, len(pairs), BLOCK // 4, BLOCK), jnp.float32)
+    vmem = pl.BlockSpec(memory_space=pltpu.VMEM)
+    return pl.pallas_call(
+        functools.partial(pairs_kernel, pairs, used),
+        out_shape=[shape] * 2,
+        in_specs=[pl.BlockSpec(memory_space=pltpu.SMEM)] + [vmem] * (len(used) * CHUNKS),
+        out_specs=[vmem] * 2,
+        scratch_shapes=[pltpu.VMEM((len(pairs), 4, BLOCK // 4, BLOCK), jnp.float32)],
+        compiler_params=pltpu.CompilerParams(vmem_limit_bytes=VMEM_LIMIT),
+        cost_estimate=pl.CostEstimate(
+            flops=2 * len(pairs) * BLOCK * CHUNKS * blocks[0][0].size,
+            bytes_accessed=2 * len(used) * CHUNKS * blocks[0][0].size + 16 * shape.size,
+            transcendentals=0,
+        ),
+        name="pairs",
+    )(meta, *[part for s in used for part in blocks[s]])
+
+
+def spread_kernel(factor, place, keep0, got0, far0, keep1, got1, far1, out, sums):
+    early = keep0.shape[1]
+    sums[:early] = (keep0[0] + got0[0] + far0[...].astype(jnp.float32)) * factor
+    sums[early:] = (keep1[0] + got1[0] + far1[...].astype(jnp.float32)) * factor
+    rows, slots, width = out.shape
+    slot = lax.broadcasted_iota(jnp.int32, (slots, width), 0)
+    source = jnp.zeros((slots, width), jnp.int32)
+    for s in range(slots):
+        source = jnp.where(slot == s, place[s], source)
+    masks = [source == k for k in range(sums.shape[0])]
+
+    def one(m, carry):
+        row = jnp.zeros((slots, width), jnp.float32)
+        for k, mask in enumerate(masks):
+            values = jnp.broadcast_to(sums[k, pl.ds(m, 1), :], (slots, width))
+            row = jnp.where(mask, values, row)
+        out[m] = row
+        return carry
+
+    lax.fori_loop(0, rows, one, 0, unroll=8)
+
+
+def spread(factor, place, early, late):
+    rows = BLOCK // 4
+    slots = place.shape[0]
+    vmem = pl.BlockSpec(memory_space=pltpu.VMEM)
+    return pl.pallas_call(
+        functools.partial(spread_kernel, factor),
+        out_shape=jax.ShapeDtypeStruct((rows, slots, BLOCK), jnp.float32),
+        in_specs=[pl.BlockSpec(memory_space=pltpu.SMEM)] + [vmem] * 6,
+        out_specs=vmem,
+        scratch_shapes=[pltpu.VMEM((len(ALL_PAIRS), rows, BLOCK), jnp.float32)],
+        compiler_params=pltpu.CompilerParams(vmem_limit_bytes=VMEM_LIMIT),
+        cost_estimate=pl.CostEstimate(
+            flops=6 * rows * slots * BLOCK, bytes_accessed=4 * rows * slots * BLOCK, transcendentals=0
+        ),
+        name="spread",
+    )(place, *early, *late)
+
+
+SWAP = [(0, 1), (1, 0)]
+
+
+def reduce_blocks(keep, give):
+    got = lax.ppermute(give, "orb", SWAP)
+    far = lax.ppermute(keep[1] + got[1], "aux", SWAP)
+    return keep, got, far
+
+
+def six_pair_body(integrals, coeffs, pair_blocks, pair_count, orbital_count):
+    orb_local = coeffs.shape[1]
+    width = orb_local // CHUNKS
+    total_aux = integrals.shape[0] * lax.axis_size("aux")
+    owners = lax.axis_size("ao")
+    here, aux, orb = lax.axis_index("ao"), lax.axis_index("aux"), lax.axis_index("orb")
+    up = [(i, i + 1) for i in range(owners - 1)]
+    down = [(i + 1, i) for i in range(owners - 1)]
+
+    parts = [lax.slice_in_dim(coeffs, c * width, (c + 1) * width, axis=1) for c in range(CHUNKS)]
+    halos = [(lax.ppermute(part, "ao", up), lax.ppermute(part, "ao", down)) for part in parts]
+
+    table = pair_blocks.reshape(owners, -1, 2)
+    slots = table.shape[1]
+    wanted = jnp.max(jnp.where(table // AO_DEV == here, table % AO_DEV, 0), axis=(1, 2))
+    partners = here ^ jnp.arange(owners, dtype=jnp.int32)
+    wanted = wanted[partners]
+    counts = lax.dynamic_slice_in_dim(orbital_count, here * AO_DEV, AO_DEV) - orb * orb_local
+
+    blocks = [[] for _ in range(owners)]
+    for c, (part, (prev, following)) in enumerate(zip(parts, halos)):
+        meta = jnp.concatenate([wanted, counts - c * width]).astype(jnp.int32)
+        for s, piece in enumerate(transform(meta, integrals, prev, part, following)):
+            blocks[s].append(piece)
+
+    def fetch(s):
+        swap = [(j, j ^ s) for j in range(owners)]
+        return [lax.ppermute(piece, "ao", swap) for piece in blocks[s]]
+
+    got = [blocks[0], None, None, None]
+    got[2] = fetch(2)
+    got[1] = fetch(1)
+    got[3] = fetch(3)
+
+    position = jnp.stack([here, aux, orb]).astype(jnp.int32)
+    early = reduce_blocks(*pair_products(EARLY_PAIRS, (0, 1, 2), position, got))
+    late = reduce_blocks(*pair_products(LATE_PAIRS, (0, 1, 2, 3), position, got))
+
+    owned = lax.dynamic_index_in_dim(table, here, 0, keepdims=False) // AO_DEV ^ here
+    lower, upper = jnp.min(owned, axis=1), jnp.max(owned, axis=1)
+    place = jnp.full((slots,), len(ALL_PAIRS), jnp.int32)
+    for k, (a, b) in enumerate(ALL_PAIRS):
+        place = jnp.where((lower == a) & (upper == b), k, place)
+    place = jnp.where(jnp.arange(slots) < pair_count[here], place, len(ALL_PAIRS))
+    return spread(1.0 / math.sqrt(total_aux * ORBS), place, early, late)
+
+
 def solution(mesh):
+    sizes = dict(mesh.shape)
+    body = general_body
+    if sizes["ao"] == 4 and sizes["aux"] == 2 and sizes["orb"] == 2:
+        body = six_pair_body
     return jax.shard_map(
         body,
         mesh=mesh,

time: 159 us -> 83.8 us (0.53)
  waiting for transfers between devices: 97.4 us -> 45.1 us
  local copies, waits for them, and re-layouts: 19.7 us -> 4.21 us
  between operations: 13.5 us -> 0.15 us
  matrix products: 12.2 us -> 0 us
  starting transfers between devices: 11.5 us -> 23 us
  Pallas kernels: 0 us -> 8.66 us
    reduce_scatter x1 -> x0, waiting for transfers between devices: 46.6 us -> none  [body(): lax.psum_scatter(term * weights[None, :, None], ('aux', 'orb'), scatter_d...]
    all_to_all x1 -> x0, waiting for transfers between devices: 43.6 us -> none  [body(): lax.all_to_all(outgoing, 'ao', split_axis=0, concat_axis=0, tiled=True)]
    ppermute x2 -> x14, waiting for transfers between devices: 7.15 us -> 45.1 us  [the longest x6 36.9 us: fetch(): return [lax.ppermute(piece, 'ao', swap) for piece in blocks[s]]]
    ppermute x2 -> x14, starting transfers between devices: 5.84 us -> 23 us  [the longest x6 8.43 us: fetch(): return [lax.ppermute(piece, 'ao', swap) for piece in blocks[s]]]
    dot_general x3 -> x0, matrix products: 12.2 us -> none  [the longest x1 10.4 us: body(): jnp.einsum('spmi,spni->msn', lefts, right_factors, preferred_element_type...]
    gather x3 -> x1, local copies, waits for them, and re-layouts: 11.2 us -> 0.64 us  [six_pair_body(): wanted = wanted[partners]]
    pallas_call x0 -> x5, Pallas kernels: none -> 8.66 us  [the longest x2 3.61 us: transform(): pl.pallas_call(transform_kernel, out_shape=[jax.ShapeDtypeStruct(shape, j...]
    all_to_all x1 -> x0, starting transfers between devices: 5.63 us -> none  [body(): lax.all_to_all(outgoing, 'ao', split_axis=0, concat_axis=0, tiled=True)]
  transfers between devices with their start and end apart: 4 -> 14, of which waited for: 4 -> 7; matrix products, arithmetic and copies ran while one was open for 3% -> 5% of each run, Pallas kernels for 0% -> 6%
where the time goes in v1:
time: 83.8 us; the launch traced here: 83.5 us
  waiting for transfers between devices  45.1 us (54%)
  starting transfers between devices  23 us (27%)
  Pallas kernels  8.66 us (10%)
  local copies, waits for them, and re-layouts  4.21 us (5%)
  other arithmetic  2.46 us (3%)
    ppermute x6, waiting for transfers between devices, fetch(): return [lax.ppermute(piece, 'ao', swap) for piece in blocks[s]]  36.9 us
    ppermute x6, starting transfers between devices, fetch(): return [lax.ppermute(piece, 'ao', swap) for piece in blocks[s]]  8.43 us
    ppermute x2, waiting for transfers between devices, reduce_blocks(): far = lax.ppermute(keep[1] + got[1], 'aux', SWAP)  8.17 us
    ppermute x2, starting transfers between devices, six_pair_body(): lax.ppermute(part, 'ao', up)  7.83 us
    ppermute x2, starting transfers between devices, six_pair_body(): lax.ppermute(part, 'ao', down)  3.85 us
    pallas_call x2, Pallas kernels, transform(): pl.pallas_call(transform_kernel, out_shape=[jax.ShapeDtypeStruct(shape, j...  3.61 us
    pallas_call x2, Pallas kernels, pair_products(): pl.pallas_call(functools.partial(pairs_kernel, pairs, used), out_shape=[s...  3.21 us
    ppermute x2, starting transfers between devices, reduce_blocks(): far = lax.ppermute(keep[1] + got[1], 'aux', SWAP)  2.26 us
  transfers between devices with their start and end apart: 14, of which 7 were waited for; matrix products, arithmetic and copies ran while one was open for 5% of the time, Pallas kernels for 6%

profile of v1, /device:TPU:8, one launch (start us, length us, event | category | flops | bytes accessed | tf_op | source)
XLA Modules:
  0.0 83.5 jit_solution(368954695401798142)
XLA Ops:
  0.0 1.1 %fusion.6 = (bf16[512,256]{1,0:T(8,128)(2,1)S(1)}, bf16[512,256]{1,0:T(8,128)(2,1)S(1)}) fusion(bf16[512,512]{1,0:T(8,128)(2,1)} %param.6), kind=kLoop, calls=%fused_computation.34 | loop fusion | bytes 1048576 | tf_op jit(solution)/shard_map/slice | solution.py:230
  1.1 1.9 %collective-permute-start.3 = (bf16[512,256]{1,0:T(8,128)(2,1)S(1)}, bf16[512,256]{1,0:T(8,128)(2,1)S(1)}, u32[]{:S(2)}, u32[]{:S(2)}) collective-permute-start(bf16[512,256]{1,0:T(8,128)(2,1)S(1)} %get-tuple-element.33.own), channel_id=1, source_target_pairs={{4,0},{8,4},{12,8},{5,1},{9,5},{13,9},{6,2},{10,6},{14,10},{7,3},{... | collective-permute-start | bytes 786440 | tf_op jit(solution)/shard_map/ppermute | solution.py:231
  3.0 3.9 %collective-permute-start.2 = (bf16[512,256]{1,0:T(8,128)(2,1)S(1)}, bf16[512,256]{1,0:T(8,128)(2,1)S(1)}, u32[]{:S(2)}, u32[]{:S(2)}) collective-permute-start(bf16[512,256]{1,0:T(8,128)(2,1)S(1)} %get-tuple-element.33.own), channel_id=1, source_target_pairs={{0,4},{4,8},{8,12},{1,5},{5,9},{9,13},{2,6},{6,10},{10,14},{3,7},{... | collective-permute-start | bytes 786440 | tf_op jit(solution)/shard_map/ppermute | solution.py:231
  6.9 1.9 %collective-permute-start.1 = (bf16[512,256]{1,0:T(8,128)(2,1)S(1)}, bf16[512,256]{1,0:T(8,128)(2,1)S(1)}, u32[]{:S(2)}, u32[]{:S(2)}) collective-permute-start(bf16[512,256]{1,0:T(8,128)(2,1)S(1)} %get-tuple-element.34.own), channel_id=1, source_target_pairs={{4,0},{8,4},{12,8},{5,1},{9,5},{13,9},{6,2},{10,6},{14,10},{7,3},{... | collective-permute-start | bytes 786440 | tf_op jit(solution)/shard_map/ppermute | solution.py:231
  8.9 3.9 %collective-permute-start = (bf16[512,256]{1,0:T(8,128)(2,1)S(1)}, bf16[512,256]{1,0:T(8,128)(2,1)S(1)}, u32[]{:S(2)}, u32[]{:S(2)}) collective-permute-start(bf16[512,256]{1,0:T(8,128)(2,1)S(1)} %get-tuple-element.34.own), channel_id=1, source_target_pairs={{0,4},{4,8},{8,12},{1,5},{5,9},{9,13},{2,6},{6,10},{10,14},{3,7},{... | collective-permute-start | bytes 786440 | tf_op jit(solution)/shard_map/ppermute | solution.py:231
  14.4 0.7 broadcast_add_fusion
  15.2 1.7 %copy-done = bf16[2,512,1280]{2,1,0:T(8,128)(2,1)S(1)} copy-done((bf16[2,512,1280]{2,1,0:T(8,128)(2,1)S(1)}, bf16[2,512,1280]{2,1,0:T(8,128)(2,1)}, u32[]{:S(2)}) %copy-start) | copy-done | bytes 2621464
  16.9 1.4 %transform.3 = (bf16[2,256,256]{2,1,0:T(8,128)(2,1)S(1)}, bf16[2,256,256]{2,1,0:T(8,128)(2,1)S(1)}, bf16[2,256,256]{2,1,0:T(8,128)(2,1)S(1)}, bf16[2,256,256]{2,1,0:T(8,128)(2,1)S(1)}) custom-call(s32[6]{0:T(128)S(1)} %get-tuple-element.35.meta, bf16[2,512,1280]{2,1,0:T(8,128)(2,1)S(1)} %copy-done, bf16[512,256]{1,0:T(8,128)(2,1)S(1)} %collective-permute-done.2.prev, ...), custom_call_target="tpu_custom_call" | custom-call | flops 671088640 | bytes 4456448 | tf_op jit(solution)/shard_map/transform/pallas_call | solution.py:102
  18.5 3.0 %collective-permute-start.7 = (bf16[2,256,256]{2,1,0:T(8,128)(2,1)S(1)}, bf16[2,256,256]{2,1,0:T(8,128)(2,1)S(1)}, u32[]{:S(2)}, u32[]{:S(2)}) collective-permute-start(bf16[2,256,256]{2,1,0:T(8,128)(2,1)S(1)} %get-tuple-element.22), channel_id=1, source_target_pairs={{0,8},{4,12},{8,0},{12,4},{1,9},{5,13},{9,1},{13,5},{2,10},{6,14},... | collective-permute-start | bytes 786440 | tf_op jit(solution)/shard_map/ppermute | solution.py:248
  22.0 2.2 %transform.2 = (bf16[2,256,256]{2,1,0:T(8,128)(2,1)S(1)}, bf16[2,256,256]{2,1,0:T(8,128)(2,1)}, bf16[2,256,256]{2,1,0:T(8,128)(2,1)S(1)}, bf16[2,256,256]{2,1,0:T(8,128)(2,1)S(1)}) custom-call(s32[6]{0:T(128)S(1)} %get-tuple-element.36.meta, bf16[2,512,1280]{2,1,0:T(8,128)(2,1)S(1)} %copy-done.1, bf16[512,256]{1,0:T(8,128)(2,1)S(1)} %collective-permute-done.prev, ...), custom_call_target="tpu_custom_call" | custom-call | flops 671088640 | bytes 4456448 | tf_op jit(solution)/shard_map/transform/pallas_call | solution.py:102
  24.1 1.0 %collective-permute-start.4 = (bf16[2,256,256]{2,1,0:T(8,128)(2,1)}, bf16[2,256,256]{2,1,0:T(8,128)(2,1)S(1)}, u32[]{:S(2)}, u32[]{:S(2)}) collective-permute-start(bf16[2,256,256]{2,1,0:T(8,128)(2,1)} %get-tuple-element.19), channel_id=1, source_target_pairs={{0,4},{4,0},{8,12},{12,8},{1,5},{5,1},{9,13},{13,9},{2,6},{6,2},{1... | collective-permute-start | bytes 786440 | tf_op jit(solution)/shard_map/ppermute | solution.py:248
  25.2 2.0 %collective-permute-start.6 = (bf16[2,256,256]{2,1,0:T(8,128)(2,1)S(1)}, bf16[2,256,256]{2,1,0:T(8,128)(2,1)S(1)}, u32[]{:S(2)}, u32[]{:S(2)}) collective-permute-start(bf16[2,256,256]{2,1,0:T(8,128)(2,1)S(1)} %get-tuple-element.21), channel_id=1, source_target_pairs={{0,8},{4,12},{8,0},{12,4},{1,9},{5,13},{9,1},{13,5},{2,10},{6,14},... | collective-permute-start | bytes 786440 | tf_op jit(solution)/shard_map/ppermute | solution.py:248
  27.2 2.6 %collective-permute-done.5.refs_3_ = bf16[2,256,256]{2,1,0:T(8,128)(2,1)S(1)} collective-permute-done((bf16[2,256,256]{2,1,0:T(8,128)(2,1)S(1)}, bf16[2,256,256]{2,1,0:T(8,128)(2,1)S(1)}, u32[]{:S(2)}, u32[]{:S(2)}) %collective-permute-start.5) | collective-permute-done | bytes 262176 | tf_op jit(solution)/shard_map/ppermute | solution.py:248
  29.8 1.8 %collective-permute-start.10 = (bf16[2,256,256]{2,1,0:T(8,128)(2,1)S(1)}, bf16[2,256,256]{2,1,0:T(8,128)(2,1)S(1)}, u32[]{:S(2)}, u32[]{:S(2)}) collective-permute-start(bf16[2,256,256]{2,1,0:T(8,128)(2,1)S(1)} %get-tuple-element.25), channel_id=1, source_target_pairs={{0,12},{4,8},{8,4},{12,0},{1,13},{5,9},{9,5},{13,1},{2,14},{6,10},... | collective-permute-start | bytes 786440 | tf_op jit(solution)/shard_map/ppermute | solution.py:248
  31.7 7.4 %collective-permute-done.7.refs_5_ = bf16[2,256,256]{2,1,0:T(8,128)(2,1)S(1)} collective-permute-done((bf16[2,256,256]{2,1,0:T(8,128)(2,1)S(1)}, bf16[2,256,256]{2,1,0:T(8,128)(2,1)S(1)}, u32[]{:S(2)}, u32[]{:S(2)}) %collective-permute-start.7) | collective-permute-done | bytes 262176 | tf_op jit(solution)/shard_map/ppermute | solution.py:248
  39.1 18.1 %collective-permute-done.11.refs_7_ = bf16[2,256,256]{2,1,0:T(8,128)(2,1)S(1)} collective-permute-done((bf16[2,256,256]{2,1,0:T(8,128)(2,1)S(1)}, bf16[2,256,256]{2,1,0:T(8,128)(2,1)S(1)}, u32[]{:S(2)}, u32[]{:S(2)}) %collective-permute-start.11) | collective-permute-done | bytes 262176 | tf_op jit(solution)/shard_map/ppermute | solution.py:248
  57.3 4.5 %collective-permute-done.6.refs_4_ = bf16[2,256,256]{2,1,0:T(8,128)(2,1)S(1)} collective-permute-done((bf16[2,256,256]{2,1,0:T(8,128)(2,1)S(1)}, bf16[2,256,256]{2,1,0:T(8,128)(2,1)S(1)}, u32[]{:S(2)}, u32[]{:S(2)}) %collective-permute-start.6) | collective-permute-done | bytes 262176 | tf_op jit(solution)/shard_map/ppermute | solution.py:248
  61.7 4.2 %collective-permute-done.10.refs_6_ = bf16[2,256,256]{2,1,0:T(8,128)(2,1)S(1)} collective-permute-done((bf16[2,256,256]{2,1,0:T(8,128)(2,1)S(1)}, bf16[2,256,256]{2,1,0:T(8,128)(2,1)S(1)}, u32[]{:S(2)}, u32[]{:S(2)}) %collective-permute-start.10) | collective-permute-done | bytes 262176 | tf_op jit(solution)/shard_map/ppermute | solution.py:248
  66.0 1.6 %pairs.3 = (f32[2,3,64,256]{3,2,1,0:T(8,128)S(1)}, f32[2,3,64,256]{3,2,1,0:T(8,128)S(1)}) custom-call(s32[3]{0:T(128)S(1)} %pad_add_fusion.meta, bf16[2,256,256]{2,1,0:T(8,128)(2,1)S(1)} %get-tuple-element.17.refs_0_, bf16[2,256,256]{2,1,0:T(8,128)(2,1)S(1)} %get-tuple-element.18.refs_1_, bf16[2,256,256]{2,1,0:T(8,128)(2,1)S(1)} %collective-permute-done.4.refs_2_, ...), custom_call_target="tpu_custom_call" | custom-call | flops 402653184 | bytes 3670016 | tf_op jit(solution)/shard_map/pairs/pallas_call | solution.py:156
  67.8 1.6 %pairs.2 = (f32[2,3,64,256]{3,2,1,0:T(8,128)S(1)}, f32[2,3,64,256]{3,2,1,0:T(8,128)S(1)}) custom-call(s32[3]{0:T(128)S(1)} %pad_add_fusion.meta, bf16[2,256,256]{2,1,0:T(8,128)(2,1)S(1)} %get-tuple-element.17.refs_0_, bf16[2,256,256]{2,1,0:T(8,128)(2,1)S(1)} %get-tuple-element.18.refs_1_, bf16[2,256,256]{2,1,0:T(8,128)(2,1)S(1)} %collective-permute-done.4.refs_2_, ...), custom_call_target="tpu_custom_call" | custom-call | flops 402653184 | bytes 3145728 | tf_op jit(solution)/shard_map/pairs/pallas_call | solution.py:156
  70.6 1.6 %collective-permute-start.13 = (f32[3,64,256]{2,1,0:T(8,128)S(1)}, f32[3,64,256]{2,1,0:T(8,128)S(1)}, u32[]{:S(2)}, u32[]{:S(2)}) collective-permute-start(f32[3,64,256]{2,1,0:T(8,128)S(1)} %fusion), channel_id=1, source_target_pairs={{0,2},{2,0},{1,3},{3,1},{4,6},{6,4},{5,7},{7,5},{8,10},{10,8},{9,1... | collective-permute-start | bytes 589832 | tf_op jit(solution)/shard_map/ppermute | solution.py:217
  73.5 4.9 %collective-permute-done.13.far1 = f32[3,64,256]{2,1,0:T(8,128)S(1)} collective-permute-done((f32[3,64,256]{2,1,0:T(8,128)S(1)}, f32[3,64,256]{2,1,0:T(8,128)S(1)}, u32[]{:S(2)}, u32[]{:S(2)}) %collective-permute-start.13) | collective-permute-done | bytes 196640 | tf_op jit(solution)/shard_map/ppermute | solution.py:217
  78.4 3.3 %collective-permute-done.9.far0 = f32[3,64,256]{2,1,0:T(8,128)S(1)} collective-permute-done((f32[3,64,256]{2,1,0:T(8,128)S(1)}, f32[3,64,256]{2,1,0:T(8,128)S(1)}, u32[]{:S(2)}, u32[]{:S(2)}) %collective-permute-start.9) | collective-permute-done | bytes 196640 | tf_op jit(solution)/shard_map/ppermute | solution.py:217
  81.7 1.8 %spread.1 = f32[64,16,256]{2,1,0:T(8,128)} custom-call(s32[16]{0:T(128)S(1)} %compare_select_fusion.2.place, f32[2,3,64,256]{3,2,1,0:T(8,128)S(1)} %get-tuple-element.23.keep0, f32[2,3,64,256]{3,2,1,0:T(8,128)S(1)} %collective-permute-done.8.got0, f32[3,64,256]{2,1,0:T(8,128)S(1)} %collective-permute-done.9.far0, ...), custom_call_target="tpu_custom_call" | custom-call | flops 1572864 | bytes 1048576 | tf_op jit(solution)/shard_map/spread/pallas_call | solution.py:198
  (34 shorter events, 5.0 us)
Async XLA Ops:
  1.1 14.1 %collective-permute-start.3 = (bf16[512,256]{1,0:T(8,128)(2,1)S(1)}, bf16[512,256]{1,0:T(8,128)(2,1)S(1)}, u32[]{:S(2)}, u32[]{:S(2)}) collective-permute-start(bf16[512,256]{1,0:T(8,128)(2,1)S(1)} %get-tuple-element.33.own), channel_id=1, source_target_pairs={{4,0},{8,4},{12,8},{5,1},{9,5},{13,9},{6,2},{10,6},{14,10},{7,3},{... | collective-permute-start | bytes 786440 | tf_op jit(solution)/shard_map/ppermute | solution.py:231
  3.0 12.2 %collective-permute-start.2 = (bf16[512,256]{1,0:T(8,128)(2,1)S(1)}, bf16[512,256]{1,0:T(8,128)(2,1)S(1)}, u32[]{:S(2)}, u32[]{:S(2)}) collective-permute-start(bf16[512,256]{1,0:T(8,128)(2,1)S(1)} %get-tuple-element.33.own), channel_id=1, source_target_pairs={{0,4},{4,8},{8,12},{1,5},{5,9},{9,13},{2,6},{6,10},{10,14},{3,7},{... | collective-permute-start | bytes 786440 | tf_op jit(solution)/shard_map/ppermute | solution.py:231
  6.9 15.0 %collective-permute-start.1 = (bf16[512,256]{1,0:T(8,128)(2,1)S(1)}, bf16[512,256]{1,0:T(8,128)(2,1)S(1)}, u32[]{:S(2)}, u32[]{:S(2)}) collective-permute-start(bf16[512,256]{1,0:T(8,128)(2,1)S(1)} %get-tuple-element.34.own), channel_id=1, source_target_pairs={{4,0},{8,4},{12,8},{5,1},{9,5},{13,9},{6,2},{10,6},{14,10},{7,3},{... | collective-permute-start | bytes 786440 | tf_op jit(solution)/shard_map/ppermute | solution.py:231
  8.9 13.1 %collective-permute-start = (bf16[512,256]{1,0:T(8,128)(2,1)S(1)}, bf16[512,256]{1,0:T(8,128)(2,1)S(1)}, u32[]{:S(2)}, u32[]{:S(2)}) collective-permute-start(bf16[512,256]{1,0:T(8,128)(2,1)S(1)} %get-tuple-element.34.own), channel_id=1, source_target_pairs={{0,4},{4,8},{8,12},{1,5},{5,9},{9,13},{2,6},{6,10},{10,14},{3,7},{... | collective-permute-start | bytes 786440 | tf_op jit(solution)/shard_map/ppermute | solution.py:231
  15.2 1.7 %copy-start = (bf16[2,512,1280]{2,1,0:T(8,128)(2,1)S(1)}, bf16[2,512,1280]{2,1,0:T(8,128)(2,1)}, u32[]{:S(2)}) copy-start(bf16[2,512,1280]{2,1,0:T(8,128)(2,1)} %integrals.3) | copy-start | bytes 7864324
  16.9 5.0 %copy-start.1 = (bf16[2,512,1280]{2,1,0:T(8,128)(2,1)S(1)}, bf16[2,512,1280]{2,1,0:T(8,128)(2,1)}, u32[]{:S(2)}) copy-start(bf16[2,512,1280]{2,1,0:T(8,128)(2,1)} %integrals.3) | copy-start | bytes 7864324
  18.4 11.4 %collective-permute-start.5 = (bf16[2,256,256]{2,1,0:T(8,128)(2,1)S(1)}, bf16[2,256,256]{2,1,0:T(8,128)(2,1)S(1)}, u32[]{:S(2)}, u32[]{:S(2)}) collective-permute-start(bf16[2,256,256]{2,1,0:T(8,128)(2,1)S(1)} %get-tuple-element.20), channel_id=1, source_target_pairs={{0,4},{4,0},{8,12},{12,8},{1,5},{5,1},{9,13},{13,9},{2,6},{6,2},{1... | collective-permute-start | bytes 786440 | tf_op jit(solution)/shard_map/ppermute | solution.py:248
  18.5 20.7 %collective-permute-start.7 = (bf16[2,256,256]{2,1,0:T(8,128)(2,1)S(1)}, bf16[2,256,256]{2,1,0:T(8,128)(2,1)S(1)}, u32[]{:S(2)}, u32[]{:S(2)}) collective-permute-start(bf16[2,256,256]{2,1,0:T(8,128)(2,1)S(1)} %get-tuple-element.22), channel_id=1, source_target_pairs={{0,8},{4,12},{8,0},{12,4},{1,9},{5,13},{9,1},{13,5},{2,10},{6,14},... | collective-permute-start | bytes 786440 | tf_op jit(solution)/shard_map/ppermute | solution.py:248
  21.5 35.8 %collective-permute-start.11 = (bf16[2,256,256]{2,1,0:T(8,128)(2,1)S(1)}, bf16[2,256,256]{2,1,0:T(8,128)(2,1)S(1)}, u32[]{:S(2)}, u32[]{:S(2)}) collective-permute-start(bf16[2,256,256]{2,1,0:T(8,128)(2,1)S(1)} %get-tuple-element.26), channel_id=1, source_target_pairs={{0,12},{4,8},{8,4},{12,0},{1,13},{5,9},{9,5},{13,1},{2,14},{6,10},... | collective-permute-start | bytes 786440 | tf_op jit(solution)/shard_map/ppermute | solution.py:248
  21.9 45.7 %copy-start.2 = (s32[64,2]{0,1:T(2,128)S(1)}, s32[64,2]{0,1:T(2,128)}, u32[]{:S(2)}) copy-start(s32[64,2]{0,1:T(2,128)} %param.7) | copy-start | bytes 1540
  24.1 45.8 %copy-start.3 = (s32[4]{0:T(128)S(1)}, s32[4]{0:T(128)}, u32[]{:S(2)}) copy-start(s32[4]{0:T(128)} %param.8) | copy-start | bytes 52
  24.1 33.2 %collective-permute-start.4 = (bf16[2,256,256]{2,1,0:T(8,128)(2,1)}, bf16[2,256,256]{2,1,0:T(8,128)(2,1)S(1)}, u32[]{:S(2)}, u32[]{:S(2)}) collective-permute-start(bf16[2,256,256]{2,1,0:T(8,128)(2,1)} %get-tuple-element.19), channel_id=1, source_target_pairs={{0,4},{4,0},{8,12},{12,8},{1,5},{5,1},{9,13},{13,9},{2,6},{6,2},{1... | collective-permute-start | bytes 786440 | tf_op jit(solution)/shard_map/ppermute | solution.py:248
  25.2 36.6 %collective-permute-start.6 = (bf16[2,256,256]{2,1,0:T(8,128)(2,1)S(1)}, bf16[2,256,256]{2,1,0:T(8,128)(2,1)S(1)}, u32[]{:S(2)}, u32[]{:S(2)}) collective-permute-start(bf16[2,256,256]{2,1,0:T(8,128)(2,1)S(1)} %get-tuple-element.21), channel_id=1, source_target_pairs={{0,8},{4,12},{8,0},{12,4},{1,9},{5,13},{9,1},{13,5},{2,10},{6,14},... | collective-permute-start | bytes 786440 | tf_op jit(solution)/shard_map/ppermute | solution.py:248
  29.8 36.2 %collective-permute-start.10 = (bf16[2,256,256]{2,1,0:T(8,128)(2,1)S(1)}, bf16[2,256,256]{2,1,0:T(8,128)(2,1)S(1)}, u32[]{:S(2)}, u32[]{:S(2)}) collective-permute-start(bf16[2,256,256]{2,1,0:T(8,128)(2,1)S(1)} %get-tuple-element.25), channel_id=1, source_target_pairs={{0,12},{4,8},{8,4},{12,0},{1,13},{5,9},{9,5},{13,1},{2,14},{6,10},... | collective-permute-start | bytes 786440 | tf_op jit(solution)/shard_map/ppermute | solution.py:248
  67.6 3.0 %collective-permute-start.12 = (f32[2,3,64,256]{3,2,1,0:T(8,128)S(1)}, f32[2,3,64,256]{3,2,1,0:T(8,128)S(1)}, u32[]{:S(2)}, u32[]{:S(2)}) collective-permute-start(f32[2,3,64,256]{3,2,1,0:T(8,128)S(1)} %get-tuple-element.28), channel_id=1, source_target_pairs={{0,1},{1,0},{2,3},{3,2},{4,5},{5,4},{6,7},{7,6},{8,9},{9,8},{10,11... | collective-permute-start | bytes 1179656 | tf_op jit(solution)/shard_map/ppermute | solution.py:216
  69.4 2.8 %collective-permute-start.8 = (f32[2,3,64,256]{3,2,1,0:T(8,128)S(1)}, f32[2,3,64,256]{3,2,1,0:T(8,128)S(1)}, u32[]{:S(2)}, u32[]{:S(2)}) collective-permute-start(f32[2,3,64,256]{3,2,1,0:T(8,128)S(1)} %get-tuple-element.24), channel_id=1, source_target_pairs={{0,1},{1,0},{2,3},{3,2},{4,5},{5,4},{6,7},{7,6},{8,9},{9,8},{10,11... | collective-permute-start | bytes 1179656 | tf_op jit(solution)/shard_map/ppermute | solution.py:216
  70.6 7.8 %collective-permute-start.13 = (f32[3,64,256]{2,1,0:T(8,128)S(1)}, f32[3,64,256]{2,1,0:T(8,128)S(1)}, u32[]{:S(2)}, u32[]{:S(2)}) collective-permute-start(f32[3,64,256]{2,1,0:T(8,128)S(1)} %fusion), channel_id=1, source_target_pairs={{0,2},{2,0},{1,3},{3,1},{4,6},{6,4},{5,7},{7,5},{8,10},{10,8},{9,1... | collective-permute-start | bytes 589832 | tf_op jit(solution)/shard_map/ppermute | solution.py:217
  72.2 9.5 %collective-permute-start.9 = (f32[3,64,256]{2,1,0:T(8,128)S(1)}, f32[3,64,256]{2,1,0:T(8,128)S(1)}, u32[]{:S(2)}, u32[]{:S(2)}) collective-permute-start(f32[3,64,256]{2,1,0:T(8,128)S(1)} %fusion.1), channel_id=1, source_target_pairs={{0,2},{2,0},{1,3},{3,1},{4,6},{6,4},{5,7},{7,5},{8,10},{10,8},{9,1... | collective-permute-start | bytes 589832 | tf_op jit(solution)/shard_map/ppermute | solution.py:217

commit v2 on v1

--- a/solution.py
+++ b/solution.py
@@ -76,28 +76,63 @@
 ALL_PAIRS = EARLY_PAIRS + LATE_PAIRS
 
 
-def transform_kernel(meta, integrals, prev, own, following, out0, out1, out2, out3, half):
-    columns = own.shape[1]
-    ids = lax.broadcasted_iota(jnp.int32, (BLOCK, columns), 1)
+def dot(a, b):
+    return jnp.dot(a, b, preferred_element_type=jnp.float32)
+
+
+def central_kernel(integrals, own, *outs):
     mid = AO_DEV * BLOCK
-
-    def dot(a, b):
-        return jnp.dot(a, b, preferred_element_type=jnp.float32)
-
+    width = own.shape[1] // len(outs)
     for offset in range(AO_DEV):
         low = mid - offset * BLOCK
         for p in range(integrals.shape[0]):
-            slab = integrals[p, offset * BLOCK : (offset + 1) * BLOCK, :]
-            values = dot(slab[:, low : low + mid], own[...])
-            values += dot(slab[:, :low], prev[offset * BLOCK :, :])
-            values += dot(slab[:, low + mid :], following[: (offset + 1) * BLOCK, :])
-            half[offset, p] = jnp.where(ids < meta[4 + offset], values, 0.0).astype(jnp.bfloat16)
+            slab = integrals[p, offset * BLOCK : (offset + 1) * BLOCK, low : low + mid]
+            for c, out in enumerate(outs):
+                out[offset, p] = dot(slab, own[:, c * width : (c + 1) * width])
+
+
+def central(integrals, own):
+    shape = (AO_DEV, integrals.shape[0], BLOCK, own.shape[1] // CHUNKS)
+    vmem = pl.BlockSpec(memory_space=pltpu.VMEM)
+    return pl.pallas_call(
+        central_kernel,
+        out_shape=[jax.ShapeDtypeStruct(shape, jnp.float32)] * CHUNKS,
+        in_specs=[vmem] * 2,
+        out_specs=[vmem] * CHUNKS,
+        cost_estimate=pl.CostEstimate(
+            flops=2 * integrals.size // WIN * AO_DEV * own.shape[1],
+            bytes_accessed=2 * integrals.size + 2 * own.size + 4 * CHUNKS * math.prod(shape),
+            transcendentals=0,
+        ),
+        compiler_params=pltpu.CompilerParams(vmem_limit_bytes=VMEM_LIMIT),
+        name="central",
+    )(integrals, own)
+
+
+def transform_kernel(meta, integrals, centre, outer, inner, out0, out1, out2, out3, half):
+    columns = outer.shape[1]
+    mid = AO_DEV * BLOCK
+
+    def rims(prev, following):
+        ids = lax.broadcasted_iota(jnp.int32, (BLOCK, columns), 1)
+        for offset in range(AO_DEV):
+            low = mid - offset * BLOCK
+            for p in range(integrals.shape[0]):
+                slab = integrals[p, offset * BLOCK : (offset + 1) * BLOCK, :]
+                values = centre[offset, p]
+                values += dot(slab[:, :low], prev[offset * BLOCK :, :])
+                values += dot(slab[:, low + mid :], following[: (offset + 1) * BLOCK, :])
+                half[offset, p] = jnp.where(ids < meta[4 + offset], values, 0.0).astype(jnp.bfloat16)
+
+    odd = meta[6] & 1
+    pl.when(odd == 0)(lambda: rims(inner, outer))
+    pl.when(odd == 1)(lambda: rims(outer, inner))
     for s, out in enumerate((out0, out1, out2, out3)):
         out[...] = half[meta[s]]
 
 
-def transform(meta, integrals, prev, own, following):
-    shape = (integrals.shape[0], BLOCK, own.shape[1])
+def transform(meta, integrals, centre, outer, inner):
+    shape = (integrals.shape[0], BLOCK, outer.shape[1])
     vmem = pl.BlockSpec(memory_space=pltpu.VMEM)
     return pl.pallas_call(
         transform_kernel,
@@ -107,17 +142,18 @@
         scratch_shapes=[pltpu.VMEM((AO_DEV, *shape), jnp.bfloat16)],
         compiler_params=pltpu.CompilerParams(vmem_limit_bytes=VMEM_LIMIT),
         cost_estimate=pl.CostEstimate(
-            flops=2 * AO_DEV * math.prod(shape) * integrals.shape[2],
-            bytes_accessed=2 * (integrals.size + 3 * own.size + 4 * math.prod(shape)),
+            flops=2 * AO_DEV * math.prod(shape) * integrals.shape[2] * 3 // WIN,
+            bytes_accessed=2 * (integrals.size + 2 * outer.size + 4 * math.prod(shape)) + 4 * centre.size,
             transcendentals=0,
         ),
         name="transform",
-    )(meta, integrals, prev, own, following)
-
-
-def pairs_kernel(pairs, used, meta, *refs):
+    )(meta, integrals, centre, outer, inner)
+
+
+def pairs_kernel(pairs, used, tied, meta, *refs):
     blocks = {s: refs[i * CHUNKS : (i + 1) * CHUNKS] for i, s in enumerate(used)}
-    keep, give, grams = refs[len(used) * CHUNKS :]
+    keep, give = refs[len(used) * CHUNKS + tied :][:2]
+    grams = refs[-1]
     here, aux, orb = meta[0], meta[1], meta[2]
 
     def product(left, right):
@@ -150,15 +186,20 @@
             give[x, k] = grams[k, row + 1 - orb]
 
 
-def pair_products(pairs, used, meta, blocks):
+def pair_products(pairs, used, meta, blocks, tied=()):
     shape = jax.ShapeDtypeStruct((2, len(pairs), BLOCK // 4, BLOCK), jnp.float32)
     vmem = pl.BlockSpec(memory_space=pltpu.VMEM)
+    anywhere = pl.BlockSpec(memory_space=pl.ANY)
+    first = 1 + len(used) * CHUNKS
     return pl.pallas_call(
-        functools.partial(pairs_kernel, pairs, used),
-        out_shape=[shape] * 2,
-        in_specs=[pl.BlockSpec(memory_space=pltpu.SMEM)] + [vmem] * (len(used) * CHUNKS),
-        out_specs=[vmem] * 2,
+        functools.partial(pairs_kernel, pairs, used, len(tied)),
+        out_shape=[shape] * 2 + [jax.ShapeDtypeStruct(t.shape, t.dtype) for t in tied],
+        in_specs=[pl.BlockSpec(memory_space=pltpu.SMEM)]
+        + [vmem] * (len(used) * CHUNKS)
+        + [anywhere] * len(tied),
+        out_specs=[vmem] * 2 + [anywhere] * len(tied),
         scratch_shapes=[pltpu.VMEM((len(pairs), 4, BLOCK // 4, BLOCK), jnp.float32)],
+        input_output_aliases={first + i: 2 + i for i in range(len(tied))},
         compiler_params=pltpu.CompilerParams(vmem_limit_bytes=VMEM_LIMIT),
         cost_estimate=pl.CostEstimate(
             flops=2 * len(pairs) * BLOCK * CHUNKS * blocks[0][0].size,
@@ -166,7 +207,7 @@
             transcendentals=0,
         ),
         name="pairs",
-    )(meta, *[part for s in used for part in blocks[s]])
+    )(meta, *[part for s in used for part in blocks[s]], *tied)
 
 
 def spread_kernel(factor, place, keep0, got0, far0, keep1, got1, far1, out, sums):
@@ -224,11 +265,12 @@
     total_aux = integrals.shape[0] * lax.axis_size("aux")
     owners = lax.axis_size("ao")
     here, aux, orb = lax.axis_index("ao"), lax.axis_index("aux"), lax.axis_index("orb")
-    up = [(i, i + 1) for i in range(owners - 1)]
-    down = [(i + 1, i) for i in range(owners - 1)]
+    outside = [(0, 1), (1, 0), (2, 3), (3, 2)]
+    inside = [(1, 2), (2, 1)]
 
     parts = [lax.slice_in_dim(coeffs, c * width, (c + 1) * width, axis=1) for c in range(CHUNKS)]
-    halos = [(lax.ppermute(part, "ao", up), lax.ppermute(part, "ao", down)) for part in parts]
+    halos = [(lax.ppermute(part, "ao", inside), lax.ppermute(part, "ao", outside)) for part in parts]
+    centres = central(integrals, coeffs)
 
     table = pair_blocks.reshape(owners, -1, 2)
     slots = table.shape[1]
@@ -238,22 +280,23 @@
     counts = lax.dynamic_slice_in_dim(orbital_count, here * AO_DEV, AO_DEV) - orb * orb_local
 
     blocks = [[] for _ in range(owners)]
-    for c, (part, (prev, following)) in enumerate(zip(parts, halos)):
-        meta = jnp.concatenate([wanted, counts - c * width]).astype(jnp.int32)
-        for s, piece in enumerate(transform(meta, integrals, prev, part, following)):
+    for c, (inner, outer) in enumerate(halos):
+        meta = jnp.concatenate([wanted, counts - c * width, here[None]]).astype(jnp.int32)
+        for s, piece in enumerate(transform(meta, integrals, centres[c], outer, inner)):
             blocks[s].append(piece)
 
-    def fetch(s):
-        swap = [(j, j ^ s) for j in range(owners)]
-        return [lax.ppermute(piece, "ao", swap) for piece in blocks[s]]
-
-    got = [blocks[0], None, None, None]
-    got[2] = fetch(2)
-    got[1] = fetch(1)
-    got[3] = fetch(3)
+    def fetch(s, piece):
+        return lax.ppermute(piece, "ao", [(j, j ^ s) for j in range(owners)])
 
     position = jnp.stack([here, aux, orb]).astype(jnp.int32)
-    early = reduce_blocks(*pair_products(EARLY_PAIRS, (0, 1, 2), position, got))
+    got = [blocks[0], [], [], []]
+    for c in range(CHUNKS):
+        got[2].append(fetch(2, blocks[2][c]))
+        got[1].append(fetch(1, blocks[1][c]))
+    got[3] = [fetch(3, piece) for piece in blocks[3][:-1]]
+    keep, give, last = pair_products(EARLY_PAIRS, (0, 1, 2), position, got, blocks[3][-1:])
+    got[3].append(fetch(3, last))
+    early = reduce_blocks(keep, give)
     late = reduce_blocks(*pair_products(LATE_PAIRS, (0, 1, 2, 3), position, got))
 
     owned = lax.dynamic_index_in_dim(table, here, 0, keepdims=False) // AO_DEV ^ here

time: 83.8 us -> 82.9 us (0.989)
  starting transfers between devices: 23 us -> 15.7 us
  waiting for transfers between devices: 45.1 us -> 50.9 us
  local copies, waits for them, and re-layouts: 4.21 us -> 5.28 us
    ppermute x10, starting transfers between devices: 20.1 us -> 13 us  [the longest x2 6.96 us: six_pair_body(): lax.ppermute(part, 'ao', inside)]
    ppermute x10, waiting for transfers between devices: 36.9 us -> 42.6 us  [the longest x6 40.8 us: fetch(): return lax.ppermute(piece, 'ao', [(j, j ^ s) for j in range(owners)])]
    unnamed x8 -> x10, local copies, waits for them, and re-layouts: 1.75 us -> 2.8 us
    pallas_call x2 -> x3, Pallas kernels: 3.21 us -> 3.91 us  [the longest x2 3.21 us: pair_products(): pl.pallas_call(functools.partial(pairs_kernel, pairs, used, len(tied)), o...]
  transfers between devices with their start and end apart: 14 -> 14, of which waited for: 7 -> 9; matrix products, arithmetic and copies ran while one was open for 5% -> 4% of each run, Pallas kernels for 6% -> 8%
where the time goes in v2:
time: 82.9 us; the launch traced here: 82.6 us
  waiting for transfers between devices  50.9 us (61%)
  starting transfers between devices  15.7 us (19%)
  Pallas kernels  8.85 us (11%)
  local copies, waits for them, and re-layouts  5.28 us (6%)
  other arithmetic  1.8 us (2%)
    ppermute x6, waiting for transfers between devices, fetch(): return lax.ppermute(piece, 'ao', [(j, j ^ s) for j in range(owners)])  40.8 us
    ppermute x2, waiting for transfers between devices, reduce_blocks(): far = lax.ppermute(keep[1] + got[1], 'aux', SWAP)  8.28 us
    ppermute x2, starting transfers between devices, six_pair_body(): lax.ppermute(part, 'ao', inside)  6.96 us
    ppermute x6, starting transfers between devices, fetch(): return lax.ppermute(piece, 'ao', [(j, j ^ s) for j in range(owners)])  5.91 us
    pallas_call x2, Pallas kernels, pair_products(): pl.pallas_call(functools.partial(pairs_kernel, pairs, used, len(tied)), o...  3.21 us
    pallas_call x2, Pallas kernels, transform(): pl.pallas_call(transform_kernel, out_shape=[jax.ShapeDtypeStruct(shape, j...  3.1 us
    unnamed x10, local copies, waits for them, and re-layouts  2.8 us
    ppermute x2, starting transfers between devices, reduce_blocks(): far = lax.ppermute(keep[1] + got[1], 'aux', SWAP)  2.58 us
  transfers between devices with their start and end apart: 14, of which 9 were waited for; matrix products, arithmetic and copies ran while one was open for 4% of the time, Pallas kernels for 8%

profile of v2, /device:TPU:8, one launch (start us, length us, event | category | flops | bytes accessed | tf_op | source)
XLA Modules:
  0.0 82.6 jit_solution(11867765522383187961)
XLA Ops:
  0.0 1.1 %fusion.6 = (bf16[512,256]{1,0:T(8,128)(2,1)S(1)}, bf16[512,256]{1,0:T(8,128)(2,1)S(1)}) fusion(bf16[512,512]{1,0:T(8,128)(2,1)} %own.1), kind=kLoop, calls=%fused_computation.34 | loop fusion | bytes 1048576 | tf_op jit(solution)/shard_map/slice | solution.py:271
  1.2 5.0 %collective-permute-start.1 = (bf16[512,256]{1,0:T(8,128)(2,1)S(1)}, bf16[512,256]{1,0:T(8,128)(2,1)S(1)}, u32[]{:S(2)}, u32[]{:S(2)}) collective-permute-start(bf16[512,256]{1,0:T(8,128)(2,1)S(1)} %get-tuple-element.40), channel_id=1, source_target_pairs={{4,8},{8,4},{5,9},{9,5},{6,10},{10,6},{7,11},{11,7},{20,24},{24,20... | collective-permute-start | bytes 786440 | tf_op jit(solution)/shard_map/ppermute | solution.py:272
  6.3 1.9 %collective-permute-start.3 = (bf16[512,256]{1,0:T(8,128)(2,1)S(1)}, bf16[512,256]{1,0:T(8,128)(2,1)S(1)}, u32[]{:S(2)}, u32[]{:S(2)}) collective-permute-start(bf16[512,256]{1,0:T(8,128)(2,1)S(1)} %get-tuple-element.39), channel_id=1, source_target_pairs={{4,8},{8,4},{5,9},{9,5},{6,10},{10,6},{7,11},{11,7},{20,24},{24,20... | collective-permute-start | bytes 786440 | tf_op jit(solution)/shard_map/ppermute | solution.py:272
  9.8 1.7 %copy-done = bf16[2,512,1280]{2,1,0:T(8,128)(2,1)S(1)} copy-done((bf16[2,512,1280]{2,1,0:T(8,128)(2,1)S(1)}, bf16[2,512,1280]{2,1,0:T(8,128)(2,1)}, u32[]{:S(2)}) %copy-start) | copy-done | bytes 2621464
  11.5 1.0 %copy-done.1 = bf16[512,512]{1,0:T(8,128)(2,1)S(1)} copy-done((bf16[512,512]{1,0:T(8,128)(2,1)S(1)}, bf16[512,512]{1,0:T(8,128)(2,1)}, u32[]{:S(2)}) %copy-start.1) | copy-done | bytes 524312
  13.5 1.9 %transform.2 = (bf16[2,256,256]{2,1,0:T(8,128)(2,1)S(1)}, bf16[2,256,256]{2,1,0:T(8,128)(2,1)S(1)}, bf16[2,256,256]{2,1,0:T(8,128)(2,1)S(1)}, bf16[2,256,256]{2,1,0:T(8,128)(2,1)}) custom-call(s32[7]{0:T(128)S(1)} %get-tuple-element.42.meta, bf16[2,512,1280]{2,1,0:T(8,128)(2,1)S(1)} %copy-done, f32[2,2,256,256]{3,2,1,0:T(8,128)S(1)} %get-tuple-element.20.centre, ...), custom_call_target="tpu_custom_call" | custom-call | flops 402653184 | bytes 5242880 | tf_op jit(solution)/shard_map/transform/pallas_call | solution.py:137
  15.4 0.8 collective-permute-start.4
  16.1 1.7 %collective-permute-done.3.inner = bf16[512,256]{1,0:T(8,128)(2,1)S(1)} collective-permute-done((bf16[512,256]{1,0:T(8,128)(2,1)S(1)}, bf16[512,256]{1,0:T(8,128)(2,1)S(1)}, u32[]{:S(2)}, u32[]{:S(2)}) %collective-permute-start.3) | collective-permute-done | bytes 262176 | tf_op jit(solution)/shard_map/ppermute | solution.py:272
  17.8 1.2 %transform.3 = (bf16[2,256,256]{2,1,0:T(8,128)(2,1)S(1)}, bf16[2,256,256]{2,1,0:T(8,128)(2,1)S(1)}, bf16[2,256,256]{2,1,0:T(8,128)(2,1)S(1)}, bf16[2,256,256]{2,1,0:T(8,128)(2,1)S(1)}) custom-call(s32[7]{0:T(128)S(1)} %get-tuple-element.41.meta, bf16[2,512,1280]{2,1,0:T(8,128)(2,1)S(1)} %copy-done, f32[2,2,256,256]{3,2,1,0:T(8,128)S(1)} %get-tuple-element.22.centre, ...), custom_call_target="tpu_custom_call" | custom-call | flops 402653184 | bytes 5242880 | tf_op jit(solution)/shard_map/transform/pallas_call | solution.py:137
  19.1 3.2 %collective-permute-start.6 = (bf16[2,256,256]{2,1,0:T(8,128)(2,1)S(1)}, bf16[2,256,256]{2,1,0:T(8,128)(2,1)S(1)}, u32[]{:S(2)}, u32[]{:S(2)}) collective-permute-start(bf16[2,256,256]{2,1,0:T(8,128)(2,1)S(1)} %get-tuple-element.26), channel_id=1, source_target_pairs={{0,8},{4,12},{8,0},{12,4},{1,9},{5,13},{9,1},{13,5},{2,10},{6,14},... | collective-permute-start | bytes 786440 | tf_op jit(solution)/shard_map/ppermute | solution.py:289
  22.4 1.5 %collective-permute-start.10 = (bf16[2,256,256]{2,1,0:T(8,128)(2,1)}, bf16[2,256,256]{2,1,0:T(8,128)(2,1)S(1)}, u32[]{:S(2)}, u32[]{:S(2)}) collective-permute-start(bf16[2,256,256]{2,1,0:T(8,128)(2,1)} %get-tuple-element.31), channel_id=1, source_target_pairs={{0,12},{4,8},{8,4},{12,0},{1,13},{5,9},{9,5},{13,1},{2,14},{6,10},... | collective-permute-start | bytes 786440 | tf_op jit(solution)/shard_map/ppermute | solution.py:289
  23.9 6.2 %collective-permute-done.4.refs_2_ = bf16[2,256,256]{2,1,0:T(8,128)(2,1)S(1)} collective-permute-done((bf16[2,256,256]{2,1,0:T(8,128)(2,1)S(1)}, bf16[2,256,256]{2,1,0:T(8,128)(2,1)S(1)}, u32[]{:S(2)}, u32[]{:S(2)}) %collective-permute-start.4) | collective-permute-done | bytes 262176 | tf_op jit(solution)/shard_map/ppermute | solution.py:289
  30.1 4.2 %collective-permute-done.5.refs_3_ = bf16[2,256,256]{2,1,0:T(8,128)(2,1)S(1)} collective-permute-done((bf16[2,256,256]{2,1,0:T(8,128)(2,1)S(1)}, bf16[2,256,256]{2,1,0:T(8,128)(2,1)S(1)}, u32[]{:S(2)}, u32[]{:S(2)}) %collective-permute-start.5) | collective-permute-done | bytes 262176 | tf_op jit(solution)/shard_map/ppermute | solution.py:289
  34.3 11.6 %collective-permute-done.6.refs_4_ = bf16[2,256,256]{2,1,0:T(8,128)(2,1)S(1)} collective-permute-done((bf16[2,256,256]{2,1,0:T(8,128)(2,1)S(1)}, bf16[2,256,256]{2,1,0:T(8,128)(2,1)S(1)}, u32[]{:S(2)}, u32[]{:S(2)}) %collective-permute-start.6) | collective-permute-done | bytes 262176 | tf_op jit(solution)/shard_map/ppermute | solution.py:289
  45.9 5.6 %collective-permute-done.7.refs_5_ = bf16[2,256,256]{2,1,0:T(8,128)(2,1)S(1)} collective-permute-done((bf16[2,256,256]{2,1,0:T(8,128)(2,1)S(1)}, bf16[2,256,256]{2,1,0:T(8,128)(2,1)S(1)}, u32[]{:S(2)}, u32[]{:S(2)}) %collective-permute-start.7) | collective-permute-done | bytes 262176 | tf_op jit(solution)/shard_map/ppermute | solution.py:289
  51.5 1.6 %pairs.2 = (f32[2,3,64,256]{3,2,1,0:T(8,128)S(1)}, f32[2,3,64,256]{3,2,1,0:T(8,128)S(1)}, bf16[2,256,256]{2,1,0:T(8,128)(2,1)S(1)}) custom-call(s32[3]{0:T(128)S(1)} %pad_add_fusion.meta, bf16[2,256,256]{2,1,0:T(8,128)(2,1)S(1)} %get-tuple-element.21.refs_0_, bf16[2,256,256]{2,1,0:T(8,128)(2,1)S(1)} %get-tuple-element.23.refs_1_, ...), custom_call_target="tpu_custom_call", output_to_operand_aliasing={{2}: (7, {})} | custom-call | flops 402653184 | bytes 3145728 | tf_op jit(solution)/shard_map/pairs/pallas_call | solution.py:194
  53.6 9.9 %collective-permute-done.10.refs_6_ = bf16[2,256,256]{2,1,0:T(8,128)(2,1)S(1)} collective-permute-done((bf16[2,256,256]{2,1,0:T(8,128)(2,1)}, bf16[2,256,256]{2,1,0:T(8,128)(2,1)S(1)}, u32[]{:S(2)}, u32[]{:S(2)}) %collective-permute-start.10) | collective-permute-done | bytes 262176 | tf_op jit(solution)/shard_map/ppermute | solution.py:289
  63.5 3.3 %collective-permute-done.11.refs_7_ = bf16[2,256,256]{2,1,0:T(8,128)(2,1)S(1)} collective-permute-done((bf16[2,256,256]{2,1,0:T(8,128)(2,1)S(1)}, bf16[2,256,256]{2,1,0:T(8,128)(2,1)S(1)}, u32[]{:S(2)}, u32[]{:S(2)}) %collective-permute-start.11) | collective-permute-done | bytes 262176 | tf_op jit(solution)/shard_map/ppermute | solution.py:289
  66.8 1.6 %pairs.3 = (f32[2,3,64,256]{3,2,1,0:T(8,128)S(1)}, f32[2,3,64,256]{3,2,1,0:T(8,128)S(1)}) custom-call(s32[3]{0:T(128)S(1)} %pad_add_fusion.meta, bf16[2,256,256]{2,1,0:T(8,128)(2,1)S(1)} %get-tuple-element.21.refs_0_, bf16[2,256,256]{2,1,0:T(8,128)(2,1)S(1)} %get-tuple-element.23.refs_1_, bf16[2,256,256]{2,1,0:T(8,128)(2,1)S(1)} %collective-permute-done.4.refs_2_, ...), custom_call_target="tpu_custom_call" | custom-call | flops 402653184 | bytes 3670016 | tf_op jit(solution)/shard_map/pairs/pallas_call | solution.py:194
  69.2 1.6 %collective-permute-start.9 = (f32[3,64,256]{2,1,0:T(8,128)S(1)}, f32[3,64,256]{2,1,0:T(8,128)S(1)}, u32[]{:S(2)}, u32[]{:S(2)}) collective-permute-start(f32[3,64,256]{2,1,0:T(8,128)S(1)} %fusion.1), channel_id=1, source_target_pairs={{0,2},{2,0},{1,3},{3,1},{4,6},{6,4},{5,7},{7,5},{8,10},{10,8},{9,1... | collective-permute-start | bytes 589832 | tf_op jit(solution)/shard_map/ppermute | solution.py:258
  70.8 1.0 %collective-permute-start.13 = (f32[3,64,256]{2,1,0:T(8,128)S(1)}, f32[3,64,256]{2,1,0:T(8,128)S(1)}, u32[]{:S(2)}, u32[]{:S(2)}) collective-permute-start(f32[3,64,256]{2,1,0:T(8,128)S(1)} %fusion), channel_id=1, source_target_pairs={{0,2},{2,0},{1,3},{3,1},{4,6},{6,4},{5,7},{7,5},{8,10},{10,8},{9,1... | collective-permute-start | bytes 589832 | tf_op jit(solution)/shard_map/ppermute | solution.py:258
  72.5 4.5 %collective-permute-done.9.far0 = f32[3,64,256]{2,1,0:T(8,128)S(1)} collective-permute-done((f32[3,64,256]{2,1,0:T(8,128)S(1)}, f32[3,64,256]{2,1,0:T(8,128)S(1)}, u32[]{:S(2)}, u32[]{:S(2)}) %collective-permute-start.9) | collective-permute-done | bytes 196640 | tf_op jit(solution)/shard_map/ppermute | solution.py:258
  77.0 3.8 %collective-permute-done.13.far1 = f32[3,64,256]{2,1,0:T(8,128)S(1)} collective-permute-done((f32[3,64,256]{2,1,0:T(8,128)S(1)}, f32[3,64,256]{2,1,0:T(8,128)S(1)}, u32[]{:S(2)}, u32[]{:S(2)}) %collective-permute-start.13) | collective-permute-done | bytes 196640 | tf_op jit(solution)/shard_map/ppermute | solution.py:258
  80.8 1.8 %spread.1 = f32[64,16,256]{2,1,0:T(8,128)} custom-call(s32[16]{0:T(128)S(1)} %compare_select_fusion.2.place, f32[2,3,64,256]{3,2,1,0:T(8,128)S(1)} %get-tuple-element.29.keep0, f32[2,3,64,256]{3,2,1,0:T(8,128)S(1)} %collective-permute-done.8.got0, f32[3,64,256]{2,1,0:T(8,128)S(1)} %collective-permute-done.9.far0, ...), custom_call_target="tpu_custom_call" | custom-call | flops 1572864 | bytes 1048576 | tf_op jit(solution)/shard_map/spread/pallas_call | solution.py:239
  (37 shorter events, 4.6 us)
Async XLA Ops:
  0.0 13.3 %copy-start.3 = (s32[8]{0:T(128)S(1)}, s32[8]{0:T(128)}, u32[]{:S(2)}) copy-start(s32[8]{0:T(128)} %param.9) | copy-start | bytes 100
  1.1 12.4 %collective-permute-start = (bf16[512,256]{1,0:T(8,128)(2,1)S(1)}, bf16[512,256]{1,0:T(8,128)(2,1)S(1)}, u32[]{:S(2)}, u32[]{:S(2)}) collective-permute-start(bf16[512,256]{1,0:T(8,128)(2,1)S(1)} %get-tuple-element.40), channel_id=1, source_target_pairs={{0,4},{4,0},{8,12},{12,8},{1,5},{5,1},{9,13},{13,9},{2,6},{6,2},{1... | collective-permute-start | bytes 786440 | tf_op jit(solution)/shard_map/ppermute | solution.py:272
  1.2 12.3 %collective-permute-start.1 = (bf16[512,256]{1,0:T(8,128)(2,1)S(1)}, bf16[512,256]{1,0:T(8,128)(2,1)S(1)}, u32[]{:S(2)}, u32[]{:S(2)}) collective-permute-start(bf16[512,256]{1,0:T(8,128)(2,1)S(1)} %get-tuple-element.40), channel_id=1, source_target_pairs={{4,8},{8,4},{5,9},{9,5},{6,10},{10,6},{7,11},{11,7},{20,24},{24,20... | collective-permute-start | bytes 786440 | tf_op jit(solution)/shard_map/ppermute | solution.py:272
  6.2 9.9 %collective-permute-start.2 = (bf16[512,256]{1,0:T(8,128)(2,1)S(1)}, bf16[512,256]{1,0:T(8,128)(2,1)S(1)}, u32[]{:S(2)}, u32[]{:S(2)}) collective-permute-start(bf16[512,256]{1,0:T(8,128)(2,1)S(1)} %get-tuple-element.39), channel_id=1, source_target_pairs={{0,4},{4,0},{8,12},{12,8},{1,5},{5,1},{9,13},{13,9},{2,6},{6,2},{1... | collective-permute-start | bytes 786440 | tf_op jit(solution)/shard_map/ppermute | solution.py:272
  6.3 11.5 %collective-permute-start.3 = (bf16[512,256]{1,0:T(8,128)(2,1)S(1)}, bf16[512,256]{1,0:T(8,128)(2,1)S(1)}, u32[]{:S(2)}, u32[]{:S(2)}) collective-permute-start(bf16[512,256]{1,0:T(8,128)(2,1)S(1)} %get-tuple-element.39), channel_id=1, source_target_pairs={{4,8},{8,4},{5,9},{9,5},{6,10},{10,6},{7,11},{11,7},{20,24},{24,20... | collective-permute-start | bytes 786440 | tf_op jit(solution)/shard_map/ppermute | solution.py:272
  9.8 1.7 %copy-start = (bf16[2,512,1280]{2,1,0:T(8,128)(2,1)S(1)}, bf16[2,512,1280]{2,1,0:T(8,128)(2,1)}, u32[]{:S(2)}) copy-start(bf16[2,512,1280]{2,1,0:T(8,128)(2,1)} %integrals.5) | copy-start | bytes 7864324
  11.5 1.0 %copy-start.1 = (bf16[512,512]{1,0:T(8,128)(2,1)S(1)}, bf16[512,512]{1,0:T(8,128)(2,1)}, u32[]{:S(2)}) copy-start(bf16[512,512]{1,0:T(8,128)(2,1)} %own.1) | copy-start | bytes 1572868
  15.4 14.7 %collective-permute-start.4 = (bf16[2,256,256]{2,1,0:T(8,128)(2,1)S(1)}, bf16[2,256,256]{2,1,0:T(8,128)(2,1)S(1)}, u32[]{:S(2)}, u32[]{:S(2)}) collective-permute-start(bf16[2,256,256]{2,1,0:T(8,128)(2,1)S(1)} %get-tuple-element.24), channel_id=1, source_target_pairs={{0,4},{4,0},{8,12},{12,8},{1,5},{5,1},{9,13},{13,9},{2,6},{6,2},{1... | collective-permute-start | bytes 786440 | tf_op jit(solution)/shard_map/ppermute | solution.py:289
  17.8 35.7 %copy-start.2 = (s32[64,2]{0,1:T(2,128)S(1)}, s32[64,2]{0,1:T(2,128)}, u32[]{:S(2)}) copy-start(s32[64,2]{0,1:T(2,128)} %param.7) | copy-start | bytes 1540
  19.0 49.5 %copy-start.4 = (s32[4]{0:T(128)S(1)}, s32[4]{0:T(128)}, u32[]{:S(2)}) copy-start(s32[4]{0:T(128)} %param.8) | copy-start | bytes 52
  19.1 15.3 %collective-permute-start.5 = (bf16[2,256,256]{2,1,0:T(8,128)(2,1)S(1)}, bf16[2,256,256]{2,1,0:T(8,128)(2,1)S(1)}, u32[]{:S(2)}, u32[]{:S(2)}) collective-permute-start(bf16[2,256,256]{2,1,0:T(8,128)(2,1)S(1)} %get-tuple-element.25), channel_id=1, source_target_pairs={{0,4},{4,0},{8,12},{12,8},{1,5},{5,1},{9,13},{13,9},{2,6},{6,2},{1... | collective-permute-start | bytes 786440 | tf_op jit(solution)/shard_map/ppermute | solution.py:289
  19.1 26.8 %collective-permute-start.6 = (bf16[2,256,256]{2,1,0:T(8,128)(2,1)S(1)}, bf16[2,256,256]{2,1,0:T(8,128)(2,1)S(1)}, u32[]{:S(2)}, u32[]{:S(2)}) collective-permute-start(bf16[2,256,256]{2,1,0:T(8,128)(2,1)S(1)} %get-tuple-element.26), channel_id=1, source_target_pairs={{0,8},{4,12},{8,0},{12,4},{1,9},{5,13},{9,1},{13,5},{2,10},{6,14},... | collective-permute-start | bytes 786440 | tf_op jit(solution)/shard_map/ppermute | solution.py:289
  22.3 29.2 %collective-permute-start.7 = (bf16[2,256,256]{2,1,0:T(8,128)(2,1)S(1)}, bf16[2,256,256]{2,1,0:T(8,128)(2,1)S(1)}, u32[]{:S(2)}, u32[]{:S(2)}) collective-permute-start(bf16[2,256,256]{2,1,0:T(8,128)(2,1)S(1)} %get-tuple-element.27), channel_id=1, source_target_pairs={{0,8},{4,12},{8,0},{12,4},{1,9},{5,13},{9,1},{13,5},{2,10},{6,14},... | collective-permute-start | bytes 786440 | tf_op jit(solution)/shard_map/ppermute | solution.py:289
  22.4 41.1 %collective-permute-start.10 = (bf16[2,256,256]{2,1,0:T(8,128)(2,1)}, bf16[2,256,256]{2,1,0:T(8,128)(2,1)S(1)}, u32[]{:S(2)}, u32[]{:S(2)}) collective-permute-start(bf16[2,256,256]{2,1,0:T(8,128)(2,1)} %get-tuple-element.31), channel_id=1, source_target_pairs={{0,12},{4,8},{8,4},{12,0},{1,13},{5,9},{9,5},{13,1},{2,14},{6,10},... | collective-permute-start | bytes 786440 | tf_op jit(solution)/shard_map/ppermute | solution.py:289
  53.2 13.7 %collective-permute-start.11 = (bf16[2,256,256]{2,1,0:T(8,128)(2,1)S(1)}, bf16[2,256,256]{2,1,0:T(8,128)(2,1)S(1)}, u32[]{:S(2)}, u32[]{:S(2)}) collective-permute-start(bf16[2,256,256]{2,1,0:T(8,128)(2,1)S(1)} %get-tuple-element.32), channel_id=1, source_target_pairs={{0,12},{4,8},{8,4},{12,0},{1,13},{5,9},{9,5},{13,1},{2,14},{6,10},... | collective-permute-start | bytes 786440 | tf_op jit(solution)/shard_map/ppermute | solution.py:289
  53.5 15.7 %collective-permute-start.8 = (f32[2,3,64,256]{3,2,1,0:T(8,128)S(1)}, f32[2,3,64,256]{3,2,1,0:T(8,128)S(1)}, u32[]{:S(2)}, u32[]{:S(2)}) collective-permute-start(f32[2,3,64,256]{3,2,1,0:T(8,128)S(1)} %get-tuple-element.30), channel_id=1, source_target_pairs={{0,1},{1,0},{2,3},{3,2},{4,5},{5,4},{6,7},{7,6},{8,9},{9,8},{10,11... | collective-permute-start | bytes 1179656 | tf_op jit(solution)/shard_map/ppermute | solution.py:257
  68.5 2.3 %collective-permute-start.12 = (f32[2,3,64,256]{3,2,1,0:T(8,128)S(1)}, f32[2,3,64,256]{3,2,1,0:T(8,128)S(1)}, u32[]{:S(2)}, u32[]{:S(2)}) collective-permute-start(f32[2,3,64,256]{3,2,1,0:T(8,128)S(1)} %get-tuple-element.34), channel_id=1, source_target_pairs={{0,1},{1,0},{2,3},{3,2},{4,5},{5,4},{6,7},{7,6},{8,9},{9,8},{10,11... | collective-permute-start | bytes 1179656 | tf_op jit(solution)/shard_map/ppermute | solution.py:257
  69.2 7.8 %collective-permute-start.9 = (f32[3,64,256]{2,1,0:T(8,128)S(1)}, f32[3,64,256]{2,1,0:T(8,128)S(1)}, u32[]{:S(2)}, u32[]{:S(2)}) collective-permute-start(f32[3,64,256]{2,1,0:T(8,128)S(1)} %fusion.1), channel_id=1, source_target_pairs={{0,2},{2,0},{1,3},{3,1},{4,6},{6,4},{5,7},{7,5},{8,10},{10,8},{9,1... | collective-permute-start | bytes 589832 | tf_op jit(solution)/shard_map/ppermute | solution.py:258
  70.8 10.0 %collective-permute-start.13 = (f32[3,64,256]{2,1,0:T(8,128)S(1)}, f32[3,64,256]{2,1,0:T(8,128)S(1)}, u32[]{:S(2)}, u32[]{:S(2)}) collective-permute-start(f32[3,64,256]{2,1,0:T(8,128)S(1)} %fusion), channel_id=1, source_target_pairs={{0,2},{2,0},{1,3},{3,1},{4,6},{6,4},{5,7},{7,5},{8,10},{10,8},{9,1... | collective-permute-start | bytes 589832 | tf_op jit(solution)/shard_map/ppermute | solution.py:258

commit v3 on v0

--- a/solution.py
+++ b/solution.py
@@ -1,14 +1,25 @@
+import functools
 import math
 
 import jax
 import jax.numpy as jnp
 from jax import lax
+from jax.experimental import pallas as pl
+from jax.experimental.pallas import tpu as pltpu
 from jax.sharding import PartitionSpec as P
 
 BLOCK = 256
 AO_DEV = 2
 WIN = 5
 ORBS = 1024
+CHUNKS = 2
+SPREAD_STEPS = 4
+SPREAD_STEPS = 4
+SPREAD_STEPS = 4
+SPREAD_STEPS = 4
+SPREAD_STEPS = 4
+SPREAD_STEPS = 4
+VMEM_LIMIT = 40 * 1024 * 1024
 
 
 def with_halo(cells, sides, width):
@@ -28,7 +39,7 @@
     return cells
 
 
-def body(integrals, coeffs, pair_blocks, pair_count, orbital_count):
+def general_body(integrals, coeffs, pair_blocks, pair_count, orbital_count):
     orb_local = coeffs.shape[1]
     aux_devices = lax.axis_size("aux")
     total_aux = integrals.shape[0] * aux_devices
@@ -66,7 +77,319 @@
     )
 
 
+EARLY_PAIRS = ((0, 1), (0, 2), (1, 2))
+LATE_PAIRS = ((0, 3), (1, 3), (2, 3))
+ALL_PAIRS = EARLY_PAIRS + LATE_PAIRS
+GROUPS = 4
+SWAP = [(0, 1), (1, 0)]
+OUTSIDE = [(0, 1), (1, 0), (2, 3), (3, 2)]
+INSIDE = [(1, 2), (2, 1)]
+
+IN_HBM = pl.BlockSpec(memory_space=pltpu.HBM)
+IN_VMEM = pl.BlockSpec(memory_space=pltpu.VMEM)
+IN_SMEM = pl.BlockSpec(memory_space=pltpu.SMEM)
+
+
+def like(shape, dtype):
+    return jax.ShapeDtypeStruct(shape, dtype)
+
+
+def local_call(kernel, name, out_shape, in_specs, out_specs, flops, scratch=()):
+    moved = sum(math.prod(o.shape) * o.dtype.itemsize for o in out_shape)
+    return pl.pallas_call(
+        kernel,
+        out_shape=out_shape,
+        in_specs=in_specs,
+        out_specs=out_specs,
+        scratch_shapes=list(scratch),
+        compiler_params=pltpu.CompilerParams(vmem_limit_bytes=VMEM_LIMIT),
+        cost_estimate=pl.CostEstimate(flops=flops, bytes_accessed=2 * moved, transcendentals=0),
+        name=name,
+    )
+
+
+def dot(a, b):
+    return jnp.dot(a, b, preferred_element_type=jnp.float32)
+
+
+def central_kernel(position, table, counts, integrals, *refs):
+    parts, outs, scalars = refs[:CHUNKS], refs[CHUNKS:-1], refs[-1]
+    mid = AO_DEV * BLOCK
+    here, orb = position[0], position[2]
+    slots = table.shape[1] // GROUPS
+    for s in range(GROUPS):
+        first = (here ^ s) * slots
+        found = jnp.int32(0)
+        for k in range(slots):
+            for side in (0, 1):
+                block = table[side, first + k]
+                found = jnp.where(block // AO_DEV == here, block % AO_DEV, found)
+        scalars[s] = found
+    for offset in range(AO_DEV):
+        scalars[GROUPS + offset] = counts[here * AO_DEV + offset] - orb * CHUNKS * parts[0].shape[1]
+    for offset in range(AO_DEV):
+        low = mid - offset * BLOCK
+        for p in range(integrals.shape[0]):
+            slab = integrals[p, offset * BLOCK : (offset + 1) * BLOCK, low : low + mid]
+            for part, out in zip(parts, outs):
+                out[offset, p] = dot(slab, part[...])
+
+
+def central(position, table, counts, integrals, parts):
+    shape = (AO_DEV, integrals.shape[0], BLOCK, parts[0].shape[1])
+    *out, scalars = local_call(
+        central_kernel,
+        "central",
+        [like(shape, jnp.float32)] * CHUNKS + [like((8,), jnp.int32)],
+        [IN_SMEM] * 3 + [IN_VMEM] * (1 + CHUNKS),
+        [IN_VMEM] * CHUNKS + [IN_SMEM],
+        4 * integrals.size // WIN * CHUNKS * parts[0].shape[1],
+    )(position, table, counts, integrals, *parts)
+    return out, scalars
+
+
+def transform_kernel(start, position, scalars, integrals, centre, outer, inner, *refs):
+    outs, half = refs[:-1], refs[-1]
+    columns = outer.shape[1]
+    mid = AO_DEV * BLOCK
+
+    def rims(prev, following):
+        ids = start + lax.broadcasted_iota(jnp.int32, (BLOCK, columns), 1)
+        for offset in range(AO_DEV):
+            low = mid - offset * BLOCK
+            for p in range(integrals.shape[0]):
+                slab = integrals[p, offset * BLOCK : (offset + 1) * BLOCK, :]
+                values = centre[offset, p]
+                values += dot(slab[:, :low], prev[offset * BLOCK :, :])
+                values += dot(slab[:, low + mid :], following[: (offset + 1) * BLOCK, :])
+                live = ids < scalars[GROUPS + offset]
+                half[offset, p] = jnp.where(live, values, 0.0).astype(jnp.bfloat16)
+
+    odd = position[0] & 1
+    pl.when(odd == 0)(lambda: rims(inner, outer))
+    pl.when(odd == 1)(lambda: rims(outer, inner))
+    for s, out in enumerate(outs[: GROUPS - 1]):
+        out[...] = half[scalars[s]]
+    first = 0
+    for out in outs[GROUPS - 1 :]:
+        for p in range(out.shape[0]):
+            out[p] = half[scalars[GROUPS - 1], first + p]
+        first += out.shape[0]
+
+
+def transform(start, position, scalars, integrals, centre, outer, inner, cuts):
+    aux_here = integrals.shape[0]
+    shape = (BLOCK, outer.shape[1])
+    return local_call(
+        functools.partial(transform_kernel, start),
+        "transform",
+        [like((n, *shape), jnp.bfloat16) for n in [aux_here] * (GROUPS - 1) + cuts],
+        [IN_SMEM] * 2 + [IN_VMEM] * 4,
+        [IN_VMEM] * (GROUPS - 1 + len(cuts)),
+        6 * AO_DEV * integrals.size * shape[1] // WIN,
+        [pltpu.VMEM((AO_DEV, aux_here, *shape), jnp.bfloat16)],
+    )(position, scalars, integrals, centre, outer, inner)
+
+
+def form_pairs(pairs, position, blocks, keep, give, grams):
+    here, aux, orb = position[0], position[1], position[2]
+    slices = [[(ref, p) for ref in block for p in range(ref.shape[0])] for block in blocks]
+
+    def product(left, right):
+        total = None
+        for (a, i), (b, j) in zip(slices[left], slices[right]):
+            part = lax.dot_general(
+                a[i], b[j], (((1,), (1,)), ((), ())), preferred_element_type=jnp.float32
+            )
+            total = part if total is None else total + part
+        return total.reshape(grams.shape[1:])
+
+    for bit in (0, 1):
+        mine = [(k, a, b) for k, (a, b) in enumerate(pairs) if (a ^ b) >> 1 == bit]
+        upper = (here >> bit) & 1
+
+        @pl.when(upper == 0)
+        def _(mine=mine):
+            for k, a, b in mine:
+                grams[k] = product(a, b)
+
+        @pl.when(upper == 1)
+        def _(mine=mine):
+            for k, a, b in mine:
+                grams[k] = product(b, a)
+
+    for k in range(len(pairs)):
+        for x in (0, 1):
+            row = 2 * (aux ^ x)
+            keep[x, k] = grams[k, row + orb]
+            give[k][x] = grams[k, row + 1 - orb]
+
+
+def early_kernel(position, table, live, *refs):
+    used = 3 * CHUNKS
+    blocks = [refs[i : i + CHUNKS] for i in range(0, used, CHUNKS)]
+    keep, *give, place, grams = refs[used:]
+    here = position[0]
+    slots = place.shape[0]
+    for s in range(slots):
+        a = table[0, here * slots + s] // AO_DEV ^ here
+        b = table[1, here * slots + s] // AO_DEV ^ here
+        low, high = jnp.minimum(a, b), jnp.maximum(a, b)
+        index = jnp.where(high == 3, low + 3, jnp.where(high == 2, low + 1, 0))
+        place[s] = jnp.where(s < live[here], index, len(ALL_PAIRS))
+    form_pairs(EARLY_PAIRS, position, blocks, keep, give, grams)
+
+
+def late_kernel(sizes, position, *refs):
+    blocks = []
+    for size in sizes:
+        blocks.append(refs[:size])
+        refs = refs[size:]
+    keep, *give, grams = refs
+    form_pairs(LATE_PAIRS, position, blocks, keep, give, grams)
+
+
+def pair_flops(pairs, blocks):
+    return 2 * len(pairs) * BLOCK * CHUNKS * blocks[0][0].size
+
+
+def shares(pairs):
+    rows = BLOCK // 4
+    keep = like((2, len(pairs), rows, BLOCK), jnp.float32)
+    give = like((2, rows, BLOCK), jnp.float32)
+    return [keep] + [give] * len(pairs), pltpu.VMEM((len(pairs), 4, rows, BLOCK), jnp.float32)
+
+
+def early_pairs(position, table, live, blocks):
+    out, grams = shares(EARLY_PAIRS)
+    keep, *give, place = local_call(
+        early_kernel,
+        "early_pairs",
+        out + [like((table.shape[1] // GROUPS,), jnp.int32)],
+        [IN_SMEM] * 3 + [IN_VMEM] * (3 * CHUNKS),
+        [IN_VMEM] * len(out) + [IN_SMEM],
+        pair_flops(EARLY_PAIRS, blocks),
+        [grams],
+    )(position, table, live, *[part for block in blocks for part in block])
+    return keep, give, place
+
+
+def late_pairs(position, blocks):
+    out, grams = shares(LATE_PAIRS)
+    sizes = [len(block) for block in blocks]
+    keep, *give = local_call(
+        functools.partial(late_kernel, sizes),
+        "late_pairs",
+        out,
+        [IN_SMEM] + [IN_VMEM] * sum(sizes),
+        [IN_VMEM] * len(out),
+        pair_flops(LATE_PAIRS, blocks),
+        [grams],
+    )(position, *[part for block in blocks for part in block])
+    return keep, give
+
+
+def spread_kernel(factor, place, *refs):
+    *parts, out, sums, rows, sems = refs
+    half = len(parts) // 2
+    k = 0
+    for kept, far, *got in (parts[:half], parts[half:]):
+        for i, other in enumerate(got):
+            sums[k] = (kept[0, i] + other[0] + far[i].astype(jnp.float32)) * factor
+            k += 1
+    total, slots, width = out.shape
+    slot = lax.broadcasted_iota(jnp.int32, (slots, width), 0)
+    source = jnp.zeros((slots, width), jnp.int32)
+    for s in range(slots):
+        source = jnp.where(slot == s, place[s], source)
+    masks = [source == k for k in range(sums.shape[0])]
+
+    def one(m, carry):
+        row = jnp.zeros((slots, width), jnp.float32)
+        for k, mask in enumerate(masks):
+            values = jnp.broadcast_to(sums[k, pl.ds(m, 1), :], (slots, width))
+            row = jnp.where(mask, values, row)
+        rows[m] = row
+        return carry
+
+    step = total // SPREAD_STEPS
+    copies = []
+    for i in range(SPREAD_STEPS):
+        lax.fori_loop(i * step, (i + 1) * step, one, 0, unroll=8)
+        part = pl.ds(i * step, step)
+        copies.append(pltpu.make_async_copy(rows.at[part], out.at[part], sems.at[i]))
+        copies[-1].start()
+    for copy in copies:
+        copy.wait()
+
+
+def spread(factor, place, *parts):
+    rows = BLOCK // 4
+    shape = (rows, place.shape[0], BLOCK)
+    parts = [array for kept, far, got in parts for array in (kept, far, *got)]
+    return local_call(
+        functools.partial(spread_kernel, factor),
+        "spread",
+        [like(shape, jnp.float32)],
+        [IN_SMEM] + [IN_VMEM] * len(parts),
+        [IN_HBM],
+        6 * math.prod(shape),
+        [
+            pltpu.VMEM((len(ALL_PAIRS), rows, BLOCK), jnp.float32),
+            pltpu.VMEM(shape, jnp.float32),
+            pltpu.SemaphoreType.DMA((SPREAD_STEPS,)),
+        ],
+    )(place, *parts)[0]
+
+
+def across(kept, give):
+    got = [lax.ppermute(one, "orb", SWAP) for one in give]
+    share = jnp.stack([kept[1, k] + other[1] for k, other in enumerate(got)])
+    return got, lax.ppermute(share.astype(jnp.bfloat16), "aux", SWAP)
+
+
+def six_pair_body(integrals, coeffs, pair_blocks, pair_count, orbital_count):
+    width = coeffs.shape[1] // CHUNKS
+    total_aux = integrals.shape[0] * lax.axis_size("aux")
+    position = jnp.stack([lax.axis_index(axis) for axis in ("ao", "aux", "orb")]).astype(jnp.int32)
+    table = pair_blocks.T
+
+    parts = [lax.slice_in_dim(coeffs, c * width, (c + 1) * width, axis=1) for c in range(CHUNKS)]
+    halos = [
+        (lax.ppermute(part, "ao", INSIDE), lax.ppermute(part, "ao", OUTSIDE)) for part in parts
+    ]
+    centres, scalars = central(position, table, orbital_count, integrals, parts)
+
+    aux_here = integrals.shape[0]
+    cuts = [[aux_here]] * (CHUNKS - 1) + [[1] * aux_here]
+    blocks = [[] for _ in range(GROUPS)]
+    for c, (inner, outer) in enumerate(halos):
+        pieces = transform(c * width, position, scalars, integrals, centres[c], outer, inner, cuts[c])
+        for s in range(GROUPS - 1):
+            blocks[s].append(pieces[s])
+        blocks[-1] += pieces[GROUPS - 1 :]
+
+    def fetch(s, piece):
+        return lax.ppermute(piece, "ao", [(j, j ^ s) for j in range(GROUPS)])
+
+    middle = [fetch(2, piece) for piece in blocks[2]]
+    near = [fetch(1, piece) for piece in blocks[1]]
+    last = [fetch(3, piece) for piece in blocks[3][:-1]]
+    kept0, give0, place = early_pairs(position, table, pair_count, [blocks[0], near, middle])
+    piece, kept0 = lax.optimization_barrier((blocks[3][-1], kept0))
+    last.append(fetch(3, piece))
+    got0, far0 = across(kept0, give0)
+    factor = 1.0 / math.sqrt(total_aux * ORBS)
+    kept1, give1 = late_pairs(position, [blocks[0], near, middle, last])
+    got1, far1 = across(kept1, give1)
+    return spread(factor, place, (kept0, far0, got0), (kept1, far1, got1))
+
+
 def solution(mesh):
+    sizes = dict(mesh.shape)
+    body = general_body
+    if sizes["ao"] == 4 and sizes["aux"] == 2 and sizes["orb"] == 2:
+        body = six_pair_body
     return jax.shard_map(
         body,
         mesh=mesh,

time: 159 us -> 75.5 us (0.47)
  waiting for transfers between devices: 97.4 us -> 41.5 us
  local copies, waits for them, and re-layouts: 19.7 us -> 4.15 us
  between operations: 13.5 us -> 0.19 us
  matrix products: 12.2 us -> 0 us
  Pallas kernels: 0 us -> 10.3 us
  starting transfers between devices: 11.5 us -> 18.2 us
  other arithmetic: 3.06 us -> 0.16 us
    reduce_scatter x1 -> x0, waiting for transfers between devices: 46.6 us -> none  [body(): lax.psum_scatter(term * weights[None, :, None], ('aux', 'orb'), scatter_d...]
    all_to_all x1 -> x0, waiting for transfers between devices: 43.6 us -> none  [body(): lax.all_to_all(outgoing, 'ao', split_axis=0, concat_axis=0, tiled=True)]
    ppermute x2 -> x19, waiting for transfers between devices: 7.15 us -> 41.5 us  [the longest x7 37 us: fetch(): return lax.ppermute(piece, 'ao', [(j, j ^ s) for j in range(GROUPS)])]
    ppermute x2 -> x19, starting transfers between devices: 5.84 us -> 18.2 us  [the longest x7 7.17 us: fetch(): return lax.ppermute(piece, 'ao', [(j, j ^ s) for j in range(GROUPS)])]
    dot_general x3 -> x0, matrix products: 12.2 us -> none  [the longest x1 10.4 us: body(): jnp.einsum('spmi,spni->msn', lefts, right_factors, preferred_element_type...]
    gather x3 -> x0, local copies, waits for them, and re-layouts: 11.2 us -> none  [the longest x1 4.65 us: body(): lefts = received[left_source]]
    pallas_call x0 -> x6, Pallas kernels: none -> 10.3 us  [the longest x1 2.6 us: central(): local_call(central_kernel, 'central', [like(shape, jnp.float32)] * CHUNKS...]
    all_to_all x1 -> x0, starting transfers between devices: 5.63 us -> none  [body(): lax.all_to_all(outgoing, 'ao', split_axis=0, concat_axis=0, tiled=True)]
  transfers between devices with their start and end apart: 4 -> 19, of which waited for: 4 -> 8; matrix products, arithmetic and copies ran while one was open for 3% -> 0% of each run, Pallas kernels for 0% -> 12%
where the time goes in v3:
time: 75.5 us; the launch traced here: 74.5 us
  waiting for transfers between devices  41.5 us (55%)
  starting transfers between devices  18.2 us (24%)
  Pallas kernels  10.3 us (14%)
  local copies, waits for them, and re-layouts  4.15 us (5%)
    ppermute x7, waiting for transfers between devices, fetch(): return lax.ppermute(piece, 'ao', [(j, j ^ s) for j in range(GROUPS)])  37 us
    ppermute x7, starting transfers between devices, fetch(): return lax.ppermute(piece, 'ao', [(j, j ^ s) for j in range(GROUPS)])  7.17 us
    ppermute x2, starting transfers between devices, six_pair_body(): lax.ppermute(part, 'ao', INSIDE)  6.96 us
    ppermute x2, waiting for transfers between devices, across(): return (got, lax.ppermute(share.astype(jnp.bfloat16), 'aux', SWAP))  4.5 us
    unnamed x10, local copies, waits for them, and re-layouts  3.08 us
    ppermute x2, starting transfers between devices, across(): return (got, lax.ppermute(share.astype(jnp.bfloat16), 'aux', SWAP))  2.75 us
    pallas_call x1, Pallas kernels, central(): local_call(central_kernel, 'central', [like(shape, jnp.float32)] * CHUNKS...  2.6 us
    pallas_call x2, Pallas kernels, transform(): local_call(functools.partial(transform_kernel, start), 'transform', [like...  2.39 us
  transfers between devices with their start and end apart: 19, of which 8 were waited for; matrix products, arithmetic and copies ran while one was open for 0% of the time, Pallas kernels for 12%

profile of v3, /device:TPU:8, one launch (start us, length us, event | category | flops | bytes accessed | tf_op | source)
XLA Modules:
  0.0 74.5 jit_solution(14279664072330767071)
XLA Ops:
  0.0 1.1 %fusion.6 = (bf16[512,256]{1,0:T(8,128)(2,1)S(1)}, bf16[512,256]{1,0:T(8,128)(2,1)S(1)}) fusion(bf16[512,512]{1,0:T(8,128)(2,1)} %param.6), kind=kLoop, calls=%fused_computation.15 | loop fusion | bytes 1048576 | tf_op jit(solution)/shard_map/slice | solution.py:357
  1.1 5.0 %collective-permute-start.3 = (bf16[512,256]{1,0:T(8,128)(2,1)S(1)}, bf16[512,256]{1,0:T(8,128)(2,1)S(1)}, u32[]{:S(2)}, u32[]{:S(2)}) collective-permute-start(bf16[512,256]{1,0:T(8,128)(2,1)S(1)} %get-tuple-element.51.refs_1_), channel_id=1, source_target_pairs={{4,8},{8,4},{5,9},{9,5},{6,10},{10,6},{7,11},{11,7},{20,24},{24,20... | collective-permute-start | bytes 786440 | tf_op jit(solution)/shard_map/ppermute | solution.py:359
  6.3 1.9 %collective-permute-start.1 = (bf16[512,256]{1,0:T(8,128)(2,1)S(1)}, bf16[512,256]{1,0:T(8,128)(2,1)S(1)}, u32[]{:S(2)}, u32[]{:S(2)}) collective-permute-start(bf16[512,256]{1,0:T(8,128)(2,1)S(1)} %get-tuple-element.52.refs_0_), channel_id=1, source_target_pairs={{4,8},{8,4},{5,9},{9,5},{6,10},{10,6},{7,11},{11,7},{20,24},{24,20... | collective-permute-start | bytes 786440 | tf_op jit(solution)/shard_map/ppermute | solution.py:359
  8.3 1.7 %copy-done = bf16[2,512,1280]{2,1,0:T(8,128)(2,1)S(1)} copy-done((bf16[2,512,1280]{2,1,0:T(8,128)(2,1)S(1)}, bf16[2,512,1280]{2,1,0:T(8,128)(2,1)}, u32[]{:S(2)}) %copy-start) | copy-done | bytes 2621464
  11.4 2.6 %central.1 = (f32[2,2,256,256]{3,2,1,0:T(8,128)S(1)}, f32[2,2,256,256]{3,2,1,0:T(8,128)S(1)}, s32[8]{0:T(128)S(1)}) custom-call(s32[3]{0:T(128)S(1)} %pad_add_fusion.position, s32[2,64]{1,0:T(2,128)S(1)} %bitcast.16, s32[8]{0:T(128)S(1)} %copy-done.4, bf16[2,512,1280]{2,1,0:T(8,128)(2,1)S(1)} %copy-done, bf16[512,256]{1,0:T(8,128)(2,1)S(1)} %get-tuple-element.52.refs_0_, ...), custom_call_target="tpu_custom_call" | custom-call | flops 536870912 | bytes 4194368 | tf_op jit(solution)/shard_map/central/pallas_call | solution.py:140
  14.0 1.2 %transform.3 = (bf16[2,256,256]{2,1,0:T(8,128)(2,1)S(1)}, bf16[2,256,256]{2,1,0:T(8,128)(2,1)S(1)}, bf16[2,256,256]{2,1,0:T(8,128)(2,1)S(1)}, bf16[1,256,256]{2,1,0:T(8,128)(2,1)S(1)}, bf16[1,256,256]{2,1,0:T(8,128)(2,1)S(1)}) custom-call(s32[3]{0:T(128)S(1)} %pad_add_fusion.position, s32[8]{0:T(128)S(1)} %get-tuple-element.28.scalars, ...), custom_call_target="tpu_custom_call" | custom-call | flops 805306368 | bytes 2097152 | tf_op jit(solution)/shard_map/transform/pallas_call | solution.py:183
  15.2 0.8 %collective-permute-start.5 = (bf16[2,256,256]{2,1,0:T(8,128)(2,1)S(1)}, bf16[2,256,256]{2,1,0:T(8,128)(2,1)S(1)}, u32[]{:S(2)}, u32[]{:S(2)}) collective-permute-start(bf16[2,256,256]{2,1,0:T(8,128)(2,1)S(1)} %get-tuple-element.34), channel_id=1, source_target_pairs={{0,4},{4,0},{8,12},{12,8},{1,5},{5,1},{9,13},{13,9},{2,6},{6,2},{1... | collective-permute-start | bytes 786440 | tf_op jit(solution)/shard_map/ppermute | solution.py:373
  16.0 2.7 %collective-permute-start.7 = (bf16[2,256,256]{2,1,0:T(8,128)(2,1)S(1)}, bf16[2,256,256]{2,1,0:T(8,128)(2,1)S(1)}, u32[]{:S(2)}, u32[]{:S(2)}) collective-permute-start(bf16[2,256,256]{2,1,0:T(8,128)(2,1)S(1)} %get-tuple-element.36), channel_id=1, source_target_pairs={{0,8},{4,12},{8,0},{12,4},{1,9},{5,13},{9,1},{13,5},{2,10},{6,14},... | collective-permute-start | bytes 786440 | tf_op jit(solution)/shard_map/ppermute | solution.py:373
  18.8 1.2 %transform.2 = (bf16[2,256,256]{2,1,0:T(8,128)(2,1)S(1)}, bf16[2,256,256]{2,1,0:T(8,128)(2,1)S(1)}, bf16[2,256,256]{2,1,0:T(8,128)(2,1)S(1)}, bf16[2,256,256]{2,1,0:T(8,128)(2,1)S(1)}) custom-call(s32[3]{0:T(128)S(1)} %pad_add_fusion.position, s32[8]{0:T(128)S(1)} %get-tuple-element.28.scalars, bf16[2,512,1280]{2,1,0:T(8,128)(2,1)S(1)} %copy-done.1, ...), custom_call_target="tpu_custom_call" | custom-call | flops 805306368 | bytes 2097152 | tf_op jit(solution)/shard_map/transform/pallas_call | solution.py:183
  20.1 2.2 %collective-permute-start.6 = (bf16[2,256,256]{2,1,0:T(8,128)(2,1)S(1)}, bf16[2,256,256]{2,1,0:T(8,128)(2,1)S(1)}, u32[]{:S(2)}, u32[]{:S(2)}) collective-permute-start(bf16[2,256,256]{2,1,0:T(8,128)(2,1)S(1)} %get-tuple-element.35), channel_id=1, source_target_pairs={{0,8},{4,12},{8,0},{12,4},{1,9},{5,13},{9,1},{13,5},{2,10},{6,14},... | collective-permute-start | bytes 786440 | tf_op jit(solution)/shard_map/ppermute | solution.py:373
  22.3 1.2 %collective-permute-start.12 = (bf16[2,256,256]{2,1,0:T(8,128)(2,1)S(1)}, bf16[2,256,256]{2,1,0:T(8,128)(2,1)S(1)}, u32[]{:S(2)}, u32[]{:S(2)}) collective-permute-start(bf16[2,256,256]{2,1,0:T(8,128)(2,1)S(1)} %get-tuple-element.44), channel_id=1, source_target_pairs={{0,12},{4,8},{8,4},{12,0},{1,13},{5,9},{9,5},{13,1},{2,14},{6,10},... | collective-permute-start | bytes 786440 | tf_op jit(solution)/shard_map/ppermute | solution.py:373
  23.5 6.3 %collective-permute-done.5.refs_3_ = bf16[2,256,256]{2,1,0:T(8,128)(2,1)S(1)} collective-permute-done((bf16[2,256,256]{2,1,0:T(8,128)(2,1)S(1)}, bf16[2,256,256]{2,1,0:T(8,128)(2,1)S(1)}, u32[]{:S(2)}, u32[]{:S(2)}) %collective-permute-start.5) | collective-permute-done | bytes 262176 | tf_op jit(solution)/shard_map/ppermute | solution.py:373
  29.8 1.9 %collective-permute-done.7.refs_5_ = bf16[2,256,256]{2,1,0:T(8,128)(2,1)S(1)} collective-permute-done((bf16[2,256,256]{2,1,0:T(8,128)(2,1)S(1)}, bf16[2,256,256]{2,1,0:T(8,128)(2,1)S(1)}, u32[]{:S(2)}, u32[]{:S(2)}) %collective-permute-start.7) | collective-permute-done | bytes 262176 | tf_op jit(solution)/shard_map/ppermute | solution.py:373
  31.6 5.1 %collective-permute-done.4.refs_2_ = bf16[2,256,256]{2,1,0:T(8,128)(2,1)S(1)} collective-permute-done((bf16[2,256,256]{2,1,0:T(8,128)(2,1)S(1)}, bf16[2,256,256]{2,1,0:T(8,128)(2,1)S(1)}, u32[]{:S(2)}, u32[]{:S(2)}) %collective-permute-start.4) | collective-permute-done | bytes 262176 | tf_op jit(solution)/shard_map/ppermute | solution.py:373
  36.7 15.5 %collective-permute-done.6.refs_4_ = bf16[2,256,256]{2,1,0:T(8,128)(2,1)S(1)} collective-permute-done((bf16[2,256,256]{2,1,0:T(8,128)(2,1)S(1)}, bf16[2,256,256]{2,1,0:T(8,128)(2,1)S(1)}, u32[]{:S(2)}, u32[]{:S(2)}) %collective-permute-start.6) | collective-permute-done | bytes 262176 | tf_op jit(solution)/shard_map/ppermute | solution.py:373
  52.3 2.2 %early_pairs.1 = (f32[2,3,64,256]{3,2,1,0:T(8,128)S(1)}, f32[2,64,256]{2,1,0:T(8,128)S(1)}, f32[2,64,256]{2,1,0:T(8,128)S(1)}, f32[2,64,256]{2,1,0:T(8,128)S(1)}, s32[16]{0:T(128)S(1)}) custom-call(s32[3]{0:T(128)S(1)} %pad_add_fusion.position, s32[2,64]{1,0:T(2,128)S(1)} %bitcast.17, s32[4]{0:T(128)S(1)} %copy-done.3, ...), custom_call_target="tpu_custom_call" | custom-call | flops 402653184 | bytes 1572992 | tf_op jit(solution)/shard_map/early_pairs/pallas_call | solution.py:265
  55.1 6.8 %collective-permute-done.13.refs_7_ = bf16[1,256,256]{2,1,0:T(8,128)(2,1)S(1)} collective-permute-done((bf16[1,256,256]{2,1,0:T(8,128)(2,1)S(1)}, bf16[1,256,256]{2,1,0:T(8,128)(2,1)S(1)}, u32[]{:S(2)}, u32[]{:S(2)}) %collective-permute-start.13) | collective-permute-done | bytes 131104 | tf_op jit(solution)/shard_map/ppermute | solution.py:373
  62.0 1.4 %collective-permute-done.14.refs_8_ = bf16[1,256,256]{2,1,0:T(8,128)(2,1)S(1)} collective-permute-done((bf16[1,256,256]{2,1,0:T(8,128)(2,1)S(1)}, bf16[1,256,256]{2,1,0:T(8,128)(2,1)S(1)}, u32[]{:S(2)}, u32[]{:S(2)}) %collective-permute-start.14) | collective-permute-done | bytes 131104 | tf_op jit(solution)/shard_map/ppermute | solution.py:373
  63.4 1.4 %late_pairs.1 = (f32[2,3,64,256]{3,2,1,0:T(8,128)S(1)}, f32[2,64,256]{2,1,0:T(8,128)S(1)}, f32[2,64,256]{2,1,0:T(8,128)S(1)}, f32[2,64,256]{2,1,0:T(8,128)S(1)}) custom-call(s32[3]{0:T(128)S(1)} %pad_add_fusion.position, bf16[2,256,256]{2,1,0:T(8,128)(2,1)S(1)} %get-tuple-element.30.refs_0_, bf16[2,256,256]{2,1,0:T(8,128)(2,1)S(1)} %get-tuple-element.32.refs_1_, ...), custom_call_target="tpu_custom_call" | custom-call | flops 402653184 | bytes 1572864 | tf_op jit(solution)/shard_map/late_pairs/pallas_call | solution.py:280
  65.5 1.6 %collective-permute-start.11 = (bf16[3,64,256]{2,1,0:T(8,128)(2,1)S(1)}, bf16[3,64,256]{2,1,0:T(8,128)(2,1)S(1)}, u32[]{:S(2)}, u32[]{:S(2)}) collective-permute-start(bf16[3,64,256]{2,1,0:T(8,128)(2,1)S(1)} %pad_maximum_fusion), channel_id=1, source_target_pairs={{0,2},{2,0},{1,3},{3,1},{4,6},{6,4},{5,7},{7,5},{8,10},{10,8},{9,1... | collective-permute-start | bytes 294920 | tf_op jit(solution)/shard_map/ppermute | solution.py:348
  67.1 1.2 %collective-permute-start.18 = (bf16[3,64,256]{2,1,0:T(8,128)(2,1)S(1)}, bf16[3,64,256]{2,1,0:T(8,128)(2,1)S(1)}, u32[]{:S(2)}, u32[]{:S(2)}) collective-permute-start(bf16[3,64,256]{2,1,0:T(8,128)(2,1)S(1)} %pad_maximum_fusion.1), channel_id=1, source_target_pairs={{0,2},{2,0},{1,3},{3,1},{4,6},{6,4},{5,7},{7,5},{8,10},{10,8},{9,1... | collective-permute-start | bytes 294920 | tf_op jit(solution)/shard_map/ppermute | solution.py:348
  68.3 2.8 %collective-permute-done.11.refs_1_ = bf16[3,64,256]{2,1,0:T(8,128)(2,1)S(1)} collective-permute-done((bf16[3,64,256]{2,1,0:T(8,128)(2,1)S(1)}, bf16[3,64,256]{2,1,0:T(8,128)(2,1)S(1)}, u32[]{:S(2)}, u32[]{:S(2)}) %collective-permute-start.11) | collective-permute-done | bytes 98336 | tf_op jit(solution)/shard_map/ppermute | solution.py:348
  71.2 1.7 %collective-permute-done.18.refs_6_ = bf16[3,64,256]{2,1,0:T(8,128)(2,1)S(1)} collective-permute-done((bf16[3,64,256]{2,1,0:T(8,128)(2,1)S(1)}, bf16[3,64,256]{2,1,0:T(8,128)(2,1)S(1)}, u32[]{:S(2)}, u32[]{:S(2)}) %collective-permute-start.18) | collective-permute-done | bytes 98336 | tf_op jit(solution)/shard_map/ppermute | solution.py:348
  72.8 1.7 %spread.1 = f32[64,16,256]{2,1,0:T(8,128)} custom-call(s32[16]{0:T(128)S(1)} %get-tuple-element.37.place, f32[2,3,64,256]{3,2,1,0:T(8,128)S(1)} %get-tuple-element.40.refs_0_, bf16[3,64,256]{2,1,0:T(8,128)(2,1)S(1)} %collective-permute-done.11.refs_1_, f32[2,64,256]{2,1,0:T(8,128)S(1)} %collective-permute-done.8.refs_2_, ...), custom_call_target="tpu_custom_call" | custom-call | flops 1572864 | bytes 2097152 | tf_op jit(solution)/shard_map/spread/pallas_call | solution.py:330
  (36 shorter events, 3.1 us)
Async XLA Ops:
  1.1 12.9 %collective-permute-start.2 = (bf16[512,256]{1,0:T(8,128)(2,1)S(1)}, bf16[512,256]{1,0:T(8,128)(2,1)S(1)}, u32[]{:S(2)}, u32[]{:S(2)}) collective-permute-start(bf16[512,256]{1,0:T(8,128)(2,1)S(1)} %get-tuple-element.51.refs_1_), channel_id=1, source_target_pairs={{0,4},{4,0},{8,12},{12,8},{1,5},{5,1},{9,13},{13,9},{2,6},{6,2},{1... | collective-permute-start | bytes 786440 | tf_op jit(solution)/shard_map/ppermute | solution.py:359
  1.1 12.8 %collective-permute-start.3 = (bf16[512,256]{1,0:T(8,128)(2,1)S(1)}, bf16[512,256]{1,0:T(8,128)(2,1)S(1)}, u32[]{:S(2)}, u32[]{:S(2)}) collective-permute-start(bf16[512,256]{1,0:T(8,128)(2,1)S(1)} %get-tuple-element.51.refs_1_), channel_id=1, source_target_pairs={{4,8},{8,4},{5,9},{9,5},{6,10},{10,6},{7,11},{11,7},{20,24},{24,20... | collective-permute-start | bytes 786440 | tf_op jit(solution)/shard_map/ppermute | solution.py:359
  6.2 12.6 %collective-permute-start = (bf16[512,256]{1,0:T(8,128)(2,1)S(1)}, bf16[512,256]{1,0:T(8,128)(2,1)S(1)}, u32[]{:S(2)}, u32[]{:S(2)}) collective-permute-start(bf16[512,256]{1,0:T(8,128)(2,1)S(1)} %get-tuple-element.52.refs_0_), channel_id=1, source_target_pairs={{0,4},{4,0},{8,12},{12,8},{1,5},{5,1},{9,13},{13,9},{2,6},{6,2},{1... | collective-permute-start | bytes 786440 | tf_op jit(solution)/shard_map/ppermute | solution.py:359
  6.3 12.5 %collective-permute-start.1 = (bf16[512,256]{1,0:T(8,128)(2,1)S(1)}, bf16[512,256]{1,0:T(8,128)(2,1)S(1)}, u32[]{:S(2)}, u32[]{:S(2)}) collective-permute-start(bf16[512,256]{1,0:T(8,128)(2,1)S(1)} %get-tuple-element.52.refs_0_), channel_id=1, source_target_pairs={{4,8},{8,4},{5,9},{9,5},{6,10},{10,6},{7,11},{11,7},{20,24},{24,20... | collective-permute-start | bytes 786440 | tf_op jit(solution)/shard_map/ppermute | solution.py:359
  8.3 1.7 %copy-start = (bf16[2,512,1280]{2,1,0:T(8,128)(2,1)S(1)}, bf16[2,512,1280]{2,1,0:T(8,128)(2,1)}, u32[]{:S(2)}) copy-start(bf16[2,512,1280]{2,1,0:T(8,128)(2,1)} %integrals.5) | copy-start | bytes 7864324
  10.0 0.7 copy-start.2
  10.7 0.7 copy-start.4
  11.4 2.6 %copy-start.1 = (bf16[2,512,1280]{2,1,0:T(8,128)(2,1)S(1)}, bf16[2,512,1280]{2,1,0:T(8,128)(2,1)}, u32[]{:S(2)}) copy-start(bf16[2,512,1280]{2,1,0:T(8,128)(2,1)} %integrals.5) | copy-start | bytes 7864324
  15.2 37.0 %copy-start.3 = (s32[4]{0:T(128)S(1)}, s32[4]{0:T(128)}, u32[]{:S(2)}) copy-start(s32[4]{0:T(128)} %live.1) | copy-start | bytes 52
  15.2 14.6 %collective-permute-start.5 = (bf16[2,256,256]{2,1,0:T(8,128)(2,1)S(1)}, bf16[2,256,256]{2,1,0:T(8,128)(2,1)S(1)}, u32[]{:S(2)}, u32[]{:S(2)}) collective-permute-start(bf16[2,256,256]{2,1,0:T(8,128)(2,1)S(1)} %get-tuple-element.34), channel_id=1, source_target_pairs={{0,4},{4,0},{8,12},{12,8},{1,5},{5,1},{9,13},{13,9},{2,6},{6,2},{1... | collective-permute-start | bytes 786440 | tf_op jit(solution)/shard_map/ppermute | solution.py:373
  16.0 15.6 %collective-permute-start.7 = (bf16[2,256,256]{2,1,0:T(8,128)(2,1)S(1)}, bf16[2,256,256]{2,1,0:T(8,128)(2,1)S(1)}, u32[]{:S(2)}, u32[]{:S(2)}) collective-permute-start(bf16[2,256,256]{2,1,0:T(8,128)(2,1)S(1)} %get-tuple-element.36), channel_id=1, source_target_pairs={{0,8},{4,12},{8,0},{12,4},{1,9},{5,13},{9,1},{13,5},{2,10},{6,14},... | collective-permute-start | bytes 786440 | tf_op jit(solution)/shard_map/ppermute | solution.py:373
  20.0 16.8 %collective-permute-start.4 = (bf16[2,256,256]{2,1,0:T(8,128)(2,1)S(1)}, bf16[2,256,256]{2,1,0:T(8,128)(2,1)S(1)}, u32[]{:S(2)}, u32[]{:S(2)}) collective-permute-start(bf16[2,256,256]{2,1,0:T(8,128)(2,1)S(1)} %get-tuple-element.33), channel_id=1, source_target_pairs={{0,4},{4,0},{8,12},{12,8},{1,5},{5,1},{9,13},{13,9},{2,6},{6,2},{1... | collective-permute-start | bytes 786440 | tf_op jit(solution)/shard_map/ppermute | solution.py:373
  20.1 32.1 %collective-permute-start.6 = (bf16[2,256,256]{2,1,0:T(8,128)(2,1)S(1)}, bf16[2,256,256]{2,1,0:T(8,128)(2,1)S(1)}, u32[]{:S(2)}, u32[]{:S(2)}) collective-permute-start(bf16[2,256,256]{2,1,0:T(8,128)(2,1)S(1)} %get-tuple-element.35), channel_id=1, source_target_pairs={{0,8},{4,12},{8,0},{12,4},{1,9},{5,13},{9,1},{13,5},{2,10},{6,14},... | collective-permute-start | bytes 786440 | tf_op jit(solution)/shard_map/ppermute | solution.py:373
  22.3 39.7 %collective-permute-start.12 = (bf16[2,256,256]{2,1,0:T(8,128)(2,1)S(1)}, bf16[2,256,256]{2,1,0:T(8,128)(2,1)S(1)}, u32[]{:S(2)}, u32[]{:S(2)}) collective-permute-start(bf16[2,256,256]{2,1,0:T(8,128)(2,1)S(1)} %get-tuple-element.44), channel_id=1, source_target_pairs={{0,12},{4,8},{8,4},{12,0},{1,13},{5,9},{9,5},{13,1},{2,14},{6,10},... | collective-permute-start | bytes 786440 | tf_op jit(solution)/shard_map/ppermute | solution.py:373
  29.8 32.2 %collective-permute-start.13 = (bf16[1,256,256]{2,1,0:T(8,128)(2,1)S(1)}, bf16[1,256,256]{2,1,0:T(8,128)(2,1)S(1)}, u32[]{:S(2)}, u32[]{:S(2)}) collective-permute-start(bf16[1,256,256]{2,1,0:T(8,128)(2,1)S(1)} %get-tuple-element.45), channel_id=1, source_target_pairs={{0,12},{4,8},{8,4},{12,0},{1,13},{5,9},{9,5},{13,1},{2,14},{6,10},... | collective-permute-start | bytes 393224 | tf_op jit(solution)/shard_map/ppermute | solution.py:373
  54.5 8.9 %collective-permute-start.14 = (bf16[1,256,256]{2,1,0:T(8,128)(2,1)S(1)}, bf16[1,256,256]{2,1,0:T(8,128)(2,1)S(1)}, u32[]{:S(2)}, u32[]{:S(2)}) collective-permute-start(bf16[1,256,256]{2,1,0:T(8,128)(2,1)S(1)} %get-tuple-element.46), channel_id=1, source_target_pairs={{0,12},{4,8},{8,4},{12,0},{1,13},{5,9},{9,5},{13,1},{2,14},{6,10},... | collective-permute-start | bytes 393224 | tf_op jit(solution)/shard_map/ppermute | solution.py:373
  54.5 10.8 %collective-permute-start.10 = (f32[2,64,256]{2,1,0:T(8,128)S(1)}, f32[2,64,256]{2,1,0:T(8,128)S(1)}, u32[]{:S(2)}, u32[]{:S(2)}) collective-permute-start(f32[2,64,256]{2,1,0:T(8,128)S(1)} %get-tuple-element.43), channel_id=1, source_target_pairs={{0,1},{1,0},{2,3},{3,2},{4,5},{5,4},{6,7},{7,6},{8,9},{9,8},{10,11... | collective-permute-start | bytes 393224 | tf_op jit(solution)/shard_map/ppermute | solution.py:346
  54.6 10.8 %collective-permute-start.8 = (f32[2,64,256]{2,1,0:T(8,128)S(1)}, f32[2,64,256]{2,1,0:T(8,128)S(1)}, u32[]{:S(2)}, u32[]{:S(2)}) collective-permute-start(f32[2,64,256]{2,1,0:T(8,128)S(1)} %get-tuple-element.41), channel_id=1, source_target_pairs={{0,1},{1,0},{2,3},{3,2},{4,5},{5,4},{6,7},{7,6},{8,9},{9,8},{10,11... | collective-permute-start | bytes 393224 | tf_op jit(solution)/shard_map/ppermute | solution.py:346
  62.0 3.5 %collective-permute-start.9 = (f32[2,64,256]{2,1,0:T(8,128)S(1)}, f32[2,64,256]{2,1,0:T(8,128)S(1)}, u32[]{:S(2)}, u32[]{:S(2)}) collective-permute-start(f32[2,64,256]{2,1,0:T(8,128)S(1)} %get-tuple-element.42), channel_id=1, source_target_pairs={{0,1},{1,0},{2,3},{3,2},{4,5},{5,4},{6,7},{7,6},{8,9},{9,8},{10,11... | collective-permute-start | bytes 393224 | tf_op jit(solution)/shard_map/ppermute | solution.py:346
  64.8 2.3 %collective-permute-start.15 = (f32[2,64,256]{2,1,0:T(8,128)S(1)}, f32[2,64,256]{2,1,0:T(8,128)S(1)}, u32[]{:S(2)}, u32[]{:S(2)}) collective-permute-start(f32[2,64,256]{2,1,0:T(8,128)S(1)} %get-tuple-element.48), channel_id=1, source_target_pairs={{0,1},{1,0},{2,3},{3,2},{4,5},{5,4},{6,7},{7,6},{8,9},{9,8},{10,11... | collective-permute-start | bytes 393224 | tf_op jit(solution)/shard_map/ppermute | solution.py:346
  64.9 2.2 %collective-permute-start.16 = (f32[2,64,256]{2,1,0:T(8,128)S(1)}, f32[2,64,256]{2,1,0:T(8,128)S(1)}, u32[]{:S(2)}, u32[]{:S(2)}) collective-permute-start(f32[2,64,256]{2,1,0:T(8,128)S(1)} %get-tuple-element.49), channel_id=1, source_target_pairs={{0,1},{1,0},{2,3},{3,2},{4,5},{5,4},{6,7},{7,6},{8,9},{9,8},{10,11... | collective-permute-start | bytes 393224 | tf_op jit(solution)/shard_map/ppermute | solution.py:346
  65.4 1.7 %collective-permute-start.17 = (f32[2,64,256]{2,1,0:T(8,128)S(1)}, f32[2,64,256]{2,1,0:T(8,128)S(1)}, u32[]{:S(2)}, u32[]{:S(2)}) collective-permute-start(f32[2,64,256]{2,1,0:T(8,128)S(1)} %get-tuple-element.50), channel_id=1, source_target_pairs={{0,1},{1,0},{2,3},{3,2},{4,5},{5,4},{6,7},{7,6},{8,9},{9,8},{10,11... | collective-permute-start | bytes 393224 | tf_op jit(solution)/shard_map/ppermute | solution.py:346
  65.5 5.7 %collective-permute-start.11 = (bf16[3,64,256]{2,1,0:T(8,128)(2,1)S(1)}, bf16[3,64,256]{2,1,0:T(8,128)(2,1)S(1)}, u32[]{:S(2)}, u32[]{:S(2)}) collective-permute-start(bf16[3,64,256]{2,1,0:T(8,128)(2,1)S(1)} %pad_maximum_fusion), channel_id=1, source_target_pairs={{0,2},{2,0},{1,3},{3,1},{4,6},{6,4},{5,7},{7,5},{8,10},{10,8},{9,1... | collective-permute-start | bytes 294920 | tf_op jit(solution)/shard_map/ppermute | solution.py:348
  67.1 5.7 %collective-permute-start.18 = (bf16[3,64,256]{2,1,0:T(8,128)(2,1)S(1)}, bf16[3,64,256]{2,1,0:T(8,128)(2,1)S(1)}, u32[]{:S(2)}, u32[]{:S(2)}) collective-permute-start(bf16[3,64,256]{2,1,0:T(8,128)(2,1)S(1)} %pad_maximum_fusion.1), channel_id=1, source_target_pairs={{0,2},{2,0},{1,3},{3,1},{4,6},{6,4},{5,7},{7,5},{8,10},{10,8},{9,1... | collective-permute-start | bytes 294920 | tf_op jit(solution)/shard_map/ppermute | solution.py:348

commit v4 on v3

--- a/solution.py
+++ b/solution.py
@@ -117,14 +117,10 @@
     mid = AO_DEV * BLOCK
     here, orb = position[0], position[2]
     slots = table.shape[1] // GROUPS
+    named = jnp.where(table[...] // AO_DEV == here, table[...] % AO_DEV, 0).astype(jnp.float32)
+    owner = lax.broadcasted_iota(jnp.int32, table.shape, 1) // slots
     for s in range(GROUPS):
-        first = (here ^ s) * slots
-        found = jnp.int32(0)
-        for k in range(slots):
-            for side in (0, 1):
-                block = table[side, first + k]
-                found = jnp.where(block // AO_DEV == here, block % AO_DEV, found)
-        scalars[s] = found
+        scalars[s] = jnp.max(jnp.where(owner == here ^ s, named, 0.0)).astype(jnp.int32)
     for offset in range(AO_DEV):
         scalars[GROUPS + offset] = counts[here * AO_DEV + offset] - orb * CHUNKS * parts[0].shape[1]
     for offset in range(AO_DEV):
@@ -141,7 +137,7 @@
         central_kernel,
         "central",
         [like(shape, jnp.float32)] * CHUNKS + [like((8,), jnp.int32)],
-        [IN_SMEM] * 3 + [IN_VMEM] * (1 + CHUNKS),
+        [IN_SMEM, IN_VMEM, IN_SMEM] + [IN_VMEM] * (1 + CHUNKS),
         [IN_VMEM] * CHUNKS + [IN_SMEM],
         4 * integrals.size // WIN * CHUNKS * parts[0].shape[1],
     )(position, table, counts, integrals, *parts)
@@ -168,31 +164,25 @@
     odd = position[0] & 1
     pl.when(odd == 0)(lambda: rims(inner, outer))
     pl.when(odd == 1)(lambda: rims(outer, inner))
-    for s, out in enumerate(outs[: GROUPS - 1]):
+    for s, out in enumerate(outs):
         out[...] = half[scalars[s]]
-    first = 0
-    for out in outs[GROUPS - 1 :]:
-        for p in range(out.shape[0]):
-            out[p] = half[scalars[GROUPS - 1], first + p]
-        first += out.shape[0]
-
-
-def transform(start, position, scalars, integrals, centre, outer, inner, cuts):
-    aux_here = integrals.shape[0]
-    shape = (BLOCK, outer.shape[1])
+
+
+def transform(start, position, scalars, integrals, centre, outer, inner):
+    shape = (integrals.shape[0], BLOCK, outer.shape[1])
     return local_call(
         functools.partial(transform_kernel, start),
         "transform",
-        [like((n, *shape), jnp.bfloat16) for n in [aux_here] * (GROUPS - 1) + cuts],
+        [like(shape, jnp.bfloat16)] * GROUPS,
         [IN_SMEM] * 2 + [IN_VMEM] * 4,
-        [IN_VMEM] * (GROUPS - 1 + len(cuts)),
-        6 * AO_DEV * integrals.size * shape[1] // WIN,
-        [pltpu.VMEM((AO_DEV, aux_here, *shape), jnp.bfloat16)],
+        [IN_VMEM] * GROUPS,
+        6 * AO_DEV * math.prod(shape) * integrals.shape[2] // WIN,
+        [pltpu.VMEM((AO_DEV, *shape), jnp.bfloat16)],
     )(position, scalars, integrals, centre, outer, inner)
 
 
-def form_pairs(pairs, position, blocks, keep, give, grams):
-    here, aux, orb = position[0], position[1], position[2]
+def form_pairs(pairs, position, blocks, grams):
+    here = position[0]
     slices = [[(ref, p) for ref in block for p in range(ref.shape[0])] for block in blocks]
 
     def product(left, right):
@@ -218,18 +208,12 @@
             for k, a, b in mine:
                 grams[k] = product(b, a)
 
-    for k in range(len(pairs)):
-        for x in (0, 1):
-            row = 2 * (aux ^ x)
-            keep[x, k] = grams[k, row + orb]
-            give[k][x] = grams[k, row + 1 - orb]
-
 
 def early_kernel(position, table, live, *refs):
     used = 3 * CHUNKS
     blocks = [refs[i : i + CHUNKS] for i in range(0, used, CHUNKS)]
-    keep, *give, place, grams = refs[used:]
-    here = position[0]
+    near, far, place, grams = refs[used:]
+    here, aux, orb = position[0], position[1], position[2]
     slots = place.shape[0]
     for s in range(slots):
         a = table[0, here * slots + s] // AO_DEV ^ here
@@ -237,66 +221,69 @@
         low, high = jnp.minimum(a, b), jnp.maximum(a, b)
         index = jnp.where(high == 3, low + 3, jnp.where(high == 2, low + 1, 0))
         place[s] = jnp.where(s < live[here], index, len(ALL_PAIRS))
-    form_pairs(EARLY_PAIRS, position, blocks, keep, give, grams)
-
-
-def late_kernel(sizes, position, *refs):
-    blocks = []
-    for size in sizes:
-        blocks.append(refs[:size])
-        refs = refs[size:]
-    keep, *give, grams = refs
-    form_pairs(LATE_PAIRS, position, blocks, keep, give, grams)
+    form_pairs(EARLY_PAIRS, position, blocks, grams)
+    for k in range(len(EARLY_PAIRS)):
+        for core in (0, 1):
+            near[core, k] = grams[k, 2 * aux + (orb ^ core)]
+            far[core, k] = grams[k, 2 * (1 - aux) + (orb ^ core)].astype(jnp.bfloat16)
+
+
+def late_kernel(position, *refs):
+    used = GROUPS * CHUNKS
+    blocks = [refs[i : i + CHUNKS] for i in range(0, used, CHUNKS)]
+    keep, give, grams = refs[used:]
+    aux, orb = position[1], position[2]
+    form_pairs(LATE_PAIRS, position, blocks, grams)
+    for k in range(len(LATE_PAIRS)):
+        for chip in (0, 1):
+            row = 2 * (aux ^ chip)
+            keep[chip, k] = grams[k, row + orb]
+            give[chip, k] = grams[k, row + 1 - orb]
 
 
 def pair_flops(pairs, blocks):
     return 2 * len(pairs) * BLOCK * CHUNKS * blocks[0][0].size
 
 
-def shares(pairs):
+def quarters(pairs):
     rows = BLOCK // 4
-    keep = like((2, len(pairs), rows, BLOCK), jnp.float32)
-    give = like((2, rows, BLOCK), jnp.float32)
-    return [keep] + [give] * len(pairs), pltpu.VMEM((len(pairs), 4, rows, BLOCK), jnp.float32)
+    return (2, len(pairs), rows, BLOCK), pltpu.VMEM((len(pairs), 4, rows, BLOCK), jnp.float32)
 
 
 def early_pairs(position, table, live, blocks):
-    out, grams = shares(EARLY_PAIRS)
-    keep, *give, place = local_call(
+    shape, grams = quarters(EARLY_PAIRS)
+    return local_call(
         early_kernel,
         "early_pairs",
-        out + [like((table.shape[1] // GROUPS,), jnp.int32)],
+        [
+            like(shape, jnp.float32),
+            like(shape, jnp.bfloat16),
+            like((table.shape[1] // GROUPS,), jnp.int32),
+        ],
         [IN_SMEM] * 3 + [IN_VMEM] * (3 * CHUNKS),
-        [IN_VMEM] * len(out) + [IN_SMEM],
+        [IN_VMEM] * 2 + [IN_SMEM],
         pair_flops(EARLY_PAIRS, blocks),
         [grams],
     )(position, table, live, *[part for block in blocks for part in block])
-    return keep, give, place
 
 
 def late_pairs(position, blocks):
-    out, grams = shares(LATE_PAIRS)
-    sizes = [len(block) for block in blocks]
-    keep, *give = local_call(
-        functools.partial(late_kernel, sizes),
+    shape, grams = quarters(LATE_PAIRS)
+    return local_call(
+        late_kernel,
         "late_pairs",
-        out,
-        [IN_SMEM] + [IN_VMEM] * sum(sizes),
-        [IN_VMEM] * len(out),
+        [like(shape, jnp.float32)] * 2,
+        [IN_SMEM] + [IN_VMEM] * (GROUPS * CHUNKS),
+        [IN_VMEM] * 2,
         pair_flops(LATE_PAIRS, blocks),
         [grams],
     )(position, *[part for block in blocks for part in block])
-    return keep, give
-
-
-def spread_kernel(factor, place, *refs):
-    *parts, out, sums, rows, sems = refs
-    half = len(parts) // 2
-    k = 0
-    for kept, far, *got in (parts[:half], parts[half:]):
-        for i, other in enumerate(got):
-            sums[k] = (kept[0, i] + other[0] + far[i].astype(jnp.float32)) * factor
-            k += 1
+
+
+def spread_kernel(factor, place, near0, far0, got0, near1, got1, far1, out, sums, rows, sems):
+    early = near0.shape[1]
+    sums[:early] = (near0[0] + far0[0].astype(jnp.float32) + got0[...]) * factor
+    sums[early:] = (near1[0] + got1[0] + far1[...].astype(jnp.float32)) * factor
     total, slots, width = out.shape
     slot = lax.broadcasted_iota(jnp.int32, (slots, width), 0)
     source = jnp.zeros((slots, width), jnp.int32)
@@ -326,7 +313,6 @@
 def spread(factor, place, *parts):
     rows = BLOCK // 4
     shape = (rows, place.shape[0], BLOCK)
-    parts = [array for kept, far, got in parts for array in (kept, far, *got)]
     return local_call(
         functools.partial(spread_kernel, factor),
         "spread",
@@ -342,12 +328,6 @@
     )(place, *parts)[0]
 
 
-def across(kept, give):
-    got = [lax.ppermute(one, "orb", SWAP) for one in give]
-    share = jnp.stack([kept[1, k] + other[1] for k, other in enumerate(got)])
-    return got, lax.ppermute(share.astype(jnp.bfloat16), "aux", SWAP)
-
-
 def six_pair_body(integrals, coeffs, pair_blocks, pair_count, orbital_count):
     width = coeffs.shape[1] // CHUNKS
     total_aux = integrals.shape[0] * lax.axis_size("aux")
@@ -360,29 +340,26 @@
     ]
     centres, scalars = central(position, table, orbital_count, integrals, parts)
 
-    aux_here = integrals.shape[0]
-    cuts = [[aux_here]] * (CHUNKS - 1) + [[1] * aux_here]
     blocks = [[] for _ in range(GROUPS)]
     for c, (inner, outer) in enumerate(halos):
-        pieces = transform(c * width, position, scalars, integrals, centres[c], outer, inner, cuts[c])
-        for s in range(GROUPS - 1):
-            blocks[s].append(pieces[s])
-        blocks[-1] += pieces[GROUPS - 1 :]
-
-    def fetch(s, piece):
-        return lax.ppermute(piece, "ao", [(j, j ^ s) for j in range(GROUPS)])
-
-    middle = [fetch(2, piece) for piece in blocks[2]]
-    near = [fetch(1, piece) for piece in blocks[1]]
-    last = [fetch(3, piece) for piece in blocks[3][:-1]]
-    kept0, give0, place = early_pairs(position, table, pair_count, [blocks[0], near, middle])
-    piece, kept0 = lax.optimization_barrier((blocks[3][-1], kept0))
-    last.append(fetch(3, piece))
-    got0, far0 = across(kept0, give0)
+        pieces = transform(c * width, position, scalars, integrals, centres[c], outer, inner)
+        for block, piece in zip(blocks, pieces):
+            block.append(piece)
+
+    def fetch(s):
+        swap = [(j, j ^ s) for j in range(GROUPS)]
+        return [lax.ppermute(piece, "ao", swap) for piece in blocks[s]]
+
+    got = [blocks[0], fetch(1), fetch(2)]
+    near0, across0, place = early_pairs(position, table, pair_count, got)
+    far0 = lax.ppermute(across0, "aux", SWAP)
+    got.append(fetch(3))
+    near1, give1 = late_pairs(position, got)
+    got1 = lax.ppermute(give1, "orb", SWAP)
+    far1 = lax.ppermute((near1[1] + got1[1]).astype(jnp.bfloat16), "aux", SWAP)
+    got0 = lax.ppermute(near0[1] + far0[1].astype(jnp.float32), "orb", SWAP)
     factor = 1.0 / math.sqrt(total_aux * ORBS)
-    kept1, give1 = late_pairs(position, [blocks[0], near, middle, last])
-    got1, far1 = across(kept1, give1)
-    return spread(factor, place, (kept0, far0, got0), (kept1, far1, got1))
+    return spread(factor, place, near0, far0, got0, near1, got1, far1)
 
 
 def solution(mesh):

time: 75.5 us -> 73 us (0.967)
  Pallas kernels: 10.3 us -> 9.44 us
    ppermute x15 -> x10, waiting for transfers between devices: 41.5 us -> 40.6 us  [the longest x6 36.2 us: fetch(): return [lax.ppermute(piece, 'ao', swap) for piece in blocks[s]]]
    pallas_call x1, Pallas kernels: 2.6 us -> 1.77 us  [central(): local_call(central_kernel, 'central', [like(shape, jnp.float32)] * CHUNKS...]
    ppermute x15 -> x10, starting transfers between devices: 11.1 us -> 10.9 us  [the longest x6 7.14 us: fetch(): return [lax.ppermute(piece, 'ao', swap) for piece in blocks[s]]]
  transfers between devices with their start and end apart: 19 -> 14, of which waited for: 8 -> 9; matrix products, arithmetic and copies ran while one was open for 0% -> 0% of each run, Pallas kernels for 12% -> 11%
where the time goes in v4:
time: 73 us; the launch traced here: 72.7 us
  waiting for transfers between devices  40.8 us (56%)
  starting transfers between devices  18 us (25%)
  Pallas kernels  9.44 us (13%)
  local copies, waits for them, and re-layouts  4.15 us (6%)
    ppermute x6, waiting for transfers between devices, fetch(): return [lax.ppermute(piece, 'ao', swap) for piece in blocks[s]]  36.2 us
    ppermute x6, starting transfers between devices, fetch(): return [lax.ppermute(piece, 'ao', swap) for piece in blocks[s]]  7.14 us
    ppermute x2, starting transfers between devices, six_pair_body(): lax.ppermute(part, 'ao', INSIDE)  6.96 us
    ppermute x1, waiting for transfers between devices, six_pair_body(): far1 = lax.ppermute((near1[1] + got1[1]).astype(jnp.bfloat16), 'aux', SWAP)  3.34 us
    unnamed x10, local copies, waits for them, and re-layouts  3.08 us
    pallas_call x2, Pallas kernels, transform(): local_call(functools.partial(transform_kernel, start), 'transform', [like...  2.39 us
    pallas_call x1, Pallas kernels, early_pairs(): local_call(early_kernel, 'early_pairs', [like(shape, jnp.float32), like(s...  2.21 us
    pallas_call x1, Pallas kernels, central(): local_call(central_kernel, 'central', [like(shape, jnp.float32)] * CHUNKS...  1.77 us
  transfers between devices with their start and end apart: 14, of which 9 were waited for; matrix products, arithmetic and copies ran while one was open for 0% of the time, Pallas kernels for 11%

profile of v4, /device:TPU:8, one launch (start us, length us, event | category | flops | bytes accessed | tf_op | source)
XLA Modules:
  0.0 72.7 jit_solution(1576079797909056077)
XLA Ops:
  0.0 1.1 %fusion.2 = (bf16[512,256]{1,0:T(8,128)(2,1)S(1)}, bf16[512,256]{1,0:T(8,128)(2,1)S(1)}) fusion(bf16[512,512]{1,0:T(8,128)(2,1)} %param.6), kind=kLoop, calls=%fused_computation.5 | loop fusion | bytes 1048576 | tf_op jit(solution)/shard_map/slice | solution.py:337
  1.1 5.0 %collective-permute-start.3 = (bf16[512,256]{1,0:T(8,128)(2,1)S(1)}, bf16[512,256]{1,0:T(8,128)(2,1)S(1)}, u32[]{:S(2)}, u32[]{:S(2)}) collective-permute-start(bf16[512,256]{1,0:T(8,128)(2,1)S(1)} %get-tuple-element.37.refs_1_), channel_id=1, source_target_pairs={{4,8},{8,4},{5,9},{9,5},{6,10},{10,6},{7,11},{11,7},{20,24},{24,20... | collective-permute-start | bytes 786440 | tf_op jit(solution)/shard_map/ppermute | solution.py:339
  6.3 1.9 %collective-permute-start.1 = (bf16[512,256]{1,0:T(8,128)(2,1)S(1)}, bf16[512,256]{1,0:T(8,128)(2,1)S(1)}, u32[]{:S(2)}, u32[]{:S(2)}) collective-permute-start(bf16[512,256]{1,0:T(8,128)(2,1)S(1)} %get-tuple-element.38.refs_0_), channel_id=1, source_target_pairs={{4,8},{8,4},{5,9},{9,5},{6,10},{10,6},{7,11},{11,7},{20,24},{24,20... | collective-permute-start | bytes 786440 | tf_op jit(solution)/shard_map/ppermute | solution.py:339
  8.3 1.7 %copy-done = bf16[2,512,1280]{2,1,0:T(8,128)(2,1)S(1)} copy-done((bf16[2,512,1280]{2,1,0:T(8,128)(2,1)S(1)}, bf16[2,512,1280]{2,1,0:T(8,128)(2,1)}, u32[]{:S(2)}) %copy-start) | copy-done | bytes 2621464
  10.0 0.7 copy-done.2
  10.7 0.7 copy-done.4
  11.4 1.8 %central.1 = (f32[2,2,256,256]{3,2,1,0:T(8,128)S(1)}, f32[2,2,256,256]{3,2,1,0:T(8,128)S(1)}, s32[8]{0:T(128)S(1)}) custom-call(s32[3]{0:T(128)S(1)} %pad_add_fusion.position, s32[2,64]{1,0:T(2,128)S(1)} %bitcast.8, s32[8]{0:T(128)S(1)} %copy-done.4, bf16[2,512,1280]{2,1,0:T(8,128)(2,1)S(1)} %copy-done, bf16[512,256]{1,0:T(8,128)(2,1)S(1)} %get-tuple-element.38.refs_0_, ...), custom_call_target="tpu_custom_call" | custom-call | flops 536870912 | bytes 4194368 | tf_op jit(solution)/shard_map/central/pallas_call | solution.py:136
  13.3 1.2 %transform.3 = (bf16[2,256,256]{2,1,0:T(8,128)(2,1)S(1)}, bf16[2,256,256]{2,1,0:T(8,128)(2,1)S(1)}, bf16[2,256,256]{2,1,0:T(8,128)(2,1)S(1)}, bf16[2,256,256]{2,1,0:T(8,128)(2,1)S(1)}) custom-call(s32[3]{0:T(128)S(1)} %pad_add_fusion.position, s32[8]{0:T(128)S(1)} %get-tuple-element.21.scalars, bf16[2,512,1280]{2,1,0:T(8,128)(2,1)S(1)} %copy-done.1, ...), custom_call_target="tpu_custom_call" | custom-call | flops 402653184 | bytes 2097152 | tf_op jit(solution)/shard_map/transform/pallas_call | solution.py:173
  15.2 2.9 %collective-permute-start.7 = (bf16[2,256,256]{2,1,0:T(8,128)(2,1)S(1)}, bf16[2,256,256]{2,1,0:T(8,128)(2,1)S(1)}, u32[]{:S(2)}, u32[]{:S(2)}) collective-permute-start(bf16[2,256,256]{2,1,0:T(8,128)(2,1)S(1)} %get-tuple-element.29), channel_id=1, source_target_pairs={{0,8},{4,12},{8,0},{12,4},{1,9},{5,13},{9,1},{13,5},{2,10},{6,14},... | collective-permute-start | bytes 786440 | tf_op jit(solution)/shard_map/ppermute | solution.py:351
  18.1 1.2 %transform.2 = (bf16[2,256,256]{2,1,0:T(8,128)(2,1)S(1)}, bf16[2,256,256]{2,1,0:T(8,128)(2,1)S(1)}, bf16[2,256,256]{2,1,0:T(8,128)(2,1)S(1)}, bf16[2,256,256]{2,1,0:T(8,128)(2,1)S(1)}) custom-call(s32[3]{0:T(128)S(1)} %pad_add_fusion.position, s32[8]{0:T(128)S(1)} %get-tuple-element.21.scalars, bf16[2,512,1280]{2,1,0:T(8,128)(2,1)S(1)} %copy-done.1, ...), custom_call_target="tpu_custom_call" | custom-call | flops 402653184 | bytes 2097152 | tf_op jit(solution)/shard_map/transform/pallas_call | solution.py:173
  19.5 3.0 %collective-permute-start.6 = (bf16[2,256,256]{2,1,0:T(8,128)(2,1)S(1)}, bf16[2,256,256]{2,1,0:T(8,128)(2,1)S(1)}, u32[]{:S(2)}, u32[]{:S(2)}) collective-permute-start(bf16[2,256,256]{2,1,0:T(8,128)(2,1)S(1)} %get-tuple-element.28), channel_id=1, source_target_pairs={{0,8},{4,12},{8,0},{12,4},{1,9},{5,13},{9,1},{13,5},{2,10},{6,14},... | collective-permute-start | bytes 786440 | tf_op jit(solution)/shard_map/ppermute | solution.py:351
  22.9 5.6 %collective-permute-done.5.refs_3_ = bf16[2,256,256]{2,1,0:T(8,128)(2,1)S(1)} collective-permute-done((bf16[2,256,256]{2,1,0:T(8,128)(2,1)S(1)}, bf16[2,256,256]{2,1,0:T(8,128)(2,1)S(1)}, u32[]{:S(2)}, u32[]{:S(2)}) %collective-permute-start.5) | collective-permute-done | bytes 262176 | tf_op jit(solution)/shard_map/ppermute | solution.py:351
  28.5 2.5 %collective-permute-done.7.refs_5_ = bf16[2,256,256]{2,1,0:T(8,128)(2,1)S(1)} collective-permute-done((bf16[2,256,256]{2,1,0:T(8,128)(2,1)S(1)}, bf16[2,256,256]{2,1,0:T(8,128)(2,1)S(1)}, u32[]{:S(2)}, u32[]{:S(2)}) %collective-permute-start.7) | collective-permute-done | bytes 262176 | tf_op jit(solution)/shard_map/ppermute | solution.py:351
  31.0 4.6 %collective-permute-done.4.refs_2_ = bf16[2,256,256]{2,1,0:T(8,128)(2,1)S(1)} collective-permute-done((bf16[2,256,256]{2,1,0:T(8,128)(2,1)S(1)}, bf16[2,256,256]{2,1,0:T(8,128)(2,1)S(1)}, u32[]{:S(2)}, u32[]{:S(2)}) %collective-permute-start.4) | collective-permute-done | bytes 262176 | tf_op jit(solution)/shard_map/ppermute | solution.py:351
  35.7 17.3 %collective-permute-done.6.refs_4_ = bf16[2,256,256]{2,1,0:T(8,128)(2,1)S(1)} collective-permute-done((bf16[2,256,256]{2,1,0:T(8,128)(2,1)S(1)}, bf16[2,256,256]{2,1,0:T(8,128)(2,1)S(1)}, u32[]{:S(2)}, u32[]{:S(2)}) %collective-permute-start.6) | collective-permute-done | bytes 262176 | tf_op jit(solution)/shard_map/ppermute | solution.py:351
  52.9 2.2 %early_pairs.1 = (f32[2,3,64,256]{3,2,1,0:T(8,128)S(1)}, bf16[2,3,64,256]{3,2,1,0:T(8,128)(2,1)S(1)}, s32[16]{0:T(128)S(1)}) custom-call(s32[3]{0:T(128)S(1)} %pad_add_fusion.position, s32[2,64]{1,0:T(2,128)S(1)} %bitcast.9, s32[4]{0:T(128)S(1)} %copy-done.3, bf16[2,256,256]{2,1,0:T(8,128)(2,1)S(1)} %get-tuple-element.23.refs_0_, ...), custom_call_target="tpu_custom_call" | custom-call | flops 402653184 | bytes 1179776 | tf_op jit(solution)/shard_map/early_pairs/pallas_call | solution.py:255
  55.1 1.6 %collective-permute-start.8 = (bf16[2,3,64,256]{3,2,1,0:T(8,128)(2,1)S(1)}, bf16[2,3,64,256]{3,2,1,0:T(8,128)(2,1)S(1)}, u32[]{:S(2)}, u32[]{:S(2)}) collective-permute-start(bf16[2,3,64,256]{3,2,1,0:T(8,128)(2,1)S(1)} %get-tuple-element.32), channel_id=1, source_target_pairs={{0,2},{2,0},{1,3},{3,1},{4,6},{6,4},{5,7},{7,5},{8,10},{10,8},{9,1... | collective-permute-start | bytes 589832 | tf_op jit(solution)/shard_map/ppermute | solution.py:355
  56.7 2.4 %collective-permute-done.11.refs_7_ = bf16[2,256,256]{2,1,0:T(8,128)(2,1)S(1)} collective-permute-done((bf16[2,256,256]{2,1,0:T(8,128)(2,1)S(1)}, bf16[2,256,256]{2,1,0:T(8,128)(2,1)S(1)}, u32[]{:S(2)}, u32[]{:S(2)}) %collective-permute-start.11) | collective-permute-done | bytes 262176 | tf_op jit(solution)/shard_map/ppermute | solution.py:351
  59.1 3.8 %collective-permute-done.10.refs_6_ = bf16[2,256,256]{2,1,0:T(8,128)(2,1)S(1)} collective-permute-done((bf16[2,256,256]{2,1,0:T(8,128)(2,1)S(1)}, bf16[2,256,256]{2,1,0:T(8,128)(2,1)S(1)}, u32[]{:S(2)}, u32[]{:S(2)}) %collective-permute-start.10) | collective-permute-done | bytes 262176 | tf_op jit(solution)/shard_map/ppermute | solution.py:351
  62.8 1.4 %late_pairs.1 = (f32[2,3,64,256]{3,2,1,0:T(8,128)S(1)}, f32[2,3,64,256]{3,2,1,0:T(8,128)S(1)}) custom-call(s32[3]{0:T(128)S(1)} %pad_add_fusion.position, bf16[2,256,256]{2,1,0:T(8,128)(2,1)S(1)} %get-tuple-element.23.refs_0_, bf16[2,256,256]{2,1,0:T(8,128)(2,1)S(1)} %get-tuple-element.25.refs_1_, bf16[2,256,256]{2,1,0:T(8,128)(2,1)S(1)} %collective-permute-done.4.refs_2_, ...), custom_call_target="tpu_custom_call" | custom-call | flops 402653184 | bytes 1572864 | tf_op jit(solution)/shard_map/late_pairs/pallas_call | solution.py:272
  64.9 1.1 %collective-permute-done.12.got1 = f32[2,3,64,256]{3,2,1,0:T(8,128)S(1)} collective-permute-done((f32[2,3,64,256]{3,2,1,0:T(8,128)S(1)}, f32[2,3,64,256]{3,2,1,0:T(8,128)S(1)}, u32[]{:S(2)}, u32[]{:S(2)}) %collective-permute-start.12) | collective-permute-done | bytes 393248 | tf_op jit(solution)/shard_map/ppermute | solution.py:358
  66.1 1.6 %collective-permute-start.13 = (bf16[3,64,256]{2,1,0:T(8,128)(2,1)S(1)}, bf16[3,64,256]{2,1,0:T(8,128)(2,1)S(1)}, u32[]{:S(2)}, u32[]{:S(2)}) collective-permute-start(bf16[3,64,256]{2,1,0:T(8,128)(2,1)S(1)} %fusion.1), channel_id=1, source_target_pairs={{0,2},{2,0},{1,3},{3,1},{4,6},{6,4},{5,7},{7,5},{8,10},{10,8},{9,1... | collective-permute-start | bytes 294920 | tf_op jit(solution)/shard_map/ppermute | solution.py:359
  67.7 3.3 %collective-permute-done.13.far1 = bf16[3,64,256]{2,1,0:T(8,128)(2,1)S(1)} collective-permute-done((bf16[3,64,256]{2,1,0:T(8,128)(2,1)S(1)}, bf16[3,64,256]{2,1,0:T(8,128)(2,1)S(1)}, u32[]{:S(2)}, u32[]{:S(2)}) %collective-permute-start.13) | collective-permute-done | bytes 98336 | tf_op jit(solution)/shard_map/ppermute | solution.py:359
  71.0 1.7 %spread.1 = f32[64,16,256]{2,1,0:T(8,128)} custom-call(s32[16]{0:T(128)S(1)} %get-tuple-element.30.place, f32[2,3,64,256]{3,2,1,0:T(8,128)S(1)} %get-tuple-element.31.near0, bf16[2,3,64,256]{3,2,1,0:T(8,128)(2,1)S(1)} %collective-permute-done.8.far0, f32[3,64,256]{2,1,0:T(8,128)S(1)} %collective-permute-done.9.got0, ...), custom_call_target="tpu_custom_call" | custom-call | flops 1572864 | bytes 2097152 | tf_op jit(solution)/shard_map/spread/pallas_call | solution.py:316
  (24 shorter events, 2.3 us)
Async XLA Ops:
  1.1 12.1 %collective-permute-start.2 = (bf16[512,256]{1,0:T(8,128)(2,1)S(1)}, bf16[512,256]{1,0:T(8,128)(2,1)S(1)}, u32[]{:S(2)}, u32[]{:S(2)}) collective-permute-start(bf16[512,256]{1,0:T(8,128)(2,1)S(1)} %get-tuple-element.37.refs_1_), channel_id=1, source_target_pairs={{0,4},{4,0},{8,12},{12,8},{1,5},{5,1},{9,13},{13,9},{2,6},{6,2},{1... | collective-permute-start | bytes 786440 | tf_op jit(solution)/shard_map/ppermute | solution.py:339
  1.1 12.2 %collective-permute-start.3 = (bf16[512,256]{1,0:T(8,128)(2,1)S(1)}, bf16[512,256]{1,0:T(8,128)(2,1)S(1)}, u32[]{:S(2)}, u32[]{:S(2)}) collective-permute-start(bf16[512,256]{1,0:T(8,128)(2,1)S(1)} %get-tuple-element.37.refs_1_), channel_id=1, source_target_pairs={{4,8},{8,4},{5,9},{9,5},{6,10},{10,6},{7,11},{11,7},{20,24},{24,20... | collective-permute-start | bytes 786440 | tf_op jit(solution)/shard_map/ppermute | solution.py:339
  6.2 12.0 %collective-permute-start = (bf16[512,256]{1,0:T(8,128)(2,1)S(1)}, bf16[512,256]{1,0:T(8,128)(2,1)S(1)}, u32[]{:S(2)}, u32[]{:S(2)}) collective-permute-start(bf16[512,256]{1,0:T(8,128)(2,1)S(1)} %get-tuple-element.38.refs_0_), channel_id=1, source_target_pairs={{0,4},{4,0},{8,12},{12,8},{1,5},{5,1},{9,13},{13,9},{2,6},{6,2},{1... | collective-permute-start | bytes 786440 | tf_op jit(solution)/shard_map/ppermute | solution.py:339
  6.3 11.9 %collective-permute-start.1 = (bf16[512,256]{1,0:T(8,128)(2,1)S(1)}, bf16[512,256]{1,0:T(8,128)(2,1)S(1)}, u32[]{:S(2)}, u32[]{:S(2)}) collective-permute-start(bf16[512,256]{1,0:T(8,128)(2,1)S(1)} %get-tuple-element.38.refs_0_), channel_id=1, source_target_pairs={{4,8},{8,4},{5,9},{9,5},{6,10},{10,6},{7,11},{11,7},{20,24},{24,20... | collective-permute-start | bytes 786440 | tf_op jit(solution)/shard_map/ppermute | solution.py:339
  8.3 1.7 %copy-start = (bf16[2,512,1280]{2,1,0:T(8,128)(2,1)S(1)}, bf16[2,512,1280]{2,1,0:T(8,128)(2,1)}, u32[]{:S(2)}) copy-start(bf16[2,512,1280]{2,1,0:T(8,128)(2,1)} %integrals.5) | copy-start | bytes 7864324
  10.0 0.7 copy-start.2
  10.7 0.7 copy-start.4
  11.4 2.0 %copy-start.1 = (bf16[2,512,1280]{2,1,0:T(8,128)(2,1)S(1)}, bf16[2,512,1280]{2,1,0:T(8,128)(2,1)}, u32[]{:S(2)}) copy-start(bf16[2,512,1280]{2,1,0:T(8,128)(2,1)} %integrals.5) | copy-start | bytes 7864324
  14.6 38.4 %copy-start.3 = (s32[4]{0:T(128)S(1)}, s32[4]{0:T(128)}, u32[]{:S(2)}) copy-start(s32[4]{0:T(128)} %live.1) | copy-start | bytes 52
  14.6 14.0 %collective-permute-start.5 = (bf16[2,256,256]{2,1,0:T(8,128)(2,1)S(1)}, bf16[2,256,256]{2,1,0:T(8,128)(2,1)S(1)}, u32[]{:S(2)}, u32[]{:S(2)}) collective-permute-start(bf16[2,256,256]{2,1,0:T(8,128)(2,1)S(1)} %get-tuple-element.27), channel_id=1, source_target_pairs={{0,4},{4,0},{8,12},{12,8},{1,5},{5,1},{9,13},{13,9},{2,6},{6,2},{1... | collective-permute-start | bytes 786440 | tf_op jit(solution)/shard_map/ppermute | solution.py:351
  15.2 15.8 %collective-permute-start.7 = (bf16[2,256,256]{2,1,0:T(8,128)(2,1)S(1)}, bf16[2,256,256]{2,1,0:T(8,128)(2,1)S(1)}, u32[]{:S(2)}, u32[]{:S(2)}) collective-permute-start(bf16[2,256,256]{2,1,0:T(8,128)(2,1)S(1)} %get-tuple-element.29), channel_id=1, source_target_pairs={{0,8},{4,12},{8,0},{12,4},{1,9},{5,13},{9,1},{13,5},{2,10},{6,14},... | collective-permute-start | bytes 786440 | tf_op jit(solution)/shard_map/ppermute | solution.py:351
  19.4 16.3 %collective-permute-start.4 = (bf16[2,256,256]{2,1,0:T(8,128)(2,1)S(1)}, bf16[2,256,256]{2,1,0:T(8,128)(2,1)S(1)}, u32[]{:S(2)}, u32[]{:S(2)}) collective-permute-start(bf16[2,256,256]{2,1,0:T(8,128)(2,1)S(1)} %get-tuple-element.26), channel_id=1, source_target_pairs={{0,4},{4,0},{8,12},{12,8},{1,5},{5,1},{9,13},{13,9},{2,6},{6,2},{1... | collective-permute-start | bytes 786440 | tf_op jit(solution)/shard_map/ppermute | solution.py:351
  19.5 33.4 %collective-permute-start.6 = (bf16[2,256,256]{2,1,0:T(8,128)(2,1)S(1)}, bf16[2,256,256]{2,1,0:T(8,128)(2,1)S(1)}, u32[]{:S(2)}, u32[]{:S(2)}) collective-permute-start(bf16[2,256,256]{2,1,0:T(8,128)(2,1)S(1)} %get-tuple-element.28), channel_id=1, source_target_pairs={{0,8},{4,12},{8,0},{12,4},{1,9},{5,13},{9,1},{13,5},{2,10},{6,14},... | collective-permute-start | bytes 786440 | tf_op jit(solution)/shard_map/ppermute | solution.py:351
  22.5 36.6 %collective-permute-start.11 = (bf16[2,256,256]{2,1,0:T(8,128)(2,1)S(1)}, bf16[2,256,256]{2,1,0:T(8,128)(2,1)S(1)}, u32[]{:S(2)}, u32[]{:S(2)}) collective-permute-start(bf16[2,256,256]{2,1,0:T(8,128)(2,1)S(1)} %get-tuple-element.34), channel_id=1, source_target_pairs={{0,12},{4,8},{8,4},{12,0},{1,13},{5,9},{9,5},{13,1},{2,14},{6,10},... | collective-permute-start | bytes 786440 | tf_op jit(solution)/shard_map/ppermute | solution.py:351
  28.5 34.3 %collective-permute-start.10 = (bf16[2,256,256]{2,1,0:T(8,128)(2,1)S(1)}, bf16[2,256,256]{2,1,0:T(8,128)(2,1)S(1)}, u32[]{:S(2)}, u32[]{:S(2)}) collective-permute-start(bf16[2,256,256]{2,1,0:T(8,128)(2,1)S(1)} %get-tuple-element.33), channel_id=1, source_target_pairs={{0,12},{4,8},{8,4},{12,0},{1,13},{5,9},{9,5},{13,1},{2,14},{6,10},... | collective-permute-start | bytes 786440 | tf_op jit(solution)/shard_map/ppermute | solution.py:351
  55.1 9.2 %collective-permute-start.8 = (bf16[2,3,64,256]{3,2,1,0:T(8,128)(2,1)S(1)}, bf16[2,3,64,256]{3,2,1,0:T(8,128)(2,1)S(1)}, u32[]{:S(2)}, u32[]{:S(2)}) collective-permute-start(bf16[2,3,64,256]{3,2,1,0:T(8,128)(2,1)S(1)} %get-tuple-element.32), channel_id=1, source_target_pairs={{0,2},{2,0},{1,3},{3,1},{4,6},{6,4},{5,7},{7,5},{8,10},{10,8},{9,1... | collective-permute-start | bytes 589832 | tf_op jit(solution)/shard_map/ppermute | solution.py:355
  64.3 1.8 %collective-permute-start.12 = (f32[2,3,64,256]{3,2,1,0:T(8,128)S(1)}, f32[2,3,64,256]{3,2,1,0:T(8,128)S(1)}, u32[]{:S(2)}, u32[]{:S(2)}) collective-permute-start(f32[2,3,64,256]{3,2,1,0:T(8,128)S(1)} %get-tuple-element.36), channel_id=1, source_target_pairs={{0,1},{1,0},{2,3},{3,2},{4,5},{5,4},{6,7},{7,6},{8,9},{9,8},{10,11... | collective-permute-start | bytes 1179656 | tf_op jit(solution)/shard_map/ppermute | solution.py:358
  64.4 3.3 %collective-permute-start.9 = (f32[3,64,256]{2,1,0:T(8,128)S(1)}, f32[3,64,256]{2,1,0:T(8,128)S(1)}, u32[]{:S(2)}, u32[]{:S(2)}) collective-permute-start(f32[3,64,256]{2,1,0:T(8,128)S(1)} %add_bitcast_fusion), channel_id=1, source_target_pairs={{0,1},{1,0},{2,3},{3,2},{4,5},{5,4},{6,7},{7,6},{8,9},{9,8},{10,11... | collective-permute-start | bytes 589832 | tf_op jit(solution)/shard_map/ppermute | solution.py:360
  66.1 4.9 %collective-permute-start.13 = (bf16[3,64,256]{2,1,0:T(8,128)(2,1)S(1)}, bf16[3,64,256]{2,1,0:T(8,128)(2,1)S(1)}, u32[]{:S(2)}, u32[]{:S(2)}) collective-permute-start(bf16[3,64,256]{2,1,0:T(8,128)(2,1)S(1)} %fusion.1), channel_id=1, source_target_pairs={{0,2},{2,0},{1,3},{3,1},{4,6},{6,4},{5,7},{7,5},{8,10},{10,8},{9,1... | collective-permute-start | bytes 294920 | tf_op jit(solution)/shard_map/ppermute | solution.py:359

commit v5 on v4

--- a/solution.py
+++ b/solution.py
@@ -20,6 +20,7 @@
 SPREAD_STEPS = 4
 SPREAD_STEPS = 4
 VMEM_LIMIT = 40 * 1024 * 1024
+LEAD_FLOPS = 1 << 32
 
 
 def with_halo(cells, sides, width):
@@ -112,9 +113,18 @@
     return jnp.dot(a, b, preferred_element_type=jnp.float32)
 
 
-def central_kernel(position, table, counts, integrals, *refs):
-    parts, outs, scalars = refs[:CHUNKS], refs[CHUNKS:-1], refs[-1]
-    mid = AO_DEV * BLOCK
+def where_kernel(position, out):
+    for i in range(position.shape[0]):
+        out[i] = position[i]
+
+
+def where(position):
+    return local_call(
+        where_kernel, "where", [like(position.shape, jnp.int32)], [IN_SMEM], [IN_SMEM], LEAD_FLOPS
+    )(position)[0]
+
+
+def tables_kernel(position, counts, table, scalars):
     here, orb = position[0], position[2]
     slots = table.shape[1] // GROUPS
     named = jnp.where(table[...] // AO_DEV == here, table[...] % AO_DEV, 0).astype(jnp.float32)
@@ -122,63 +132,54 @@
     for s in range(GROUPS):
         scalars[s] = jnp.max(jnp.where(owner == here ^ s, named, 0.0)).astype(jnp.int32)
     for offset in range(AO_DEV):
-        scalars[GROUPS + offset] = counts[here * AO_DEV + offset] - orb * CHUNKS * parts[0].shape[1]
-    for offset in range(AO_DEV):
-        low = mid - offset * BLOCK
-        for p in range(integrals.shape[0]):
-            slab = integrals[p, offset * BLOCK : (offset + 1) * BLOCK, low : low + mid]
-            for part, out in zip(parts, outs):
-                out[offset, p] = dot(slab, part[...])
-
-
-def central(position, table, counts, integrals, parts):
-    shape = (AO_DEV, integrals.shape[0], BLOCK, parts[0].shape[1])
-    *out, scalars = local_call(
-        central_kernel,
-        "central",
-        [like(shape, jnp.float32)] * CHUNKS + [like((8,), jnp.int32)],
-        [IN_SMEM, IN_VMEM, IN_SMEM] + [IN_VMEM] * (1 + CHUNKS),
-        [IN_VMEM] * CHUNKS + [IN_SMEM],
-        4 * integrals.size // WIN * CHUNKS * parts[0].shape[1],
-    )(position, table, counts, integrals, *parts)
-    return out, scalars
-
-
-def transform_kernel(start, position, scalars, integrals, centre, outer, inner, *refs):
+        scalars[GROUPS + offset] = counts[here * AO_DEV + offset] - orb * (ORBS // 2)
+
+
+def tables(position, counts, table):
+    return local_call(
+        tables_kernel,
+        "tables",
+        [like((8,), jnp.int32)],
+        [IN_SMEM] * 2 + [IN_VMEM],
+        [IN_SMEM],
+        table.size,
+    )(position, counts, table)[0]
+
+
+def transform_kernel(start, position, scalars, integrals, own, outer, inner, *refs):
     outs, half = refs[:-1], refs[-1]
-    columns = outer.shape[1]
     mid = AO_DEV * BLOCK
 
-    def rims(prev, following):
-        ids = start + lax.broadcasted_iota(jnp.int32, (BLOCK, columns), 1)
+    def blocks(prev, following):
+        ids = start + lax.broadcasted_iota(jnp.int32, (BLOCK, own.shape[1]), 1)
         for offset in range(AO_DEV):
             low = mid - offset * BLOCK
+            live = ids < scalars[GROUPS + offset]
             for p in range(integrals.shape[0]):
                 slab = integrals[p, offset * BLOCK : (offset + 1) * BLOCK, :]
-                values = centre[offset, p]
+                values = dot(slab[:, low : low + mid], own[...])
                 values += dot(slab[:, :low], prev[offset * BLOCK :, :])
                 values += dot(slab[:, low + mid :], following[: (offset + 1) * BLOCK, :])
-                live = ids < scalars[GROUPS + offset]
                 half[offset, p] = jnp.where(live, values, 0.0).astype(jnp.bfloat16)
 
     odd = position[0] & 1
-    pl.when(odd == 0)(lambda: rims(inner, outer))
-    pl.when(odd == 1)(lambda: rims(outer, inner))
+    pl.when(odd == 0)(lambda: blocks(inner, outer))
+    pl.when(odd == 1)(lambda: blocks(outer, inner))
     for s, out in enumerate(outs):
         out[...] = half[scalars[s]]
 
 
-def transform(start, position, scalars, integrals, centre, outer, inner):
-    shape = (integrals.shape[0], BLOCK, outer.shape[1])
+def transform(start, position, scalars, integrals, own, outer, inner):
+    shape = (integrals.shape[0], BLOCK, own.shape[1])
     return local_call(
         functools.partial(transform_kernel, start),
         "transform",
         [like(shape, jnp.bfloat16)] * GROUPS,
         [IN_SMEM] * 2 + [IN_VMEM] * 4,
         [IN_VMEM] * GROUPS,
-        6 * AO_DEV * math.prod(shape) * integrals.shape[2] // WIN,
+        2 * AO_DEV * math.prod(shape) * integrals.shape[2],
         [pltpu.VMEM((AO_DEV, *shape), jnp.bfloat16)],
-    )(position, scalars, integrals, centre, outer, inner)
+    )(position, scalars, integrals, own, outer, inner)
 
 
 def form_pairs(pairs, position, blocks, grams):
@@ -334,15 +335,17 @@
     position = jnp.stack([lax.axis_index(axis) for axis in ("ao", "aux", "orb")]).astype(jnp.int32)
     table = pair_blocks.T
 
-    parts = [lax.slice_in_dim(coeffs, c * width, (c + 1) * width, axis=1) for c in range(CHUNKS)]
-    halos = [
-        (lax.ppermute(part, "ao", INSIDE), lax.ppermute(part, "ao", OUTSIDE)) for part in parts
-    ]
-    centres, scalars = central(position, table, orbital_count, integrals, parts)
+    parts = [lax.slice_in_dim(coeffs, 0, width, axis=1)]
+    position, rest = lax.optimization_barrier((where(position), coeffs))
+    for c in range(1, CHUNKS):
+        parts.append(lax.slice_in_dim(rest, c * width, (c + 1) * width, axis=1))
+    inner = [lax.ppermute(part, "ao", INSIDE) for part in parts]
+    outer = [lax.ppermute(part, "ao", OUTSIDE) for part in parts]
+    scalars = tables(position, orbital_count, table)
 
     blocks = [[] for _ in range(GROUPS)]
-    for c, (inner, outer) in enumerate(halos):
-        pieces = transform(c * width, position, scalars, integrals, centres[c], outer, inner)
+    for c, part in enumerate(parts):
+        pieces = transform(c * width, position, scalars, integrals, part, outer[c], inner[c])
         for block, piece in zip(blocks, pieces):
             block.append(piece)
 

time: 73 us -> 72.5 us (level)
  local copies, waits for them, and re-layouts: 4.15 us -> 1.01 us
  starting transfers between devices: 18 us -> 19.6 us
  Pallas kernels: 9.44 us -> 10.6 us
    ppermute x4, waiting for transfers between devices: 0.2 us -> 6.7 us  [the longest x2 4.64 us: six_pair_body(): outer = [lax.ppermute(part, 'ao', OUTSIDE) for part in parts]]
    ppermute x6, waiting for transfers between devices: 36.2 us -> 29.7 us  [fetch(): return [lax.ppermute(piece, 'ao', swap) for piece in blocks[s]]]
    unnamed x10, local copies, waits for them, and re-layouts: 3.08 us -> 0.02 us
    ppermute x6, starting transfers between devices: 7.14 us -> 9.54 us  [fetch(): return [lax.ppermute(piece, 'ao', swap) for piece in blocks[s]]]
    ppermute x4, starting transfers between devices: 7.1 us -> 6.3 us  [the longest x2 5.84 us: six_pair_body(): inner = [lax.ppermute(part, 'ao', INSIDE) for part in parts]]
    pallas_call x1 -> x2, Pallas kernels: 1.77 us -> 2.41 us  [the longest x1 1.27 us: tables(): local_call(tables_kernel, 'tables', [like((8,), jnp.int32)], [IN_SMEM] *...]
  transfers between devices with their start and end apart: 14 -> 14, of which waited for: 9 -> 10; matrix products, arithmetic and copies ran while one was open for 0% -> 0% of each run, Pallas kernels for 11% -> 12%
where the time goes in v5:
time: 72.5 us; the launch traced here: 72.4 us
  waiting for transfers between devices  40.9 us (56%)
  starting transfers between devices  19.6 us (27%)
  Pallas kernels  10.6 us (15%)
  local copies, waits for them, and re-layouts  1.01 us (1%)
    ppermute x6, waiting for transfers between devices, fetch(): return [lax.ppermute(piece, 'ao', swap) for piece in blocks[s]]  29.7 us
    ppermute x6, starting transfers between devices, fetch(): return [lax.ppermute(piece, 'ao', swap) for piece in blocks[s]]  9.54 us
    ppermute x2, starting transfers between devices, six_pair_body(): inner = [lax.ppermute(part, 'ao', INSIDE) for part in parts]  5.84 us
    ppermute x2, waiting for transfers between devices, six_pair_body(): outer = [lax.ppermute(part, 'ao', OUTSIDE) for part in parts]  4.64 us
    ppermute x1, waiting for transfers between devices, six_pair_body(): far1 = lax.ppermute((near1[1] + got1[1]).astype(jnp.bfloat16), 'aux', SWAP)  3.34 us
    pallas_call x2, Pallas kernels, transform(): local_call(functools.partial(transform_kernel, start), 'transform', [like...  2.94 us
    pallas_call x1, Pallas kernels, early_pairs(): local_call(early_kernel, 'early_pairs', [like(shape, jnp.float32), like(s...  2.2 us
    ppermute x2, waiting for transfers between devices, six_pair_body(): inner = [lax.ppermute(part, 'ao', INSIDE) for part in parts]  2.05 us
  transfers between devices with their start and end apart: 14, of which 10 were waited for; matrix products, arithmetic and copies ran while one was open for 0% of the time, Pallas kernels for 12%

profile of v5, /device:TPU:8, one launch (start us, length us, event | category | flops | bytes accessed | tf_op | source)
XLA Modules:
  0.0 72.4 jit_solution(12804325867083903385)
XLA Ops:
  1.0 3.5 %collective-permute-start.1 = (bf16[512,256]{1,0:T(8,128)(2,1)S(1)}, bf16[512,256]{1,0:T(8,128)(2,1)S(1)}, u32[]{:S(2)}, u32[]{:S(2)}) collective-permute-start(bf16[512,256]{1,0:T(8,128)(2,1)S(1)} %slice.18.own), channel_id=1, source_target_pairs={{4,8},{8,4},{5,9},{9,5},{6,10},{10,6},{7,11},{11,7},{20,24},{24,20... | collective-permute-start | bytes 786440 | tf_op jit(solution)/shard_map/ppermute | solution.py:342
  4.6 1.1 %where.1.position = s32[3]{0:T(128)S(1)} custom-call(s32[3]{0:T(128)S(1)} %pad_add_fusion.position), custom_call_target="tpu_custom_call" | custom-call | flops 4294967296 | bytes 24 | tf_op jit(solution)/shard_map/where/pallas_call | solution.py:122
  5.8 2.4 %collective-permute-start.3 = (bf16[512,256]{1,0:T(8,128)(2,1)S(1)}, bf16[512,256]{1,0:T(8,128)(2,1)S(1)}, u32[]{:S(2)}, u32[]{:S(2)}) collective-permute-start(bf16[512,256]{1,0:T(8,128)(2,1)S(1)} %slice.19.own), channel_id=1, source_target_pairs={{4,8},{8,4},{5,9},{9,5},{6,10},{10,6},{7,11},{11,7},{20,24},{24,20... | collective-permute-start | bytes 786440 | tf_op jit(solution)/shard_map/ppermute | solution.py:342
  8.6 1.3 %tables.1.scalars = s32[8]{0:T(128)S(1)} custom-call(s32[3]{0:T(128)S(1)} %where.1.position, s32[8]{0:T(128)S(1)} %copy-done.3, s32[2,64]{1,0:T(2,128)S(1)} %bitcast.8), custom_call_target="tpu_custom_call" | custom-call | flops 128 | bytes 64 | tf_op jit(solution)/shard_map/tables/pallas_call | solution.py:139
  9.9 2.0 %collective-permute-done.1.inner = bf16[512,256]{1,0:T(8,128)(2,1)S(1)} collective-permute-done((bf16[512,256]{1,0:T(8,128)(2,1)S(1)}, bf16[512,256]{1,0:T(8,128)(2,1)S(1)}, u32[]{:S(2)}, u32[]{:S(2)}) %collective-permute-start.1) | collective-permute-done | bytes 262176 | tf_op jit(solution)/shard_map/ppermute | solution.py:342
  11.9 1.9 %collective-permute-done.outer = bf16[512,256]{1,0:T(8,128)(2,1)S(1)} collective-permute-done((bf16[512,256]{1,0:T(8,128)(2,1)S(1)}, bf16[512,256]{1,0:T(8,128)(2,1)S(1)}, u32[]{:S(2)}, u32[]{:S(2)}) %collective-permute-start) | collective-permute-done | bytes 262176 | tf_op jit(solution)/shard_map/ppermute | solution.py:343
  13.8 1.5 %transform.2 = (bf16[2,256,256]{2,1,0:T(8,128)(2,1)S(1)}, bf16[2,256,256]{2,1,0:T(8,128)(2,1)S(1)}, bf16[2,256,256]{2,1,0:T(8,128)(2,1)S(1)}, bf16[2,256,256]{2,1,0:T(8,128)(2,1)S(1)}) custom-call(s32[3]{0:T(128)S(1)} %where.1.position, s32[8]{0:T(128)S(1)} %tables.1.scalars, bf16[2,512,1280]{2,1,0:T(8,128)(2,1)S(1)} %copy-done, ...), custom_call_target="tpu_custom_call" | custom-call | flops 671088640 | bytes 2097152 | tf_op jit(solution)/shard_map/transform/pallas_call | solution.py:174
  15.3 1.4 %collective-permute-start.6 = (bf16[2,256,256]{2,1,0:T(8,128)(2,1)S(1)}, bf16[2,256,256]{2,1,0:T(8,128)(2,1)S(1)}, u32[]{:S(2)}, u32[]{:S(2)}) collective-permute-start(bf16[2,256,256]{2,1,0:T(8,128)(2,1)S(1)} %get-tuple-element.26), channel_id=1, source_target_pairs={{0,8},{4,12},{8,0},{12,4},{1,9},{5,13},{9,1},{13,5},{2,10},{6,14},... | collective-permute-start | bytes 786440 | tf_op jit(solution)/shard_map/ppermute | solution.py:354
  16.8 2.8 %collective-permute-done.2.outer = bf16[512,256]{1,0:T(8,128)(2,1)S(1)} collective-permute-done((bf16[512,256]{1,0:T(8,128)(2,1)S(1)}, bf16[512,256]{1,0:T(8,128)(2,1)S(1)}, u32[]{:S(2)}, u32[]{:S(2)}) %collective-permute-start.2) | collective-permute-done | bytes 262176 | tf_op jit(solution)/shard_map/ppermute | solution.py:343
  19.5 1.5 %transform.3 = (bf16[2,256,256]{2,1,0:T(8,128)(2,1)S(1)}, bf16[2,256,256]{2,1,0:T(8,128)(2,1)S(1)}, bf16[2,256,256]{2,1,0:T(8,128)(2,1)S(1)}, bf16[2,256,256]{2,1,0:T(8,128)(2,1)S(1)}) custom-call(s32[3]{0:T(128)S(1)} %where.1.position, s32[8]{0:T(128)S(1)} %tables.1.scalars, bf16[2,512,1280]{2,1,0:T(8,128)(2,1)S(1)} %copy-done, ...), custom_call_target="tpu_custom_call" | custom-call | flops 671088640 | bytes 2097152 | tf_op jit(solution)/shard_map/transform/pallas_call | solution.py:174
  21.0 5.1 %collective-permute-start.5 = (bf16[2,256,256]{2,1,0:T(8,128)(2,1)S(1)}, bf16[2,256,256]{2,1,0:T(8,128)(2,1)S(1)}, u32[]{:S(2)}, u32[]{:S(2)}) collective-permute-start(bf16[2,256,256]{2,1,0:T(8,128)(2,1)S(1)} %get-tuple-element.25), channel_id=1, source_target_pairs={{0,4},{4,0},{8,12},{12,8},{1,5},{5,1},{9,13},{13,9},{2,6},{6,2},{1... | collective-permute-start | bytes 786440 | tf_op jit(solution)/shard_map/ppermute | solution.py:354
  26.1 1.5 %collective-permute-start.10 = (bf16[2,256,256]{2,1,0:T(8,128)(2,1)S(1)}, bf16[2,256,256]{2,1,0:T(8,128)(2,1)S(1)}, u32[]{:S(2)}, u32[]{:S(2)}) collective-permute-start(bf16[2,256,256]{2,1,0:T(8,128)(2,1)S(1)} %get-tuple-element.31), channel_id=1, source_target_pairs={{0,12},{4,8},{8,4},{12,0},{1,13},{5,9},{9,5},{13,1},{2,14},{6,10},... | collective-permute-start | bytes 786440 | tf_op jit(solution)/shard_map/ppermute | solution.py:354
  27.6 1.6 %collective-permute-done.4.refs_2_ = bf16[2,256,256]{2,1,0:T(8,128)(2,1)S(1)} collective-permute-done((bf16[2,256,256]{2,1,0:T(8,128)(2,1)S(1)}, bf16[2,256,256]{2,1,0:T(8,128)(2,1)S(1)}, u32[]{:S(2)}, u32[]{:S(2)}) %collective-permute-start.4) | collective-permute-done | bytes 262176 | tf_op jit(solution)/shard_map/ppermute | solution.py:354
  29.2 1.5 %collective-permute-start.11 = (bf16[2,256,256]{2,1,0:T(8,128)(2,1)S(1)}, bf16[2,256,256]{2,1,0:T(8,128)(2,1)S(1)}, u32[]{:S(2)}, u32[]{:S(2)}) collective-permute-start(bf16[2,256,256]{2,1,0:T(8,128)(2,1)S(1)} %get-tuple-element.32), channel_id=1, source_target_pairs={{0,12},{4,8},{8,4},{12,0},{1,13},{5,9},{9,5},{13,1},{2,14},{6,10},... | collective-permute-start | bytes 786440 | tf_op jit(solution)/shard_map/ppermute | solution.py:354
  30.6 7.1 %collective-permute-done.5.refs_3_ = bf16[2,256,256]{2,1,0:T(8,128)(2,1)S(1)} collective-permute-done((bf16[2,256,256]{2,1,0:T(8,128)(2,1)S(1)}, bf16[2,256,256]{2,1,0:T(8,128)(2,1)S(1)}, u32[]{:S(2)}, u32[]{:S(2)}) %collective-permute-start.5) | collective-permute-done | bytes 262176 | tf_op jit(solution)/shard_map/ppermute | solution.py:354
  37.7 3.7 %collective-permute-done.7.refs_5_ = bf16[2,256,256]{2,1,0:T(8,128)(2,1)S(1)} collective-permute-done((bf16[2,256,256]{2,1,0:T(8,128)(2,1)S(1)}, bf16[2,256,256]{2,1,0:T(8,128)(2,1)S(1)}, u32[]{:S(2)}, u32[]{:S(2)}) %collective-permute-start.7) | collective-permute-done | bytes 262176 | tf_op jit(solution)/shard_map/ppermute | solution.py:354
  41.4 2.2 %early_pairs.1 = (f32[2,3,64,256]{3,2,1,0:T(8,128)S(1)}, bf16[2,3,64,256]{3,2,1,0:T(8,128)(2,1)S(1)}, s32[16]{0:T(128)S(1)}) custom-call(s32[3]{0:T(128)S(1)} %where.1.position, s32[2,64]{1,0:T(2,128)S(1)} %bitcast.9, s32[4]{0:T(128)S(1)} %copy-done.2, bf16[2,256,256]{2,1,0:T(8,128)(2,1)S(1)} %get-tuple-element.21.refs_0_, ...), custom_call_target="tpu_custom_call" | custom-call | flops 402653184 | bytes 1179776 | tf_op jit(solution)/shard_map/early_pairs/pallas_call | solution.py:256
  43.6 1.6 %collective-permute-start.8 = (bf16[2,3,64,256]{3,2,1,0:T(8,128)(2,1)S(1)}, bf16[2,3,64,256]{3,2,1,0:T(8,128)(2,1)S(1)}, u32[]{:S(2)}, u32[]{:S(2)}) collective-permute-start(bf16[2,3,64,256]{3,2,1,0:T(8,128)(2,1)S(1)} %get-tuple-element.30), channel_id=1, source_target_pairs={{0,2},{2,0},{1,3},{3,1},{4,6},{6,4},{5,7},{7,5},{8,10},{10,8},{9,1... | collective-permute-start | bytes 589832 | tf_op jit(solution)/shard_map/ppermute | solution.py:358
  45.2 13.0 %collective-permute-done.10.refs_6_ = bf16[2,256,256]{2,1,0:T(8,128)(2,1)S(1)} collective-permute-done((bf16[2,256,256]{2,1,0:T(8,128)(2,1)S(1)}, bf16[2,256,256]{2,1,0:T(8,128)(2,1)S(1)}, u32[]{:S(2)}, u32[]{:S(2)}) %collective-permute-start.10) | collective-permute-done | bytes 262176 | tf_op jit(solution)/shard_map/ppermute | solution.py:354
  58.2 4.4 %collective-permute-done.11.refs_7_ = bf16[2,256,256]{2,1,0:T(8,128)(2,1)S(1)} collective-permute-done((bf16[2,256,256]{2,1,0:T(8,128)(2,1)S(1)}, bf16[2,256,256]{2,1,0:T(8,128)(2,1)S(1)}, u32[]{:S(2)}, u32[]{:S(2)}) %collective-permute-start.11) | collective-permute-done | bytes 262176 | tf_op jit(solution)/shard_map/ppermute | solution.py:354
  62.6 1.4 %late_pairs.1 = (f32[2,3,64,256]{3,2,1,0:T(8,128)S(1)}, f32[2,3,64,256]{3,2,1,0:T(8,128)S(1)}) custom-call(s32[3]{0:T(128)S(1)} %where.1.position, bf16[2,256,256]{2,1,0:T(8,128)(2,1)S(1)} %get-tuple-element.21.refs_0_, bf16[2,256,256]{2,1,0:T(8,128)(2,1)S(1)} %get-tuple-element.23.refs_1_, bf16[2,256,256]{2,1,0:T(8,128)(2,1)S(1)} %collective-permute-done.4.refs_2_, ...), custom_call_target="tpu_custom_call" | custom-call | flops 402653184 | bytes 1572864 | tf_op jit(solution)/shard_map/late_pairs/pallas_call | solution.py:273
  65.8 1.6 %collective-permute-start.13 = (bf16[3,64,256]{2,1,0:T(8,128)(2,1)S(1)}, bf16[3,64,256]{2,1,0:T(8,128)(2,1)S(1)}, u32[]{:S(2)}, u32[]{:S(2)}) collective-permute-start(bf16[3,64,256]{2,1,0:T(8,128)(2,1)S(1)} %fusion.1), channel_id=1, source_target_pairs={{0,2},{2,0},{1,3},{3,1},{4,6},{6,4},{5,7},{7,5},{8,10},{10,8},{9,1... | collective-permute-start | bytes 294920 | tf_op jit(solution)/shard_map/ppermute | solution.py:362
  67.4 3.3 %collective-permute-done.13.far1 = bf16[3,64,256]{2,1,0:T(8,128)(2,1)S(1)} collective-permute-done((bf16[3,64,256]{2,1,0:T(8,128)(2,1)S(1)}, bf16[3,64,256]{2,1,0:T(8,128)(2,1)S(1)}, u32[]{:S(2)}, u32[]{:S(2)}) %collective-permute-start.13) | collective-permute-done | bytes 98336 | tf_op jit(solution)/shard_map/ppermute | solution.py:362
  70.7 1.7 %spread.1 = f32[64,16,256]{2,1,0:T(8,128)} custom-call(s32[16]{0:T(128)S(1)} %get-tuple-element.28.place, f32[2,3,64,256]{3,2,1,0:T(8,128)S(1)} %get-tuple-element.29.near0, bf16[2,3,64,256]{3,2,1,0:T(8,128)(2,1)S(1)} %collective-permute-done.8.far0, f32[3,64,256]{2,1,0:T(8,128)S(1)} %collective-permute-done.9.got0, ...), custom_call_target="tpu_custom_call" | custom-call | flops 1572864 | bytes 2097152 | tf_op jit(solution)/shard_map/spread/pallas_call | solution.py:317
  (26 shorter events, 3.5 us)
Async XLA Ops:
  1.0 10.9 %collective-permute-start.1 = (bf16[512,256]{1,0:T(8,128)(2,1)S(1)}, bf16[512,256]{1,0:T(8,128)(2,1)S(1)}, u32[]{:S(2)}, u32[]{:S(2)}) collective-permute-start(bf16[512,256]{1,0:T(8,128)(2,1)S(1)} %slice.18.own), channel_id=1, source_target_pairs={{4,8},{8,4},{5,9},{9,5},{6,10},{10,6},{7,11},{11,7},{20,24},{24,20... | collective-permute-start | bytes 786440 | tf_op jit(solution)/shard_map/ppermute | solution.py:342
  4.5 9.3 %collective-permute-start = (bf16[512,256]{1,0:T(8,128)(2,1)S(1)}, bf16[512,256]{1,0:T(8,128)(2,1)S(1)}, u32[]{:S(2)}, u32[]{:S(2)}) collective-permute-start(bf16[512,256]{1,0:T(8,128)(2,1)S(1)} %slice.18.own), channel_id=1, source_target_pairs={{0,4},{4,0},{8,12},{12,8},{1,5},{5,1},{9,13},{13,9},{2,6},{6,2},{1... | collective-permute-start | bytes 786440 | tf_op jit(solution)/shard_map/ppermute | solution.py:343
  4.6 1.2 %copy-start.4 = (bf16[512,512]{1,0:T(8,128)(2,1)S(1)}, bf16[512,512]{1,0:T(8,128)(2,1)}, u32[]{:S(2)}) copy-start(bf16[512,512]{1,0:T(8,128)(2,1)} %param.6) | copy-start | bytes 1572868
  4.6 4.0 %copy-start.1 = (s32[64,2]{0,1:T(2,128)S(1)}, s32[64,2]{0,1:T(2,128)}, u32[]{:S(2)}) copy-start(s32[64,2]{0,1:T(2,128)} %param.7) | copy-start | bytes 1540
  4.6 4.0 %copy-start.3 = (s32[8]{0:T(128)S(1)}, s32[8]{0:T(128)}, u32[]{:S(2)}) copy-start(s32[8]{0:T(128)} %counts.1) | copy-start | bytes 100
  4.6 9.1 %copy-start = (bf16[2,512,1280]{2,1,0:T(8,128)(2,1)S(1)}, bf16[2,512,1280]{2,1,0:T(8,128)(2,1)}, u32[]{:S(2)}) copy-start(bf16[2,512,1280]{2,1,0:T(8,128)(2,1)} %integrals.3) | copy-start | bytes 7864324
  5.8 10.9 %collective-permute-start.3 = (bf16[512,256]{1,0:T(8,128)(2,1)S(1)}, bf16[512,256]{1,0:T(8,128)(2,1)S(1)}, u32[]{:S(2)}, u32[]{:S(2)}) collective-permute-start(bf16[512,256]{1,0:T(8,128)(2,1)S(1)} %slice.19.own), channel_id=1, source_target_pairs={{4,8},{8,4},{5,9},{9,5},{6,10},{10,6},{7,11},{11,7},{20,24},{24,20... | collective-permute-start | bytes 786440 | tf_op jit(solution)/shard_map/ppermute | solution.py:342
  8.2 11.4 %collective-permute-start.2 = (bf16[512,256]{1,0:T(8,128)(2,1)S(1)}, bf16[512,256]{1,0:T(8,128)(2,1)S(1)}, u32[]{:S(2)}, u32[]{:S(2)}) collective-permute-start(bf16[512,256]{1,0:T(8,128)(2,1)S(1)} %slice.19.own), channel_id=1, source_target_pairs={{0,4},{4,0},{8,12},{12,8},{1,5},{5,1},{9,13},{13,9},{2,6},{6,2},{1... | collective-permute-start | bytes 786440 | tf_op jit(solution)/shard_map/ppermute | solution.py:343
  9.9 31.5 %copy-start.2 = (s32[4]{0:T(128)S(1)}, s32[4]{0:T(128)}, u32[]{:S(2)}) copy-start(s32[4]{0:T(128)} %live.1) | copy-start | bytes 52
  15.2 13.9 %collective-permute-start.4 = (bf16[2,256,256]{2,1,0:T(8,128)(2,1)S(1)}, bf16[2,256,256]{2,1,0:T(8,128)(2,1)S(1)}, u32[]{:S(2)}, u32[]{:S(2)}) collective-permute-start(bf16[2,256,256]{2,1,0:T(8,128)(2,1)S(1)} %get-tuple-element.24), channel_id=1, source_target_pairs={{0,4},{4,0},{8,12},{12,8},{1,5},{5,1},{9,13},{13,9},{2,6},{6,2},{1... | collective-permute-start | bytes 786440 | tf_op jit(solution)/shard_map/ppermute | solution.py:354
  15.3 15.3 %collective-permute-start.6 = (bf16[2,256,256]{2,1,0:T(8,128)(2,1)S(1)}, bf16[2,256,256]{2,1,0:T(8,128)(2,1)S(1)}, u32[]{:S(2)}, u32[]{:S(2)}) collective-permute-start(bf16[2,256,256]{2,1,0:T(8,128)(2,1)S(1)} %get-tuple-element.26), channel_id=1, source_target_pairs={{0,8},{4,12},{8,0},{12,4},{1,9},{5,13},{9,1},{13,5},{2,10},{6,14},... | collective-permute-start | bytes 786440 | tf_op jit(solution)/shard_map/ppermute | solution.py:354
  21.0 16.7 %collective-permute-start.5 = (bf16[2,256,256]{2,1,0:T(8,128)(2,1)S(1)}, bf16[2,256,256]{2,1,0:T(8,128)(2,1)S(1)}, u32[]{:S(2)}, u32[]{:S(2)}) collective-permute-start(bf16[2,256,256]{2,1,0:T(8,128)(2,1)S(1)} %get-tuple-element.25), channel_id=1, source_target_pairs={{0,4},{4,0},{8,12},{12,8},{1,5},{5,1},{9,13},{13,9},{2,6},{6,2},{1... | collective-permute-start | bytes 786440 | tf_op jit(solution)/shard_map/ppermute | solution.py:354
  26.1 15.3 %collective-permute-start.7 = (bf16[2,256,256]{2,1,0:T(8,128)(2,1)S(1)}, bf16[2,256,256]{2,1,0:T(8,128)(2,1)S(1)}, u32[]{:S(2)}, u32[]{:S(2)}) collective-permute-start(bf16[2,256,256]{2,1,0:T(8,128)(2,1)S(1)} %get-tuple-element.27), channel_id=1, source_target_pairs={{0,8},{4,12},{8,0},{12,4},{1,9},{5,13},{9,1},{13,5},{2,10},{6,14},... | collective-permute-start | bytes 786440 | tf_op jit(solution)/shard_map/ppermute | solution.py:354
  26.1 32.1 %collective-permute-start.10 = (bf16[2,256,256]{2,1,0:T(8,128)(2,1)S(1)}, bf16[2,256,256]{2,1,0:T(8,128)(2,1)S(1)}, u32[]{:S(2)}, u32[]{:S(2)}) collective-permute-start(bf16[2,256,256]{2,1,0:T(8,128)(2,1)S(1)} %get-tuple-element.31), channel_id=1, source_target_pairs={{0,12},{4,8},{8,4},{12,0},{1,13},{5,9},{9,5},{13,1},{2,14},{6,10},... | collective-permute-start | bytes 786440 | tf_op jit(solution)/shard_map/ppermute | solution.py:354
  29.2 33.4 %collective-permute-start.11 = (bf16[2,256,256]{2,1,0:T(8,128)(2,1)S(1)}, bf16[2,256,256]{2,1,0:T(8,128)(2,1)S(1)}, u32[]{:S(2)}, u32[]{:S(2)}) collective-permute-start(bf16[2,256,256]{2,1,0:T(8,128)(2,1)S(1)} %get-tuple-element.32), channel_id=1, source_target_pairs={{0,12},{4,8},{8,4},{12,0},{1,13},{5,9},{9,5},{13,1},{2,14},{6,10},... | collective-permute-start | bytes 786440 | tf_op jit(solution)/shard_map/ppermute | solution.py:354
  43.6 20.4 %collective-permute-start.8 = (bf16[2,3,64,256]{3,2,1,0:T(8,128)(2,1)S(1)}, bf16[2,3,64,256]{3,2,1,0:T(8,128)(2,1)S(1)}, u32[]{:S(2)}, u32[]{:S(2)}) collective-permute-start(bf16[2,3,64,256]{3,2,1,0:T(8,128)(2,1)S(1)} %get-tuple-element.30), channel_id=1, source_target_pairs={{0,2},{2,0},{1,3},{3,1},{4,6},{6,4},{5,7},{7,5},{8,10},{10,8},{9,1... | collective-permute-start | bytes 589832 | tf_op jit(solution)/shard_map/ppermute | solution.py:358
  64.0 1.8 %collective-permute-start.12 = (f32[2,3,64,256]{3,2,1,0:T(8,128)S(1)}, f32[2,3,64,256]{3,2,1,0:T(8,128)S(1)}, u32[]{:S(2)}, u32[]{:S(2)}) collective-permute-start(f32[2,3,64,256]{3,2,1,0:T(8,128)S(1)} %get-tuple-element.34), channel_id=1, source_target_pairs={{0,1},{1,0},{2,3},{3,2},{4,5},{5,4},{6,7},{7,6},{8,9},{9,8},{10,11... | collective-permute-start | bytes 1179656 | tf_op jit(solution)/shard_map/ppermute | solution.py:361
  64.1 3.3 %collective-permute-start.9 = (f32[3,64,256]{2,1,0:T(8,128)S(1)}, f32[3,64,256]{2,1,0:T(8,128)S(1)}, u32[]{:S(2)}, u32[]{:S(2)}) collective-permute-start(f32[3,64,256]{2,1,0:T(8,128)S(1)} %add_bitcast_fusion), channel_id=1, source_target_pairs={{0,1},{1,0},{2,3},{3,2},{4,5},{5,4},{6,7},{7,6},{8,9},{9,8},{10,11... | collective-permute-start | bytes 589832 | tf_op jit(solution)/shard_map/ppermute | solution.py:363
  65.8 4.9 %collective-permute-start.13 = (bf16[3,64,256]{2,1,0:T(8,128)(2,1)S(1)}, bf16[3,64,256]{2,1,0:T(8,128)(2,1)S(1)}, u32[]{:S(2)}, u32[]{:S(2)}) collective-permute-start(bf16[3,64,256]{2,1,0:T(8,128)(2,1)S(1)} %fusion.1), channel_id=1, source_target_pairs={{0,2},{2,0},{1,3},{3,1},{4,6},{6,4},{5,7},{7,5},{8,10},{10,8},{9,1... | collective-permute-start | bytes 294920 | tf_op jit(solution)/shard_map/ppermute | solution.py:362

commit v6 on v5

--- a/solution.py
+++ b/solution.py
@@ -88,20 +88,19 @@
 
 IN_HBM = pl.BlockSpec(memory_space=pltpu.HBM)
 IN_VMEM = pl.BlockSpec(memory_space=pltpu.VMEM)
-IN_SMEM = pl.BlockSpec(memory_space=pltpu.SMEM)
 
 
 def like(shape, dtype):
     return jax.ShapeDtypeStruct(shape, dtype)
 
 
-def local_call(kernel, name, out_shape, in_specs, out_specs, flops, scratch=()):
+def local_call(kernel, name, out_shape, inputs, flops, scratch=(), out_spec=IN_VMEM):
     moved = sum(math.prod(o.shape) * o.dtype.itemsize for o in out_shape)
     return pl.pallas_call(
         kernel,
         out_shape=out_shape,
-        in_specs=in_specs,
-        out_specs=out_specs,
+        in_specs=[IN_VMEM] * inputs,
+        out_specs=[out_spec] * len(out_shape),
         scratch_shapes=list(scratch),
         compiler_params=pltpu.CompilerParams(vmem_limit_bytes=VMEM_LIMIT),
         cost_estimate=pl.CostEstimate(flops=flops, bytes_accessed=2 * moved, transcendentals=0),
@@ -113,77 +112,77 @@
     return jnp.dot(a, b, preferred_element_type=jnp.float32)
 
 
-def where_kernel(position, out):
-    for i in range(position.shape[0]):
-        out[i] = position[i]
-
-
-def where(position):
-    return local_call(
-        where_kernel, "where", [like(position.shape, jnp.int32)], [IN_SMEM], [IN_SMEM], LEAD_FLOPS
-    )(position)[0]
-
-
-def tables_kernel(position, counts, table, scalars):
-    here, orb = position[0], position[2]
+def lead_kernel(out):
+    out[...] = jnp.zeros_like(out)
+
+
+def lead():
+    return local_call(lead_kernel, "lead", [like((8, 128), jnp.int32)], 0, LEAD_FLOPS)()[0]
+
+
+def scalar_at(values, index):
+    ids = lax.broadcasted_iota(jnp.int32, values.shape, 1)
+    return jnp.sum(jnp.where(ids == index, values, 0).astype(jnp.float32))
+
+
+def tables_kernel(first, counts, table, wants):
+    here, orb = lax.axis_index("ao"), lax.axis_index("orb")
     slots = table.shape[1] // GROUPS
     named = jnp.where(table[...] // AO_DEV == here, table[...] % AO_DEV, 0).astype(jnp.float32)
     owner = lax.broadcasted_iota(jnp.int32, table.shape, 1) // slots
-    for s in range(GROUPS):
-        scalars[s] = jnp.max(jnp.where(owner == here ^ s, named, 0.0)).astype(jnp.int32)
+    rows = [jnp.max(jnp.where(owner == here ^ s, named, 0.0)) for s in range(GROUPS)]
     for offset in range(AO_DEV):
-        scalars[GROUPS + offset] = counts[here * AO_DEV + offset] - orb * (ORBS // 2)
-
-
-def tables(position, counts, table):
-    return local_call(
-        tables_kernel,
-        "tables",
-        [like((8,), jnp.int32)],
-        [IN_SMEM] * 2 + [IN_VMEM],
-        [IN_SMEM],
-        table.size,
-    )(position, counts, table)[0]
-
-
-def transform_kernel(start, position, scalars, integrals, own, outer, inner, *refs):
-    outs, half = refs[:-1], refs[-1]
+        count = scalar_at(counts[...], here * AO_DEV + offset)
+        rows.append(count - (orb * (ORBS // 2)).astype(jnp.float32))
+    row = lax.broadcasted_iota(jnp.int32, wants.shape, 0)
+    out = first[0, 0:1].astype(jnp.float32).reshape(1, 1) + jnp.zeros(wants.shape, jnp.float32)
+    for k, value in enumerate(rows):
+        out = jnp.where(row == k, value, out)
+    wants[...] = out.astype(jnp.int32)
+
+
+def tables(first, counts, table, width):
+    return local_call(
+        tables_kernel, "tables", [like((8, width), jnp.int32)], 3, table.size
+    )(first, counts.reshape(1, -1), table)[0]
+
+
+def transform_kernel(start, wants, integrals, own, outer, inner, *outs):
     mid = AO_DEV * BLOCK
 
     def blocks(prev, following):
         ids = start + lax.broadcasted_iota(jnp.int32, (BLOCK, own.shape[1]), 1)
-        for offset in range(AO_DEV):
-            low = mid - offset * BLOCK
-            live = ids < scalars[GROUPS + offset]
-            for p in range(integrals.shape[0]):
+        for p in range(integrals.shape[0]):
+            both = []
+            for offset in range(AO_DEV):
+                low = mid - offset * BLOCK
                 slab = integrals[p, offset * BLOCK : (offset + 1) * BLOCK, :]
                 values = dot(slab[:, low : low + mid], own[...])
                 values += dot(slab[:, :low], prev[offset * BLOCK :, :])
                 values += dot(slab[:, low + mid :], following[: (offset + 1) * BLOCK, :])
-                half[offset, p] = jnp.where(live, values, 0.0).astype(jnp.bfloat16)
-
-    odd = position[0] & 1
+                live = ids < wants[GROUPS + offset : GROUPS + offset + 1, :]
+                both.append(jnp.where(live, values, 0.0))
+            for s, out in enumerate(outs):
+                out[p] = jnp.where(wants[s : s + 1, :] == 0, *both).astype(jnp.bfloat16)
+
+    odd = lax.axis_index("ao") & 1
     pl.when(odd == 0)(lambda: blocks(inner, outer))
     pl.when(odd == 1)(lambda: blocks(outer, inner))
-    for s, out in enumerate(outs):
-        out[...] = half[scalars[s]]
-
-
-def transform(start, position, scalars, integrals, own, outer, inner):
+
+
+def transform(start, wants, integrals, own, outer, inner):
     shape = (integrals.shape[0], BLOCK, own.shape[1])
     return local_call(
         functools.partial(transform_kernel, start),
         "transform",
         [like(shape, jnp.bfloat16)] * GROUPS,
-        [IN_SMEM] * 2 + [IN_VMEM] * 4,
-        [IN_VMEM] * GROUPS,
+        5,
         2 * AO_DEV * math.prod(shape) * integrals.shape[2],
-        [pltpu.VMEM((AO_DEV, *shape), jnp.bfloat16)],
-    )(position, scalars, integrals, own, outer, inner)
-
-
-def form_pairs(pairs, position, blocks, grams):
-    here = position[0]
+    )(wants, integrals, own, outer, inner)
+
+
+def form_pairs(pairs, blocks, grams):
+    here = lax.axis_index("ao")
     slices = [[(ref, p) for ref in block for p in range(ref.shape[0])] for block in blocks]
 
     def product(left, right):
@@ -210,31 +209,38 @@
                 grams[k] = product(b, a)
 
 
-def early_kernel(position, table, live, *refs):
+def early_kernel(live, table, *refs):
     used = 3 * CHUNKS
     blocks = [refs[i : i + CHUNKS] for i in range(0, used, CHUNKS)]
     near, far, place, grams = refs[used:]
-    here, aux, orb = position[0], position[1], position[2]
-    slots = place.shape[0]
-    for s in range(slots):
-        a = table[0, here * slots + s] // AO_DEV ^ here
-        b = table[1, here * slots + s] // AO_DEV ^ here
-        low, high = jnp.minimum(a, b), jnp.maximum(a, b)
-        index = jnp.where(high == 3, low + 3, jnp.where(high == 2, low + 1, 0))
-        place[s] = jnp.where(s < live[here], index, len(ALL_PAIRS))
-    form_pairs(EARLY_PAIRS, position, blocks, grams)
+    here, aux, orb = (lax.axis_index(axis) for axis in ("ao", "aux", "orb"))
+    slots, width = place.shape
+    slot = lax.broadcasted_iota(jnp.int32, (slots, table.shape[1]), 0)
+    column = lax.broadcasted_iota(jnp.int32, (slots, table.shape[1]), 1)
+    shown = column == here * slots + slot
+    sides = []
+    for side in (0, 1):
+        group = (table[side : side + 1, :] // AO_DEV).astype(jnp.float32)
+        group = jnp.sum(jnp.where(shown, group, 0.0), axis=1, keepdims=True)
+        sides.append(group.astype(jnp.int32) ^ here)
+    low, high = jnp.minimum(*sides), jnp.maximum(*sides)
+    index = jnp.where(high == 3, low + 3, jnp.where(high == 2, low + 1, 0))
+    slot = lax.broadcasted_iota(jnp.int32, (slots, width), 0)
+    count = scalar_at(live[...], here).astype(jnp.int32)
+    place[...] = jnp.where(slot < count, index, len(ALL_PAIRS))
+    form_pairs(EARLY_PAIRS, blocks, grams)
     for k in range(len(EARLY_PAIRS)):
         for core in (0, 1):
             near[core, k] = grams[k, 2 * aux + (orb ^ core)]
             far[core, k] = grams[k, 2 * (1 - aux) + (orb ^ core)].astype(jnp.bfloat16)
 
 
-def late_kernel(position, *refs):
+def late_kernel(*refs):
     used = GROUPS * CHUNKS
     blocks = [refs[i : i + CHUNKS] for i in range(0, used, CHUNKS)]
     keep, give, grams = refs[used:]
-    aux, orb = position[1], position[2]
-    form_pairs(LATE_PAIRS, position, blocks, grams)
+    aux, orb = lax.axis_index("aux"), lax.axis_index("orb")
+    form_pairs(LATE_PAIRS, blocks, grams)
     for k in range(len(LATE_PAIRS)):
         for chip in (0, 1):
             row = 2 * (aux ^ chip)
@@ -251,7 +257,7 @@
     return (2, len(pairs), rows, BLOCK), pltpu.VMEM((len(pairs), 4, rows, BLOCK), jnp.float32)
 
 
-def early_pairs(position, table, live, blocks):
+def early_pairs(live, table, blocks):
     shape, grams = quarters(EARLY_PAIRS)
     return local_call(
         early_kernel,
@@ -259,26 +265,24 @@
         [
             like(shape, jnp.float32),
             like(shape, jnp.bfloat16),
-            like((table.shape[1] // GROUPS,), jnp.int32),
+            like((table.shape[1] // GROUPS, BLOCK), jnp.int32),
         ],
-        [IN_SMEM] * 3 + [IN_VMEM] * (3 * CHUNKS),
-        [IN_VMEM] * 2 + [IN_SMEM],
+        2 + 3 * CHUNKS,
         pair_flops(EARLY_PAIRS, blocks),
         [grams],
-    )(position, table, live, *[part for block in blocks for part in block])
-
-
-def late_pairs(position, blocks):
+    )(live.reshape(1, -1), table, *[part for block in blocks for part in block])
+
+
+def late_pairs(blocks):
     shape, grams = quarters(LATE_PAIRS)
     return local_call(
         late_kernel,
         "late_pairs",
         [like(shape, jnp.float32)] * 2,
-        [IN_SMEM] + [IN_VMEM] * (GROUPS * CHUNKS),
-        [IN_VMEM] * 2,
+        GROUPS * CHUNKS,
         pair_flops(LATE_PAIRS, blocks),
         [grams],
-    )(position, *[part for block in blocks for part in block])
+    )(*[part for block in blocks for part in block])
 
 
 def spread_kernel(factor, place, near0, far0, got0, near1, got1, far1, out, sums, rows, sems):
@@ -286,11 +290,7 @@
     sums[:early] = (near0[0] + far0[0].astype(jnp.float32) + got0[...]) * factor
     sums[early:] = (near1[0] + got1[0] + far1[...].astype(jnp.float32)) * factor
     total, slots, width = out.shape
-    slot = lax.broadcasted_iota(jnp.int32, (slots, width), 0)
-    source = jnp.zeros((slots, width), jnp.int32)
-    for s in range(slots):
-        source = jnp.where(slot == s, place[s], source)
-    masks = [source == k for k in range(sums.shape[0])]
+    masks = [place[...] == k for k in range(sums.shape[0])]
 
     def one(m, carry):
         row = jnp.zeros((slots, width), jnp.float32)
@@ -318,34 +318,33 @@
         functools.partial(spread_kernel, factor),
         "spread",
         [like(shape, jnp.float32)],
-        [IN_SMEM] + [IN_VMEM] * len(parts),
-        [IN_HBM],
+        1 + len(parts),
         6 * math.prod(shape),
         [
             pltpu.VMEM((len(ALL_PAIRS), rows, BLOCK), jnp.float32),
             pltpu.VMEM(shape, jnp.float32),
             pltpu.SemaphoreType.DMA((SPREAD_STEPS,)),
         ],
+        IN_HBM,
     )(place, *parts)[0]
 
 
 def six_pair_body(integrals, coeffs, pair_blocks, pair_count, orbital_count):
     width = coeffs.shape[1] // CHUNKS
     total_aux = integrals.shape[0] * lax.axis_size("aux")
-    position = jnp.stack([lax.axis_index(axis) for axis in ("ao", "aux", "orb")]).astype(jnp.int32)
     table = pair_blocks.T
 
     parts = [lax.slice_in_dim(coeffs, 0, width, axis=1)]
-    position, rest = lax.optimization_barrier((where(position), coeffs))
+    first, rest = lax.optimization_barrier((lead(), coeffs))
     for c in range(1, CHUNKS):
         parts.append(lax.slice_in_dim(rest, c * width, (c + 1) * width, axis=1))
     inner = [lax.ppermute(part, "ao", INSIDE) for part in parts]
     outer = [lax.ppermute(part, "ao", OUTSIDE) for part in parts]
-    scalars = tables(position, orbital_count, table)
+    wants = tables(first, orbital_count, table, width)
 
     blocks = [[] for _ in range(GROUPS)]
     for c, part in enumerate(parts):
-        pieces = transform(c * width, position, scalars, integrals, part, outer[c], inner[c])
+        pieces = transform(c * width, wants, integrals, part, outer[c], inner[c])
         for block, piece in zip(blocks, pieces):
             block.append(piece)
 
@@ -354,10 +353,10 @@
         return [lax.ppermute(piece, "ao", swap) for piece in blocks[s]]
 
     got = [blocks[0], fetch(1), fetch(2)]
-    near0, across0, place = early_pairs(position, table, pair_count, got)
+    near0, across0, place = early_pairs(pair_count, table, got)
     far0 = lax.ppermute(across0, "aux", SWAP)
     got.append(fetch(3))
-    near1, give1 = late_pairs(position, got)
+    near1, give1 = late_pairs(got)
     got1 = lax.ppermute(give1, "orb", SWAP)
     far1 = lax.ppermute((near1[1] + got1[1]).astype(jnp.bfloat16), "aux", SWAP)
     got0 = lax.ppermute(near0[1] + far0[1].astype(jnp.float32), "orb", SWAP)

time: 72.5 us -> 71.1 us (0.981)
  waiting for transfers between devices: 40.9 us -> 48 us
  Pallas kernels: 10.6 us -> 4.85 us
  starting transfers between devices: 19.6 us -> 16.8 us
    ppermute x2, waiting for transfers between devices: 2.05 us -> 5.3 us  [six_pair_body(): inner = [lax.ppermute(part, 'ao', INSIDE) for part in parts]]
    ppermute x6, starting transfers between devices: 9.54 us -> 6.56 us  [fetch(): return [lax.ppermute(piece, 'ao', swap) for piece in blocks[s]]]
    pallas_call x3, Pallas kernels: 3.8 us -> 1.01 us  [the longest x1 0.87 us: late_pairs(): local_call(late_kernel, 'late_pairs', [like(shape, jnp.float32)] * 2, GRO...]
    ppermute x2, waiting for transfers between devices: 4.64 us -> 6.74 us  [six_pair_body(): outer = [lax.ppermute(part, 'ao', OUTSIDE) for part in parts]]
    ppermute x6, waiting for transfers between devices: 29.7 us -> 31.5 us  [fetch(): return [lax.ppermute(piece, 'ao', swap) for piece in blocks[s]]]
    pallas_call x2, Pallas kernels: 2.94 us -> 1.71 us  [transform(): local_call(functools.partial(transform_kernel, start), 'transform', [like...]
    pallas_call x1, Pallas kernels: 2.2 us -> 0.98 us  [early_pairs(): local_call(early_kernel, 'early_pairs', [like(shape, jnp.float32), like(s...]
  transfers between devices with their start and end apart: 14 -> 14, of which waited for: 10 -> 11; matrix products, arithmetic and copies ran while one was open for 0% -> 0% of each run, Pallas kernels for 12% -> 5%
where the time goes in v6:
time: 71.1 us; the launch traced here: 71 us
  waiting for transfers between devices  48 us (68%)
  starting transfers between devices  16.8 us (24%)
  Pallas kernels  4.85 us (7%)
  local copies, waits for them, and re-layouts  1.02 us (1%)
    ppermute x6, waiting for transfers between devices, fetch(): return [lax.ppermute(piece, 'ao', swap) for piece in blocks[s]]  31.5 us
    ppermute x2, waiting for transfers between devices, six_pair_body(): outer = [lax.ppermute(part, 'ao', OUTSIDE) for part in parts]  6.74 us
    ppermute x6, starting transfers between devices, fetch(): return [lax.ppermute(piece, 'ao', swap) for piece in blocks[s]]  6.56 us
    ppermute x2, starting transfers between devices, six_pair_body(): inner = [lax.ppermute(part, 'ao', INSIDE) for part in parts]  6.11 us
    ppermute x2, waiting for transfers between devices, six_pair_body(): inner = [lax.ppermute(part, 'ao', INSIDE) for part in parts]  5.3 us
    ppermute x1, waiting for transfers between devices, six_pair_body(): far1 = lax.ppermute((near1[1] + got1[1]).astype(jnp.bfloat16), 'aux', SWAP)  3.34 us
    pallas_call x2, Pallas kernels, transform(): local_call(functools.partial(transform_kernel, start), 'transform', [like...  1.71 us
    ppermute x1, starting transfers between devices, six_pair_body(): far1 = lax.ppermute((near1[1] + got1[1]).astype(jnp.bfloat16), 'aux', SWAP)  1.55 us
  transfers between devices with their start and end apart: 14, of which 11 were waited for; matrix products, arithmetic and copies ran while one was open for 0% of the time, Pallas kernels for 5%

profile of v6, /device:TPU:8, one launch (start us, length us, event | category | flops | bytes accessed | tf_op | source)
XLA Modules:
  0.0 71.0 jit_solution(5202011182092268290)
XLA Ops:
  0.0 1.0 %slice.18.own = bf16[512,256]{1,0:T(8,128)(2,1)S(1)} slice(bf16[512,512]{1,0:T(8,128)(2,1)} %param.6), slice={[0:512], [0:256]} | slice | bytes 524288 | tf_op jit(solution)/shard_map/slice | solution.py:337
  1.0 3.7 %collective-permute-start.1 = (bf16[512,256]{1,0:T(8,128)(2,1)S(1)}, bf16[512,256]{1,0:T(8,128)(2,1)S(1)}, u32[]{:S(2)}, u32[]{:S(2)}) collective-permute-start(bf16[512,256]{1,0:T(8,128)(2,1)S(1)} %slice.18.own), channel_id=1, source_target_pairs={{4,8},{8,4},{5,9},{9,5},{6,10},{10,6},{7,11},{11,7},{20,24},{24,20... | collective-permute-start | bytes 786440 | tf_op jit(solution)/shard_map/ppermute | solution.py:341
  4.9 2.4 %collective-permute-start.3 = (bf16[512,256]{1,0:T(8,128)(2,1)S(1)}, bf16[512,256]{1,0:T(8,128)(2,1)S(1)}, u32[]{:S(2)}, u32[]{:S(2)}) collective-permute-start(bf16[512,256]{1,0:T(8,128)(2,1)S(1)} %slice.19.own), channel_id=1, source_target_pairs={{4,8},{8,4},{5,9},{9,5},{6,10},{10,6},{7,11},{11,7},{20,24},{24,20... | collective-permute-start | bytes 786440 | tf_op jit(solution)/shard_map/ppermute | solution.py:341
  7.8 4.6 %collective-permute-done.1.inner = bf16[512,256]{1,0:T(8,128)(2,1)S(1)} collective-permute-done((bf16[512,256]{1,0:T(8,128)(2,1)S(1)}, bf16[512,256]{1,0:T(8,128)(2,1)S(1)}, u32[]{:S(2)}, u32[]{:S(2)}) %collective-permute-start.1) | collective-permute-done | bytes 262176 | tf_op jit(solution)/shard_map/ppermute | solution.py:341
  12.4 1.7 %collective-permute-done.outer = bf16[512,256]{1,0:T(8,128)(2,1)S(1)} collective-permute-done((bf16[512,256]{1,0:T(8,128)(2,1)S(1)}, bf16[512,256]{1,0:T(8,128)(2,1)S(1)}, u32[]{:S(2)}, u32[]{:S(2)}) %collective-permute-start) | collective-permute-done | bytes 262176 | tf_op jit(solution)/shard_map/ppermute | solution.py:342
  14.1 0.9 %transform.2 = (bf16[2,256,256]{2,1,0:T(8,128)(2,1)S(1)}, bf16[2,256,256]{2,1,0:T(8,128)(2,1)S(1)}, bf16[2,256,256]{2,1,0:T(8,128)(2,1)S(1)}, bf16[2,256,256]{2,1,0:T(8,128)(2,1)S(1)}) custom-call(s32[8,256]{1,0:T(8,128)S(1)} %tables.1.wants, bf16[2,512,1280]{2,1,0:T(8,128)(2,1)S(1)} %copy-done, bf16[512,256]{1,0:T(8,128)(2,1)S(1)} %slice.18.own, ...), custom_call_target="tpu_custom_call" | custom-call | flops 671088640 | bytes 2097152 | tf_op jit(solution)/shard_map/transform/pallas_call | solution.py:175
  15.0 1.9 %collective-permute-start.6 = (bf16[2,256,256]{2,1,0:T(8,128)(2,1)S(1)}, bf16[2,256,256]{2,1,0:T(8,128)(2,1)S(1)}, u32[]{:S(2)}, u32[]{:S(2)}) collective-permute-start(bf16[2,256,256]{2,1,0:T(8,128)(2,1)S(1)} %get-tuple-element.26), channel_id=1, source_target_pairs={{0,8},{4,12},{8,0},{12,4},{1,9},{5,13},{9,1},{13,5},{2,10},{6,14},... | collective-permute-start | bytes 786440 | tf_op jit(solution)/shard_map/ppermute | solution.py:353
  16.9 0.7 %collective-permute-done.3.inner = bf16[512,256]{1,0:T(8,128)(2,1)S(1)} collective-permute-done((bf16[512,256]{1,0:T(8,128)(2,1)S(1)}, bf16[512,256]{1,0:T(8,128)(2,1)S(1)}, u32[]{:S(2)}, u32[]{:S(2)}) %collective-permute-start.3) | collective-permute-done | bytes 262176 | tf_op jit(solution)/shard_map/ppermute | solution.py:341
  17.7 5.0 %collective-permute-done.2.outer = bf16[512,256]{1,0:T(8,128)(2,1)S(1)} collective-permute-done((bf16[512,256]{1,0:T(8,128)(2,1)S(1)}, bf16[512,256]{1,0:T(8,128)(2,1)S(1)}, u32[]{:S(2)}, u32[]{:S(2)}) %collective-permute-start.2) | collective-permute-done | bytes 262176 | tf_op jit(solution)/shard_map/ppermute | solution.py:342
  22.7 0.9 %transform.3 = (bf16[2,256,256]{2,1,0:T(8,128)(2,1)S(1)}, bf16[2,256,256]{2,1,0:T(8,128)(2,1)S(1)}, bf16[2,256,256]{2,1,0:T(8,128)(2,1)S(1)}, bf16[2,256,256]{2,1,0:T(8,128)(2,1)S(1)}) custom-call(s32[8,256]{1,0:T(8,128)S(1)} %tables.1.wants, bf16[2,512,1280]{2,1,0:T(8,128)(2,1)S(1)} %copy-done, bf16[512,256]{1,0:T(8,128)(2,1)S(1)} %slice.19.own, ...), custom_call_target="tpu_custom_call" | custom-call | flops 671088640 | bytes 2097152 | tf_op jit(solution)/shard_map/transform/pallas_call | solution.py:175
  23.6 3.0 %collective-permute-start.5 = (bf16[2,256,256]{2,1,0:T(8,128)(2,1)S(1)}, bf16[2,256,256]{2,1,0:T(8,128)(2,1)S(1)}, u32[]{:S(2)}, u32[]{:S(2)}) collective-permute-start(bf16[2,256,256]{2,1,0:T(8,128)(2,1)S(1)} %get-tuple-element.25), channel_id=1, source_target_pairs={{0,4},{4,0},{8,12},{12,8},{1,5},{5,1},{9,13},{13,9},{2,6},{6,2},{1... | collective-permute-start | bytes 786440 | tf_op jit(solution)/shard_map/ppermute | solution.py:353
  26.6 1.5 %collective-permute-start.10 = (bf16[2,256,256]{2,1,0:T(8,128)(2,1)S(1)}, bf16[2,256,256]{2,1,0:T(8,128)(2,1)S(1)}, u32[]{:S(2)}, u32[]{:S(2)}) collective-permute-start(bf16[2,256,256]{2,1,0:T(8,128)(2,1)S(1)} %get-tuple-element.31), channel_id=1, source_target_pairs={{0,12},{4,8},{8,4},{12,0},{1,13},{5,9},{9,5},{13,1},{2,14},{6,10},... | collective-permute-start | bytes 786440 | tf_op jit(solution)/shard_map/ppermute | solution.py:353
  28.2 4.4 %collective-permute-done.4.refs_2_ = bf16[2,256,256]{2,1,0:T(8,128)(2,1)S(1)} collective-permute-done((bf16[2,256,256]{2,1,0:T(8,128)(2,1)S(1)}, bf16[2,256,256]{2,1,0:T(8,128)(2,1)S(1)}, u32[]{:S(2)}, u32[]{:S(2)}) %collective-permute-start.4) | collective-permute-done | bytes 262176 | tf_op jit(solution)/shard_map/ppermute | solution.py:353
  32.6 5.5 %collective-permute-done.5.refs_3_ = bf16[2,256,256]{2,1,0:T(8,128)(2,1)S(1)} collective-permute-done((bf16[2,256,256]{2,1,0:T(8,128)(2,1)S(1)}, bf16[2,256,256]{2,1,0:T(8,128)(2,1)S(1)}, u32[]{:S(2)}, u32[]{:S(2)}) %collective-permute-start.5) | collective-permute-done | bytes 262176 | tf_op jit(solution)/shard_map/ppermute | solution.py:353
  38.1 13.4 %collective-permute-done.7.refs_5_ = bf16[2,256,256]{2,1,0:T(8,128)(2,1)S(1)} collective-permute-done((bf16[2,256,256]{2,1,0:T(8,128)(2,1)S(1)}, bf16[2,256,256]{2,1,0:T(8,128)(2,1)S(1)}, u32[]{:S(2)}, u32[]{:S(2)}) %collective-permute-start.7) | collective-permute-done | bytes 262176 | tf_op jit(solution)/shard_map/ppermute | solution.py:353
  51.5 1.0 %early_pairs.1 = (f32[2,3,64,256]{3,2,1,0:T(8,128)S(1)}, bf16[2,3,64,256]{3,2,1,0:T(8,128)(2,1)S(1)}, s32[16,256]{1,0:T(8,128)S(1)}) custom-call(s32[1,4]{1,0:T(1,128)S(1)} %bitcast.9, s32[2,64]{1,0:T(2,128)S(1)} %bitcast.8, bf16[2,256,256]{2,1,0:T(8,128)(2,1)S(1)} %get-tuple-element.21.refs_0_, bf16[2,256,256]{2,1,0:T(8,128)(2,1)S(1)} %get-tuple-element.23.refs_1_, ...), custom_call_target="tpu_custom_call" | custom-call | flops 402653184 | bytes 1212416 | tf_op jit(solution)/shard_map/early_pairs/pallas_call | solution.py:262
  52.5 1.6 %collective-permute-start.8 = (bf16[2,3,64,256]{3,2,1,0:T(8,128)(2,1)S(1)}, bf16[2,3,64,256]{3,2,1,0:T(8,128)(2,1)S(1)}, u32[]{:S(2)}, u32[]{:S(2)}) collective-permute-start(bf16[2,3,64,256]{3,2,1,0:T(8,128)(2,1)S(1)} %get-tuple-element.30), channel_id=1, source_target_pairs={{0,2},{2,0},{1,3},{3,1},{4,6},{6,4},{5,7},{7,5},{8,10},{10,8},{9,1... | collective-permute-start | bytes 589832 | tf_op jit(solution)/shard_map/ppermute | solution.py:357
  54.0 4.4 %collective-permute-done.10.refs_6_ = bf16[2,256,256]{2,1,0:T(8,128)(2,1)S(1)} collective-permute-done((bf16[2,256,256]{2,1,0:T(8,128)(2,1)S(1)}, bf16[2,256,256]{2,1,0:T(8,128)(2,1)S(1)}, u32[]{:S(2)}, u32[]{:S(2)}) %collective-permute-start.10) | collective-permute-done | bytes 262176 | tf_op jit(solution)/shard_map/ppermute | solution.py:353
  58.5 3.7 %collective-permute-done.11.refs_7_ = bf16[2,256,256]{2,1,0:T(8,128)(2,1)S(1)} collective-permute-done((bf16[2,256,256]{2,1,0:T(8,128)(2,1)S(1)}, bf16[2,256,256]{2,1,0:T(8,128)(2,1)S(1)}, u32[]{:S(2)}, u32[]{:S(2)}) %collective-permute-start.11) | collective-permute-done | bytes 262176 | tf_op jit(solution)/shard_map/ppermute | solution.py:353
  62.2 0.9 %late_pairs.1 = (f32[2,3,64,256]{3,2,1,0:T(8,128)S(1)}, f32[2,3,64,256]{3,2,1,0:T(8,128)S(1)}) custom-call(bf16[2,256,256]{2,1,0:T(8,128)(2,1)S(1)} %get-tuple-element.21.refs_0_, bf16[2,256,256]{2,1,0:T(8,128)(2,1)S(1)} %get-tuple-element.23.refs_1_, bf16[2,256,256]{2,1,0:T(8,128)(2,1)S(1)} %collective-permute-done.4.refs_2_, ...), custom_call_target="tpu_custom_call" | custom-call | flops 402653184 | bytes 1572864 | tf_op jit(solution)/shard_map/late_pairs/pallas_call | solution.py:278
  63.7 1.1 %collective-permute-done.12.got1 = f32[2,3,64,256]{3,2,1,0:T(8,128)S(1)} collective-permute-done((f32[2,3,64,256]{3,2,1,0:T(8,128)S(1)}, f32[2,3,64,256]{3,2,1,0:T(8,128)S(1)}, u32[]{:S(2)}, u32[]{:S(2)}) %collective-permute-start.12) | collective-permute-done | bytes 393248 | tf_op jit(solution)/shard_map/ppermute | solution.py:360
  64.9 1.6 %collective-permute-start.13 = (bf16[3,64,256]{2,1,0:T(8,128)(2,1)S(1)}, bf16[3,64,256]{2,1,0:T(8,128)(2,1)S(1)}, u32[]{:S(2)}, u32[]{:S(2)}) collective-permute-start(bf16[3,64,256]{2,1,0:T(8,128)(2,1)S(1)} %fusion.1), channel_id=1, source_target_pairs={{0,2},{2,0},{1,3},{3,1},{4,6},{6,4},{5,7},{7,5},{8,10},{10,8},{9,1... | collective-permute-start | bytes 294920 | tf_op jit(solution)/shard_map/ppermute | solution.py:361
  66.5 3.3 %collective-permute-done.13.far1 = bf16[3,64,256]{2,1,0:T(8,128)(2,1)S(1)} collective-permute-done((bf16[3,64,256]{2,1,0:T(8,128)(2,1)S(1)}, bf16[3,64,256]{2,1,0:T(8,128)(2,1)S(1)}, u32[]{:S(2)}, u32[]{:S(2)}) %collective-permute-start.13) | collective-permute-done | bytes 98336 | tf_op jit(solution)/shard_map/ppermute | solution.py:361
  69.8 1.2 %spread.1 = f32[64,16,256]{2,1,0:T(8,128)} custom-call(s32[16,256]{1,0:T(8,128)S(1)} %get-tuple-element.28.place, f32[2,3,64,256]{3,2,1,0:T(8,128)S(1)} %get-tuple-element.29.near0, bf16[2,3,64,256]{3,2,1,0:T(8,128)(2,1)S(1)} %collective-permute-done.8.far0, f32[3,64,256]{2,1,0:T(8,128)S(1)} %collective-permute-done.9.got0, ...), custom_call_target="tpu_custom_call" | custom-call | flops 1572864 | bytes 2097152 | tf_op jit(solution)/shard_map/spread/pallas_call | solution.py:317
  (25 shorter events, 1.4 us)
Async XLA Ops:
  1.0 3.9 %copy-start.4 = (bf16[512,512]{1,0:T(8,128)(2,1)S(1)}, bf16[512,512]{1,0:T(8,128)(2,1)}, u32[]{:S(2)}) copy-start(bf16[512,512]{1,0:T(8,128)(2,1)} %param.6) | copy-start | bytes 1572868
  1.0 6.7 %copy-start.1 = (s32[64,2]{0,1:T(2,128)S(1)}, s32[64,2]{0,1:T(2,128)}, u32[]{:S(2)}) copy-start(s32[64,2]{0,1:T(2,128)} %param.7) | copy-start | bytes 1540
  1.0 6.7 %copy-start.3 = (s32[8]{0:T(128)S(1)}, s32[8]{0:T(128)}, u32[]{:S(2)}) copy-start(s32[8]{0:T(128)} %param.9) | copy-start | bytes 100
  1.0 13.1 %copy-start = (bf16[2,512,1280]{2,1,0:T(8,128)(2,1)S(1)}, bf16[2,512,1280]{2,1,0:T(8,128)(2,1)}, u32[]{:S(2)}) copy-start(bf16[2,512,1280]{2,1,0:T(8,128)(2,1)} %integrals.3) | copy-start | bytes 7864324
  1.0 11.3 %collective-permute-start.1 = (bf16[512,256]{1,0:T(8,128)(2,1)S(1)}, bf16[512,256]{1,0:T(8,128)(2,1)S(1)}, u32[]{:S(2)}, u32[]{:S(2)}) collective-permute-start(bf16[512,256]{1,0:T(8,128)(2,1)S(1)} %slice.18.own), channel_id=1, source_target_pairs={{4,8},{8,4},{5,9},{9,5},{6,10},{10,6},{7,11},{11,7},{20,24},{24,20... | collective-permute-start | bytes 786440 | tf_op jit(solution)/shard_map/ppermute | solution.py:341
  4.8 9.3 %collective-permute-start = (bf16[512,256]{1,0:T(8,128)(2,1)S(1)}, bf16[512,256]{1,0:T(8,128)(2,1)S(1)}, u32[]{:S(2)}, u32[]{:S(2)}) collective-permute-start(bf16[512,256]{1,0:T(8,128)(2,1)S(1)} %slice.18.own), channel_id=1, source_target_pairs={{0,4},{4,0},{8,12},{12,8},{1,5},{5,1},{9,13},{13,9},{2,6},{6,2},{1... | collective-permute-start | bytes 786440 | tf_op jit(solution)/shard_map/ppermute | solution.py:342
  4.9 12.8 %collective-permute-start.3 = (bf16[512,256]{1,0:T(8,128)(2,1)S(1)}, bf16[512,256]{1,0:T(8,128)(2,1)S(1)}, u32[]{:S(2)}, u32[]{:S(2)}) collective-permute-start(bf16[512,256]{1,0:T(8,128)(2,1)S(1)} %slice.19.own), channel_id=1, source_target_pairs={{4,8},{8,4},{5,9},{9,5},{6,10},{10,6},{7,11},{11,7},{20,24},{24,20... | collective-permute-start | bytes 786440 | tf_op jit(solution)/shard_map/ppermute | solution.py:341
  7.3 15.4 %collective-permute-start.2 = (bf16[512,256]{1,0:T(8,128)(2,1)S(1)}, bf16[512,256]{1,0:T(8,128)(2,1)S(1)}, u32[]{:S(2)}, u32[]{:S(2)}) collective-permute-start(bf16[512,256]{1,0:T(8,128)(2,1)S(1)} %slice.19.own), channel_id=1, source_target_pairs={{0,4},{4,0},{8,12},{12,8},{1,5},{5,1},{9,13},{13,9},{2,6},{6,2},{1... | collective-permute-start | bytes 786440 | tf_op jit(solution)/shard_map/ppermute | solution.py:342
  7.8 43.7 %copy-start.2 = (s32[4]{0:T(128)S(1)}, s32[4]{0:T(128)}, u32[]{:S(2)}) copy-start(s32[4]{0:T(128)} %param.8) | copy-start | bytes 52
  14.9 17.6 %collective-permute-start.4 = (bf16[2,256,256]{2,1,0:T(8,128)(2,1)S(1)}, bf16[2,256,256]{2,1,0:T(8,128)(2,1)S(1)}, u32[]{:S(2)}, u32[]{:S(2)}) collective-permute-start(bf16[2,256,256]{2,1,0:T(8,128)(2,1)S(1)} %get-tuple-element.24), channel_id=1, source_target_pairs={{0,4},{4,0},{8,12},{12,8},{1,5},{5,1},{9,13},{13,9},{2,6},{6,2},{1... | collective-permute-start | bytes 786440 | tf_op jit(solution)/shard_map/ppermute | solution.py:353
  15.0 17.6 %collective-permute-start.6 = (bf16[2,256,256]{2,1,0:T(8,128)(2,1)S(1)}, bf16[2,256,256]{2,1,0:T(8,128)(2,1)S(1)}, u32[]{:S(2)}, u32[]{:S(2)}) collective-permute-start(bf16[2,256,256]{2,1,0:T(8,128)(2,1)S(1)} %get-tuple-element.26), channel_id=1, source_target_pairs={{0,8},{4,12},{8,0},{12,4},{1,9},{5,13},{9,1},{13,5},{2,10},{6,14},... | collective-permute-start | bytes 786440 | tf_op jit(solution)/shard_map/ppermute | solution.py:353
  23.6 14.5 %collective-permute-start.5 = (bf16[2,256,256]{2,1,0:T(8,128)(2,1)S(1)}, bf16[2,256,256]{2,1,0:T(8,128)(2,1)S(1)}, u32[]{:S(2)}, u32[]{:S(2)}) collective-permute-start(bf16[2,256,256]{2,1,0:T(8,128)(2,1)S(1)} %get-tuple-element.25), channel_id=1, source_target_pairs={{0,4},{4,0},{8,12},{12,8},{1,5},{5,1},{9,13},{13,9},{2,6},{6,2},{1... | collective-permute-start | bytes 786440 | tf_op jit(solution)/shard_map/ppermute | solution.py:353
  26.6 24.9 %collective-permute-start.7 = (bf16[2,256,256]{2,1,0:T(8,128)(2,1)S(1)}, bf16[2,256,256]{2,1,0:T(8,128)(2,1)S(1)}, u32[]{:S(2)}, u32[]{:S(2)}) collective-permute-start(bf16[2,256,256]{2,1,0:T(8,128)(2,1)S(1)} %get-tuple-element.27), channel_id=1, source_target_pairs={{0,8},{4,12},{8,0},{12,4},{1,9},{5,13},{9,1},{13,5},{2,10},{6,14},... | collective-permute-start | bytes 786440 | tf_op jit(solution)/shard_map/ppermute | solution.py:353
  26.6 31.9 %collective-permute-start.10 = (bf16[2,256,256]{2,1,0:T(8,128)(2,1)S(1)}, bf16[2,256,256]{2,1,0:T(8,128)(2,1)S(1)}, u32[]{:S(2)}, u32[]{:S(2)}) collective-permute-start(bf16[2,256,256]{2,1,0:T(8,128)(2,1)S(1)} %get-tuple-element.31), channel_id=1, source_target_pairs={{0,12},{4,8},{8,4},{12,0},{1,13},{5,9},{9,5},{13,1},{2,14},{6,10},... | collective-permute-start | bytes 786440 | tf_op jit(solution)/shard_map/ppermute | solution.py:353
  32.6 29.6 %collective-permute-start.11 = (bf16[2,256,256]{2,1,0:T(8,128)(2,1)S(1)}, bf16[2,256,256]{2,1,0:T(8,128)(2,1)S(1)}, u32[]{:S(2)}, u32[]{:S(2)}) collective-permute-start(bf16[2,256,256]{2,1,0:T(8,128)(2,1)S(1)} %get-tuple-element.32), channel_id=1, source_target_pairs={{0,12},{4,8},{8,4},{12,0},{1,13},{5,9},{9,5},{13,1},{2,14},{6,10},... | collective-permute-start | bytes 786440 | tf_op jit(solution)/shard_map/ppermute | solution.py:353
  52.5 10.7 %collective-permute-start.8 = (bf16[2,3,64,256]{3,2,1,0:T(8,128)(2,1)S(1)}, bf16[2,3,64,256]{3,2,1,0:T(8,128)(2,1)S(1)}, u32[]{:S(2)}, u32[]{:S(2)}) collective-permute-start(bf16[2,3,64,256]{3,2,1,0:T(8,128)(2,1)S(1)} %get-tuple-element.30), channel_id=1, source_target_pairs={{0,2},{2,0},{1,3},{3,1},{4,6},{6,4},{5,7},{7,5},{8,10},{10,8},{9,1... | collective-permute-start | bytes 589832 | tf_op jit(solution)/shard_map/ppermute | solution.py:357
  63.1 1.8 %collective-permute-start.12 = (f32[2,3,64,256]{3,2,1,0:T(8,128)S(1)}, f32[2,3,64,256]{3,2,1,0:T(8,128)S(1)}, u32[]{:S(2)}, u32[]{:S(2)}) collective-permute-start(f32[2,3,64,256]{3,2,1,0:T(8,128)S(1)} %get-tuple-element.34), channel_id=1, source_target_pairs={{0,1},{1,0},{2,3},{3,2},{4,5},{5,4},{6,7},{7,6},{8,9},{9,8},{10,11... | collective-permute-start | bytes 1179656 | tf_op jit(solution)/shard_map/ppermute | solution.py:360
  63.2 3.3 %collective-permute-start.9 = (f32[3,64,256]{2,1,0:T(8,128)S(1)}, f32[3,64,256]{2,1,0:T(8,128)S(1)}, u32[]{:S(2)}, u32[]{:S(2)}) collective-permute-start(f32[3,64,256]{2,1,0:T(8,128)S(1)} %add_bitcast_fusion), channel_id=1, source_target_pairs={{0,1},{1,0},{2,3},{3,2},{4,5},{5,4},{6,7},{7,6},{8,9},{9,8},{10,11... | collective-permute-start | bytes 589832 | tf_op jit(solution)/shard_map/ppermute | solution.py:362
  64.9 4.9 %collective-permute-start.13 = (bf16[3,64,256]{2,1,0:T(8,128)(2,1)S(1)}, bf16[3,64,256]{2,1,0:T(8,128)(2,1)S(1)}, u32[]{:S(2)}, u32[]{:S(2)}) collective-permute-start(bf16[3,64,256]{2,1,0:T(8,128)(2,1)S(1)} %fusion.1), channel_id=1, source_target_pairs={{0,2},{2,0},{1,3},{3,1},{4,6},{6,4},{5,7},{7,5},{8,10},{10,8},{9,1... | collective-permute-start | bytes 294920 | tf_op jit(solution)/shard_map/ppermute | solution.py:361

commit v7 on v6

--- a/solution.py
+++ b/solution.py
@@ -170,6 +170,27 @@
     pl.when(odd == 1)(lambda: blocks(outer, inner))
 
 
+def shared_kernel(start, wants, integrals, own, outer, inner, swapped, *refs):
+    *outs, whole = refs
+    aux = lax.axis_index("aux")
+    width = inner.shape[1]
+    whole[:, pl.ds(pl.multiple_of(aux * width, width), width)] = inner[...]
+    whole[:, pl.ds(pl.multiple_of((1 - aux) * width, width), width)] = swapped[...]
+    transform_kernel(start, wants, integrals, own, outer, whole, *outs)
+
+
+def shared_transform(start, wants, integrals, own, outer, inner, swapped):
+    shape = (integrals.shape[0], BLOCK, own.shape[1])
+    return local_call(
+        functools.partial(shared_kernel, start),
+        "transform",
+        [like(shape, jnp.bfloat16)] * GROUPS,
+        6,
+        2 * AO_DEV * math.prod(shape) * integrals.shape[2],
+        [pltpu.VMEM(own.shape, jnp.bfloat16)],
+    )(wants, integrals, own, outer, inner, swapped)
+
+
 def transform(start, wants, integrals, own, outer, inner):
     shape = (integrals.shape[0], BLOCK, own.shape[1])
     return local_call(
@@ -211,7 +232,8 @@
 
 def early_kernel(live, table, *refs):
     used = 3 * CHUNKS
-    blocks = [refs[i : i + CHUNKS] for i in range(0, used, CHUNKS)]
+    own, middle, next_to = [refs[i : i + CHUNKS] for i in range(0, used, CHUNKS)]
+    blocks = own, next_to, middle
     near, far, place, grams = refs[used:]
     here, aux, orb = (lax.axis_index(axis) for axis in ("ao", "aux", "orb"))
     slots, width = place.shape
@@ -237,7 +259,8 @@
 
 def late_kernel(*refs):
     used = GROUPS * CHUNKS
-    blocks = [refs[i : i + CHUNKS] for i in range(0, used, CHUNKS)]
+    own, middle, next_to, last = [refs[i : i + CHUNKS] for i in range(0, used, CHUNKS)]
+    blocks = own, next_to, middle, last
     keep, give, grams = refs[used:]
     aux, orb = lax.axis_index("aux"), lax.axis_index("orb")
     form_pairs(LATE_PAIRS, blocks, grams)
@@ -270,7 +293,7 @@
         2 + 3 * CHUNKS,
         pair_flops(EARLY_PAIRS, blocks),
         [grams],
-    )(live.reshape(1, -1), table, *[part for block in blocks for part in block])
+    )(live.reshape(1, -1), table, *blocks[0], *blocks[2], *blocks[1])
 
 
 def late_pairs(blocks):
@@ -282,7 +305,7 @@
         GROUPS * CHUNKS,
         pair_flops(LATE_PAIRS, blocks),
         [grams],
-    )(*[part for block in blocks for part in block])
+    )(*blocks[0], *blocks[2], *blocks[1], *blocks[3])
 
 
 def spread_kernel(factor, place, near0, far0, got0, near1, got1, far1, out, sums, rows, sems):
@@ -334,25 +357,31 @@
     total_aux = integrals.shape[0] * lax.axis_size("aux")
     table = pair_blocks.T
 
+    half = width // 2
     parts = [lax.slice_in_dim(coeffs, 0, width, axis=1)]
     first, rest = lax.optimization_barrier((lead(), coeffs))
-    for c in range(1, CHUNKS):
-        parts.append(lax.slice_in_dim(rest, c * width, (c + 1) * width, axis=1))
-    inner = [lax.ppermute(part, "ao", INSIDE) for part in parts]
+    parts.append(lax.slice_in_dim(rest, width, 2 * width, axis=1))
+    mine = lax.dynamic_slice_in_dim(rest, width + lax.axis_index("aux") * half, half, axis=1)
+    inner = [lax.ppermute(part, "ao", INSIDE) for part in (parts[0], mine)]
     outer = [lax.ppermute(part, "ao", OUTSIDE) for part in parts]
     wants = tables(first, orbital_count, table, width)
 
-    blocks = [[] for _ in range(GROUPS)]
-    for c, part in enumerate(parts):
-        pieces = transform(c * width, wants, integrals, part, outer[c], inner[c])
-        for block, piece in zip(blocks, pieces):
-            block.append(piece)
+    pieces = list(transform(0, wants, integrals, parts[0], outer[0], inner[0]))
+    blocks = [[piece] for piece in pieces]
+    inner[1], blocks[0][0] = lax.optimization_barrier((inner[1], blocks[0][0]))
+    swapped = lax.ppermute(inner[1], "aux", SWAP)
+    pieces = shared_transform(
+        width, wants, integrals, parts[1], outer[1], inner[1], swapped
+    )
+    for block, piece in zip(blocks, pieces):
+        block.append(piece)
 
     def fetch(s):
         swap = [(j, j ^ s) for j in range(GROUPS)]
         return [lax.ppermute(piece, "ao", swap) for piece in blocks[s]]
 
-    got = [blocks[0], fetch(1), fetch(2)]
+    middle = fetch(2)
+    got = [blocks[0], fetch(1), middle]
     near0, across0, place = early_pairs(pair_count, table, got)
     far0 = lax.ppermute(across0, "aux", SWAP)
     got.append(fetch(3))

time: 71.1 us -> 68.8 us (0.968)
  waiting for transfers between devices: 48 us -> 41.6 us
  starting transfers between devices: 16.8 us -> 18.9 us
  local copies, waits for them, and re-layouts: 1.02 us -> 2.88 us
    ppermute x2 -> x3, waiting for transfers between devices: 5.3 us -> 2.71 us  [the longest x2 2.71 us: six_pair_body(): inner = [lax.ppermute(part, 'ao', INSIDE) for part in (parts[0], mine)]]
    ppermute x2, waiting for transfers between devices: 6.74 us -> 4.39 us  [six_pair_body(): outer = [lax.ppermute(part, 'ao', OUTSIDE) for part in parts]]
    ppermute x2 -> x3, starting transfers between devices: 6.11 us -> 7.66 us  [the longest x2 6.11 us: six_pair_body(): inner = [lax.ppermute(part, 'ao', INSIDE) for part in (parts[0], mine)]]
    ppermute x6, waiting for transfers between devices: 31.5 us -> 30.1 us  [fetch(): return [lax.ppermute(piece, 'ao', swap) for piece in blocks[s]]]
    slice x1, local copies, waits for them, and re-layouts: 0.02 us -> 0.97 us  [six_pair_body(): parts.append(lax.slice_in_dim(rest, width, 2 * width, axis=1))]
    pallas_call x0 -> x1, Pallas kernels: none -> 0.93 us  [shared_transform(): local_call(functools.partial(shared_kernel, start), 'transform', [like(sh...]
    dynamic_slice x0 -> x1, local copies, waits for them, and re-layouts: none -> 0.92 us  [six_pair_body(): lax.dynamic_slice_in_dim(rest, width + lax.axis_index('aux') * half, half...]
    pallas_call x2 -> x1, Pallas kernels: 1.71 us -> 0.85 us  [transform(): local_call(functools.partial(transform_kernel, start), 'transform', [like...]
  transfers between devices with their start and end apart: 14 -> 15, of which waited for: 11 -> 11; matrix products, arithmetic and copies ran while one was open for 0% -> 3% of each run, Pallas kernels for 5% -> 6%
where the time goes in v7:
time: 68.8 us; the launch traced here: 68.6 us
  waiting for transfers between devices  41.6 us (60%)
  starting transfers between devices  18.9 us (27%)
  Pallas kernels  4.93 us (7%)
  local copies, waits for them, and re-layouts  2.88 us (4%)
    ppermute x6, waiting for transfers between devices, fetch(): return [lax.ppermute(piece, 'ao', swap) for piece in blocks[s]]  30.1 us
    ppermute x6, starting transfers between devices, fetch(): return [lax.ppermute(piece, 'ao', swap) for piece in blocks[s]]  7.09 us
    ppermute x2, starting transfers between devices, six_pair_body(): inner = [lax.ppermute(part, 'ao', INSIDE) for part in (parts[0], mine)]  6.11 us
    ppermute x2, waiting for transfers between devices, six_pair_body(): outer = [lax.ppermute(part, 'ao', OUTSIDE) for part in parts]  4.39 us
    ppermute x1, waiting for transfers between devices, six_pair_body(): far1 = lax.ppermute((near1[1] + got1[1]).astype(jnp.bfloat16), 'aux', SWAP)  3.34 us
    ppermute x2, waiting for transfers between devices, six_pair_body(): inner = [lax.ppermute(part, 'ao', INSIDE) for part in (parts[0], mine)]  2.71 us
    ppermute x1, starting transfers between devices, six_pair_body(): swapped = lax.ppermute(inner[1], 'aux', SWAP)  1.56 us
    ppermute x1, starting transfers between devices, six_pair_body(): far0 = lax.ppermute(across0, 'aux', SWAP)  1.55 us
  transfers between devices with their start and end apart: 15, of which 11 were waited for; matrix products, arithmetic and copies ran while one was open for 3% of the time, Pallas kernels for 6%

profile of v7, /device:TPU:8, one launch (start us, length us, event | category | flops | bytes accessed | tf_op | source)
XLA Modules:
  0.0 68.6 jit_solution(7880730918119232950)
XLA Ops:
  0.0 1.0 %slice.18.own = bf16[512,256]{1,0:T(8,128)(2,1)S(1)} slice(bf16[512,512]{1,0:T(8,128)(2,1)} %param.6), slice={[0:512], [0:256]} | slice | bytes 524288 | tf_op jit(solution)/shard_map/slice | solution.py:361
  1.0 3.7 %collective-permute-start.2 = (bf16[512,256]{1,0:T(8,128)(2,1)S(1)}, bf16[512,256]{1,0:T(8,128)(2,1)S(1)}, u32[]{:S(2)}, u32[]{:S(2)}) collective-permute-start(bf16[512,256]{1,0:T(8,128)(2,1)S(1)} %slice.18.own), channel_id=1, source_target_pairs={{4,8},{8,4},{5,9},{9,5},{6,10},{10,6},{7,11},{11,7},{20,24},{24,20... | collective-permute-start | bytes 786440 | tf_op jit(solution)/shard_map/ppermute | solution.py:365
  4.9 0.9 %constant_dynamic-slice_fusion = bf16[512,128]{1,0:T(8,128)(2,1)S(1)} fusion(bf16[512,512]{1,0:T(8,128)(2,1)} %param.6, s32[]{:T(128)S(6)} %select_n.3), kind=kLoop, calls=%fused_computation.4 | loop fusion | bytes 262148 | tf_op jit(solution)/shard_map/dynamic_slice | solution.py:364
  5.8 2.4 %collective-permute-start = (bf16[512,128]{1,0:T(8,128)(2,1)S(1)}, bf16[512,128]{1,0:T(8,128)(2,1)S(1)}, u32[]{:S(2)}, u32[]{:S(2)}) collective-permute-start(bf16[512,128]{1,0:T(8,128)(2,1)S(1)} %constant_dynamic-slice_fusion), channel_id=1, source_target_pairs={{4,8},{8,4},{5,9},{9,5},{6,10},{10,6},{7,11},{11,7},{20,24},{24,20... | collective-permute-start | bytes 393224 | tf_op jit(solution)/shard_map/ppermute | solution.py:365
  8.1 1.0 %slice.19.own = bf16[512,256]{1,0:T(8,128)(2,1)S(1)} slice(bf16[512,512]{1,0:T(8,128)(2,1)} %param.6), slice={[0:512], [256:512]} | slice | bytes 524288 | tf_op jit(solution)/shard_map/slice | solution.py:363
  9.7 2.7 %collective-permute-done.2.inner = bf16[512,256]{1,0:T(8,128)(2,1)S(1)} collective-permute-done((bf16[512,256]{1,0:T(8,128)(2,1)S(1)}, bf16[512,256]{1,0:T(8,128)(2,1)S(1)}, u32[]{:S(2)}, u32[]{:S(2)}) %collective-permute-start.2) | collective-permute-done | bytes 262176 | tf_op jit(solution)/shard_map/ppermute | solution.py:365
  12.4 1.7 %collective-permute-done.1.outer = bf16[512,256]{1,0:T(8,128)(2,1)S(1)} collective-permute-done((bf16[512,256]{1,0:T(8,128)(2,1)S(1)}, bf16[512,256]{1,0:T(8,128)(2,1)S(1)}, u32[]{:S(2)}, u32[]{:S(2)}) %collective-permute-start.1) | collective-permute-done | bytes 262176 | tf_op jit(solution)/shard_map/ppermute | solution.py:366
  15.0 1.6 %collective-permute-start.4 = (bf16[512,128]{1,0:T(8,128)(2,1)S(1)}, bf16[512,128]{1,0:T(8,128)(2,1)S(1)}, u32[]{:S(2)}, u32[]{:S(2)}) collective-permute-start(bf16[512,128]{1,0:T(8,128)(2,1)S(1)} %collective-permute-done.inner), channel_id=1, source_target_pairs={{0,2},{2,0},{1,3},{3,1},{4,6},{6,4},{5,7},{7,5},{8,10},{10,8},{9,1... | collective-permute-start | bytes 393224 | tf_op jit(solution)/shard_map/ppermute | solution.py:372
  16.6 1.3 %collective-permute-start.7 = (bf16[2,256,256]{2,1,0:T(8,128)(2,1)S(1)}, bf16[2,256,256]{2,1,0:T(8,128)(2,1)S(1)}, u32[]{:S(2)}, u32[]{:S(2)}) collective-permute-start(bf16[2,256,256]{2,1,0:T(8,128)(2,1)S(1)} %get-tuple-element.30), channel_id=1, source_target_pairs={{0,4},{4,0},{8,12},{12,8},{1,5},{5,1},{9,13},{13,9},{2,6},{6,2},{1... | collective-permute-start | bytes 786440 | tf_op jit(solution)/shard_map/ppermute | solution.py:381
  17.8 2.7 %collective-permute-done.3.outer = bf16[512,256]{1,0:T(8,128)(2,1)S(1)} collective-permute-done((bf16[512,256]{1,0:T(8,128)(2,1)S(1)}, bf16[512,256]{1,0:T(8,128)(2,1)S(1)}, u32[]{:S(2)}, u32[]{:S(2)}) %collective-permute-start.3) | collective-permute-done | bytes 262176 | tf_op jit(solution)/shard_map/ppermute | solution.py:366
  20.5 0.9 %transform.3 = (bf16[2,256,256]{2,1,0:T(8,128)(2,1)S(1)}, bf16[2,256,256]{2,1,0:T(8,128)(2,1)S(1)}, bf16[2,256,256]{2,1,0:T(8,128)(2,1)S(1)}, bf16[2,256,256]{2,1,0:T(8,128)(2,1)S(1)}) custom-call(s32[8,256]{1,0:T(8,128)S(1)} %tables.1.wants, bf16[2,512,1280]{2,1,0:T(8,128)(2,1)S(1)} %copy-done, bf16[512,256]{1,0:T(8,128)(2,1)S(1)} %slice.19.own, ...), custom_call_target="tpu_custom_call" | custom-call | flops 671088640 | bytes 2097152 | tf_op jit(solution)/shard_map/transform/pallas_call | solution.py:184
  21.5 3.1 %collective-permute-start.6 = (bf16[2,256,256]{2,1,0:T(8,128)(2,1)S(1)}, bf16[2,256,256]{2,1,0:T(8,128)(2,1)S(1)}, u32[]{:S(2)}, u32[]{:S(2)}) collective-permute-start(bf16[2,256,256]{2,1,0:T(8,128)(2,1)S(1)} %get-tuple-element.29), channel_id=1, source_target_pairs={{0,8},{4,12},{8,0},{12,4},{1,9},{5,13},{9,1},{13,5},{2,10},{6,14},... | collective-permute-start | bytes 786440 | tf_op jit(solution)/shard_map/ppermute | solution.py:381
  25.6 1.7 %collective-permute-start.12 = (bf16[2,256,256]{2,1,0:T(8,128)(2,1)S(1)}, bf16[2,256,256]{2,1,0:T(8,128)(2,1)S(1)}, u32[]{:S(2)}, u32[]{:S(2)}) collective-permute-start(bf16[2,256,256]{2,1,0:T(8,128)(2,1)S(1)} %get-tuple-element.36), channel_id=1, source_target_pairs={{0,12},{4,8},{8,4},{12,0},{1,13},{5,9},{9,5},{13,1},{2,14},{6,10},... | collective-permute-start | bytes 786440 | tf_op jit(solution)/shard_map/ppermute | solution.py:381
  27.4 4.4 %collective-permute-done.7.refs_4_ = bf16[2,256,256]{2,1,0:T(8,128)(2,1)S(1)} collective-permute-done((bf16[2,256,256]{2,1,0:T(8,128)(2,1)S(1)}, bf16[2,256,256]{2,1,0:T(8,128)(2,1)S(1)}, u32[]{:S(2)}, u32[]{:S(2)}) %collective-permute-start.7) | collective-permute-done | bytes 262176 | tf_op jit(solution)/shard_map/ppermute | solution.py:381
  31.7 5.2 %collective-permute-done.6.refs_3_ = bf16[2,256,256]{2,1,0:T(8,128)(2,1)S(1)} collective-permute-done((bf16[2,256,256]{2,1,0:T(8,128)(2,1)S(1)}, bf16[2,256,256]{2,1,0:T(8,128)(2,1)S(1)}, u32[]{:S(2)}, u32[]{:S(2)}) %collective-permute-start.6) | collective-permute-done | bytes 262176 | tf_op jit(solution)/shard_map/ppermute | solution.py:381
  37.0 5.3 %collective-permute-done.8.refs_5_ = bf16[2,256,256]{2,1,0:T(8,128)(2,1)S(1)} collective-permute-done((bf16[2,256,256]{2,1,0:T(8,128)(2,1)S(1)}, bf16[2,256,256]{2,1,0:T(8,128)(2,1)S(1)}, u32[]{:S(2)}, u32[]{:S(2)}) %collective-permute-start.8) | collective-permute-done | bytes 262176 | tf_op jit(solution)/shard_map/ppermute | solution.py:381
  42.2 1.0 %early_pairs.1 = (f32[2,3,64,256]{3,2,1,0:T(8,128)S(1)}, bf16[2,3,64,256]{3,2,1,0:T(8,128)(2,1)S(1)}, s32[16,256]{1,0:T(8,128)S(1)}) custom-call(s32[1,4]{1,0:T(1,128)S(1)} %bitcast.9, s32[2,64]{1,0:T(2,128)S(1)} %bitcast.8, bf16[2,256,256]{2,1,0:T(8,128)(2,1)S(1)} %get-tuple-element.25.refs_0_, bf16[2,256,256]{2,1,0:T(8,128)(2,1)S(1)} %get-tuple-element.27.refs_1_, ...), custom_call_target="tpu_custom_call" | custom-call | flops 402653184 | bytes 1212416 | tf_op jit(solution)/shard_map/early_pairs/pallas_call | solution.py:285
  43.2 1.6 %collective-permute-start.9 = (bf16[2,3,64,256]{3,2,1,0:T(8,128)(2,1)S(1)}, bf16[2,3,64,256]{3,2,1,0:T(8,128)(2,1)S(1)}, u32[]{:S(2)}, u32[]{:S(2)}) collective-permute-start(bf16[2,3,64,256]{3,2,1,0:T(8,128)(2,1)S(1)} %get-tuple-element.34), channel_id=1, source_target_pairs={{0,2},{2,0},{1,3},{3,1},{4,6},{6,4},{5,7},{7,5},{8,10},{10,8},{9,1... | collective-permute-start | bytes 589832 | tf_op jit(solution)/shard_map/ppermute | solution.py:386
  44.8 11.1 %collective-permute-done.11.refs_6_ = bf16[2,256,256]{2,1,0:T(8,128)(2,1)S(1)} collective-permute-done((bf16[2,256,256]{2,1,0:T(8,128)(2,1)S(1)}, bf16[2,256,256]{2,1,0:T(8,128)(2,1)S(1)}, u32[]{:S(2)}, u32[]{:S(2)}) %collective-permute-start.11) | collective-permute-done | bytes 262176 | tf_op jit(solution)/shard_map/ppermute | solution.py:381
  55.9 3.9 %collective-permute-done.12.refs_7_ = bf16[2,256,256]{2,1,0:T(8,128)(2,1)S(1)} collective-permute-done((bf16[2,256,256]{2,1,0:T(8,128)(2,1)S(1)}, bf16[2,256,256]{2,1,0:T(8,128)(2,1)S(1)}, u32[]{:S(2)}, u32[]{:S(2)}) %collective-permute-start.12) | collective-permute-done | bytes 262176 | tf_op jit(solution)/shard_map/ppermute | solution.py:381
  61.4 1.1 %collective-permute-done.13.got1 = f32[2,3,64,256]{3,2,1,0:T(8,128)S(1)} collective-permute-done((f32[2,3,64,256]{3,2,1,0:T(8,128)S(1)}, f32[2,3,64,256]{3,2,1,0:T(8,128)S(1)}, u32[]{:S(2)}, u32[]{:S(2)}) %collective-permute-start.13) | collective-permute-done | bytes 393248 | tf_op jit(solution)/shard_map/ppermute | solution.py:389
  62.5 1.6 %collective-permute-start.14 = (bf16[3,64,256]{2,1,0:T(8,128)(2,1)S(1)}, bf16[3,64,256]{2,1,0:T(8,128)(2,1)S(1)}, u32[]{:S(2)}, u32[]{:S(2)}) collective-permute-start(bf16[3,64,256]{2,1,0:T(8,128)(2,1)S(1)} %fusion.1), channel_id=1, source_target_pairs={{0,2},{2,0},{1,3},{3,1},{4,6},{6,4},{5,7},{7,5},{8,10},{10,8},{9,1... | collective-permute-start | bytes 294920 | tf_op jit(solution)/shard_map/ppermute | solution.py:390
  64.1 3.3 %collective-permute-done.14.far1 = bf16[3,64,256]{2,1,0:T(8,128)(2,1)S(1)} collective-permute-done((bf16[3,64,256]{2,1,0:T(8,128)(2,1)S(1)}, bf16[3,64,256]{2,1,0:T(8,128)(2,1)S(1)}, u32[]{:S(2)}, u32[]{:S(2)}) %collective-permute-start.14) | collective-permute-done | bytes 98336 | tf_op jit(solution)/shard_map/ppermute | solution.py:390
  67.4 1.2 %spread.1 = f32[64,16,256]{2,1,0:T(8,128)} custom-call(s32[16,256]{1,0:T(8,128)S(1)} %get-tuple-element.32.place, f32[2,3,64,256]{3,2,1,0:T(8,128)S(1)} %get-tuple-element.33.near0, bf16[2,3,64,256]{3,2,1,0:T(8,128)(2,1)S(1)} %collective-permute-done.9.far0, f32[3,64,256]{2,1,0:T(8,128)S(1)} %collective-permute-done.10.got0, ...), custom_call_target="tpu_custom_call" | custom-call | flops 1572864 | bytes 2097152 | tf_op jit(solution)/shard_map/spread/pallas_call | solution.py:340
  (26 shorter events, 4.1 us)
Async XLA Ops:
  1.0 8.5 %copy-start.1 = (s32[64,2]{0,1:T(2,128)S(1)}, s32[64,2]{0,1:T(2,128)}, u32[]{:S(2)}) copy-start(s32[64,2]{0,1:T(2,128)} %param.7) | copy-start | bytes 1540
  1.0 8.5 %copy-start.3 = (s32[8]{0:T(128)S(1)}, s32[8]{0:T(128)}, u32[]{:S(2)}) copy-start(s32[8]{0:T(128)} %param.9) | copy-start | bytes 100
  1.0 13.1 %copy-start = (bf16[2,512,1280]{2,1,0:T(8,128)(2,1)S(1)}, bf16[2,512,1280]{2,1,0:T(8,128)(2,1)}, u32[]{:S(2)}) copy-start(bf16[2,512,1280]{2,1,0:T(8,128)(2,1)} %integrals.3) | copy-start | bytes 7864324
  1.0 11.3 %collective-permute-start.2 = (bf16[512,256]{1,0:T(8,128)(2,1)S(1)}, bf16[512,256]{1,0:T(8,128)(2,1)S(1)}, u32[]{:S(2)}, u32[]{:S(2)}) collective-permute-start(bf16[512,256]{1,0:T(8,128)(2,1)S(1)} %slice.18.own), channel_id=1, source_target_pairs={{4,8},{8,4},{5,9},{9,5},{6,10},{10,6},{7,11},{11,7},{20,24},{24,20... | collective-permute-start | bytes 786440 | tf_op jit(solution)/shard_map/ppermute | solution.py:365
  4.8 9.3 %collective-permute-start.1 = (bf16[512,256]{1,0:T(8,128)(2,1)S(1)}, bf16[512,256]{1,0:T(8,128)(2,1)S(1)}, u32[]{:S(2)}, u32[]{:S(2)}) collective-permute-start(bf16[512,256]{1,0:T(8,128)(2,1)S(1)} %slice.18.own), channel_id=1, source_target_pairs={{0,4},{4,0},{8,12},{12,8},{1,5},{5,1},{9,13},{13,9},{2,6},{6,2},{1... | collective-permute-start | bytes 786440 | tf_op jit(solution)/shard_map/ppermute | solution.py:366
  5.8 9.2 %collective-permute-start = (bf16[512,128]{1,0:T(8,128)(2,1)S(1)}, bf16[512,128]{1,0:T(8,128)(2,1)S(1)}, u32[]{:S(2)}, u32[]{:S(2)}) collective-permute-start(bf16[512,128]{1,0:T(8,128)(2,1)S(1)} %constant_dynamic-slice_fusion), channel_id=1, source_target_pairs={{4,8},{8,4},{5,9},{9,5},{6,10},{10,6},{7,11},{11,7},{20,24},{24,20... | collective-permute-start | bytes 393224 | tf_op jit(solution)/shard_map/ppermute | solution.py:365
  9.1 11.4 %collective-permute-start.3 = (bf16[512,256]{1,0:T(8,128)(2,1)S(1)}, bf16[512,256]{1,0:T(8,128)(2,1)S(1)}, u32[]{:S(2)}, u32[]{:S(2)}) collective-permute-start(bf16[512,256]{1,0:T(8,128)(2,1)S(1)} %slice.19.own), channel_id=1, source_target_pairs={{0,4},{4,0},{8,12},{12,8},{1,5},{5,1},{9,13},{13,9},{2,6},{6,2},{1... | collective-permute-start | bytes 786440 | tf_op jit(solution)/shard_map/ppermute | solution.py:366
  9.6 32.6 %copy-start.2 = (s32[4]{0:T(128)S(1)}, s32[4]{0:T(128)}, u32[]{:S(2)}) copy-start(s32[4]{0:T(128)} %param.8) | copy-start | bytes 52
  14.9 10.7 %collective-permute-start.5 = (bf16[2,256,256]{2,1,0:T(8,128)(2,1)S(1)}, bf16[2,256,256]{2,1,0:T(8,128)(2,1)S(1)}, u32[]{:S(2)}, u32[]{:S(2)}) collective-permute-start(bf16[2,256,256]{2,1,0:T(8,128)(2,1)S(1)} %get-tuple-element.28), channel_id=1, source_target_pairs={{0,8},{4,12},{8,0},{12,4},{1,9},{5,13},{9,1},{13,5},{2,10},{6,14},... | collective-permute-start | bytes 786440 | tf_op jit(solution)/shard_map/ppermute | solution.py:381
  15.0 5.5 %collective-permute-start.4 = (bf16[512,128]{1,0:T(8,128)(2,1)S(1)}, bf16[512,128]{1,0:T(8,128)(2,1)S(1)}, u32[]{:S(2)}, u32[]{:S(2)}) collective-permute-start(bf16[512,128]{1,0:T(8,128)(2,1)S(1)} %collective-permute-done.inner), channel_id=1, source_target_pairs={{0,2},{2,0},{1,3},{3,1},{4,6},{6,4},{5,7},{7,5},{8,10},{10,8},{9,1... | collective-permute-start | bytes 393224 | tf_op jit(solution)/shard_map/ppermute | solution.py:372
  16.6 15.2 %collective-permute-start.7 = (bf16[2,256,256]{2,1,0:T(8,128)(2,1)S(1)}, bf16[2,256,256]{2,1,0:T(8,128)(2,1)S(1)}, u32[]{:S(2)}, u32[]{:S(2)}) collective-permute-start(bf16[2,256,256]{2,1,0:T(8,128)(2,1)S(1)} %get-tuple-element.30), channel_id=1, source_target_pairs={{0,4},{4,0},{8,12},{12,8},{1,5},{5,1},{9,13},{13,9},{2,6},{6,2},{1... | collective-permute-start | bytes 786440 | tf_op jit(solution)/shard_map/ppermute | solution.py:381
  21.5 15.5 %collective-permute-start.6 = (bf16[2,256,256]{2,1,0:T(8,128)(2,1)S(1)}, bf16[2,256,256]{2,1,0:T(8,128)(2,1)S(1)}, u32[]{:S(2)}, u32[]{:S(2)}) collective-permute-start(bf16[2,256,256]{2,1,0:T(8,128)(2,1)S(1)} %get-tuple-element.29), channel_id=1, source_target_pairs={{0,8},{4,12},{8,0},{12,4},{1,9},{5,13},{9,1},{13,5},{2,10},{6,14},... | collective-permute-start | bytes 786440 | tf_op jit(solution)/shard_map/ppermute | solution.py:381
  24.6 17.7 %collective-permute-start.8 = (bf16[2,256,256]{2,1,0:T(8,128)(2,1)S(1)}, bf16[2,256,256]{2,1,0:T(8,128)(2,1)S(1)}, u32[]{:S(2)}, u32[]{:S(2)}) collective-permute-start(bf16[2,256,256]{2,1,0:T(8,128)(2,1)S(1)} %get-tuple-element.31), channel_id=1, source_target_pairs={{0,4},{4,0},{8,12},{12,8},{1,5},{5,1},{9,13},{13,9},{2,6},{6,2},{1... | collective-permute-start | bytes 786440 | tf_op jit(solution)/shard_map/ppermute | solution.py:381
  24.6 31.4 %collective-permute-start.11 = (bf16[2,256,256]{2,1,0:T(8,128)(2,1)S(1)}, bf16[2,256,256]{2,1,0:T(8,128)(2,1)S(1)}, u32[]{:S(2)}, u32[]{:S(2)}) collective-permute-start(bf16[2,256,256]{2,1,0:T(8,128)(2,1)S(1)} %get-tuple-element.35), channel_id=1, source_target_pairs={{0,12},{4,8},{8,4},{12,0},{1,13},{5,9},{9,5},{13,1},{2,14},{6,10},... | collective-permute-start | bytes 786440 | tf_op jit(solution)/shard_map/ppermute | solution.py:381
  25.6 34.2 %collective-permute-start.12 = (bf16[2,256,256]{2,1,0:T(8,128)(2,1)S(1)}, bf16[2,256,256]{2,1,0:T(8,128)(2,1)S(1)}, u32[]{:S(2)}, u32[]{:S(2)}) collective-permute-start(bf16[2,256,256]{2,1,0:T(8,128)(2,1)S(1)} %get-tuple-element.36), channel_id=1, source_target_pairs={{0,12},{4,8},{8,4},{12,0},{1,13},{5,9},{9,5},{13,1},{2,14},{6,10},... | collective-permute-start | bytes 786440 | tf_op jit(solution)/shard_map/ppermute | solution.py:381
  43.2 17.6 %collective-permute-start.9 = (bf16[2,3,64,256]{3,2,1,0:T(8,128)(2,1)S(1)}, bf16[2,3,64,256]{3,2,1,0:T(8,128)(2,1)S(1)}, u32[]{:S(2)}, u32[]{:S(2)}) collective-permute-start(bf16[2,3,64,256]{3,2,1,0:T(8,128)(2,1)S(1)} %get-tuple-element.34), channel_id=1, source_target_pairs={{0,2},{2,0},{1,3},{3,1},{4,6},{6,4},{5,7},{7,5},{8,10},{10,8},{9,1... | collective-permute-start | bytes 589832 | tf_op jit(solution)/shard_map/ppermute | solution.py:386
  60.7 1.8 %collective-permute-start.13 = (f32[2,3,64,256]{3,2,1,0:T(8,128)S(1)}, f32[2,3,64,256]{3,2,1,0:T(8,128)S(1)}, u32[]{:S(2)}, u32[]{:S(2)}) collective-permute-start(f32[2,3,64,256]{3,2,1,0:T(8,128)S(1)} %get-tuple-element.38), channel_id=1, source_target_pairs={{0,1},{1,0},{2,3},{3,2},{4,5},{5,4},{6,7},{7,6},{8,9},{9,8},{10,11... | collective-permute-start | bytes 1179656 | tf_op jit(solution)/shard_map/ppermute | solution.py:389
  60.8 3.3 %collective-permute-start.10 = (f32[3,64,256]{2,1,0:T(8,128)S(1)}, f32[3,64,256]{2,1,0:T(8,128)S(1)}, u32[]{:S(2)}, u32[]{:S(2)}) collective-permute-start(f32[3,64,256]{2,1,0:T(8,128)S(1)} %add_bitcast_fusion), channel_id=1, source_target_pairs={{0,1},{1,0},{2,3},{3,2},{4,5},{5,4},{6,7},{7,6},{8,9},{9,8},{10,11... | collective-permute-start | bytes 589832 | tf_op jit(solution)/shard_map/ppermute | solution.py:391
  62.5 4.9 %collective-permute-start.14 = (bf16[3,64,256]{2,1,0:T(8,128)(2,1)S(1)}, bf16[3,64,256]{2,1,0:T(8,128)(2,1)S(1)}, u32[]{:S(2)}, u32[]{:S(2)}) collective-permute-start(bf16[3,64,256]{2,1,0:T(8,128)(2,1)S(1)} %fusion.1), channel_id=1, source_target_pairs={{0,2},{2,0},{1,3},{3,1},{4,6},{6,4},{5,7},{7,5},{8,10},{10,8},{9,1... | collective-permute-start | bytes 294920 | tf_op jit(solution)/shard_map/ppermute | solution.py:390

commit v8 on v7

--- a/solution.py
+++ b/solution.py
@@ -147,17 +147,39 @@
     )(first, counts.reshape(1, -1), table)[0]
 
 
-def transform_kernel(start, wants, integrals, own, outer, inner, *outs):
+def central_kernel(integrals, coeffs, *outs):
     mid = AO_DEV * BLOCK
+    width = coeffs.shape[1] // len(outs)
+    for offset in range(AO_DEV):
+        low = mid - offset * BLOCK
+        for p in range(integrals.shape[0]):
+            slab = integrals[p, offset * BLOCK : (offset + 1) * BLOCK, low : low + mid]
+            for c, out in enumerate(outs):
+                out[offset, p] = dot(slab, coeffs[:, c * width : (c + 1) * width])
+
+
+def central(integrals, coeffs):
+    shape = (AO_DEV, integrals.shape[0], BLOCK, coeffs.shape[1] // CHUNKS)
+    return local_call(
+        central_kernel,
+        "central",
+        [like(shape, jnp.float32)] * CHUNKS,
+        2,
+        4 * integrals.size // WIN * coeffs.shape[1],
+    )(integrals, coeffs)
+
+
+def transform_kernel(start, wants, integrals, centre, inner, outer, *outs):
+    mid = AO_DEV * BLOCK
 
     def blocks(prev, following):
-        ids = start + lax.broadcasted_iota(jnp.int32, (BLOCK, own.shape[1]), 1)
+        ids = start + lax.broadcasted_iota(jnp.int32, (BLOCK, outer.shape[1]), 1)
         for p in range(integrals.shape[0]):
             both = []
             for offset in range(AO_DEV):
                 low = mid - offset * BLOCK
                 slab = integrals[p, offset * BLOCK : (offset + 1) * BLOCK, :]
-                values = dot(slab[:, low : low + mid], own[...])
+                values = centre[offset, p]
                 values += dot(slab[:, :low], prev[offset * BLOCK :, :])
                 values += dot(slab[:, low + mid :], following[: (offset + 1) * BLOCK, :])
                 live = ids < wants[GROUPS + offset : GROUPS + offset + 1, :]
@@ -170,36 +192,25 @@
     pl.when(odd == 1)(lambda: blocks(outer, inner))
 
 
-def shared_kernel(start, wants, integrals, own, outer, inner, swapped, *refs):
+def shared_kernel(start, wants, integrals, centre, inner, outer, swapped, *refs):
     *outs, whole = refs
     aux = lax.axis_index("aux")
     width = inner.shape[1]
     whole[:, pl.ds(pl.multiple_of(aux * width, width), width)] = inner[...]
     whole[:, pl.ds(pl.multiple_of((1 - aux) * width, width), width)] = swapped[...]
-    transform_kernel(start, wants, integrals, own, outer, whole, *outs)
-
-
-def shared_transform(start, wants, integrals, own, outer, inner, swapped):
-    shape = (integrals.shape[0], BLOCK, own.shape[1])
-    return local_call(
-        functools.partial(shared_kernel, start),
+    transform_kernel(start, wants, integrals, centre, whole, outer, *outs)
+
+
+def transform(kernel, start, wants, integrals, centre, inner, outer, *swapped):
+    shape = (integrals.shape[0], BLOCK, outer.shape[1])
+    return local_call(
+        functools.partial(kernel, start),
         "transform",
         [like(shape, jnp.bfloat16)] * GROUPS,
-        6,
-        2 * AO_DEV * math.prod(shape) * integrals.shape[2],
-        [pltpu.VMEM(own.shape, jnp.bfloat16)],
-    )(wants, integrals, own, outer, inner, swapped)
-
-
-def transform(start, wants, integrals, own, outer, inner):
-    shape = (integrals.shape[0], BLOCK, own.shape[1])
-    return local_call(
-        functools.partial(transform_kernel, start),
-        "transform",
-        [like(shape, jnp.bfloat16)] * GROUPS,
-        5,
-        2 * AO_DEV * math.prod(shape) * integrals.shape[2],
-    )(wants, integrals, own, outer, inner)
+        5 + len(swapped),
+        6 * AO_DEV * math.prod(shape) * integrals.shape[2] // WIN,
+        [pltpu.VMEM(outer.shape, jnp.bfloat16)] * len(swapped),
+    )(wants, integrals, centre, inner, outer, *swapped)
 
 
 def form_pairs(pairs, blocks, grams):
@@ -358,20 +369,23 @@
     table = pair_blocks.T
 
     half = width // 2
-    parts = [lax.slice_in_dim(coeffs, 0, width, axis=1)]
+    direct = lax.slice_in_dim(coeffs, 0, width, axis=1)
+    inner0 = lax.ppermute(direct, "ao", INSIDE)
+    outer0 = lax.ppermute(direct, "ao", OUTSIDE)
     first, rest = lax.optimization_barrier((lead(), coeffs))
-    parts.append(lax.slice_in_dim(rest, width, 2 * width, axis=1))
+    wants = tables(first, orbital_count, table, width)
+    centres = central(integrals, rest)
+    wants, centres, rest = lax.optimization_barrier((wants, centres, rest))
     mine = lax.dynamic_slice_in_dim(rest, width + lax.axis_index("aux") * half, half, axis=1)
-    inner = [lax.ppermute(part, "ao", INSIDE) for part in (parts[0], mine)]
-    outer = [lax.ppermute(part, "ao", OUTSIDE) for part in parts]
-    wants = tables(first, orbital_count, table, width)
-
-    pieces = list(transform(0, wants, integrals, parts[0], outer[0], inner[0]))
+    inner1 = lax.ppermute(mine, "ao", INSIDE)
+    outer1 = lax.ppermute(lax.slice_in_dim(rest, width, 2 * width, axis=1), "ao", OUTSIDE)
+
+    pieces = list(transform(transform_kernel, 0, wants, integrals, centres[0], inner0, outer0))
     blocks = [[piece] for piece in pieces]
-    inner[1], blocks[0][0] = lax.optimization_barrier((inner[1], blocks[0][0]))
-    swapped = lax.ppermute(inner[1], "aux", SWAP)
-    pieces = shared_transform(
-        width, wants, integrals, parts[1], outer[1], inner[1], swapped
+    inner1, blocks[0][0] = lax.optimization_barrier((inner1, blocks[0][0]))
+    swapped = lax.ppermute(inner1, "aux", SWAP)
+    pieces = transform(
+        shared_kernel, width, wants, integrals, centres[1], inner1, outer1, swapped
     )
     for block, piece in zip(blocks, pieces):
         block.append(piece)

time: 68.8 us -> 71.7 us (1.042)
  local copies, waits for them, and re-layouts: 2.88 us -> 4.93 us
  waiting for transfers between devices: 41.6 us -> 40.3 us
  Pallas kernels: 4.93 us -> 6.14 us
  starting transfers between devices: 18.9 us -> 19.9 us
    unnamed x8 -> x18, local copies, waits for them, and re-layouts: 0.03 us -> 3.22 us
    ppermute x5, waiting for transfers between devices: 7.1 us -> 4.75 us  [the longest x1 2 us: six_pair_body(): outer0 = lax.ppermute(direct, 'ao', OUTSIDE)]
    pallas_call x2 -> x3, Pallas kernels: 1.78 us -> 2.98 us  [the longest x2 2.28 us: transform(): local_call(functools.partial(kernel, start), 'transform', [like(shape, jn...]
    ppermute x6, waiting for transfers between devices: 30.1 us -> 31 us  [fetch(): return [lax.ppermute(piece, 'ao', swap) for piece in blocks[s]]]
    dynamic_slice x1, local copies, waits for them, and re-layouts: 0.92 us -> 0.02 us  [six_pair_body(): lax.dynamic_slice_in_dim(rest, width + lax.axis_index('aux') * half, half...]
    ppermute x6, starting transfers between devices: 7.09 us -> 7.96 us  [fetch(): return [lax.ppermute(piece, 'ao', swap) for piece in blocks[s]]]
  transfers between devices with their start and end apart: 15 -> 15, of which waited for: 11 -> 11; matrix products, arithmetic and copies ran while one was open for 3% -> 0% of each run, Pallas kernels for 6% -> 7%
where the time goes in v8:
time: 71.7 us; the launch traced here: 71.5 us
  waiting for transfers between devices  40.3 us (56%)
  starting transfers between devices  19.9 us (28%)
  Pallas kernels  6.14 us (9%)
  local copies, waits for them, and re-layouts  4.93 us (7%)
    ppermute x6, waiting for transfers between devices, fetch(): return [lax.ppermute(piece, 'ao', swap) for piece in blocks[s]]  31 us
    ppermute x6, starting transfers between devices, fetch(): return [lax.ppermute(piece, 'ao', swap) for piece in blocks[s]]  7.96 us
    ppermute x1, starting transfers between devices, six_pair_body(): inner0 = lax.ppermute(direct, 'ao', INSIDE)  3.75 us
    ppermute x1, waiting for transfers between devices, six_pair_body(): far1 = lax.ppermute((near1[1] + got1[1]).astype(jnp.bfloat16), 'aux', SWAP)  3.34 us
    unnamed x18, local copies, waits for them, and re-layouts  3.22 us
    ppermute x1, starting transfers between devices, six_pair_body(): inner1 = lax.ppermute(mine, 'ao', INSIDE)  2.49 us
    pallas_call x2, Pallas kernels, transform(): local_call(functools.partial(kernel, start), 'transform', [like(shape, jn...  2.28 us
    ppermute x1, waiting for transfers between devices, six_pair_body(): outer0 = lax.ppermute(direct, 'ao', OUTSIDE)  2 us
  transfers between devices with their start and end apart: 15, of which 11 were waited for; matrix products, arithmetic and copies ran while one was open for 0% of the time, Pallas kernels for 7%

profile of v8, /device:TPU:8, one launch (start us, length us, event | category | flops | bytes accessed | tf_op | source)
XLA Modules:
  0.0 71.5 jit_solution(6976199284181682974)
XLA Ops:
  0.0 1.7 %slice.18 = bf16[512,256]{1,0:T(8,128)(2,1)} slice(bf16[512,512]{1,0:T(8,128)(2,1)} %coeffs), slice={[0:512], [0:256]} | slice | bytes 524288 | tf_op jit(solution)/shard_map/slice | solution.py:372
  1.7 3.7 %collective-permute-start.1 = (bf16[512,256]{1,0:T(8,128)(2,1)}, bf16[512,256]{1,0:T(8,128)(2,1)S(1)}, u32[]{:S(2)}, u32[]{:S(2)}) collective-permute-start(bf16[512,256]{1,0:T(8,128)(2,1)} %slice.18), channel_id=1, source_target_pairs={{4,8},{8,4},{5,9},{9,5},{6,10},{10,6},{7,11},{11,7},{20,24},{24,20... | collective-permute-start | bytes 786440 | tf_op jit(solution)/shard_map/ppermute | solution.py:373
  6.4 1.0 %copy-done.2 = f32[2,2,256,256]{3,2,1,0:T(8,128)} copy-done((f32[2,2,256,256]{3,2,1,0:T(8,128)}, f32[2,2,256,256]{3,2,1,0:T(8,128)S(1)}, u32[]{:S(2)}) %copy-start.2) | copy-done | bytes 1048600
  7.4 1.0 %copy-done.4 = f32[2,2,256,256]{3,2,1,0:T(8,128)} copy-done((f32[2,2,256,256]{3,2,1,0:T(8,128)}, f32[2,2,256,256]{3,2,1,0:T(8,128)S(1)}, u32[]{:S(2)}) %copy-start.4) | copy-done | bytes 1048600
  8.4 2.5 %collective-permute-start = (bf16[512,128]{1,0:T(8,128)(2,1)S(1)}, bf16[512,128]{1,0:T(8,128)(2,1)S(1)}, u32[]{:S(2)}, u32[]{:S(2)}) collective-permute-start(bf16[512,128]{1,0:T(8,128)(2,1)S(1)} %constant_dynamic-slice_fusion), channel_id=1, source_target_pairs={{4,8},{8,4},{5,9},{9,5},{6,10},{10,6},{7,11},{11,7},{20,24},{24,20... | collective-permute-start | bytes 393224 | tf_op jit(solution)/shard_map/ppermute | solution.py:380
  12.1 2.0 %collective-permute-done.2.outer = bf16[512,256]{1,0:T(8,128)(2,1)} collective-permute-done((bf16[512,256]{1,0:T(8,128)(2,1)}, bf16[512,256]{1,0:T(8,128)(2,1)}, u32[]{:S(2)}, u32[]{:S(2)}) %collective-permute-start.2) | collective-permute-done | bytes 262176 | tf_op jit(solution)/shard_map/ppermute | solution.py:374
  14.1 1.2 %copy-done.5 = f32[2,2,256,256]{3,2,1,0:T(8,128)S(1)} copy-done((f32[2,2,256,256]{3,2,1,0:T(8,128)S(1)}, f32[2,2,256,256]{3,2,1,0:T(8,128)}, u32[]{:S(2)}) %copy-start.5) | copy-done | bytes 1048600
  15.3 1.6 %transform.2 = (bf16[2,256,256]{2,1,0:T(8,128)(2,1)S(1)}, bf16[2,256,256]{2,1,0:T(8,128)(2,1)S(1)}, bf16[2,256,256]{2,1,0:T(8,128)(2,1)S(1)}, bf16[2,256,256]{2,1,0:T(8,128)(2,1)S(1)}) custom-call(s32[8,256]{1,0:T(8,128)S(1)} %tables.1.wants, bf16[2,512,1280]{2,1,0:T(8,128)(2,1)S(1)} %copy-done, f32[2,2,256,256]{3,2,1,0:T(8,128)S(1)} %copy-done.5, ...), custom_call_target="tpu_custom_call" | custom-call | flops 402653184 | bytes 2097152 | tf_op jit(solution)/shard_map/transform/pallas_call | solution.py:206
  17.0 1.6 %collective-permute-start.4 = (bf16[512,128]{1,0:T(8,128)(2,1)S(1)}, bf16[512,128]{1,0:T(8,128)(2,1)S(1)}, u32[]{:S(2)}, u32[]{:S(2)}) collective-permute-start(bf16[512,128]{1,0:T(8,128)(2,1)S(1)} %collective-permute-done.inner), channel_id=1, source_target_pairs={{0,2},{2,0},{1,3},{3,1},{4,6},{6,4},{5,7},{7,5},{8,10},{10,8},{9,1... | collective-permute-start | bytes 393224 | tf_op jit(solution)/shard_map/ppermute | solution.py:386
  18.6 1.5 %collective-permute-start.7 = (bf16[2,256,256]{2,1,0:T(8,128)(2,1)S(1)}, bf16[2,256,256]{2,1,0:T(8,128)(2,1)S(1)}, u32[]{:S(2)}, u32[]{:S(2)}) collective-permute-start(bf16[2,256,256]{2,1,0:T(8,128)(2,1)S(1)} %get-tuple-element.42), channel_id=1, source_target_pairs={{0,4},{4,0},{8,12},{12,8},{1,5},{5,1},{9,13},{13,9},{2,6},{6,2},{1... | collective-permute-start | bytes 786440 | tf_op jit(solution)/shard_map/ppermute | solution.py:395
  20.3 1.8 %collective-permute-done.4.swapped = bf16[512,128]{1,0:T(8,128)(2,1)S(1)} collective-permute-done((bf16[512,128]{1,0:T(8,128)(2,1)S(1)}, bf16[512,128]{1,0:T(8,128)(2,1)S(1)}, u32[]{:S(2)}, u32[]{:S(2)}) %collective-permute-start.4) | collective-permute-done | bytes 131104 | tf_op jit(solution)/shard_map/ppermute | solution.py:386
  22.8 2.9 %collective-permute-start.6 = (bf16[2,256,256]{2,1,0:T(8,128)(2,1)S(1)}, bf16[2,256,256]{2,1,0:T(8,128)(2,1)S(1)}, u32[]{:S(2)}, u32[]{:S(2)}) collective-permute-start(bf16[2,256,256]{2,1,0:T(8,128)(2,1)S(1)} %get-tuple-element.41), channel_id=1, source_target_pairs={{0,8},{4,12},{8,0},{12,4},{1,9},{5,13},{9,1},{13,5},{2,10},{6,14},... | collective-permute-start | bytes 786440 | tf_op jit(solution)/shard_map/ppermute | solution.py:395
  26.3 2.7 %collective-permute-done.5.refs_2_ = bf16[2,256,256]{2,1,0:T(8,128)(2,1)S(1)} collective-permute-done((bf16[2,256,256]{2,1,0:T(8,128)(2,1)S(1)}, bf16[2,256,256]{2,1,0:T(8,128)(2,1)S(1)}, u32[]{:S(2)}, u32[]{:S(2)}) %collective-permute-start.5) | collective-permute-done | bytes 262176 | tf_op jit(solution)/shard_map/ppermute | solution.py:395
  29.0 2.8 %collective-permute-start.12 = (bf16[2,256,256]{2,1,0:T(8,128)(2,1)S(1)}, bf16[2,256,256]{2,1,0:T(8,128)(2,1)S(1)}, u32[]{:S(2)}, u32[]{:S(2)}) collective-permute-start(bf16[2,256,256]{2,1,0:T(8,128)(2,1)S(1)} %get-tuple-element.48), channel_id=1, source_target_pairs={{0,12},{4,8},{8,4},{12,0},{1,13},{5,9},{9,5},{13,1},{2,14},{6,10},... | collective-permute-start | bytes 786440 | tf_op jit(solution)/shard_map/ppermute | solution.py:395
  31.8 8.4 %collective-permute-done.6.refs_3_ = bf16[2,256,256]{2,1,0:T(8,128)(2,1)S(1)} collective-permute-done((bf16[2,256,256]{2,1,0:T(8,128)(2,1)S(1)}, bf16[2,256,256]{2,1,0:T(8,128)(2,1)S(1)}, u32[]{:S(2)}, u32[]{:S(2)}) %collective-permute-start.6) | collective-permute-done | bytes 262176 | tf_op jit(solution)/shard_map/ppermute | solution.py:395
  40.2 2.7 %collective-permute-done.8.refs_5_ = bf16[2,256,256]{2,1,0:T(8,128)(2,1)S(1)} collective-permute-done((bf16[2,256,256]{2,1,0:T(8,128)(2,1)S(1)}, bf16[2,256,256]{2,1,0:T(8,128)(2,1)S(1)}, u32[]{:S(2)}, u32[]{:S(2)}) %collective-permute-start.8) | collective-permute-done | bytes 262176 | tf_op jit(solution)/shard_map/ppermute | solution.py:395
  42.8 1.0 %early_pairs.1 = (f32[2,3,64,256]{3,2,1,0:T(8,128)S(1)}, bf16[2,3,64,256]{3,2,1,0:T(8,128)(2,1)S(1)}, s32[16,256]{1,0:T(8,128)S(1)}) custom-call(s32[1,4]{1,0:T(1,128)S(1)} %bitcast.9, s32[2,64]{1,0:T(2,128)S(1)} %bitcast.8, bf16[2,256,256]{2,1,0:T(8,128)(2,1)S(1)} %get-tuple-element.36.refs_0_, bf16[2,256,256]{2,1,0:T(8,128)(2,1)S(1)} %get-tuple-element.39.refs_1_, ...), custom_call_target="tpu_custom_call" | custom-call | flops 402653184 | bytes 1212416 | tf_op jit(solution)/shard_map/early_pairs/pallas_call | solution.py:296
  43.8 1.6 %collective-permute-start.9 = (bf16[2,3,64,256]{3,2,1,0:T(8,128)(2,1)S(1)}, bf16[2,3,64,256]{3,2,1,0:T(8,128)(2,1)S(1)}, u32[]{:S(2)}, u32[]{:S(2)}) collective-permute-start(bf16[2,3,64,256]{3,2,1,0:T(8,128)(2,1)S(1)} %get-tuple-element.46), channel_id=1, source_target_pairs={{0,2},{2,0},{1,3},{3,1},{4,6},{6,4},{5,7},{7,5},{8,10},{10,8},{9,1... | collective-permute-start | bytes 589832 | tf_op jit(solution)/shard_map/ppermute | solution.py:400
  45.4 13.5 %collective-permute-done.11.refs_6_ = bf16[2,256,256]{2,1,0:T(8,128)(2,1)S(1)} collective-permute-done((bf16[2,256,256]{2,1,0:T(8,128)(2,1)S(1)}, bf16[2,256,256]{2,1,0:T(8,128)(2,1)S(1)}, u32[]{:S(2)}, u32[]{:S(2)}) %collective-permute-start.11) | collective-permute-done | bytes 262176 | tf_op jit(solution)/shard_map/ppermute | solution.py:395
  58.9 3.8 %collective-permute-done.12.refs_7_ = bf16[2,256,256]{2,1,0:T(8,128)(2,1)S(1)} collective-permute-done((bf16[2,256,256]{2,1,0:T(8,128)(2,1)S(1)}, bf16[2,256,256]{2,1,0:T(8,128)(2,1)S(1)}, u32[]{:S(2)}, u32[]{:S(2)}) %collective-permute-start.12) | collective-permute-done | bytes 262176 | tf_op jit(solution)/shard_map/ppermute | solution.py:395
  64.3 1.1 %collective-permute-done.13.got1 = f32[2,3,64,256]{3,2,1,0:T(8,128)S(1)} collective-permute-done((f32[2,3,64,256]{3,2,1,0:T(8,128)S(1)}, f32[2,3,64,256]{3,2,1,0:T(8,128)S(1)}, u32[]{:S(2)}, u32[]{:S(2)}) %collective-permute-start.13) | collective-permute-done | bytes 393248 | tf_op jit(solution)/shard_map/ppermute | solution.py:403
  65.4 1.6 %collective-permute-start.14 = (bf16[3,64,256]{2,1,0:T(8,128)(2,1)S(1)}, bf16[3,64,256]{2,1,0:T(8,128)(2,1)S(1)}, u32[]{:S(2)}, u32[]{:S(2)}) collective-permute-start(bf16[3,64,256]{2,1,0:T(8,128)(2,1)S(1)} %fusion.1), channel_id=1, source_target_pairs={{0,2},{2,0},{1,3},{3,1},{4,6},{6,4},{5,7},{7,5},{8,10},{10,8},{9,1... | collective-permute-start | bytes 294920 | tf_op jit(solution)/shard_map/ppermute | solution.py:404
  67.0 3.3 %collective-permute-done.14.far1 = bf16[3,64,256]{2,1,0:T(8,128)(2,1)S(1)} collective-permute-done((bf16[3,64,256]{2,1,0:T(8,128)(2,1)S(1)}, bf16[3,64,256]{2,1,0:T(8,128)(2,1)S(1)}, u32[]{:S(2)}, u32[]{:S(2)}) %collective-permute-start.14) | collective-permute-done | bytes 98336 | tf_op jit(solution)/shard_map/ppermute | solution.py:404
  70.3 1.2 %spread.1 = f32[64,16,256]{2,1,0:T(8,128)} custom-call(s32[16,256]{1,0:T(8,128)S(1)} %get-tuple-element.44.place, f32[2,3,64,256]{3,2,1,0:T(8,128)S(1)} %get-tuple-element.45.near0, bf16[2,3,64,256]{3,2,1,0:T(8,128)(2,1)S(1)} %collective-permute-done.9.far0, f32[3,64,256]{2,1,0:T(8,128)S(1)} %collective-permute-done.10.got0, ...), custom_call_target="tpu_custom_call" | custom-call | flops 1572864 | bytes 2097152 | tf_op jit(solution)/shard_map/spread/pallas_call | solution.py:351
  (37 shorter events, 5.3 us)
Async XLA Ops:
  1.7 3.9 %copy-start.6 = (s32[64,2]{0,1:T(2,128)S(1)}, s32[64,2]{0,1:T(2,128)}, u32[]{:S(2)}) copy-start(s32[64,2]{0,1:T(2,128)} %param.7) | copy-start | bytes 1540
  1.7 3.9 %copy-start.8 = (s32[8]{0:T(128)S(1)}, s32[8]{0:T(128)}, u32[]{:S(2)}) copy-start(s32[8]{0:T(128)} %param.9) | copy-start | bytes 100
  1.7 4.0 %copy-start = (bf16[2,512,1280]{2,1,0:T(8,128)(2,1)S(1)}, bf16[2,512,1280]{2,1,0:T(8,128)(2,1)}, u32[]{:S(2)}) copy-start(bf16[2,512,1280]{2,1,0:T(8,128)(2,1)} %integrals.5) | copy-start | bytes 7864324
  1.7 4.0 %copy-start.1 = (bf16[512,512]{1,0:T(8,128)(2,1)S(1)}, bf16[512,512]{1,0:T(8,128)(2,1)}, u32[]{:S(2)}) copy-start(bf16[512,512]{1,0:T(8,128)(2,1)} %coeffs) | copy-start | bytes 1572868
  1.7 10.4 %collective-permute-start.1 = (bf16[512,256]{1,0:T(8,128)(2,1)}, bf16[512,256]{1,0:T(8,128)(2,1)S(1)}, u32[]{:S(2)}, u32[]{:S(2)}) collective-permute-start(bf16[512,256]{1,0:T(8,128)(2,1)} %slice.18), channel_id=1, source_target_pairs={{4,8},{8,4},{5,9},{9,5},{6,10},{10,6},{7,11},{11,7},{20,24},{24,20... | collective-permute-start | bytes 786440 | tf_op jit(solution)/shard_map/ppermute | solution.py:373
  5.4 8.7 %collective-permute-start.2 = (bf16[512,256]{1,0:T(8,128)(2,1)}, bf16[512,256]{1,0:T(8,128)(2,1)}, u32[]{:S(2)}, u32[]{:S(2)}) collective-permute-start(bf16[512,256]{1,0:T(8,128)(2,1)} %slice.18), channel_id=1, source_target_pairs={{0,4},{4,0},{8,12},{12,8},{1,5},{5,1},{9,13},{13,9},{2,6},{6,2},{1... | collective-permute-start | bytes 786440 | tf_op jit(solution)/shard_map/ppermute | solution.py:374
  6.4 1.0 %copy-start.2 = (f32[2,2,256,256]{3,2,1,0:T(8,128)}, f32[2,2,256,256]{3,2,1,0:T(8,128)S(1)}, u32[]{:S(2)}) copy-start(f32[2,2,256,256]{3,2,1,0:T(8,128)S(1)} %get-tuple-element.37.centre) | copy-start | bytes 3145732
  7.4 1.0 %copy-start.4 = (f32[2,2,256,256]{3,2,1,0:T(8,128)}, f32[2,2,256,256]{3,2,1,0:T(8,128)S(1)}, u32[]{:S(2)}) copy-start(f32[2,2,256,256]{3,2,1,0:T(8,128)S(1)} %get-tuple-element.34.centre) | copy-start | bytes 3145732
  8.4 13.6 %copy-start.3 = (f32[2,2,256,256]{3,2,1,0:T(8,128)S(1)}, f32[2,2,256,256]{3,2,1,0:T(8,128)}, u32[]{:S(2)}) copy-start(f32[2,2,256,256]{3,2,1,0:T(8,128)} %copy-done.2) | copy-start | bytes 3145732
  8.4 8.6 %collective-permute-start = (bf16[512,128]{1,0:T(8,128)(2,1)S(1)}, bf16[512,128]{1,0:T(8,128)(2,1)S(1)}, u32[]{:S(2)}, u32[]{:S(2)}) collective-permute-start(bf16[512,128]{1,0:T(8,128)(2,1)S(1)} %constant_dynamic-slice_fusion), channel_id=1, source_target_pairs={{4,8},{8,4},{5,9},{9,5},{6,10},{10,6},{7,11},{11,7},{20,24},{24,20... | collective-permute-start | bytes 393224 | tf_op jit(solution)/shard_map/ppermute | solution.py:380
  11.0 9.3 %collective-permute-start.3 = (bf16[512,256]{1,0:T(8,128)(2,1)S(1)}, bf16[512,256]{1,0:T(8,128)(2,1)S(1)}, u32[]{:S(2)}, u32[]{:S(2)}) collective-permute-start(bf16[512,256]{1,0:T(8,128)(2,1)S(1)} %slice.19), channel_id=1, source_target_pairs={{0,4},{4,0},{8,12},{12,8},{1,5},{5,1},{9,13},{13,9},{2,6},{6,2},{1... | collective-permute-start | bytes 786440 | tf_op jit(solution)/shard_map/ppermute | solution.py:381
  14.1 1.2 %copy-start.5 = (f32[2,2,256,256]{3,2,1,0:T(8,128)S(1)}, f32[2,2,256,256]{3,2,1,0:T(8,128)}, u32[]{:S(2)}) copy-start(f32[2,2,256,256]{3,2,1,0:T(8,128)} %copy-done.4) | copy-start | bytes 3145732
  16.9 25.9 %copy-start.7 = (s32[4]{0:T(128)S(1)}, s32[4]{0:T(128)}, u32[]{:S(2)}) copy-start(s32[4]{0:T(128)} %param.8) | copy-start | bytes 52
  16.9 12.1 %collective-permute-start.5 = (bf16[2,256,256]{2,1,0:T(8,128)(2,1)S(1)}, bf16[2,256,256]{2,1,0:T(8,128)(2,1)S(1)}, u32[]{:S(2)}, u32[]{:S(2)}) collective-permute-start(bf16[2,256,256]{2,1,0:T(8,128)(2,1)S(1)} %get-tuple-element.40), channel_id=1, source_target_pairs={{0,8},{4,12},{8,0},{12,4},{1,9},{5,13},{9,1},{13,5},{2,10},{6,14},... | collective-permute-start | bytes 786440 | tf_op jit(solution)/shard_map/ppermute | solution.py:395
  17.0 5.0 %collective-permute-start.4 = (bf16[512,128]{1,0:T(8,128)(2,1)S(1)}, bf16[512,128]{1,0:T(8,128)(2,1)S(1)}, u32[]{:S(2)}, u32[]{:S(2)}) collective-permute-start(bf16[512,128]{1,0:T(8,128)(2,1)S(1)} %collective-permute-done.inner), channel_id=1, source_target_pairs={{0,2},{2,0},{1,3},{3,1},{4,6},{6,4},{5,7},{7,5},{8,10},{10,8},{9,1... | collective-permute-start | bytes 393224 | tf_op jit(solution)/shard_map/ppermute | solution.py:386
  18.6 13.2 %collective-permute-start.7 = (bf16[2,256,256]{2,1,0:T(8,128)(2,1)S(1)}, bf16[2,256,256]{2,1,0:T(8,128)(2,1)S(1)}, u32[]{:S(2)}, u32[]{:S(2)}) collective-permute-start(bf16[2,256,256]{2,1,0:T(8,128)(2,1)S(1)} %get-tuple-element.42), channel_id=1, source_target_pairs={{0,4},{4,0},{8,12},{12,8},{1,5},{5,1},{9,13},{13,9},{2,6},{6,2},{1... | collective-permute-start | bytes 786440 | tf_op jit(solution)/shard_map/ppermute | solution.py:395
  22.8 17.4 %collective-permute-start.6 = (bf16[2,256,256]{2,1,0:T(8,128)(2,1)S(1)}, bf16[2,256,256]{2,1,0:T(8,128)(2,1)S(1)}, u32[]{:S(2)}, u32[]{:S(2)}) collective-permute-start(bf16[2,256,256]{2,1,0:T(8,128)(2,1)S(1)} %get-tuple-element.41), channel_id=1, source_target_pairs={{0,8},{4,12},{8,0},{12,4},{1,9},{5,13},{9,1},{13,5},{2,10},{6,14},... | collective-permute-start | bytes 786440 | tf_op jit(solution)/shard_map/ppermute | solution.py:395
  25.7 17.2 %collective-permute-start.8 = (bf16[2,256,256]{2,1,0:T(8,128)(2,1)S(1)}, bf16[2,256,256]{2,1,0:T(8,128)(2,1)S(1)}, u32[]{:S(2)}, u32[]{:S(2)}) collective-permute-start(bf16[2,256,256]{2,1,0:T(8,128)(2,1)S(1)} %get-tuple-element.43), channel_id=1, source_target_pairs={{0,4},{4,0},{8,12},{12,8},{1,5},{5,1},{9,13},{13,9},{2,6},{6,2},{1... | collective-permute-start | bytes 786440 | tf_op jit(solution)/shard_map/ppermute | solution.py:395
  25.9 33.0 %collective-permute-start.11 = (bf16[2,256,256]{2,1,0:T(8,128)(2,1)S(1)}, bf16[2,256,256]{2,1,0:T(8,128)(2,1)S(1)}, u32[]{:S(2)}, u32[]{:S(2)}) collective-permute-start(bf16[2,256,256]{2,1,0:T(8,128)(2,1)S(1)} %get-tuple-element.47), channel_id=1, source_target_pairs={{0,12},{4,8},{8,4},{12,0},{1,13},{5,9},{9,5},{13,1},{2,14},{6,10},... | collective-permute-start | bytes 786440 | tf_op jit(solution)/shard_map/ppermute | solution.py:395
  29.0 33.8 %collective-permute-start.12 = (bf16[2,256,256]{2,1,0:T(8,128)(2,1)S(1)}, bf16[2,256,256]{2,1,0:T(8,128)(2,1)S(1)}, u32[]{:S(2)}, u32[]{:S(2)}) collective-permute-start(bf16[2,256,256]{2,1,0:T(8,128)(2,1)S(1)} %get-tuple-element.48), channel_id=1, source_target_pairs={{0,12},{4,8},{8,4},{12,0},{1,13},{5,9},{9,5},{13,1},{2,14},{6,10},... | collective-permute-start | bytes 786440 | tf_op jit(solution)/shard_map/ppermute | solution.py:395
  43.8 19.9 %collective-permute-start.9 = (bf16[2,3,64,256]{3,2,1,0:T(8,128)(2,1)S(1)}, bf16[2,3,64,256]{3,2,1,0:T(8,128)(2,1)S(1)}, u32[]{:S(2)}, u32[]{:S(2)}) collective-permute-start(bf16[2,3,64,256]{3,2,1,0:T(8,128)(2,1)S(1)} %get-tuple-element.46), channel_id=1, source_target_pairs={{0,2},{2,0},{1,3},{3,1},{4,6},{6,4},{5,7},{7,5},{8,10},{10,8},{9,1... | collective-permute-start | bytes 589832 | tf_op jit(solution)/shard_map/ppermute | solution.py:400
  63.6 1.8 %collective-permute-start.13 = (f32[2,3,64,256]{3,2,1,0:T(8,128)S(1)}, f32[2,3,64,256]{3,2,1,0:T(8,128)S(1)}, u32[]{:S(2)}, u32[]{:S(2)}) collective-permute-start(f32[2,3,64,256]{3,2,1,0:T(8,128)S(1)} %get-tuple-element.50), channel_id=1, source_target_pairs={{0,1},{1,0},{2,3},{3,2},{4,5},{5,4},{6,7},{7,6},{8,9},{9,8},{10,11... | collective-permute-start | bytes 1179656 | tf_op jit(solution)/shard_map/ppermute | solution.py:403
  63.7 3.3 %collective-permute-start.10 = (f32[3,64,256]{2,1,0:T(8,128)S(1)}, f32[3,64,256]{2,1,0:T(8,128)S(1)}, u32[]{:S(2)}, u32[]{:S(2)}) collective-permute-start(f32[3,64,256]{2,1,0:T(8,128)S(1)} %add_bitcast_fusion), channel_id=1, source_target_pairs={{0,1},{1,0},{2,3},{3,2},{4,5},{5,4},{6,7},{7,6},{8,9},{9,8},{10,11... | collective-permute-start | bytes 589832 | tf_op jit(solution)/shard_map/ppermute | solution.py:405
  65.4 4.9 %collective-permute-start.14 = (bf16[3,64,256]{2,1,0:T(8,128)(2,1)S(1)}, bf16[3,64,256]{2,1,0:T(8,128)(2,1)S(1)}, u32[]{:S(2)}, u32[]{:S(2)}) collective-permute-start(bf16[3,64,256]{2,1,0:T(8,128)(2,1)S(1)} %fusion.1), channel_id=1, source_target_pairs={{0,2},{2,0},{1,3},{3,1},{4,6},{6,4},{5,7},{7,5},{8,10},{10,8},{9,1... | collective-permute-start | bytes 294920 | tf_op jit(solution)/shard_map/ppermute | solution.py:404

commit v9 on v7

--- a/solution.py
+++ b/solution.py
@@ -79,8 +79,8 @@
 
 
 EARLY_PAIRS = ((0, 1), (0, 2), (1, 2))
-LATE_PAIRS = ((0, 3), (1, 3), (2, 3))
-ALL_PAIRS = EARLY_PAIRS + LATE_PAIRS
+LATE_PAIRS = ((0, 3),), ((1, 3), (2, 3))
+ALL_PAIRS = EARLY_PAIRS + LATE_PAIRS[0] + LATE_PAIRS[1]
 GROUPS = 4
 SWAP = [(0, 1), (1, 0)]
 OUTSIDE = [(0, 1), (1, 0), (2, 3), (3, 2)]
@@ -257,14 +257,14 @@
             far[core, k] = grams[k, 2 * (1 - aux) + (orb ^ core)].astype(jnp.bfloat16)
 
 
-def late_kernel(*refs):
+def late_kernel(pairs, *refs):
     used = GROUPS * CHUNKS
     own, middle, next_to, last = [refs[i : i + CHUNKS] for i in range(0, used, CHUNKS)]
     blocks = own, next_to, middle, last
     keep, give, grams = refs[used:]
     aux, orb = lax.axis_index("aux"), lax.axis_index("orb")
-    form_pairs(LATE_PAIRS, blocks, grams)
-    for k in range(len(LATE_PAIRS)):
+    form_pairs(pairs, blocks, grams)
+    for k in range(len(pairs)):
         for chip in (0, 1):
             row = 2 * (aux ^ chip)
             keep[chip, k] = grams[k, row + orb]
@@ -296,22 +296,27 @@
     )(live.reshape(1, -1), table, *blocks[0], *blocks[2], *blocks[1])
 
 
-def late_pairs(blocks):
-    shape, grams = quarters(LATE_PAIRS)
-    return local_call(
-        late_kernel,
+def late_pairs(pairs, blocks):
+    shape, grams = quarters(pairs)
+    return local_call(
+        functools.partial(late_kernel, pairs),
         "late_pairs",
         [like(shape, jnp.float32)] * 2,
         GROUPS * CHUNKS,
-        pair_flops(LATE_PAIRS, blocks),
+        pair_flops(pairs, blocks),
         [grams],
     )(*blocks[0], *blocks[2], *blocks[1], *blocks[3])
 
 
-def spread_kernel(factor, place, near0, far0, got0, near1, got1, far1, out, sums, rows, sems):
-    early = near0.shape[1]
-    sums[:early] = (near0[0] + far0[0].astype(jnp.float32) + got0[...]) * factor
-    sums[early:] = (near1[0] + got1[0] + far1[...].astype(jnp.float32)) * factor
+def spread_kernel(factor, place, near, far, got, *refs):
+    *late, out, sums, rows, sems = refs
+    done = near.shape[1]
+    sums[:done] = (near[0] + far[0].astype(jnp.float32) + got[...]) * factor
+    for i in range(0, len(late), 3):
+        near, got, far = late[i : i + 3]
+        more = done + near.shape[1]
+        sums[done:more] = (near[0] + got[0] + far[...].astype(jnp.float32)) * factor
+        done = more
     total, slots, width = out.shape
     masks = [place[...] == k for k in range(sums.shape[0])]
 
@@ -385,12 +390,14 @@
     near0, across0, place = early_pairs(pair_count, table, got)
     far0 = lax.ppermute(across0, "aux", SWAP)
     got.append(fetch(3))
-    near1, give1 = late_pairs(got)
-    got1 = lax.ppermute(give1, "orb", SWAP)
-    far1 = lax.ppermute((near1[1] + got1[1]).astype(jnp.bfloat16), "aux", SWAP)
+    late = []
+    for near1, give1 in [late_pairs(pairs, got) for pairs in LATE_PAIRS]:
+        got1 = lax.ppermute(give1, "orb", SWAP)
+        far1 = lax.ppermute((near1[1] + got1[1]).astype(jnp.bfloat16), "aux", SWAP)
+        late += [near1, got1, far1]
     got0 = lax.ppermute(near0[1] + far0[1].astype(jnp.float32), "orb", SWAP)
     factor = 1.0 / math.sqrt(total_aux * ORBS)
-    return spread(factor, place, near0, far0, got0, near1, got1, far1)
+    return spread(factor, place, near0, far0, got0, *late)
 
 
 def solution(mesh):

time: 68.8 us -> 70.2 us (1.020)
  waiting for transfers between devices: 41.6 us -> 42.7 us
    ppermute x6, waiting for transfers between devices: 30.1 us -> 33.7 us  [fetch(): return [lax.ppermute(piece, 'ao', swap) for piece in blocks[s]]]
    ppermute x2, waiting for transfers between devices: 4.39 us -> 1.71 us  [six_pair_body(): outer = [lax.ppermute(part, 'ao', OUTSIDE) for part in parts]]
    ppermute x1, waiting for transfers between devices: 0.01 us -> 1.4 us  [six_pair_body(): swapped = lax.ppermute(inner[1], 'aux', SWAP)]
    ppermute x1 -> x2, waiting for transfers between devices: 3.34 us -> 2.73 us  [six_pair_body(): far1 = lax.ppermute((near1[1] + got1[1]).astype(jnp.bfloat16), 'aux', SWAP)]
    ppermute x1 -> x2, starting transfers between devices: 1.55 us -> 2.16 us  [six_pair_body(): far1 = lax.ppermute((near1[1] + got1[1]).astype(jnp.bfloat16), 'aux', SWAP)]
  transfers between devices with their start and end apart: 15 -> 17, of which waited for: 11 -> 10; matrix products, arithmetic and copies ran while one was open for 3% -> 3% of each run, Pallas kernels for 6% -> 6%
where the time goes in v9:
time: 70.2 us; the launch traced here: 70 us
  waiting for transfers between devices  42.7 us (61%)
  starting transfers between devices  19 us (27%)
  Pallas kernels  5.19 us (7%)
  local copies, waits for them, and re-layouts  2.88 us (4%)
    ppermute x6, waiting for transfers between devices, fetch(): return [lax.ppermute(piece, 'ao', swap) for piece in blocks[s]]  33.7 us
    ppermute x6, starting transfers between devices, fetch(): return [lax.ppermute(piece, 'ao', swap) for piece in blocks[s]]  7.11 us
    ppermute x2, starting transfers between devices, six_pair_body(): inner = [lax.ppermute(part, 'ao', INSIDE) for part in (parts[0], mine)]  6.11 us
    ppermute x2, waiting for transfers between devices, six_pair_body(): far1 = lax.ppermute((near1[1] + got1[1]).astype(jnp.bfloat16), 'aux', SWAP)  2.73 us
    ppermute x2, waiting for transfers between devices, six_pair_body(): inner = [lax.ppermute(part, 'ao', INSIDE) for part in (parts[0], mine)]  2.71 us
    ppermute x2, starting transfers between devices, six_pair_body(): far1 = lax.ppermute((near1[1] + got1[1]).astype(jnp.bfloat16), 'aux', SWAP)  2.16 us
    ppermute x2, waiting for transfers between devices, six_pair_body(): outer = [lax.ppermute(part, 'ao', OUTSIDE) for part in parts]  1.71 us
    ppermute x1, starting transfers between devices, six_pair_body(): swapped = lax.ppermute(inner[1], 'aux', SWAP)  1.56 us
  transfers between devices with their start and end apart: 17, of which 10 were waited for; matrix products, arithmetic and copies ran while one was open for 3% of the time, Pallas kernels for 6%

profile of v9, /device:TPU:8, one launch (start us, length us, event | category | flops | bytes accessed | tf_op | source)
XLA Modules:
  0.0 70.0 jit_solution(13454989162913553866)
XLA Ops:
  0.0 1.0 %slice.24.own = bf16[512,256]{1,0:T(8,128)(2,1)S(1)} slice(bf16[512,512]{1,0:T(8,128)(2,1)} %param.6), slice={[0:512], [0:256]} | slice | bytes 524288 | tf_op jit(solution)/shard_map/slice | solution.py:366
  1.0 3.7 %collective-permute-start.2 = (bf16[512,256]{1,0:T(8,128)(2,1)S(1)}, bf16[512,256]{1,0:T(8,128)(2,1)S(1)}, u32[]{:S(2)}, u32[]{:S(2)}) collective-permute-start(bf16[512,256]{1,0:T(8,128)(2,1)S(1)} %slice.24.own), channel_id=1, source_target_pairs={{4,8},{8,4},{5,9},{9,5},{6,10},{10,6},{7,11},{11,7},{20,24},{24,20... | collective-permute-start | bytes 786440 | tf_op jit(solution)/shard_map/ppermute | solution.py:370
  4.9 0.9 %constant_dynamic-slice_fusion = bf16[512,128]{1,0:T(8,128)(2,1)S(1)} fusion(bf16[512,512]{1,0:T(8,128)(2,1)} %param.6, s32[]{:T(128)S(6)} %select_n.3), kind=kLoop, calls=%fused_computation.7 | loop fusion | bytes 262148 | tf_op jit(solution)/shard_map/dynamic_slice | solution.py:369
  5.8 2.4 %collective-permute-start = (bf16[512,128]{1,0:T(8,128)(2,1)S(1)}, bf16[512,128]{1,0:T(8,128)(2,1)S(1)}, u32[]{:S(2)}, u32[]{:S(2)}) collective-permute-start(bf16[512,128]{1,0:T(8,128)(2,1)S(1)} %constant_dynamic-slice_fusion), channel_id=1, source_target_pairs={{4,8},{8,4},{5,9},{9,5},{6,10},{10,6},{7,11},{11,7},{20,24},{24,20... | collective-permute-start | bytes 393224 | tf_op jit(solution)/shard_map/ppermute | solution.py:370
  8.1 1.0 %slice.25.own = bf16[512,256]{1,0:T(8,128)(2,1)S(1)} slice(bf16[512,512]{1,0:T(8,128)(2,1)} %param.6), slice={[0:512], [256:512]} | slice | bytes 524288 | tf_op jit(solution)/shard_map/slice | solution.py:368
  9.7 2.7 %collective-permute-done.2.inner = bf16[512,256]{1,0:T(8,128)(2,1)S(1)} collective-permute-done((bf16[512,256]{1,0:T(8,128)(2,1)S(1)}, bf16[512,256]{1,0:T(8,128)(2,1)S(1)}, u32[]{:S(2)}, u32[]{:S(2)}) %collective-permute-start.2) | collective-permute-done | bytes 262176 | tf_op jit(solution)/shard_map/ppermute | solution.py:370
  12.4 1.7 %collective-permute-done.1.outer = bf16[512,256]{1,0:T(8,128)(2,1)S(1)} collective-permute-done((bf16[512,256]{1,0:T(8,128)(2,1)S(1)}, bf16[512,256]{1,0:T(8,128)(2,1)S(1)}, u32[]{:S(2)}, u32[]{:S(2)}) %collective-permute-start.1) | collective-permute-done | bytes 262176 | tf_op jit(solution)/shard_map/ppermute | solution.py:371
  14.9 1.6 %collective-permute-start.4 = (bf16[512,128]{1,0:T(8,128)(2,1)S(1)}, bf16[512,128]{1,0:T(8,128)(2,1)S(1)}, u32[]{:S(2)}, u32[]{:S(2)}) collective-permute-start(bf16[512,128]{1,0:T(8,128)(2,1)S(1)} %collective-permute-done.inner), channel_id=1, source_target_pairs={{0,2},{2,0},{1,3},{3,1},{4,6},{6,4},{5,7},{7,5},{8,10},{10,8},{9,1... | collective-permute-start | bytes 393224 | tf_op jit(solution)/shard_map/ppermute | solution.py:377
  16.5 2.1 %collective-permute-start.7 = (bf16[2,256,256]{2,1,0:T(8,128)(2,1)S(1)}, bf16[2,256,256]{2,1,0:T(8,128)(2,1)S(1)}, u32[]{:S(2)}, u32[]{:S(2)}) collective-permute-start(bf16[2,256,256]{2,1,0:T(8,128)(2,1)S(1)} %get-tuple-element.32), channel_id=1, source_target_pairs={{0,4},{4,0},{8,12},{12,8},{1,5},{5,1},{9,13},{13,9},{2,6},{6,2},{1... | collective-permute-start | bytes 786440 | tf_op jit(solution)/shard_map/ppermute | solution.py:386
  18.6 1.4 %collective-permute-done.4.swapped = bf16[512,128]{1,0:T(8,128)(2,1)S(1)} collective-permute-done((bf16[512,128]{1,0:T(8,128)(2,1)S(1)}, bf16[512,128]{1,0:T(8,128)(2,1)S(1)}, u32[]{:S(2)}, u32[]{:S(2)}) %collective-permute-start.4) | collective-permute-done | bytes 131104 | tf_op jit(solution)/shard_map/ppermute | solution.py:377
  20.0 1.0 %transform.3 = (bf16[2,256,256]{2,1,0:T(8,128)(2,1)S(1)}, bf16[2,256,256]{2,1,0:T(8,128)(2,1)S(1)}, bf16[2,256,256]{2,1,0:T(8,128)(2,1)S(1)}, bf16[2,256,256]{2,1,0:T(8,128)(2,1)S(1)}) custom-call(s32[8,256]{1,0:T(8,128)S(1)} %tables.1.wants, bf16[2,512,1280]{2,1,0:T(8,128)(2,1)S(1)} %copy-done, bf16[512,256]{1,0:T(8,128)(2,1)S(1)} %slice.25.own, ...), custom_call_target="tpu_custom_call" | custom-call | flops 671088640 | bytes 2097152 | tf_op jit(solution)/shard_map/transform/pallas_call | solution.py:184
  20.9 1.4 %collective-permute-start.6 = (bf16[2,256,256]{2,1,0:T(8,128)(2,1)S(1)}, bf16[2,256,256]{2,1,0:T(8,128)(2,1)S(1)}, u32[]{:S(2)}, u32[]{:S(2)}) collective-permute-start(bf16[2,256,256]{2,1,0:T(8,128)(2,1)S(1)} %get-tuple-element.31), channel_id=1, source_target_pairs={{0,8},{4,12},{8,0},{12,4},{1,9},{5,13},{9,1},{13,5},{2,10},{6,14},... | collective-permute-start | bytes 786440 | tf_op jit(solution)/shard_map/ppermute | solution.py:386
  23.1 1.4 %collective-permute-start.11 = (bf16[2,256,256]{2,1,0:T(8,128)(2,1)S(1)}, bf16[2,256,256]{2,1,0:T(8,128)(2,1)S(1)}, u32[]{:S(2)}, u32[]{:S(2)}) collective-permute-start(bf16[2,256,256]{2,1,0:T(8,128)(2,1)S(1)} %get-tuple-element.37), channel_id=1, source_target_pairs={{0,12},{4,8},{8,4},{12,0},{1,13},{5,9},{9,5},{13,1},{2,14},{6,10},... | collective-permute-start | bytes 786440 | tf_op jit(solution)/shard_map/ppermute | solution.py:386
  24.5 5.6 %collective-permute-done.5.refs_2_ = bf16[2,256,256]{2,1,0:T(8,128)(2,1)S(1)} collective-permute-done((bf16[2,256,256]{2,1,0:T(8,128)(2,1)S(1)}, bf16[2,256,256]{2,1,0:T(8,128)(2,1)S(1)}, u32[]{:S(2)}, u32[]{:S(2)}) %collective-permute-start.5) | collective-permute-done | bytes 262176 | tf_op jit(solution)/shard_map/ppermute | solution.py:386
  30.0 1.5 %collective-permute-start.12 = (bf16[2,256,256]{2,1,0:T(8,128)(2,1)S(1)}, bf16[2,256,256]{2,1,0:T(8,128)(2,1)S(1)}, u32[]{:S(2)}, u32[]{:S(2)}) collective-permute-start(bf16[2,256,256]{2,1,0:T(8,128)(2,1)S(1)} %get-tuple-element.38), channel_id=1, source_target_pairs={{0,12},{4,8},{8,4},{12,0},{1,13},{5,9},{9,5},{13,1},{2,14},{6,10},... | collective-permute-start | bytes 786440 | tf_op jit(solution)/shard_map/ppermute | solution.py:386
  31.5 9.7 %collective-permute-done.6.refs_3_ = bf16[2,256,256]{2,1,0:T(8,128)(2,1)S(1)} collective-permute-done((bf16[2,256,256]{2,1,0:T(8,128)(2,1)S(1)}, bf16[2,256,256]{2,1,0:T(8,128)(2,1)S(1)}, u32[]{:S(2)}, u32[]{:S(2)}) %collective-permute-start.6) | collective-permute-done | bytes 262176 | tf_op jit(solution)/shard_map/ppermute | solution.py:386
  41.2 1.4 %collective-permute-done.8.refs_5_ = bf16[2,256,256]{2,1,0:T(8,128)(2,1)S(1)} collective-permute-done((bf16[2,256,256]{2,1,0:T(8,128)(2,1)S(1)}, bf16[2,256,256]{2,1,0:T(8,128)(2,1)S(1)}, u32[]{:S(2)}, u32[]{:S(2)}) %collective-permute-start.8) | collective-permute-done | bytes 262176 | tf_op jit(solution)/shard_map/ppermute | solution.py:386
  42.7 1.0 %early_pairs.1 = (f32[2,3,64,256]{3,2,1,0:T(8,128)S(1)}, bf16[2,3,64,256]{3,2,1,0:T(8,128)(2,1)S(1)}, s32[16,256]{1,0:T(8,128)S(1)}) custom-call(s32[1,4]{1,0:T(1,128)S(1)} %bitcast.11, s32[2,64]{1,0:T(2,128)S(1)} %bitcast.10, bf16[2,256,256]{2,1,0:T(8,128)(2,1)S(1)} %get-tuple-element.27.refs_0_, bf16[2,256,256]{2,1,0:T(8,128)(2,1)S(1)} %get-tuple-element.29.refs_1_, ...), custom_call_target="tpu_custom_call" | custom-call | flops 402653184 | bytes 1212416 | tf_op jit(solution)/shard_map/early_pairs/pallas_call | solution.py:285
  43.7 1.0 %collective-permute-start.9 = (bf16[2,3,64,256]{3,2,1,0:T(8,128)(2,1)S(1)}, bf16[2,3,64,256]{3,2,1,0:T(8,128)(2,1)S(1)}, u32[]{:S(2)}, u32[]{:S(2)}) collective-permute-start(bf16[2,3,64,256]{3,2,1,0:T(8,128)(2,1)S(1)} %get-tuple-element.36), channel_id=1, source_target_pairs={{0,2},{2,0},{1,3},{3,1},{4,6},{6,4},{5,7},{7,5},{8,10},{10,8},{9,1... | collective-permute-start | bytes 589832 | tf_op jit(solution)/shard_map/ppermute | solution.py:391
  44.6 12.9 %collective-permute-done.11.refs_6_ = bf16[2,256,256]{2,1,0:T(8,128)(2,1)S(1)} collective-permute-done((bf16[2,256,256]{2,1,0:T(8,128)(2,1)S(1)}, bf16[2,256,256]{2,1,0:T(8,128)(2,1)S(1)}, u32[]{:S(2)}, u32[]{:S(2)}) %collective-permute-start.11) | collective-permute-done | bytes 262176 | tf_op jit(solution)/shard_map/ppermute | solution.py:386
  57.6 4.0 %collective-permute-done.12.refs_7_ = bf16[2,256,256]{2,1,0:T(8,128)(2,1)S(1)} collective-permute-done((bf16[2,256,256]{2,1,0:T(8,128)(2,1)S(1)}, bf16[2,256,256]{2,1,0:T(8,128)(2,1)S(1)}, u32[]{:S(2)}, u32[]{:S(2)}) %collective-permute-start.12) | collective-permute-done | bytes 262176 | tf_op jit(solution)/shard_map/ppermute | solution.py:386
  64.6 1.5 %collective-permute-start.14 = (bf16[1,64,256]{2,1,0:T(8,128)(2,1)S(1)}, bf16[1,64,256]{2,1,0:T(8,128)(2,1)S(1)}, u32[]{:S(2)}, u32[]{:S(2)}) collective-permute-start(bf16[1,64,256]{2,1,0:T(8,128)(2,1)S(1)} %fusion.3), channel_id=1, source_target_pairs={{0,2},{2,0},{1,3},{3,1},{4,6},{6,4},{5,7},{7,5},{8,10},{10,8},{9,1... | collective-permute-start | bytes 98312 | tf_op jit(solution)/shard_map/ppermute | solution.py:396
  66.1 2.7 %collective-permute-done.14.refs_2_ = bf16[1,64,256]{2,1,0:T(8,128)(2,1)S(1)} collective-permute-done((bf16[1,64,256]{2,1,0:T(8,128)(2,1)S(1)}, bf16[1,64,256]{2,1,0:T(8,128)(2,1)S(1)}, u32[]{:S(2)}, u32[]{:S(2)}) %collective-permute-start.14) | collective-permute-done | bytes 32800 | tf_op jit(solution)/shard_map/ppermute | solution.py:396
  68.9 1.2 %spread.1 = f32[64,16,256]{2,1,0:T(8,128)} custom-call(s32[16,256]{1,0:T(8,128)S(1)} %get-tuple-element.34.place, f32[2,3,64,256]{3,2,1,0:T(8,128)S(1)} %get-tuple-element.35.near, bf16[2,3,64,256]{3,2,1,0:T(8,128)(2,1)S(1)} %collective-permute-done.9.far, f32[3,64,256]{2,1,0:T(8,128)S(1)} %collective-permute-done.10.got, ...), custom_call_target="tpu_custom_call" | custom-call | flops 1572864 | bytes 2097152 | tf_op jit(solution)/shard_map/spread/pallas_call | solution.py:345
  (32 shorter events, 5.2 us)
Async XLA Ops:
  1.0 8.5 %copy-start.1 = (s32[64,2]{0,1:T(2,128)S(1)}, s32[64,2]{0,1:T(2,128)}, u32[]{:S(2)}) copy-start(s32[64,2]{0,1:T(2,128)} %param.7) | copy-start | bytes 1540
  1.0 8.5 %copy-start.3 = (s32[8]{0:T(128)S(1)}, s32[8]{0:T(128)}, u32[]{:S(2)}) copy-start(s32[8]{0:T(128)} %param.9) | copy-start | bytes 100
  1.0 13.1 %copy-start = (bf16[2,512,1280]{2,1,0:T(8,128)(2,1)S(1)}, bf16[2,512,1280]{2,1,0:T(8,128)(2,1)}, u32[]{:S(2)}) copy-start(bf16[2,512,1280]{2,1,0:T(8,128)(2,1)} %integrals.3) | copy-start | bytes 7864324
  1.0 11.3 %collective-permute-start.2 = (bf16[512,256]{1,0:T(8,128)(2,1)S(1)}, bf16[512,256]{1,0:T(8,128)(2,1)S(1)}, u32[]{:S(2)}, u32[]{:S(2)}) collective-permute-start(bf16[512,256]{1,0:T(8,128)(2,1)S(1)} %slice.24.own), channel_id=1, source_target_pairs={{4,8},{8,4},{5,9},{9,5},{6,10},{10,6},{7,11},{11,7},{20,24},{24,20... | collective-permute-start | bytes 786440 | tf_op jit(solution)/shard_map/ppermute | solution.py:370
  4.8 9.3 %collective-permute-start.1 = (bf16[512,256]{1,0:T(8,128)(2,1)S(1)}, bf16[512,256]{1,0:T(8,128)(2,1)S(1)}, u32[]{:S(2)}, u32[]{:S(2)}) collective-permute-start(bf16[512,256]{1,0:T(8,128)(2,1)S(1)} %slice.24.own), channel_id=1, source_target_pairs={{0,4},{4,0},{8,12},{12,8},{1,5},{5,1},{9,13},{13,9},{2,6},{6,2},{1... | collective-permute-start | bytes 786440 | tf_op jit(solution)/shard_map/ppermute | solution.py:371
  5.8 9.1 %collective-permute-start = (bf16[512,128]{1,0:T(8,128)(2,1)S(1)}, bf16[512,128]{1,0:T(8,128)(2,1)S(1)}, u32[]{:S(2)}, u32[]{:S(2)}) collective-permute-start(bf16[512,128]{1,0:T(8,128)(2,1)S(1)} %constant_dynamic-slice_fusion), channel_id=1, source_target_pairs={{4,8},{8,4},{5,9},{9,5},{6,10},{10,6},{7,11},{11,7},{20,24},{24,20... | collective-permute-start | bytes 393224 | tf_op jit(solution)/shard_map/ppermute | solution.py:370
  9.1 9.4 %collective-permute-start.3 = (bf16[512,256]{1,0:T(8,128)(2,1)S(1)}, bf16[512,256]{1,0:T(8,128)(2,1)S(1)}, u32[]{:S(2)}, u32[]{:S(2)}) collective-permute-start(bf16[512,256]{1,0:T(8,128)(2,1)S(1)} %slice.25.own), channel_id=1, source_target_pairs={{0,4},{4,0},{8,12},{12,8},{1,5},{5,1},{9,13},{13,9},{2,6},{6,2},{1... | collective-permute-start | bytes 786440 | tf_op jit(solution)/shard_map/ppermute | solution.py:371
  9.6 33.0 %copy-start.2 = (s32[4]{0:T(128)S(1)}, s32[4]{0:T(128)}, u32[]{:S(2)}) copy-start(s32[4]{0:T(128)} %param.8) | copy-start | bytes 52
  14.9 5.0 %collective-permute-start.4 = (bf16[512,128]{1,0:T(8,128)(2,1)S(1)}, bf16[512,128]{1,0:T(8,128)(2,1)S(1)}, u32[]{:S(2)}, u32[]{:S(2)}) collective-permute-start(bf16[512,128]{1,0:T(8,128)(2,1)S(1)} %collective-permute-done.inner), channel_id=1, source_target_pairs={{0,2},{2,0},{1,3},{3,1},{4,6},{6,4},{5,7},{7,5},{8,10},{10,8},{9,1... | collective-permute-start | bytes 393224 | tf_op jit(solution)/shard_map/ppermute | solution.py:377
  16.5 13.6 %collective-permute-start.5 = (bf16[2,256,256]{2,1,0:T(8,128)(2,1)S(1)}, bf16[2,256,256]{2,1,0:T(8,128)(2,1)S(1)}, u32[]{:S(2)}, u32[]{:S(2)}) collective-permute-start(bf16[2,256,256]{2,1,0:T(8,128)(2,1)S(1)} %get-tuple-element.30), channel_id=1, source_target_pairs={{0,8},{4,12},{8,0},{12,4},{1,9},{5,13},{9,1},{13,5},{2,10},{6,14},... | collective-permute-start | bytes 786440 | tf_op jit(solution)/shard_map/ppermute | solution.py:386
  16.5 15.0 %collective-permute-start.7 = (bf16[2,256,256]{2,1,0:T(8,128)(2,1)S(1)}, bf16[2,256,256]{2,1,0:T(8,128)(2,1)S(1)}, u32[]{:S(2)}, u32[]{:S(2)}) collective-permute-start(bf16[2,256,256]{2,1,0:T(8,128)(2,1)S(1)} %get-tuple-element.32), channel_id=1, source_target_pairs={{0,4},{4,0},{8,12},{12,8},{1,5},{5,1},{9,13},{13,9},{2,6},{6,2},{1... | collective-permute-start | bytes 786440 | tf_op jit(solution)/shard_map/ppermute | solution.py:386
  20.9 20.3 %collective-permute-start.6 = (bf16[2,256,256]{2,1,0:T(8,128)(2,1)S(1)}, bf16[2,256,256]{2,1,0:T(8,128)(2,1)S(1)}, u32[]{:S(2)}, u32[]{:S(2)}) collective-permute-start(bf16[2,256,256]{2,1,0:T(8,128)(2,1)S(1)} %get-tuple-element.31), channel_id=1, source_target_pairs={{0,8},{4,12},{8,0},{12,4},{1,9},{5,13},{9,1},{13,5},{2,10},{6,14},... | collective-permute-start | bytes 786440 | tf_op jit(solution)/shard_map/ppermute | solution.py:386
  22.3 20.3 %collective-permute-start.8 = (bf16[2,256,256]{2,1,0:T(8,128)(2,1)S(1)}, bf16[2,256,256]{2,1,0:T(8,128)(2,1)S(1)}, u32[]{:S(2)}, u32[]{:S(2)}) collective-permute-start(bf16[2,256,256]{2,1,0:T(8,128)(2,1)S(1)} %get-tuple-element.33), channel_id=1, source_target_pairs={{0,4},{4,0},{8,12},{12,8},{1,5},{5,1},{9,13},{13,9},{2,6},{6,2},{1... | collective-permute-start | bytes 786440 | tf_op jit(solution)/shard_map/ppermute | solution.py:386
  23.1 34.5 %collective-permute-start.11 = (bf16[2,256,256]{2,1,0:T(8,128)(2,1)S(1)}, bf16[2,256,256]{2,1,0:T(8,128)(2,1)S(1)}, u32[]{:S(2)}, u32[]{:S(2)}) collective-permute-start(bf16[2,256,256]{2,1,0:T(8,128)(2,1)S(1)} %get-tuple-element.37), channel_id=1, source_target_pairs={{0,12},{4,8},{8,4},{12,0},{1,13},{5,9},{9,5},{13,1},{2,14},{6,10},... | collective-permute-start | bytes 786440 | tf_op jit(solution)/shard_map/ppermute | solution.py:386
  30.0 31.6 %collective-permute-start.12 = (bf16[2,256,256]{2,1,0:T(8,128)(2,1)S(1)}, bf16[2,256,256]{2,1,0:T(8,128)(2,1)S(1)}, u32[]{:S(2)}, u32[]{:S(2)}) collective-permute-start(bf16[2,256,256]{2,1,0:T(8,128)(2,1)S(1)} %get-tuple-element.38), channel_id=1, source_target_pairs={{0,12},{4,8},{8,4},{12,0},{1,13},{5,9},{9,5},{13,1},{2,14},{6,10},... | collective-permute-start | bytes 786440 | tf_op jit(solution)/shard_map/ppermute | solution.py:386
  43.7 19.7 %collective-permute-start.9 = (bf16[2,3,64,256]{3,2,1,0:T(8,128)(2,1)S(1)}, bf16[2,3,64,256]{3,2,1,0:T(8,128)(2,1)S(1)}, u32[]{:S(2)}, u32[]{:S(2)}) collective-permute-start(bf16[2,3,64,256]{3,2,1,0:T(8,128)(2,1)S(1)} %get-tuple-element.36), channel_id=1, source_target_pairs={{0,2},{2,0},{1,3},{3,1},{4,6},{6,4},{5,7},{7,5},{8,10},{10,8},{9,1... | collective-permute-start | bytes 589832 | tf_op jit(solution)/shard_map/ppermute | solution.py:391
  62.3 1.6 %collective-permute-start.15 = (f32[2,2,64,256]{3,2,1,0:T(8,128)S(1)}, f32[2,2,64,256]{3,2,1,0:T(8,128)S(1)}, u32[]{:S(2)}, u32[]{:S(2)}) collective-permute-start(f32[2,2,64,256]{3,2,1,0:T(8,128)S(1)} %get-tuple-element.42), channel_id=1, source_target_pairs={{0,1},{1,0},{2,3},{3,2},{4,5},{5,4},{6,7},{7,6},{8,9},{9,8},{10,11... | collective-permute-start | bytes 786440 | tf_op jit(solution)/shard_map/ppermute | solution.py:395
  62.8 1.8 %collective-permute-start.13 = (f32[2,1,64,256]{3,2,1,0:T(8,128)S(1)}, f32[2,1,64,256]{3,2,1,0:T(8,128)S(1)}, u32[]{:S(2)}, u32[]{:S(2)}) collective-permute-start(f32[2,1,64,256]{3,2,1,0:T(8,128)S(1)} %get-tuple-element.40), channel_id=1, source_target_pairs={{0,1},{1,0},{2,3},{3,2},{4,5},{5,4},{6,7},{7,6},{8,9},{9,8},{10,11... | collective-permute-start | bytes 393224 | tf_op jit(solution)/shard_map/ppermute | solution.py:395
  63.4 5.5 %collective-permute-start.10 = (f32[3,64,256]{2,1,0:T(8,128)S(1)}, f32[3,64,256]{2,1,0:T(8,128)S(1)}, u32[]{:S(2)}, u32[]{:S(2)}) collective-permute-start(f32[3,64,256]{2,1,0:T(8,128)S(1)} %add_bitcast_fusion), channel_id=1, source_target_pairs={{0,1},{1,0},{2,3},{3,2},{4,5},{5,4},{6,7},{7,6},{8,9},{9,8},{10,11... | collective-permute-start | bytes 589832 | tf_op jit(solution)/shard_map/ppermute | solution.py:398
  64.0 4.9 %collective-permute-start.16 = (bf16[2,64,256]{2,1,0:T(8,128)(2,1)S(1)}, bf16[2,64,256]{2,1,0:T(8,128)(2,1)S(1)}, u32[]{:S(2)}, u32[]{:S(2)}) collective-permute-start(bf16[2,64,256]{2,1,0:T(8,128)(2,1)S(1)} %fusion.1), channel_id=1, source_target_pairs={{0,2},{2,0},{1,3},{3,1},{4,6},{6,4},{5,7},{7,5},{8,10},{10,8},{9,1... | collective-permute-start | bytes 196616 | tf_op jit(solution)/shard_map/ppermute | solution.py:396
  64.6 4.2 %collective-permute-start.14 = (bf16[1,64,256]{2,1,0:T(8,128)(2,1)S(1)}, bf16[1,64,256]{2,1,0:T(8,128)(2,1)S(1)}, u32[]{:S(2)}, u32[]{:S(2)}) collective-permute-start(bf16[1,64,256]{2,1,0:T(8,128)(2,1)S(1)} %fusion.3), channel_id=1, source_target_pairs={{0,2},{2,0},{1,3},{3,1},{4,6},{6,4},{5,7},{7,5},{8,10},{10,8},{9,1... | collective-permute-start | bytes 98312 | tf_op jit(solution)/shard_map/ppermute | solution.py:396

commit v10 on v7

--- a/solution.py
+++ b/solution.py
@@ -231,10 +231,9 @@
 
 
 def early_kernel(live, table, *refs):
-    used = 3 * CHUNKS
-    own, middle, next_to = [refs[i : i + CHUNKS] for i in range(0, used, CHUNKS)]
-    blocks = own, next_to, middle
-    near, far, place, grams = refs[used:]
+    own, (middle0, next0, _, middle1, next1), refs = refs[:CHUNKS], refs[CHUNKS:-4], refs[-4:]
+    blocks = own, (next0, next1), (middle0, middle1)
+    near, far, place, grams = refs
     here, aux, orb = (lax.axis_index(axis) for axis in ("ao", "aux", "orb"))
     slots, width = place.shape
     slot = lax.broadcasted_iota(jnp.int32, (slots, table.shape[1]), 0)
@@ -282,6 +281,8 @@
 
 def early_pairs(live, table, blocks):
     shape, grams = quarters(EARLY_PAIRS)
+    own, (next0, next1), (middle0, middle1), (last0, _) = blocks
+    order = middle0, next0, last0, middle1, next1
     return local_call(
         early_kernel,
         "early_pairs",
@@ -290,10 +291,10 @@
             like(shape, jnp.bfloat16),
             like((table.shape[1] // GROUPS, BLOCK), jnp.int32),
         ],
-        2 + 3 * CHUNKS,
+        3 + 3 * CHUNKS,
         pair_flops(EARLY_PAIRS, blocks),
         [grams],
-    )(live.reshape(1, -1), table, *blocks[0], *blocks[2], *blocks[1])
+    )(live.reshape(1, -1), table, *blocks[0], *order)
 
 
 def late_pairs(blocks):
@@ -382,9 +383,9 @@
 
     middle = fetch(2)
     got = [blocks[0], fetch(1), middle]
+    got.append(fetch(3))
     near0, across0, place = early_pairs(pair_count, table, got)
     far0 = lax.ppermute(across0, "aux", SWAP)
-    got.append(fetch(3))
     near1, give1 = late_pairs(got)
     got1 = lax.ppermute(give1, "orb", SWAP)
     far1 = lax.ppermute((near1[1] + got1[1]).astype(jnp.bfloat16), "aux", SWAP)

time: 68.8 us -> 72.7 us (1.057)
  the two profiles are of different devices: /device:TPU:8 before, /device:TPU:0 now
where the time goes in v10:
time: 72.7 us; the launch traced here: 72.5 us
  waiting for transfers between devices  42.5 us (58%)
  starting transfers between devices  22 us (30%)
  Pallas kernels  4.91 us (7%)
  local copies, waits for them, and re-layouts  2.88 us (4%)
    ppermute x6, waiting for transfers between devices, fetch(): return [lax.ppermute(piece, 'ao', swap) for piece in blocks[s]]  30.9 us
    ppermute x6, starting transfers between devices, fetch(): return [lax.ppermute(piece, 'ao', swap) for piece in blocks[s]]  7.96 us
    ppermute x2, starting transfers between devices, six_pair_body(): outer = [lax.ppermute(part, 'ao', OUTSIDE) for part in parts]  7.81 us
    ppermute x2, waiting for transfers between devices, six_pair_body(): outer = [lax.ppermute(part, 'ao', OUTSIDE) for part in parts]  4.61 us
    ppermute x1, waiting for transfers between devices, six_pair_body(): far1 = lax.ppermute((near1[1] + got1[1]).astype(jnp.bfloat16), 'aux', SWAP)  3.69 us
    ppermute x1, waiting for transfers between devices, six_pair_body(): far0 = lax.ppermute(across0, 'aux', SWAP)  3.23 us
    ppermute x1, starting transfers between devices, six_pair_body(): far0 = lax.ppermute(across0, 'aux', SWAP)  1.56 us
    ppermute x1, starting transfers between devices, six_pair_body(): far1 = lax.ppermute((near1[1] + got1[1]).astype(jnp.bfloat16), 'aux', SWAP)  1.56 us
  transfers between devices with their start and end apart: 15, of which 8 were waited for; matrix products, arithmetic and copies ran while one was open for 3% of the time, Pallas kernels for 5%

profile of v10, /device:TPU:0, one launch (start us, length us, event | category | flops | bytes accessed | tf_op | source)
XLA Modules:
  0.0 72.5 jit_solution(5566549540340836436)
XLA Ops:
  0.0 1.0 %slice.18.own = bf16[512,256]{1,0:T(8,128)(2,1)S(1)} slice(bf16[512,512]{1,0:T(8,128)(2,1)} %param.6), slice={[0:512], [0:256]} | slice | bytes 524288 | tf_op jit(solution)/shard_map/slice | solution.py:362
  1.8 6.0 %collective-permute-start.1 = (bf16[512,256]{1,0:T(8,128)(2,1)S(1)}, bf16[512,256]{1,0:T(8,128)(2,1)S(1)}, u32[]{:S(2)}, u32[]{:S(2)}) collective-permute-start(bf16[512,256]{1,0:T(8,128)(2,1)S(1)} %slice.18.own), channel_id=1, source_target_pairs={{0,4},{4,0},{8,12},{12,8},{1,5},{5,1},{9,13},{13,9},{2,6},{6,2},{1... | collective-permute-start | bytes 786440 | tf_op jit(solution)/shard_map/ppermute | solution.py:367
  7.9 0.9 %constant_dynamic-slice_fusion = bf16[512,128]{1,0:T(8,128)(2,1)S(1)} fusion(bf16[512,512]{1,0:T(8,128)(2,1)} %param.6, s32[]{:T(128)S(6)} %select_n.3), kind=kLoop, calls=%fused_computation.4 | loop fusion | bytes 262148 | tf_op jit(solution)/shard_map/dynamic_slice | solution.py:365
  9.4 1.0 %slice.19.own = bf16[512,256]{1,0:T(8,128)(2,1)S(1)} slice(bf16[512,512]{1,0:T(8,128)(2,1)} %param.6), slice={[0:512], [256:512]} | slice | bytes 524288 | tf_op jit(solution)/shard_map/slice | solution.py:364
  10.4 1.8 %collective-permute-start.3 = (bf16[512,256]{1,0:T(8,128)(2,1)S(1)}, bf16[512,256]{1,0:T(8,128)(2,1)S(1)}, u32[]{:S(2)}, u32[]{:S(2)}) collective-permute-start(bf16[512,256]{1,0:T(8,128)(2,1)S(1)} %slice.19.own), channel_id=1, source_target_pairs={{0,4},{4,0},{8,12},{12,8},{1,5},{5,1},{9,13},{13,9},{2,6},{6,2},{1... | collective-permute-start | bytes 786440 | tf_op jit(solution)/shard_map/ppermute | solution.py:367
  12.4 2.6 %collective-permute-done.1.outer = bf16[512,256]{1,0:T(8,128)(2,1)S(1)} collective-permute-done((bf16[512,256]{1,0:T(8,128)(2,1)S(1)}, bf16[512,256]{1,0:T(8,128)(2,1)S(1)}, u32[]{:S(2)}, u32[]{:S(2)}) %collective-permute-start.1) | collective-permute-done | bytes 262176 | tf_op jit(solution)/shard_map/ppermute | solution.py:367
  15.9 1.4 %collective-permute-start.5 = (bf16[2,256,256]{2,1,0:T(8,128)(2,1)S(1)}, bf16[2,256,256]{2,1,0:T(8,128)(2,1)S(1)}, u32[]{:S(2)}, u32[]{:S(2)}) collective-permute-start(bf16[2,256,256]{2,1,0:T(8,128)(2,1)S(1)} %get-tuple-element.28), channel_id=1, source_target_pairs={{0,8},{4,12},{8,0},{12,4},{1,9},{5,13},{9,1},{13,5},{2,10},{6,14},... | collective-permute-start | bytes 786440 | tf_op jit(solution)/shard_map/ppermute | solution.py:382
  17.3 1.5 %collective-permute-start.4 = (bf16[512,128]{1,0:T(8,128)(2,1)S(1)}, bf16[512,128]{1,0:T(8,128)(2,1)S(1)}, u32[]{:S(2)}, u32[]{:S(2)}) collective-permute-start(bf16[512,128]{1,0:T(8,128)(2,1)S(1)} %collective-permute-done.inner), channel_id=1, source_target_pairs={{0,2},{2,0},{1,3},{3,1},{4,6},{6,4},{5,7},{7,5},{8,10},{10,8},{9,1... | collective-permute-start | bytes 393224 | tf_op jit(solution)/shard_map/ppermute | solution.py:373
  19.6 2.3 %collective-permute-start.7 = (bf16[2,256,256]{2,1,0:T(8,128)(2,1)S(1)}, bf16[2,256,256]{2,1,0:T(8,128)(2,1)S(1)}, u32[]{:S(2)}, u32[]{:S(2)}) collective-permute-start(bf16[2,256,256]{2,1,0:T(8,128)(2,1)S(1)} %get-tuple-element.30), channel_id=1, source_target_pairs={{0,12},{4,8},{8,4},{12,0},{1,13},{5,9},{9,5},{13,1},{2,14},{6,10},... | collective-permute-start | bytes 786440 | tf_op jit(solution)/shard_map/ppermute | solution.py:382
  21.9 2.0 %collective-permute-done.3.outer = bf16[512,256]{1,0:T(8,128)(2,1)S(1)} collective-permute-done((bf16[512,256]{1,0:T(8,128)(2,1)S(1)}, bf16[512,256]{1,0:T(8,128)(2,1)S(1)}, u32[]{:S(2)}, u32[]{:S(2)}) %collective-permute-start.3) | collective-permute-done | bytes 262176 | tf_op jit(solution)/shard_map/ppermute | solution.py:367
  23.8 0.9 %transform.3 = (bf16[2,256,256]{2,1,0:T(8,128)(2,1)S(1)}, bf16[2,256,256]{2,1,0:T(8,128)(2,1)S(1)}, bf16[2,256,256]{2,1,0:T(8,128)(2,1)S(1)}, bf16[2,256,256]{2,1,0:T(8,128)(2,1)S(1)}) custom-call(s32[8,256]{1,0:T(8,128)S(1)} %tables.1.wants, bf16[2,512,1280]{2,1,0:T(8,128)(2,1)S(1)} %copy-done, bf16[512,256]{1,0:T(8,128)(2,1)S(1)} %slice.19.own, ...), custom_call_target="tpu_custom_call" | custom-call | flops 671088640 | bytes 2097152 | tf_op jit(solution)/shard_map/transform/pallas_call | solution.py:184
  24.9 2.1 %collective-permute-start.9 = (bf16[2,256,256]{2,1,0:T(8,128)(2,1)S(1)}, bf16[2,256,256]{2,1,0:T(8,128)(2,1)S(1)}, u32[]{:S(2)}, u32[]{:S(2)}) collective-permute-start(bf16[2,256,256]{2,1,0:T(8,128)(2,1)S(1)} %get-tuple-element.32), channel_id=1, source_target_pairs={{0,4},{4,0},{8,12},{12,8},{1,5},{5,1},{9,13},{13,9},{2,6},{6,2},{1... | collective-permute-start | bytes 786440 | tf_op jit(solution)/shard_map/ppermute | solution.py:382
  27.0 4.8 %collective-permute-done.5.refs_2_ = bf16[2,256,256]{2,1,0:T(8,128)(2,1)S(1)} collective-permute-done((bf16[2,256,256]{2,1,0:T(8,128)(2,1)S(1)}, bf16[2,256,256]{2,1,0:T(8,128)(2,1)S(1)}, u32[]{:S(2)}, u32[]{:S(2)}) %collective-permute-start.5) | collective-permute-done | bytes 262176 | tf_op jit(solution)/shard_map/ppermute | solution.py:382
  31.8 1.3 %collective-permute-start.12 = (bf16[2,256,256]{2,1,0:T(8,128)(2,1)S(1)}, bf16[2,256,256]{2,1,0:T(8,128)(2,1)S(1)}, u32[]{:S(2)}, u32[]{:S(2)}) collective-permute-start(bf16[2,256,256]{2,1,0:T(8,128)(2,1)S(1)} %get-tuple-element.36), channel_id=1, source_target_pairs={{0,12},{4,8},{8,4},{12,0},{1,13},{5,9},{9,5},{13,1},{2,14},{6,10},... | collective-permute-start | bytes 786440 | tf_op jit(solution)/shard_map/ppermute | solution.py:382
  33.1 3.3 %collective-permute-done.6.refs_3_.refs_4_ = bf16[2,256,256]{2,1,0:T(8,128)(2,1)S(1)} collective-permute-done((bf16[2,256,256]{2,1,0:T(8,128)(2,1)S(1)}, bf16[2,256,256]{2,1,0:T(8,128)(2,1)S(1)}, u32[]{:S(2)}, u32[]{:S(2)}) %collective-permute-start.6) | collective-permute-done | bytes 262176 | tf_op jit(solution)/shard_map/ppermute | solution.py:382
  36.4 2.6 %collective-permute-done.7.refs_4_.refs_6_ = bf16[2,256,256]{2,1,0:T(8,128)(2,1)S(1)} collective-permute-done((bf16[2,256,256]{2,1,0:T(8,128)(2,1)S(1)}, bf16[2,256,256]{2,1,0:T(8,128)(2,1)S(1)}, u32[]{:S(2)}, u32[]{:S(2)}) %collective-permute-start.7) | collective-permute-done | bytes 262176 | tf_op jit(solution)/shard_map/ppermute | solution.py:382
  39.0 20.2 %collective-permute-done.8.refs_5_.refs_3_ = bf16[2,256,256]{2,1,0:T(8,128)(2,1)S(1)} collective-permute-done((bf16[2,256,256]{2,1,0:T(8,128)(2,1)S(1)}, bf16[2,256,256]{2,1,0:T(8,128)(2,1)S(1)}, u32[]{:S(2)}, u32[]{:S(2)}) %collective-permute-start.8) | collective-permute-done | bytes 262176 | tf_op jit(solution)/shard_map/ppermute | solution.py:382
  59.2 1.0 %early_pairs.1 = (f32[2,3,64,256]{3,2,1,0:T(8,128)S(1)}, bf16[2,3,64,256]{3,2,1,0:T(8,128)(2,1)S(1)}, s32[16,256]{1,0:T(8,128)S(1)}) custom-call(s32[1,4]{1,0:T(1,128)S(1)} %bitcast.10, s32[2,64]{1,0:T(2,128)S(1)} %bitcast.8, bf16[2,256,256]{2,1,0:T(8,128)(2,1)S(1)} %get-tuple-element.25.refs_0_, bf16[2,256,256]{2,1,0:T(8,128)(2,1)S(1)} %get-tuple-element.27.refs_1_, ...), custom_call_target="tpu_custom_call" | custom-call | flops 402653184 | bytes 1212416 | tf_op jit(solution)/shard_map/early_pairs/pallas_call | solution.py:286
  60.2 1.6 %collective-permute-start.10 = (bf16[2,3,64,256]{3,2,1,0:T(8,128)(2,1)S(1)}, bf16[2,3,64,256]{3,2,1,0:T(8,128)(2,1)S(1)}, u32[]{:S(2)}, u32[]{:S(2)}) collective-permute-start(bf16[2,3,64,256]{3,2,1,0:T(8,128)(2,1)S(1)} %get-tuple-element.35), channel_id=1, source_target_pairs={{0,2},{2,0},{1,3},{3,1},{4,6},{6,4},{5,7},{7,5},{8,10},{10,8},{9,1... | collective-permute-start | bytes 589832 | tf_op jit(solution)/shard_map/ppermute | solution.py:388
  61.8 0.9 %late_pairs.1 = (f32[2,3,64,256]{3,2,1,0:T(8,128)S(1)}, f32[2,3,64,256]{3,2,1,0:T(8,128)S(1)}) custom-call(bf16[2,256,256]{2,1,0:T(8,128)(2,1)S(1)} %get-tuple-element.25.refs_0_, bf16[2,256,256]{2,1,0:T(8,128)(2,1)S(1)} %get-tuple-element.27.refs_1_, bf16[2,256,256]{2,1,0:T(8,128)(2,1)S(1)} %collective-permute-done.5.refs_2_, ...), custom_call_target="tpu_custom_call" | custom-call | flops 402653184 | bytes 1572864 | tf_op jit(solution)/shard_map/late_pairs/pallas_call | solution.py:302
  62.7 3.2 %collective-permute-done.10.far0 = bf16[2,3,64,256]{3,2,1,0:T(8,128)(2,1)S(1)} collective-permute-done((bf16[2,3,64,256]{3,2,1,0:T(8,128)(2,1)S(1)}, bf16[2,3,64,256]{3,2,1,0:T(8,128)(2,1)S(1)}, u32[]{:S(2)}, u32[]{:S(2)}) %collective-permute-start.10) | collective-permute-done | bytes 196640 | tf_op jit(solution)/shard_map/ppermute | solution.py:388
  66.1 1.6 %collective-permute-start.14 = (bf16[3,64,256]{2,1,0:T(8,128)(2,1)S(1)}, bf16[3,64,256]{2,1,0:T(8,128)(2,1)S(1)}, u32[]{:S(2)}, u32[]{:S(2)}) collective-permute-start(bf16[3,64,256]{2,1,0:T(8,128)(2,1)S(1)} %fusion.1), channel_id=1, source_target_pairs={{0,2},{2,0},{1,3},{3,1},{4,6},{6,4},{5,7},{7,5},{8,10},{10,8},{9,1... | collective-permute-start | bytes 294920 | tf_op jit(solution)/shard_map/ppermute | solution.py:391
  67.6 3.7 %collective-permute-done.14.far1 = bf16[3,64,256]{2,1,0:T(8,128)(2,1)S(1)} collective-permute-done((bf16[3,64,256]{2,1,0:T(8,128)(2,1)S(1)}, bf16[3,64,256]{2,1,0:T(8,128)(2,1)S(1)}, u32[]{:S(2)}, u32[]{:S(2)}) %collective-permute-start.14) | collective-permute-done | bytes 98336 | tf_op jit(solution)/shard_map/ppermute | solution.py:391
  71.3 1.1 %spread.1 = f32[64,16,256]{2,1,0:T(8,128)} custom-call(s32[16,256]{1,0:T(8,128)S(1)} %get-tuple-element.33.place, f32[2,3,64,256]{3,2,1,0:T(8,128)S(1)} %get-tuple-element.34.near0, bf16[2,3,64,256]{3,2,1,0:T(8,128)(2,1)S(1)} %collective-permute-done.10.far0, f32[3,64,256]{2,1,0:T(8,128)S(1)} %collective-permute-done.11.got0, ...), custom_call_target="tpu_custom_call" | custom-call | flops 1572864 | bytes 2097152 | tf_op jit(solution)/shard_map/spread/pallas_call | solution.py:341
  (26 shorter events, 3.5 us)
Async XLA Ops:
  1.0 11.2 %copy-start.1 = (s32[64,2]{0,1:T(2,128)S(1)}, s32[64,2]{0,1:T(2,128)}, u32[]{:S(2)}) copy-start(s32[64,2]{0,1:T(2,128)} %param.7) | copy-start | bytes 1540
  1.0 11.2 %copy-start.2 = (s32[8]{0:T(128)S(1)}, s32[8]{0:T(128)}, u32[]{:S(2)}) copy-start(s32[8]{0:T(128)} %param.9) | copy-start | bytes 100
  1.0 14.0 %copy-start = (bf16[2,512,1280]{2,1,0:T(8,128)(2,1)S(1)}, bf16[2,512,1280]{2,1,0:T(8,128)(2,1)}, u32[]{:S(2)}) copy-start(bf16[2,512,1280]{2,1,0:T(8,128)(2,1)} %integrals.3) | copy-start | bytes 7864324
  1.0 11.4 %collective-permute-start.2 = (bf16[512,256]{1,0:T(8,128)(2,1)S(1)}, bf16[512,256]{1,0:T(8,128)(2,1)S(1)}, u32[]{:S(2)}, u32[]{:S(2)}) collective-permute-start(bf16[512,256]{1,0:T(8,128)(2,1)S(1)} %slice.18.own), channel_id=1, source_target_pairs={{4,8},{8,4},{5,9},{9,5},{6,10},{10,6},{7,11},{11,7},{20,24},{24,20... | collective-permute-start | bytes 786440 | tf_op jit(solution)/shard_map/ppermute | solution.py:366
  1.8 13.2 %collective-permute-start.1 = (bf16[512,256]{1,0:T(8,128)(2,1)S(1)}, bf16[512,256]{1,0:T(8,128)(2,1)S(1)}, u32[]{:S(2)}, u32[]{:S(2)}) collective-permute-start(bf16[512,256]{1,0:T(8,128)(2,1)S(1)} %slice.18.own), channel_id=1, source_target_pairs={{0,4},{4,0},{8,12},{12,8},{1,5},{5,1},{9,13},{13,9},{2,6},{6,2},{1... | collective-permute-start | bytes 786440 | tf_op jit(solution)/shard_map/ppermute | solution.py:367
  8.8 8.6 %collective-permute-start = (bf16[512,128]{1,0:T(8,128)(2,1)S(1)}, bf16[512,128]{1,0:T(8,128)(2,1)S(1)}, u32[]{:S(2)}, u32[]{:S(2)}) collective-permute-start(bf16[512,128]{1,0:T(8,128)(2,1)S(1)} %constant_dynamic-slice_fusion), channel_id=1, source_target_pairs={{4,8},{8,4},{5,9},{9,5},{6,10},{10,6},{7,11},{11,7},{20,24},{24,20... | collective-permute-start | bytes 393224 | tf_op jit(solution)/shard_map/ppermute | solution.py:366
  10.4 13.4 %collective-permute-start.3 = (bf16[512,256]{1,0:T(8,128)(2,1)S(1)}, bf16[512,256]{1,0:T(8,128)(2,1)S(1)}, u32[]{:S(2)}, u32[]{:S(2)}) collective-permute-start(bf16[512,256]{1,0:T(8,128)(2,1)S(1)} %slice.19.own), channel_id=1, source_target_pairs={{0,4},{4,0},{8,12},{12,8},{1,5},{5,1},{9,13},{13,9},{2,6},{6,2},{1... | collective-permute-start | bytes 786440 | tf_op jit(solution)/shard_map/ppermute | solution.py:367
  12.4 46.8 %copy-start.3 = (s32[4]{0:T(128)S(1)}, s32[4]{0:T(128)}, u32[]{:S(2)}) copy-start(s32[4]{0:T(128)} %param.8) | copy-start | bytes 52
  15.9 15.9 %collective-permute-start.5 = (bf16[2,256,256]{2,1,0:T(8,128)(2,1)S(1)}, bf16[2,256,256]{2,1,0:T(8,128)(2,1)S(1)}, u32[]{:S(2)}, u32[]{:S(2)}) collective-permute-start(bf16[2,256,256]{2,1,0:T(8,128)(2,1)S(1)} %get-tuple-element.28), channel_id=1, source_target_pairs={{0,8},{4,12},{8,0},{12,4},{1,9},{5,13},{9,1},{13,5},{2,10},{6,14},... | collective-permute-start | bytes 786440 | tf_op jit(solution)/shard_map/ppermute | solution.py:382
  17.3 6.5 %collective-permute-start.4 = (bf16[512,128]{1,0:T(8,128)(2,1)S(1)}, bf16[512,128]{1,0:T(8,128)(2,1)S(1)}, u32[]{:S(2)}, u32[]{:S(2)}) collective-permute-start(bf16[512,128]{1,0:T(8,128)(2,1)S(1)} %collective-permute-done.inner), channel_id=1, source_target_pairs={{0,2},{2,0},{1,3},{3,1},{4,6},{6,4},{5,7},{7,5},{8,10},{10,8},{9,1... | collective-permute-start | bytes 393224 | tf_op jit(solution)/shard_map/ppermute | solution.py:373
  18.8 17.5 %collective-permute-start.6 = (bf16[2,256,256]{2,1,0:T(8,128)(2,1)S(1)}, bf16[2,256,256]{2,1,0:T(8,128)(2,1)S(1)}, u32[]{:S(2)}, u32[]{:S(2)}) collective-permute-start(bf16[2,256,256]{2,1,0:T(8,128)(2,1)S(1)} %get-tuple-element.29), channel_id=1, source_target_pairs={{0,4},{4,0},{8,12},{12,8},{1,5},{5,1},{9,13},{13,9},{2,6},{6,2},{1... | collective-permute-start | bytes 786440 | tf_op jit(solution)/shard_map/ppermute | solution.py:382
  19.6 19.4 %collective-permute-start.7 = (bf16[2,256,256]{2,1,0:T(8,128)(2,1)S(1)}, bf16[2,256,256]{2,1,0:T(8,128)(2,1)S(1)}, u32[]{:S(2)}, u32[]{:S(2)}) collective-permute-start(bf16[2,256,256]{2,1,0:T(8,128)(2,1)S(1)} %get-tuple-element.30), channel_id=1, source_target_pairs={{0,12},{4,8},{8,4},{12,0},{1,13},{5,9},{9,5},{13,1},{2,14},{6,10},... | collective-permute-start | bytes 786440 | tf_op jit(solution)/shard_map/ppermute | solution.py:382
  24.8 34.4 %collective-permute-start.8 = (bf16[2,256,256]{2,1,0:T(8,128)(2,1)S(1)}, bf16[2,256,256]{2,1,0:T(8,128)(2,1)S(1)}, u32[]{:S(2)}, u32[]{:S(2)}) collective-permute-start(bf16[2,256,256]{2,1,0:T(8,128)(2,1)S(1)} %get-tuple-element.31), channel_id=1, source_target_pairs={{0,8},{4,12},{8,0},{12,4},{1,9},{5,13},{9,1},{13,5},{2,10},{6,14},... | collective-permute-start | bytes 786440 | tf_op jit(solution)/shard_map/ppermute | solution.py:382
  24.9 34.3 %collective-permute-start.9 = (bf16[2,256,256]{2,1,0:T(8,128)(2,1)S(1)}, bf16[2,256,256]{2,1,0:T(8,128)(2,1)S(1)}, u32[]{:S(2)}, u32[]{:S(2)}) collective-permute-start(bf16[2,256,256]{2,1,0:T(8,128)(2,1)S(1)} %get-tuple-element.32), channel_id=1, source_target_pairs={{0,4},{4,0},{8,12},{12,8},{1,5},{5,1},{9,13},{13,9},{2,6},{6,2},{1... | collective-permute-start | bytes 786440 | tf_op jit(solution)/shard_map/ppermute | solution.py:382
  31.8 30.0 %collective-permute-start.12 = (bf16[2,256,256]{2,1,0:T(8,128)(2,1)S(1)}, bf16[2,256,256]{2,1,0:T(8,128)(2,1)S(1)}, u32[]{:S(2)}, u32[]{:S(2)}) collective-permute-start(bf16[2,256,256]{2,1,0:T(8,128)(2,1)S(1)} %get-tuple-element.36), channel_id=1, source_target_pairs={{0,12},{4,8},{8,4},{12,0},{1,13},{5,9},{9,5},{13,1},{2,14},{6,10},... | collective-permute-start | bytes 786440 | tf_op jit(solution)/shard_map/ppermute | solution.py:382
  60.2 5.7 %collective-permute-start.10 = (bf16[2,3,64,256]{3,2,1,0:T(8,128)(2,1)S(1)}, bf16[2,3,64,256]{3,2,1,0:T(8,128)(2,1)S(1)}, u32[]{:S(2)}, u32[]{:S(2)}) collective-permute-start(bf16[2,3,64,256]{3,2,1,0:T(8,128)(2,1)S(1)} %get-tuple-element.35), channel_id=1, source_target_pairs={{0,2},{2,0},{1,3},{3,1},{4,6},{6,4},{5,7},{7,5},{8,10},{10,8},{9,1... | collective-permute-start | bytes 589832 | tf_op jit(solution)/shard_map/ppermute | solution.py:388
  62.6 3.4 %collective-permute-start.13 = (f32[2,3,64,256]{3,2,1,0:T(8,128)S(1)}, f32[2,3,64,256]{3,2,1,0:T(8,128)S(1)}, u32[]{:S(2)}, u32[]{:S(2)}) collective-permute-start(f32[2,3,64,256]{3,2,1,0:T(8,128)S(1)} %get-tuple-element.38), channel_id=1, source_target_pairs={{0,1},{1,0},{2,3},{3,2},{4,5},{5,4},{6,7},{7,6},{8,9},{9,8},{10,11... | collective-permute-start | bytes 1179656 | tf_op jit(solution)/shard_map/ppermute | solution.py:390
  65.9 1.7 %collective-permute-start.11 = (f32[3,64,256]{2,1,0:T(8,128)S(1)}, f32[3,64,256]{2,1,0:T(8,128)S(1)}, u32[]{:S(2)}, u32[]{:S(2)}) collective-permute-start(f32[3,64,256]{2,1,0:T(8,128)S(1)} %add_bitcast_fusion), channel_id=1, source_target_pairs={{0,1},{1,0},{2,3},{3,2},{4,5},{5,4},{6,7},{7,6},{8,9},{9,8},{10,11... | collective-permute-start | bytes 589832 | tf_op jit(solution)/shard_map/ppermute | solution.py:392
  66.1 5.2 %collective-permute-start.14 = (bf16[3,64,256]{2,1,0:T(8,128)(2,1)S(1)}, bf16[3,64,256]{2,1,0:T(8,128)(2,1)S(1)}, u32[]{:S(2)}, u32[]{:S(2)}) collective-permute-start(bf16[3,64,256]{2,1,0:T(8,128)(2,1)S(1)} %fusion.1), channel_id=1, source_target_pairs={{0,2},{2,0},{1,3},{3,1},{4,6},{6,4},{5,7},{7,5},{8,10},{10,8},{9,1... | collective-permute-start | bytes 294920 | tf_op jit(solution)/shard_map/ppermute | solution.py:391

commit v11 on v7

--- a/solution.py
+++ b/solution.py
@@ -21,6 +21,7 @@
 SPREAD_STEPS = 4
 VMEM_LIMIT = 40 * 1024 * 1024
 LEAD_FLOPS = 1 << 32
+CUT_LIMIT = 63 * 1024 * 1024
 
 
 def with_halo(cells, sides, width):
@@ -112,12 +113,34 @@
     return jnp.dot(a, b, preferred_element_type=jnp.float32)
 
 
-def lead_kernel(out):
-    out[...] = jnp.zeros_like(out)
-
-
-def lead():
-    return local_call(lead_kernel, "lead", [like((8, 128), jnp.int32)], 0, LEAD_FLOPS)()[0]
+def cut_kernel(coeffs, direct, shared, mine, sems):
+    width, half = direct.shape[1], mine.shape[1]
+    start = pl.multiple_of(width + lax.axis_index("aux") * half, half)
+    copies = [
+        pltpu.make_async_copy(coeffs.at[:, columns], out, sems.at[i])
+        for i, (columns, out) in enumerate(
+            ((pl.ds(0, width), direct), (pl.ds(start, half), mine), (pl.ds(width, width), shared))
+        )
+    ]
+    for copy in copies:
+        copy.start()
+    for copy in copies:
+        copy.wait()
+
+
+def cut(coeffs):
+    rows, columns = coeffs.shape
+    width = columns // CHUNKS
+    return pl.pallas_call(
+        cut_kernel,
+        out_shape=[like((rows, n), coeffs.dtype) for n in (width, width, width // 2)],
+        in_specs=[IN_HBM],
+        out_specs=[IN_HBM] * 3,
+        scratch_shapes=[pltpu.SemaphoreType.DMA((3,))],
+        compiler_params=pltpu.CompilerParams(vmem_limit_bytes=CUT_LIMIT),
+        cost_estimate=pl.CostEstimate(flops=LEAD_FLOPS, bytes_accessed=0, transcendentals=0),
+        name="cut",
+    )(coeffs)
 
 
 def scalar_at(values, index):
@@ -125,7 +148,7 @@
     return jnp.sum(jnp.where(ids == index, values, 0).astype(jnp.float32))
 
 
-def tables_kernel(first, counts, table, wants):
+def tables_kernel(counts, table, wants):
     here, orb = lax.axis_index("ao"), lax.axis_index("orb")
     slots = table.shape[1] // GROUPS
     named = jnp.where(table[...] // AO_DEV == here, table[...] % AO_DEV, 0).astype(jnp.float32)
@@ -135,16 +158,16 @@
         count = scalar_at(counts[...], here * AO_DEV + offset)
         rows.append(count - (orb * (ORBS // 2)).astype(jnp.float32))
     row = lax.broadcasted_iota(jnp.int32, wants.shape, 0)
-    out = first[0, 0:1].astype(jnp.float32).reshape(1, 1) + jnp.zeros(wants.shape, jnp.float32)
+    out = jnp.zeros(wants.shape, jnp.float32)
     for k, value in enumerate(rows):
         out = jnp.where(row == k, value, out)
     wants[...] = out.astype(jnp.int32)
 
 
-def tables(first, counts, table, width):
-    return local_call(
-        tables_kernel, "tables", [like((8, width), jnp.int32)], 3, table.size
-    )(first, counts.reshape(1, -1), table)[0]
+def tables(counts, table, width):
+    return local_call(
+        tables_kernel, "tables", [like((8, width), jnp.int32)], 2, LEAD_FLOPS
+    )(counts.reshape(1, -1), table)[0]
 
 
 def transform_kernel(start, wants, integrals, own, outer, inner, *outs):
@@ -357,14 +380,10 @@
     total_aux = integrals.shape[0] * lax.axis_size("aux")
     table = pair_blocks.T
 
-    half = width // 2
-    parts = [lax.slice_in_dim(coeffs, 0, width, axis=1)]
-    first, rest = lax.optimization_barrier((lead(), coeffs))
-    parts.append(lax.slice_in_dim(rest, width, 2 * width, axis=1))
-    mine = lax.dynamic_slice_in_dim(rest, width + lax.axis_index("aux") * half, half, axis=1)
+    *parts, mine = cut(coeffs)
     inner = [lax.ppermute(part, "ao", INSIDE) for part in (parts[0], mine)]
     outer = [lax.ppermute(part, "ao", OUTSIDE) for part in parts]
-    wants = tables(first, orbital_count, table, width)
+    wants = tables(orbital_count, table, width)
 
     pieces = list(transform(0, wants, integrals, parts[0], outer[0], inner[0]))
     blocks = [[piece] for piece in pieces]

time: 68.8 us -> 88.7 us (1.29)
  Pallas kernels: 4.93 us -> 25.9 us
  local copies, waits for them, and re-layouts: 2.88 us -> 0.03 us
  waiting for transfers between devices: 41.6 us -> 43.3 us
    pallas_call x2, Pallas kernels: 0.14 us -> 21.1 us  [the longest x1 21 us: cut(): pl.pallas_call(cut_kernel, out_shape=[like((rows, n), coeffs.dtype) for n...]
    ppermute x2, waiting for transfers between devices: 2.71 us -> 4.8 us  [six_pair_body(): inner = [lax.ppermute(part, 'ao', INSIDE) for part in (parts[0], mine)]]
    slice x2 -> x0, local copies, waits for them, and re-layouts: 1.94 us -> none  [the longest x1 0.97 us: six_pair_body(): parts.append(lax.slice_in_dim(rest, width, 2 * width, axis=1))]
    dynamic_slice x1 -> x0, local copies, waits for them, and re-layouts: 0.92 us -> none  [six_pair_body(): lax.dynamic_slice_in_dim(rest, width + lax.axis_index('aux') * half, half...]
  transfers between devices with their start and end apart: 15 -> 15, of which waited for: 11 -> 11; matrix products, arithmetic and copies ran while one was open for 3% -> 0% of each run, Pallas kernels for 6% -> 4%
where the time goes in v11:
time: 88.7 us; the launch traced here: 88.5 us
  waiting for transfers between devices  43.3 us (49%)
  Pallas kernels  25.9 us (29%)
  starting transfers between devices  19.1 us (22%)
    ppermute x6, waiting for transfers between devices, fetch(): return [lax.ppermute(piece, 'ao', swap) for piece in blocks[s]]  30.1 us
    pallas_call x1, Pallas kernels, cut(): pl.pallas_call(cut_kernel, out_shape=[like((rows, n), coeffs.dtype) for n...  21 us
    ppermute x6, starting transfers between devices, fetch(): return [lax.ppermute(piece, 'ao', swap) for piece in blocks[s]]  7.5 us
    ppermute x2, starting transfers between devices, six_pair_body(): inner = [lax.ppermute(part, 'ao', INSIDE) for part in (parts[0], mine)]  5.84 us
    ppermute x2, waiting for transfers between devices, six_pair_body(): inner = [lax.ppermute(part, 'ao', INSIDE) for part in (parts[0], mine)]  4.8 us
    ppermute x2, waiting for transfers between devices, six_pair_body(): outer = [lax.ppermute(part, 'ao', OUTSIDE) for part in parts]  3.92 us
    ppermute x1, waiting for transfers between devices, six_pair_body(): far1 = lax.ppermute((near1[1] + got1[1]).astype(jnp.bfloat16), 'aux', SWAP)  3.33 us
  transfers between devices with their start and end apart: 15, of which 11 were waited for; matrix products, arithmetic and copies ran while one was open for 0% of the time, Pallas kernels for 4%

profile of v11, /device:TPU:8, one launch (start us, length us, event | category | flops | bytes accessed | tf_op | source)
XLA Modules:
  0.0 88.5 jit_solution(11879589738755836746)
XLA Ops:
  0.0 21.0 %cut.1 = (bf16[512,256]{1,0:T(8,128)(2,1)}, bf16[512,256]{1,0:T(8,128)(2,1)}, bf16[512,128]{1,0:T(8,128)(2,1)}) custom-call(bf16[512,512]{1,0:T(8,128)(2,1)} %coeffs.1), custom_call_target="tpu_custom_call" | custom-call | flops 4294967296 | tf_op jit(solution)/shard_map/cut/pallas_call | solution.py:134
  21.0 3.5 %collective-permute-start.2 = (bf16[512,256]{1,0:T(8,128)(2,1)}, bf16[512,256]{1,0:T(8,128)(2,1)S(1)}, u32[]{:S(2)}, u32[]{:S(2)}) collective-permute-start(bf16[512,256]{1,0:T(8,128)(2,1)} %get-tuple-element.24.own), channel_id=1, source_target_pairs={{4,8},{8,4},{5,9},{9,5},{6,10},{10,6},{7,11},{11,7},{20,24},{24,20... | collective-permute-start | bytes 786440 | tf_op jit(solution)/shard_map/ppermute | solution.py:384
  24.6 2.4 %collective-permute-start = (bf16[512,128]{1,0:T(8,128)(2,1)}, bf16[512,128]{1,0:T(8,128)(2,1)S(1)}, u32[]{:S(2)}, u32[]{:S(2)}) collective-permute-start(bf16[512,128]{1,0:T(8,128)(2,1)} %get-tuple-element.23), channel_id=1, source_target_pairs={{4,8},{8,4},{5,9},{9,5},{6,10},{10,6},{7,11},{11,7},{20,24},{24,20... | collective-permute-start | bytes 393224 | tf_op jit(solution)/shard_map/ppermute | solution.py:384
  27.5 4.8 %collective-permute-done.2.inner = bf16[512,256]{1,0:T(8,128)(2,1)S(1)} collective-permute-done((bf16[512,256]{1,0:T(8,128)(2,1)}, bf16[512,256]{1,0:T(8,128)(2,1)S(1)}, u32[]{:S(2)}, u32[]{:S(2)}) %collective-permute-start.2) | collective-permute-done | bytes 262176 | tf_op jit(solution)/shard_map/ppermute | solution.py:384
  32.3 1.7 %collective-permute-done.1.outer = bf16[512,256]{1,0:T(8,128)(2,1)S(1)} collective-permute-done((bf16[512,256]{1,0:T(8,128)(2,1)}, bf16[512,256]{1,0:T(8,128)(2,1)S(1)}, u32[]{:S(2)}, u32[]{:S(2)}) %collective-permute-start.1) | collective-permute-done | bytes 262176 | tf_op jit(solution)/shard_map/ppermute | solution.py:385
  34.0 0.8 transform.2
  34.9 1.6 %collective-permute-start.4 = (bf16[512,128]{1,0:T(8,128)(2,1)S(1)}, bf16[512,128]{1,0:T(8,128)(2,1)S(1)}, u32[]{:S(2)}, u32[]{:S(2)}) collective-permute-start(bf16[512,128]{1,0:T(8,128)(2,1)S(1)} %collective-permute-done.inner), channel_id=1, source_target_pairs={{0,2},{2,0},{1,3},{3,1},{4,6},{6,4},{5,7},{7,5},{8,10},{10,8},{9,1... | collective-permute-start | bytes 393224 | tf_op jit(solution)/shard_map/ppermute | solution.py:391
  36.5 1.8 %collective-permute-start.7 = (bf16[2,256,256]{2,1,0:T(8,128)(2,1)S(1)}, bf16[2,256,256]{2,1,0:T(8,128)(2,1)S(1)}, u32[]{:S(2)}, u32[]{:S(2)}) collective-permute-start(bf16[2,256,256]{2,1,0:T(8,128)(2,1)S(1)} %get-tuple-element.32), channel_id=1, source_target_pairs={{0,4},{4,0},{8,12},{12,8},{1,5},{5,1},{9,13},{13,9},{2,6},{6,2},{1... | collective-permute-start | bytes 786440 | tf_op jit(solution)/shard_map/ppermute | solution.py:400
  38.3 2.2 %collective-permute-done.3.outer = bf16[512,256]{1,0:T(8,128)(2,1)S(1)} collective-permute-done((bf16[512,256]{1,0:T(8,128)(2,1)}, bf16[512,256]{1,0:T(8,128)(2,1)S(1)}, u32[]{:S(2)}, u32[]{:S(2)}) %collective-permute-start.3) | collective-permute-done | bytes 262176 | tf_op jit(solution)/shard_map/ppermute | solution.py:385
  40.6 0.9 %transform.3 = (bf16[2,256,256]{2,1,0:T(8,128)(2,1)S(1)}, bf16[2,256,256]{2,1,0:T(8,128)(2,1)S(1)}, bf16[2,256,256]{2,1,0:T(8,128)(2,1)S(1)}, bf16[2,256,256]{2,1,0:T(8,128)(2,1)S(1)}) custom-call(s32[8,256]{1,0:T(8,128)S(1)} %tables.1.wants, bf16[2,512,1280]{2,1,0:T(8,128)(2,1)S(1)} %copy-done, bf16[512,256]{1,0:T(8,128)(2,1)S(1)} %copy-done.1, ...), custom_call_target="tpu_custom_call" | custom-call | flops 671088640 | bytes 2097152 | tf_op jit(solution)/shard_map/transform/pallas_call | solution.py:207
  41.5 3.1 %collective-permute-start.6 = (bf16[2,256,256]{2,1,0:T(8,128)(2,1)S(1)}, bf16[2,256,256]{2,1,0:T(8,128)(2,1)S(1)}, u32[]{:S(2)}, u32[]{:S(2)}) collective-permute-start(bf16[2,256,256]{2,1,0:T(8,128)(2,1)S(1)} %get-tuple-element.31), channel_id=1, source_target_pairs={{0,8},{4,12},{8,0},{12,4},{1,9},{5,13},{9,1},{13,5},{2,10},{6,14},... | collective-permute-start | bytes 786440 | tf_op jit(solution)/shard_map/ppermute | solution.py:400
  45.7 1.7 %collective-permute-start.12 = (bf16[2,256,256]{2,1,0:T(8,128)(2,1)S(1)}, bf16[2,256,256]{2,1,0:T(8,128)(2,1)S(1)}, u32[]{:S(2)}, u32[]{:S(2)}) collective-permute-start(bf16[2,256,256]{2,1,0:T(8,128)(2,1)S(1)} %get-tuple-element.38), channel_id=1, source_target_pairs={{0,12},{4,8},{8,4},{12,0},{1,13},{5,9},{9,5},{13,1},{2,14},{6,10},... | collective-permute-start | bytes 786440 | tf_op jit(solution)/shard_map/ppermute | solution.py:400
  47.4 4.3 %collective-permute-done.7.refs_4_ = bf16[2,256,256]{2,1,0:T(8,128)(2,1)S(1)} collective-permute-done((bf16[2,256,256]{2,1,0:T(8,128)(2,1)S(1)}, bf16[2,256,256]{2,1,0:T(8,128)(2,1)S(1)}, u32[]{:S(2)}, u32[]{:S(2)}) %collective-permute-start.7) | collective-permute-done | bytes 262176 | tf_op jit(solution)/shard_map/ppermute | solution.py:400
  51.7 5.3 %collective-permute-done.6.refs_3_ = bf16[2,256,256]{2,1,0:T(8,128)(2,1)S(1)} collective-permute-done((bf16[2,256,256]{2,1,0:T(8,128)(2,1)S(1)}, bf16[2,256,256]{2,1,0:T(8,128)(2,1)S(1)}, u32[]{:S(2)}, u32[]{:S(2)}) %collective-permute-start.6) | collective-permute-done | bytes 262176 | tf_op jit(solution)/shard_map/ppermute | solution.py:400
  57.0 5.2 %collective-permute-done.8.refs_5_ = bf16[2,256,256]{2,1,0:T(8,128)(2,1)S(1)} collective-permute-done((bf16[2,256,256]{2,1,0:T(8,128)(2,1)S(1)}, bf16[2,256,256]{2,1,0:T(8,128)(2,1)S(1)}, u32[]{:S(2)}, u32[]{:S(2)}) %collective-permute-start.8) | collective-permute-done | bytes 262176 | tf_op jit(solution)/shard_map/ppermute | solution.py:400
  62.2 1.0 %early_pairs.1 = (f32[2,3,64,256]{3,2,1,0:T(8,128)S(1)}, bf16[2,3,64,256]{3,2,1,0:T(8,128)(2,1)S(1)}, s32[16,256]{1,0:T(8,128)S(1)}) custom-call(s32[1,4]{1,0:T(1,128)S(1)} %bitcast.9, s32[2,64]{1,0:T(2,128)S(1)} %bitcast.8, bf16[2,256,256]{2,1,0:T(8,128)(2,1)S(1)} %get-tuple-element.26.refs_0_, bf16[2,256,256]{2,1,0:T(8,128)(2,1)S(1)} %get-tuple-element.29.refs_1_, ...), custom_call_target="tpu_custom_call" | custom-call | flops 402653184 | bytes 1212416 | tf_op jit(solution)/shard_map/early_pairs/pallas_call | solution.py:308
  63.2 1.6 %collective-permute-start.9 = (bf16[2,3,64,256]{3,2,1,0:T(8,128)(2,1)S(1)}, bf16[2,3,64,256]{3,2,1,0:T(8,128)(2,1)S(1)}, u32[]{:S(2)}, u32[]{:S(2)}) collective-permute-start(bf16[2,3,64,256]{3,2,1,0:T(8,128)(2,1)S(1)} %get-tuple-element.36), channel_id=1, source_target_pairs={{0,2},{2,0},{1,3},{3,1},{4,6},{6,4},{5,7},{7,5},{8,10},{10,8},{9,1... | collective-permute-start | bytes 589832 | tf_op jit(solution)/shard_map/ppermute | solution.py:405
  64.7 11.2 %collective-permute-done.11.refs_6_ = bf16[2,256,256]{2,1,0:T(8,128)(2,1)S(1)} collective-permute-done((bf16[2,256,256]{2,1,0:T(8,128)(2,1)S(1)}, bf16[2,256,256]{2,1,0:T(8,128)(2,1)S(1)}, u32[]{:S(2)}, u32[]{:S(2)}) %collective-permute-start.11) | collective-permute-done | bytes 262176 | tf_op jit(solution)/shard_map/ppermute | solution.py:400
  75.9 3.9 %collective-permute-done.12.refs_7_ = bf16[2,256,256]{2,1,0:T(8,128)(2,1)S(1)} collective-permute-done((bf16[2,256,256]{2,1,0:T(8,128)(2,1)S(1)}, bf16[2,256,256]{2,1,0:T(8,128)(2,1)S(1)}, u32[]{:S(2)}, u32[]{:S(2)}) %collective-permute-start.12) | collective-permute-done | bytes 262176 | tf_op jit(solution)/shard_map/ppermute | solution.py:400
  79.8 0.9 late_pairs.1
  81.3 1.1 %collective-permute-done.13.got1 = f32[2,3,64,256]{3,2,1,0:T(8,128)S(1)} collective-permute-done((f32[2,3,64,256]{3,2,1,0:T(8,128)S(1)}, f32[2,3,64,256]{3,2,1,0:T(8,128)S(1)}, u32[]{:S(2)}, u32[]{:S(2)}) %collective-permute-start.13) | collective-permute-done | bytes 393248 | tf_op jit(solution)/shard_map/ppermute | solution.py:408
  82.5 1.6 %collective-permute-start.14 = (bf16[3,64,256]{2,1,0:T(8,128)(2,1)S(1)}, bf16[3,64,256]{2,1,0:T(8,128)(2,1)S(1)}, u32[]{:S(2)}, u32[]{:S(2)}) collective-permute-start(bf16[3,64,256]{2,1,0:T(8,128)(2,1)S(1)} %fusion.1), channel_id=1, source_target_pairs={{0,2},{2,0},{1,3},{3,1},{4,6},{6,4},{5,7},{7,5},{8,10},{10,8},{9,1... | collective-permute-start | bytes 294920 | tf_op jit(solution)/shard_map/ppermute | solution.py:409
  84.0 3.3 %collective-permute-done.14.far1 = bf16[3,64,256]{2,1,0:T(8,128)(2,1)S(1)} collective-permute-done((bf16[3,64,256]{2,1,0:T(8,128)(2,1)S(1)}, bf16[3,64,256]{2,1,0:T(8,128)(2,1)S(1)}, u32[]{:S(2)}, u32[]{:S(2)}) %collective-permute-start.14) | collective-permute-done | bytes 98336 | tf_op jit(solution)/shard_map/ppermute | solution.py:409
  87.4 1.2 %spread.1 = f32[64,16,256]{2,1,0:T(8,128)} custom-call(s32[16,256]{1,0:T(8,128)S(1)} %get-tuple-element.34.place, f32[2,3,64,256]{3,2,1,0:T(8,128)S(1)} %get-tuple-element.35.near0, bf16[2,3,64,256]{3,2,1,0:T(8,128)(2,1)S(1)} %collective-permute-done.9.far0, f32[3,64,256]{2,1,0:T(8,128)S(1)} %collective-permute-done.10.got0, ...), custom_call_target="tpu_custom_call" | custom-call | flops 1572864 | bytes 2097152 | tf_op jit(solution)/shard_map/spread/pallas_call | solution.py:363
  (27 shorter events, 2.4 us)
Async XLA Ops:
  0.0 27.3 %copy-start.5 = (s32[8]{0:T(128)S(1)}, s32[8]{0:T(128)}, u32[]{:S(2)}) copy-start(s32[8]{0:T(128)} %param.9) | copy-start | bytes 100
  0.0 27.3 %copy-start.3 = (s32[64,2]{0,1:T(2,128)S(1)}, s32[64,2]{0,1:T(2,128)}, u32[]{:S(2)}) copy-start(s32[64,2]{0,1:T(2,128)} %param.7) | copy-start | bytes 1540
  21.0 11.3 %collective-permute-start.2 = (bf16[512,256]{1,0:T(8,128)(2,1)}, bf16[512,256]{1,0:T(8,128)(2,1)S(1)}, u32[]{:S(2)}, u32[]{:S(2)}) collective-permute-start(bf16[512,256]{1,0:T(8,128)(2,1)} %get-tuple-element.24.own), channel_id=1, source_target_pairs={{4,8},{8,4},{5,9},{9,5},{6,10},{10,6},{7,11},{11,7},{20,24},{24,20... | collective-permute-start | bytes 786440 | tf_op jit(solution)/shard_map/ppermute | solution.py:384
  24.5 9.5 %collective-permute-start.1 = (bf16[512,256]{1,0:T(8,128)(2,1)}, bf16[512,256]{1,0:T(8,128)(2,1)S(1)}, u32[]{:S(2)}, u32[]{:S(2)}) collective-permute-start(bf16[512,256]{1,0:T(8,128)(2,1)} %get-tuple-element.24.own), channel_id=1, source_target_pairs={{0,4},{4,0},{8,12},{12,8},{1,5},{5,1},{9,13},{13,9},{2,6},{6,2},{1... | collective-permute-start | bytes 786440 | tf_op jit(solution)/shard_map/ppermute | solution.py:385
  24.6 10.4 %collective-permute-start = (bf16[512,128]{1,0:T(8,128)(2,1)}, bf16[512,128]{1,0:T(8,128)(2,1)S(1)}, u32[]{:S(2)}, u32[]{:S(2)}) collective-permute-start(bf16[512,128]{1,0:T(8,128)(2,1)} %get-tuple-element.23), channel_id=1, source_target_pairs={{4,8},{8,4},{5,9},{9,5},{6,10},{10,6},{7,11},{11,7},{20,24},{24,20... | collective-permute-start | bytes 393224 | tf_op jit(solution)/shard_map/ppermute | solution.py:384
  26.9 13.6 %collective-permute-start.3 = (bf16[512,256]{1,0:T(8,128)(2,1)}, bf16[512,256]{1,0:T(8,128)(2,1)S(1)}, u32[]{:S(2)}, u32[]{:S(2)}) collective-permute-start(bf16[512,256]{1,0:T(8,128)(2,1)} %get-tuple-element.27.own), channel_id=1, source_target_pairs={{0,4},{4,0},{8,12},{12,8},{1,5},{5,1},{9,13},{13,9},{2,6},{6,2},{1... | collective-permute-start | bytes 786440 | tf_op jit(solution)/shard_map/ppermute | solution.py:385
  27.3 6.7 %copy-start = (bf16[2,512,1280]{2,1,0:T(8,128)(2,1)S(1)}, bf16[2,512,1280]{2,1,0:T(8,128)(2,1)}, u32[]{:S(2)}) copy-start(bf16[2,512,1280]{2,1,0:T(8,128)(2,1)} %integrals.3) | copy-start | bytes 7864324
  27.3 6.7 %copy-start.2 = (bf16[512,256]{1,0:T(8,128)(2,1)S(1)}, bf16[512,256]{1,0:T(8,128)(2,1)}, u32[]{:S(2)}) copy-start(bf16[512,256]{1,0:T(8,128)(2,1)} %get-tuple-element.24.own) | copy-start | bytes 786436
  27.5 13.1 %copy-start.1 = (bf16[512,256]{1,0:T(8,128)(2,1)S(1)}, bf16[512,256]{1,0:T(8,128)(2,1)}, u32[]{:S(2)}) copy-start(bf16[512,256]{1,0:T(8,128)(2,1)} %get-tuple-element.27.own) | copy-start | bytes 786436
  27.5 34.7 %copy-start.4 = (s32[4]{0:T(128)S(1)}, s32[4]{0:T(128)}, u32[]{:S(2)}) copy-start(s32[4]{0:T(128)} %param.8) | copy-start | bytes 52
  34.9 10.8 %collective-permute-start.5 = (bf16[2,256,256]{2,1,0:T(8,128)(2,1)S(1)}, bf16[2,256,256]{2,1,0:T(8,128)(2,1)S(1)}, u32[]{:S(2)}, u32[]{:S(2)}) collective-permute-start(bf16[2,256,256]{2,1,0:T(8,128)(2,1)S(1)} %get-tuple-element.30), channel_id=1, source_target_pairs={{0,8},{4,12},{8,0},{12,4},{1,9},{5,13},{9,1},{13,5},{2,10},{6,14},... | collective-permute-start | bytes 786440 | tf_op jit(solution)/shard_map/ppermute | solution.py:400
  34.9 5.6 %collective-permute-start.4 = (bf16[512,128]{1,0:T(8,128)(2,1)S(1)}, bf16[512,128]{1,0:T(8,128)(2,1)S(1)}, u32[]{:S(2)}, u32[]{:S(2)}) collective-permute-start(bf16[512,128]{1,0:T(8,128)(2,1)S(1)} %collective-permute-done.inner), channel_id=1, source_target_pairs={{0,2},{2,0},{1,3},{3,1},{4,6},{6,4},{5,7},{7,5},{8,10},{10,8},{9,1... | collective-permute-start | bytes 393224 | tf_op jit(solution)/shard_map/ppermute | solution.py:391
  36.5 15.2 %collective-permute-start.7 = (bf16[2,256,256]{2,1,0:T(8,128)(2,1)S(1)}, bf16[2,256,256]{2,1,0:T(8,128)(2,1)S(1)}, u32[]{:S(2)}, u32[]{:S(2)}) collective-permute-start(bf16[2,256,256]{2,1,0:T(8,128)(2,1)S(1)} %get-tuple-element.32), channel_id=1, source_target_pairs={{0,4},{4,0},{8,12},{12,8},{1,5},{5,1},{9,13},{13,9},{2,6},{6,2},{1... | collective-permute-start | bytes 786440 | tf_op jit(solution)/shard_map/ppermute | solution.py:400
  41.5 15.5 %collective-permute-start.6 = (bf16[2,256,256]{2,1,0:T(8,128)(2,1)S(1)}, bf16[2,256,256]{2,1,0:T(8,128)(2,1)S(1)}, u32[]{:S(2)}, u32[]{:S(2)}) collective-permute-start(bf16[2,256,256]{2,1,0:T(8,128)(2,1)S(1)} %get-tuple-element.31), channel_id=1, source_target_pairs={{0,8},{4,12},{8,0},{12,4},{1,9},{5,13},{9,1},{13,5},{2,10},{6,14},... | collective-permute-start | bytes 786440 | tf_op jit(solution)/shard_map/ppermute | solution.py:400
  44.6 17.6 %collective-permute-start.8 = (bf16[2,256,256]{2,1,0:T(8,128)(2,1)S(1)}, bf16[2,256,256]{2,1,0:T(8,128)(2,1)S(1)}, u32[]{:S(2)}, u32[]{:S(2)}) collective-permute-start(bf16[2,256,256]{2,1,0:T(8,128)(2,1)S(1)} %get-tuple-element.33), channel_id=1, source_target_pairs={{0,4},{4,0},{8,12},{12,8},{1,5},{5,1},{9,13},{13,9},{2,6},{6,2},{1... | collective-permute-start | bytes 786440 | tf_op jit(solution)/shard_map/ppermute | solution.py:400
  44.6 31.3 %collective-permute-start.11 = (bf16[2,256,256]{2,1,0:T(8,128)(2,1)S(1)}, bf16[2,256,256]{2,1,0:T(8,128)(2,1)S(1)}, u32[]{:S(2)}, u32[]{:S(2)}) collective-permute-start(bf16[2,256,256]{2,1,0:T(8,128)(2,1)S(1)} %get-tuple-element.37), channel_id=1, source_target_pairs={{0,12},{4,8},{8,4},{12,0},{1,13},{5,9},{9,5},{13,1},{2,14},{6,10},... | collective-permute-start | bytes 786440 | tf_op jit(solution)/shard_map/ppermute | solution.py:400
  45.7 34.1 %collective-permute-start.12 = (bf16[2,256,256]{2,1,0:T(8,128)(2,1)S(1)}, bf16[2,256,256]{2,1,0:T(8,128)(2,1)S(1)}, u32[]{:S(2)}, u32[]{:S(2)}) collective-permute-start(bf16[2,256,256]{2,1,0:T(8,128)(2,1)S(1)} %get-tuple-element.38), channel_id=1, source_target_pairs={{0,12},{4,8},{8,4},{12,0},{1,13},{5,9},{9,5},{13,1},{2,14},{6,10},... | collective-permute-start | bytes 786440 | tf_op jit(solution)/shard_map/ppermute | solution.py:400
  63.2 17.6 %collective-permute-start.9 = (bf16[2,3,64,256]{3,2,1,0:T(8,128)(2,1)S(1)}, bf16[2,3,64,256]{3,2,1,0:T(8,128)(2,1)S(1)}, u32[]{:S(2)}, u32[]{:S(2)}) collective-permute-start(bf16[2,3,64,256]{3,2,1,0:T(8,128)(2,1)S(1)} %get-tuple-element.36), channel_id=1, source_target_pairs={{0,2},{2,0},{1,3},{3,1},{4,6},{6,4},{5,7},{7,5},{8,10},{10,8},{9,1... | collective-permute-start | bytes 589832 | tf_op jit(solution)/shard_map/ppermute | solution.py:405
  80.6 1.8 %collective-permute-start.13 = (f32[2,3,64,256]{3,2,1,0:T(8,128)S(1)}, f32[2,3,64,256]{3,2,1,0:T(8,128)S(1)}, u32[]{:S(2)}, u32[]{:S(2)}) collective-permute-start(f32[2,3,64,256]{3,2,1,0:T(8,128)S(1)} %get-tuple-element.40), channel_id=1, source_target_pairs={{0,1},{1,0},{2,3},{3,2},{4,5},{5,4},{6,7},{7,6},{8,9},{9,8},{10,11... | collective-permute-start | bytes 1179656 | tf_op jit(solution)/shard_map/ppermute | solution.py:408
  80.8 3.3 %collective-permute-start.10 = (f32[3,64,256]{2,1,0:T(8,128)S(1)}, f32[3,64,256]{2,1,0:T(8,128)S(1)}, u32[]{:S(2)}, u32[]{:S(2)}) collective-permute-start(f32[3,64,256]{2,1,0:T(8,128)S(1)} %add_bitcast_fusion), channel_id=1, source_target_pairs={{0,1},{1,0},{2,3},{3,2},{4,5},{5,4},{6,7},{7,6},{8,9},{9,8},{10,11... | collective-permute-start | bytes 589832 | tf_op jit(solution)/shard_map/ppermute | solution.py:410
  82.5 4.9 %collective-permute-start.14 = (bf16[3,64,256]{2,1,0:T(8,128)(2,1)S(1)}, bf16[3,64,256]{2,1,0:T(8,128)(2,1)S(1)}, u32[]{:S(2)}, u32[]{:S(2)}) collective-permute-start(bf16[3,64,256]{2,1,0:T(8,128)(2,1)S(1)} %fusion.1), channel_id=1, source_target_pairs={{0,2},{2,0},{1,3},{3,1},{4,6},{6,4},{5,7},{7,5},{8,10},{10,8},{9,1... | collective-permute-start | bytes 294920 | tf_op jit(solution)/shard_map/ppermute | solution.py:409

commit v12 on v11

--- a/solution.py
+++ b/solution.py
@@ -21,7 +21,7 @@
 SPREAD_STEPS = 4
 VMEM_LIMIT = 40 * 1024 * 1024
 LEAD_FLOPS = 1 << 32
-CUT_LIMIT = 63 * 1024 * 1024
+CUT_LIMIT = 53 * 1024 * 1024 + 256 * 1024
 
 
 def with_halo(cells, sides, width):
@@ -135,7 +135,7 @@
         cut_kernel,
         out_shape=[like((rows, n), coeffs.dtype) for n in (width, width, width // 2)],
         in_specs=[IN_HBM],
-        out_specs=[IN_HBM] * 3,
+        out_specs=[IN_VMEM] * 3,
         scratch_shapes=[pltpu.SemaphoreType.DMA((3,))],
         compiler_params=pltpu.CompilerParams(vmem_limit_bytes=CUT_LIMIT),
         cost_estimate=pl.CostEstimate(flops=LEAD_FLOPS, bytes_accessed=0, transcendentals=0),

time: 88.7 us -> 68.6 us (0.77)
  Pallas kernels: 25.9 us -> 6.07 us
    pallas_call x1, Pallas kernels: 21 us -> 1.15 us  [cut(): pl.pallas_call(cut_kernel, out_shape=[like((rows, n), coeffs.dtype) for n...]
  transfers between devices with their start and end apart: 15 -> 15, of which waited for: 11 -> 11; matrix products, arithmetic and copies ran while one was open for 0% -> 0% of each run, Pallas kernels for 4% -> 5%
where the time goes in v12:
time: 68.6 us; the launch traced here: 68.5 us
  waiting for transfers between devices  43 us (63%)
  starting transfers between devices  19.2 us (28%)
  Pallas kernels  6.07 us (9%)
    ppermute x6, waiting for transfers between devices, fetch(): return [lax.ppermute(piece, 'ao', swap) for piece in blocks[s]]  30.1 us
    ppermute x6, starting transfers between devices, fetch(): return [lax.ppermute(piece, 'ao', swap) for piece in blocks[s]]  7.62 us
    ppermute x2, starting transfers between devices, six_pair_body(): inner = [lax.ppermute(part, 'ao', INSIDE) for part in (parts[0], mine)]  5.84 us
    ppermute x2, waiting for transfers between devices, six_pair_body(): inner = [lax.ppermute(part, 'ao', INSIDE) for part in (parts[0], mine)]  4.61 us
    ppermute x2, waiting for transfers between devices, six_pair_body(): outer = [lax.ppermute(part, 'ao', OUTSIDE) for part in parts]  3.8 us
    ppermute x1, waiting for transfers between devices, six_pair_body(): far1 = lax.ppermute((near1[1] + got1[1]).astype(jnp.bfloat16), 'aux', SWAP)  3.33 us
    ppermute x1, starting transfers between devices, six_pair_body(): far1 = lax.ppermute((near1[1] + got1[1]).astype(jnp.bfloat16), 'aux', SWAP)  1.56 us
    ppermute x1, starting transfers between devices, six_pair_body(): swapped = lax.ppermute(inner[1], 'aux', SWAP)  1.56 us
  transfers between devices with their start and end apart: 15, of which 11 were waited for; matrix products, arithmetic and copies ran while one was open for 0% of the time, Pallas kernels for 5%

profile of v12, /device:TPU:8, one launch (start us, length us, event | category | flops | bytes accessed | tf_op | source)
XLA Modules:
  0.0 68.5 jit_solution(6562871482856439088)
XLA Ops:
  0.0 1.1 %cut.1 = (bf16[512,256]{1,0:T(8,128)(2,1)S(1)}, bf16[512,256]{1,0:T(8,128)(2,1)S(1)}, bf16[512,128]{1,0:T(8,128)(2,1)S(1)}) custom-call(bf16[512,512]{1,0:T(8,128)(2,1)} %coeffs.1), custom_call_target="tpu_custom_call" | custom-call | flops 4294967296 | tf_op jit(solution)/shard_map/cut/pallas_call | solution.py:134
  1.2 3.5 %collective-permute-start.2 = (bf16[512,256]{1,0:T(8,128)(2,1)S(1)}, bf16[512,256]{1,0:T(8,128)(2,1)S(1)}, u32[]{:S(2)}, u32[]{:S(2)}) collective-permute-start(bf16[512,256]{1,0:T(8,128)(2,1)S(1)} %get-tuple-element.24.own), channel_id=1, source_target_pairs={{4,8},{8,4},{5,9},{9,5},{6,10},{10,6},{7,11},{11,7},{20,24},{24,20... | collective-permute-start | bytes 786440 | tf_op jit(solution)/shard_map/ppermute | solution.py:384
  4.7 2.4 %collective-permute-start = (bf16[512,128]{1,0:T(8,128)(2,1)S(1)}, bf16[512,128]{1,0:T(8,128)(2,1)S(1)}, u32[]{:S(2)}, u32[]{:S(2)}) collective-permute-start(bf16[512,128]{1,0:T(8,128)(2,1)S(1)} %get-tuple-element.23), channel_id=1, source_target_pairs={{4,8},{8,4},{5,9},{9,5},{6,10},{10,6},{7,11},{11,7},{20,24},{24,20... | collective-permute-start | bytes 393224 | tf_op jit(solution)/shard_map/ppermute | solution.py:384
  7.6 4.6 %collective-permute-done.2.inner = bf16[512,256]{1,0:T(8,128)(2,1)S(1)} collective-permute-done((bf16[512,256]{1,0:T(8,128)(2,1)S(1)}, bf16[512,256]{1,0:T(8,128)(2,1)S(1)}, u32[]{:S(2)}, u32[]{:S(2)}) %collective-permute-start.2) | collective-permute-done | bytes 262176 | tf_op jit(solution)/shard_map/ppermute | solution.py:384
  12.2 1.7 %collective-permute-done.1.outer = bf16[512,256]{1,0:T(8,128)(2,1)S(1)} collective-permute-done((bf16[512,256]{1,0:T(8,128)(2,1)S(1)}, bf16[512,256]{1,0:T(8,128)(2,1)S(1)}, u32[]{:S(2)}, u32[]{:S(2)}) %collective-permute-start.1) | collective-permute-done | bytes 262176 | tf_op jit(solution)/shard_map/ppermute | solution.py:385
  14.0 0.9 %transform.2 = (bf16[2,256,256]{2,1,0:T(8,128)(2,1)S(1)}, bf16[2,256,256]{2,1,0:T(8,128)(2,1)S(1)}, bf16[2,256,256]{2,1,0:T(8,128)(2,1)S(1)}, bf16[2,256,256]{2,1,0:T(8,128)(2,1)S(1)}) custom-call(s32[8,256]{1,0:T(8,128)S(1)} %tables.1.wants, bf16[2,512,1280]{2,1,0:T(8,128)(2,1)S(1)} %copy-done, bf16[512,256]{1,0:T(8,128)(2,1)S(1)} %get-tuple-element.24.own, ...), custom_call_target="tpu_custom_call" | custom-call | flops 671088640 | bytes 2097152 | tf_op jit(solution)/shard_map/transform/pallas_call | solution.py:219
  14.9 1.6 %collective-permute-start.4 = (bf16[512,128]{1,0:T(8,128)(2,1)S(1)}, bf16[512,128]{1,0:T(8,128)(2,1)S(1)}, u32[]{:S(2)}, u32[]{:S(2)}) collective-permute-start(bf16[512,128]{1,0:T(8,128)(2,1)S(1)} %collective-permute-done.inner), channel_id=1, source_target_pairs={{0,2},{2,0},{1,3},{3,1},{4,6},{6,4},{5,7},{7,5},{8,10},{10,8},{9,1... | collective-permute-start | bytes 393224 | tf_op jit(solution)/shard_map/ppermute | solution.py:391
  16.5 1.8 %collective-permute-start.7 = (bf16[2,256,256]{2,1,0:T(8,128)(2,1)S(1)}, bf16[2,256,256]{2,1,0:T(8,128)(2,1)S(1)}, u32[]{:S(2)}, u32[]{:S(2)}) collective-permute-start(bf16[2,256,256]{2,1,0:T(8,128)(2,1)S(1)} %get-tuple-element.32), channel_id=1, source_target_pairs={{0,4},{4,0},{8,12},{12,8},{1,5},{5,1},{9,13},{13,9},{2,6},{6,2},{1... | collective-permute-start | bytes 786440 | tf_op jit(solution)/shard_map/ppermute | solution.py:400
  18.3 2.1 %collective-permute-done.3.outer = bf16[512,256]{1,0:T(8,128)(2,1)S(1)} collective-permute-done((bf16[512,256]{1,0:T(8,128)(2,1)S(1)}, bf16[512,256]{1,0:T(8,128)(2,1)S(1)}, u32[]{:S(2)}, u32[]{:S(2)}) %collective-permute-start.3) | collective-permute-done | bytes 262176 | tf_op jit(solution)/shard_map/ppermute | solution.py:385
  20.4 0.9 %transform.3 = (bf16[2,256,256]{2,1,0:T(8,128)(2,1)S(1)}, bf16[2,256,256]{2,1,0:T(8,128)(2,1)S(1)}, bf16[2,256,256]{2,1,0:T(8,128)(2,1)S(1)}, bf16[2,256,256]{2,1,0:T(8,128)(2,1)S(1)}) custom-call(s32[8,256]{1,0:T(8,128)S(1)} %tables.1.wants, bf16[2,512,1280]{2,1,0:T(8,128)(2,1)S(1)} %copy-done, bf16[512,256]{1,0:T(8,128)(2,1)S(1)} %get-tuple-element.27.own, ...), custom_call_target="tpu_custom_call" | custom-call | flops 671088640 | bytes 2097152 | tf_op jit(solution)/shard_map/transform/pallas_call | solution.py:207
  21.3 3.2 %collective-permute-start.6 = (bf16[2,256,256]{2,1,0:T(8,128)(2,1)S(1)}, bf16[2,256,256]{2,1,0:T(8,128)(2,1)S(1)}, u32[]{:S(2)}, u32[]{:S(2)}) collective-permute-start(bf16[2,256,256]{2,1,0:T(8,128)(2,1)S(1)} %get-tuple-element.31), channel_id=1, source_target_pairs={{0,8},{4,12},{8,0},{12,4},{1,9},{5,13},{9,1},{13,5},{2,10},{6,14},... | collective-permute-start | bytes 786440 | tf_op jit(solution)/shard_map/ppermute | solution.py:400
  25.6 1.7 %collective-permute-start.12 = (bf16[2,256,256]{2,1,0:T(8,128)(2,1)S(1)}, bf16[2,256,256]{2,1,0:T(8,128)(2,1)S(1)}, u32[]{:S(2)}, u32[]{:S(2)}) collective-permute-start(bf16[2,256,256]{2,1,0:T(8,128)(2,1)S(1)} %get-tuple-element.38), channel_id=1, source_target_pairs={{0,12},{4,8},{8,4},{12,0},{1,13},{5,9},{9,5},{13,1},{2,14},{6,10},... | collective-permute-start | bytes 786440 | tf_op jit(solution)/shard_map/ppermute | solution.py:400
  27.3 4.3 %collective-permute-done.7.refs_4_ = bf16[2,256,256]{2,1,0:T(8,128)(2,1)S(1)} collective-permute-done((bf16[2,256,256]{2,1,0:T(8,128)(2,1)S(1)}, bf16[2,256,256]{2,1,0:T(8,128)(2,1)S(1)}, u32[]{:S(2)}, u32[]{:S(2)}) %collective-permute-start.7) | collective-permute-done | bytes 262176 | tf_op jit(solution)/shard_map/ppermute | solution.py:400
  31.6 5.3 %collective-permute-done.6.refs_3_ = bf16[2,256,256]{2,1,0:T(8,128)(2,1)S(1)} collective-permute-done((bf16[2,256,256]{2,1,0:T(8,128)(2,1)S(1)}, bf16[2,256,256]{2,1,0:T(8,128)(2,1)S(1)}, u32[]{:S(2)}, u32[]{:S(2)}) %collective-permute-start.6) | collective-permute-done | bytes 262176 | tf_op jit(solution)/shard_map/ppermute | solution.py:400
  36.9 5.2 %collective-permute-done.8.refs_5_ = bf16[2,256,256]{2,1,0:T(8,128)(2,1)S(1)} collective-permute-done((bf16[2,256,256]{2,1,0:T(8,128)(2,1)S(1)}, bf16[2,256,256]{2,1,0:T(8,128)(2,1)S(1)}, u32[]{:S(2)}, u32[]{:S(2)}) %collective-permute-start.8) | collective-permute-done | bytes 262176 | tf_op jit(solution)/shard_map/ppermute | solution.py:400
  42.1 1.0 %early_pairs.1 = (f32[2,3,64,256]{3,2,1,0:T(8,128)S(1)}, bf16[2,3,64,256]{3,2,1,0:T(8,128)(2,1)S(1)}, s32[16,256]{1,0:T(8,128)S(1)}) custom-call(s32[1,4]{1,0:T(1,128)S(1)} %bitcast.9, s32[2,64]{1,0:T(2,128)S(1)} %bitcast.8, bf16[2,256,256]{2,1,0:T(8,128)(2,1)S(1)} %get-tuple-element.26.refs_0_, bf16[2,256,256]{2,1,0:T(8,128)(2,1)S(1)} %get-tuple-element.29.refs_1_, ...), custom_call_target="tpu_custom_call" | custom-call | flops 402653184 | bytes 1212416 | tf_op jit(solution)/shard_map/early_pairs/pallas_call | solution.py:308
  43.1 1.6 %collective-permute-start.9 = (bf16[2,3,64,256]{3,2,1,0:T(8,128)(2,1)S(1)}, bf16[2,3,64,256]{3,2,1,0:T(8,128)(2,1)S(1)}, u32[]{:S(2)}, u32[]{:S(2)}) collective-permute-start(bf16[2,3,64,256]{3,2,1,0:T(8,128)(2,1)S(1)} %get-tuple-element.36), channel_id=1, source_target_pairs={{0,2},{2,0},{1,3},{3,1},{4,6},{6,4},{5,7},{7,5},{8,10},{10,8},{9,1... | collective-permute-start | bytes 589832 | tf_op jit(solution)/shard_map/ppermute | solution.py:405
  44.7 11.2 %collective-permute-done.11.refs_6_ = bf16[2,256,256]{2,1,0:T(8,128)(2,1)S(1)} collective-permute-done((bf16[2,256,256]{2,1,0:T(8,128)(2,1)S(1)}, bf16[2,256,256]{2,1,0:T(8,128)(2,1)S(1)}, u32[]{:S(2)}, u32[]{:S(2)}) %collective-permute-start.11) | collective-permute-done | bytes 262176 | tf_op jit(solution)/shard_map/ppermute | solution.py:400
  55.9 3.9 %collective-permute-done.12.refs_7_ = bf16[2,256,256]{2,1,0:T(8,128)(2,1)S(1)} collective-permute-done((bf16[2,256,256]{2,1,0:T(8,128)(2,1)S(1)}, bf16[2,256,256]{2,1,0:T(8,128)(2,1)S(1)}, u32[]{:S(2)}, u32[]{:S(2)}) %collective-permute-start.12) | collective-permute-done | bytes 262176 | tf_op jit(solution)/shard_map/ppermute | solution.py:400
  59.7 0.9 %late_pairs.1 = (f32[2,3,64,256]{3,2,1,0:T(8,128)S(1)}, f32[2,3,64,256]{3,2,1,0:T(8,128)S(1)}) custom-call(bf16[2,256,256]{2,1,0:T(8,128)(2,1)S(1)} %get-tuple-element.26.refs_0_, bf16[2,256,256]{2,1,0:T(8,128)(2,1)S(1)} %get-tuple-element.29.refs_1_, bf16[2,256,256]{2,1,0:T(8,128)(2,1)S(1)} %collective-permute-done.5.refs_2_, ...), custom_call_target="tpu_custom_call" | custom-call | flops 402653184 | bytes 1572864 | tf_op jit(solution)/shard_map/late_pairs/pallas_call | solution.py:324
  61.3 1.1 %collective-permute-done.13.got1 = f32[2,3,64,256]{3,2,1,0:T(8,128)S(1)} collective-permute-done((f32[2,3,64,256]{3,2,1,0:T(8,128)S(1)}, f32[2,3,64,256]{3,2,1,0:T(8,128)S(1)}, u32[]{:S(2)}, u32[]{:S(2)}) %collective-permute-start.13) | collective-permute-done | bytes 393248 | tf_op jit(solution)/shard_map/ppermute | solution.py:408
  62.4 1.6 %collective-permute-start.14 = (bf16[3,64,256]{2,1,0:T(8,128)(2,1)S(1)}, bf16[3,64,256]{2,1,0:T(8,128)(2,1)S(1)}, u32[]{:S(2)}, u32[]{:S(2)}) collective-permute-start(bf16[3,64,256]{2,1,0:T(8,128)(2,1)S(1)} %fusion.1), channel_id=1, source_target_pairs={{0,2},{2,0},{1,3},{3,1},{4,6},{6,4},{5,7},{7,5},{8,10},{10,8},{9,1... | collective-permute-start | bytes 294920 | tf_op jit(solution)/shard_map/ppermute | solution.py:409
  64.0 3.3 %collective-permute-done.14.far1 = bf16[3,64,256]{2,1,0:T(8,128)(2,1)S(1)} collective-permute-done((bf16[3,64,256]{2,1,0:T(8,128)(2,1)S(1)}, bf16[3,64,256]{2,1,0:T(8,128)(2,1)S(1)}, u32[]{:S(2)}, u32[]{:S(2)}) %collective-permute-start.14) | collective-permute-done | bytes 98336 | tf_op jit(solution)/shard_map/ppermute | solution.py:409
  67.3 1.2 %spread.1 = f32[64,16,256]{2,1,0:T(8,128)} custom-call(s32[16,256]{1,0:T(8,128)S(1)} %get-tuple-element.34.place, f32[2,3,64,256]{3,2,1,0:T(8,128)S(1)} %get-tuple-element.35.near0, bf16[2,3,64,256]{3,2,1,0:T(8,128)(2,1)S(1)} %collective-permute-done.9.far0, f32[3,64,256]{2,1,0:T(8,128)S(1)} %collective-permute-done.10.got0, ...), custom_call_target="tpu_custom_call" | custom-call | flops 1572864 | bytes 2097152 | tf_op jit(solution)/shard_map/spread/pallas_call | solution.py:363
  (23 shorter events, 2.4 us)
Async XLA Ops:
  0.0 7.5 %copy-start.3 = (s32[8]{0:T(128)S(1)}, s32[8]{0:T(128)}, u32[]{:S(2)}) copy-start(s32[8]{0:T(128)} %param.9) | copy-start | bytes 100
  0.0 7.5 %copy-start.1 = (s32[64,2]{0,1:T(2,128)S(1)}, s32[64,2]{0,1:T(2,128)}, u32[]{:S(2)}) copy-start(s32[64,2]{0,1:T(2,128)} %param.7) | copy-start | bytes 1540
  1.2 11.1 %collective-permute-start.2 = (bf16[512,256]{1,0:T(8,128)(2,1)S(1)}, bf16[512,256]{1,0:T(8,128)(2,1)S(1)}, u32[]{:S(2)}, u32[]{:S(2)}) collective-permute-start(bf16[512,256]{1,0:T(8,128)(2,1)S(1)} %get-tuple-element.24.own), channel_id=1, source_target_pairs={{4,8},{8,4},{5,9},{9,5},{6,10},{10,6},{7,11},{11,7},{20,24},{24,20... | collective-permute-start | bytes 786440 | tf_op jit(solution)/shard_map/ppermute | solution.py:384
  4.7 9.3 %collective-permute-start.1 = (bf16[512,256]{1,0:T(8,128)(2,1)S(1)}, bf16[512,256]{1,0:T(8,128)(2,1)S(1)}, u32[]{:S(2)}, u32[]{:S(2)}) collective-permute-start(bf16[512,256]{1,0:T(8,128)(2,1)S(1)} %get-tuple-element.24.own), channel_id=1, source_target_pairs={{0,4},{4,0},{8,12},{12,8},{1,5},{5,1},{9,13},{13,9},{2,6},{6,2},{1... | collective-permute-start | bytes 786440 | tf_op jit(solution)/shard_map/ppermute | solution.py:385
  4.7 10.2 %collective-permute-start = (bf16[512,128]{1,0:T(8,128)(2,1)S(1)}, bf16[512,128]{1,0:T(8,128)(2,1)S(1)}, u32[]{:S(2)}, u32[]{:S(2)}) collective-permute-start(bf16[512,128]{1,0:T(8,128)(2,1)S(1)} %get-tuple-element.23), channel_id=1, source_target_pairs={{4,8},{8,4},{5,9},{9,5},{6,10},{10,6},{7,11},{11,7},{20,24},{24,20... | collective-permute-start | bytes 393224 | tf_op jit(solution)/shard_map/ppermute | solution.py:384
  7.1 13.3 %collective-permute-start.3 = (bf16[512,256]{1,0:T(8,128)(2,1)S(1)}, bf16[512,256]{1,0:T(8,128)(2,1)S(1)}, u32[]{:S(2)}, u32[]{:S(2)}) collective-permute-start(bf16[512,256]{1,0:T(8,128)(2,1)S(1)} %get-tuple-element.27.own), channel_id=1, source_target_pairs={{0,4},{4,0},{8,12},{12,8},{1,5},{5,1},{9,13},{13,9},{2,6},{6,2},{1... | collective-permute-start | bytes 786440 | tf_op jit(solution)/shard_map/ppermute | solution.py:385
  7.5 6.5 %copy-start = (bf16[2,512,1280]{2,1,0:T(8,128)(2,1)S(1)}, bf16[2,512,1280]{2,1,0:T(8,128)(2,1)}, u32[]{:S(2)}) copy-start(bf16[2,512,1280]{2,1,0:T(8,128)(2,1)} %integrals.3) | copy-start | bytes 7864324
  7.6 34.5 %copy-start.2 = (s32[4]{0:T(128)S(1)}, s32[4]{0:T(128)}, u32[]{:S(2)}) copy-start(s32[4]{0:T(128)} %param.8) | copy-start | bytes 52
  14.8 10.8 %collective-permute-start.5 = (bf16[2,256,256]{2,1,0:T(8,128)(2,1)S(1)}, bf16[2,256,256]{2,1,0:T(8,128)(2,1)S(1)}, u32[]{:S(2)}, u32[]{:S(2)}) collective-permute-start(bf16[2,256,256]{2,1,0:T(8,128)(2,1)S(1)} %get-tuple-element.30), channel_id=1, source_target_pairs={{0,8},{4,12},{8,0},{12,4},{1,9},{5,13},{9,1},{13,5},{2,10},{6,14},... | collective-permute-start | bytes 786440 | tf_op jit(solution)/shard_map/ppermute | solution.py:400
  14.9 5.5 %collective-permute-start.4 = (bf16[512,128]{1,0:T(8,128)(2,1)S(1)}, bf16[512,128]{1,0:T(8,128)(2,1)S(1)}, u32[]{:S(2)}, u32[]{:S(2)}) collective-permute-start(bf16[512,128]{1,0:T(8,128)(2,1)S(1)} %collective-permute-done.inner), channel_id=1, source_target_pairs={{0,2},{2,0},{1,3},{3,1},{4,6},{6,4},{5,7},{7,5},{8,10},{10,8},{9,1... | collective-permute-start | bytes 393224 | tf_op jit(solution)/shard_map/ppermute | solution.py:391
  16.5 15.2 %collective-permute-start.7 = (bf16[2,256,256]{2,1,0:T(8,128)(2,1)S(1)}, bf16[2,256,256]{2,1,0:T(8,128)(2,1)S(1)}, u32[]{:S(2)}, u32[]{:S(2)}) collective-permute-start(bf16[2,256,256]{2,1,0:T(8,128)(2,1)S(1)} %get-tuple-element.32), channel_id=1, source_target_pairs={{0,4},{4,0},{8,12},{12,8},{1,5},{5,1},{9,13},{13,9},{2,6},{6,2},{1... | collective-permute-start | bytes 786440 | tf_op jit(solution)/shard_map/ppermute | solution.py:400
  21.3 15.6 %collective-permute-start.6 = (bf16[2,256,256]{2,1,0:T(8,128)(2,1)S(1)}, bf16[2,256,256]{2,1,0:T(8,128)(2,1)S(1)}, u32[]{:S(2)}, u32[]{:S(2)}) collective-permute-start(bf16[2,256,256]{2,1,0:T(8,128)(2,1)S(1)} %get-tuple-element.31), channel_id=1, source_target_pairs={{0,8},{4,12},{8,0},{12,4},{1,9},{5,13},{9,1},{13,5},{2,10},{6,14},... | collective-permute-start | bytes 786440 | tf_op jit(solution)/shard_map/ppermute | solution.py:400
  24.6 17.6 %collective-permute-start.8 = (bf16[2,256,256]{2,1,0:T(8,128)(2,1)S(1)}, bf16[2,256,256]{2,1,0:T(8,128)(2,1)S(1)}, u32[]{:S(2)}, u32[]{:S(2)}) collective-permute-start(bf16[2,256,256]{2,1,0:T(8,128)(2,1)S(1)} %get-tuple-element.33), channel_id=1, source_target_pairs={{0,4},{4,0},{8,12},{12,8},{1,5},{5,1},{9,13},{13,9},{2,6},{6,2},{1... | collective-permute-start | bytes 786440 | tf_op jit(solution)/shard_map/ppermute | solution.py:400
  24.6 31.3 %collective-permute-start.11 = (bf16[2,256,256]{2,1,0:T(8,128)(2,1)S(1)}, bf16[2,256,256]{2,1,0:T(8,128)(2,1)S(1)}, u32[]{:S(2)}, u32[]{:S(2)}) collective-permute-start(bf16[2,256,256]{2,1,0:T(8,128)(2,1)S(1)} %get-tuple-element.37), channel_id=1, source_target_pairs={{0,12},{4,8},{8,4},{12,0},{1,13},{5,9},{9,5},{13,1},{2,14},{6,10},... | collective-permute-start | bytes 786440 | tf_op jit(solution)/shard_map/ppermute | solution.py:400
  25.6 34.1 %collective-permute-start.12 = (bf16[2,256,256]{2,1,0:T(8,128)(2,1)S(1)}, bf16[2,256,256]{2,1,0:T(8,128)(2,1)S(1)}, u32[]{:S(2)}, u32[]{:S(2)}) collective-permute-start(bf16[2,256,256]{2,1,0:T(8,128)(2,1)S(1)} %get-tuple-element.38), channel_id=1, source_target_pairs={{0,12},{4,8},{8,4},{12,0},{1,13},{5,9},{9,5},{13,1},{2,14},{6,10},... | collective-permute-start | bytes 786440 | tf_op jit(solution)/shard_map/ppermute | solution.py:400
  43.1 17.6 %collective-permute-start.9 = (bf16[2,3,64,256]{3,2,1,0:T(8,128)(2,1)S(1)}, bf16[2,3,64,256]{3,2,1,0:T(8,128)(2,1)S(1)}, u32[]{:S(2)}, u32[]{:S(2)}) collective-permute-start(bf16[2,3,64,256]{3,2,1,0:T(8,128)(2,1)S(1)} %get-tuple-element.36), channel_id=1, source_target_pairs={{0,2},{2,0},{1,3},{3,1},{4,6},{6,4},{5,7},{7,5},{8,10},{10,8},{9,1... | collective-permute-start | bytes 589832 | tf_op jit(solution)/shard_map/ppermute | solution.py:405
  60.6 1.8 %collective-permute-start.13 = (f32[2,3,64,256]{3,2,1,0:T(8,128)S(1)}, f32[2,3,64,256]{3,2,1,0:T(8,128)S(1)}, u32[]{:S(2)}, u32[]{:S(2)}) collective-permute-start(f32[2,3,64,256]{3,2,1,0:T(8,128)S(1)} %get-tuple-element.40), channel_id=1, source_target_pairs={{0,1},{1,0},{2,3},{3,2},{4,5},{5,4},{6,7},{7,6},{8,9},{9,8},{10,11... | collective-permute-start | bytes 1179656 | tf_op jit(solution)/shard_map/ppermute | solution.py:408
  60.7 3.3 %collective-permute-start.10 = (f32[3,64,256]{2,1,0:T(8,128)S(1)}, f32[3,64,256]{2,1,0:T(8,128)S(1)}, u32[]{:S(2)}, u32[]{:S(2)}) collective-permute-start(f32[3,64,256]{2,1,0:T(8,128)S(1)} %add_bitcast_fusion), channel_id=1, source_target_pairs={{0,1},{1,0},{2,3},{3,2},{4,5},{5,4},{6,7},{7,6},{8,9},{9,8},{10,11... | collective-permute-start | bytes 589832 | tf_op jit(solution)/shard_map/ppermute | solution.py:410
  62.4 4.9 %collective-permute-start.14 = (bf16[3,64,256]{2,1,0:T(8,128)(2,1)S(1)}, bf16[3,64,256]{2,1,0:T(8,128)(2,1)S(1)}, u32[]{:S(2)}, u32[]{:S(2)}) collective-permute-start(bf16[3,64,256]{2,1,0:T(8,128)(2,1)S(1)} %fusion.1), channel_id=1, source_target_pairs={{0,2},{2,0},{1,3},{3,1},{4,6},{6,4},{5,7},{7,5},{8,10},{10,8},{9,1... | collective-permute-start | bytes 294920 | tf_op jit(solution)/shard_map/ppermute | solution.py:409

commit v13 on v12

--- a/solution.py
+++ b/solution.py
@@ -225,7 +225,7 @@
     )(wants, integrals, own, outer, inner)
 
 
-def form_pairs(pairs, blocks, grams):
+def form_pairs(pairs, blocks, grams, before=None):
     here = lax.axis_index("ao")
     slices = [[(ref, p) for ref in block for p in range(ref.shape[0])] for block in blocks]
 
@@ -238,6 +238,10 @@
             total = part if total is None else total + part
         return total.reshape(grams.shape[1:])
 
+    def formed(k, left, right):
+        gram = product(left, right)
+        return gram if before is None else gram + before[k]
+
     for bit in (0, 1):
         mine = [(k, a, b) for k, (a, b) in enumerate(pairs) if (a ^ b) >> 1 == bit]
         upper = (here >> bit) & 1
@@ -245,12 +249,12 @@
         @pl.when(upper == 0)
         def _(mine=mine):
             for k, a, b in mine:
-                grams[k] = product(a, b)
+                grams[k] = formed(k, a, b)
 
         @pl.when(upper == 1)
         def _(mine=mine):
             for k, a, b in mine:
-                grams[k] = product(b, a)
+                grams[k] = formed(k, b, a)
 
 
 def early_kernel(live, table, *refs):
@@ -280,13 +284,15 @@
             far[core, k] = grams[k, 2 * (1 - aux) + (orb ^ core)].astype(jnp.bfloat16)
 
 
-def late_kernel(*refs):
-    used = GROUPS * CHUNKS
-    own, middle, next_to, last = [refs[i : i + CHUNKS] for i in range(0, used, CHUNKS)]
-    blocks = own, next_to, middle, last
-    keep, give, grams = refs[used:]
+def begin_kernel(own, middle, next_to, last, grams):
+    form_pairs(LATE_PAIRS, ([own], [next_to], [middle], [last]), grams)
+
+
+def late_kernel(own, middle, next_to, last, before, *refs):
+    keep, give, grams = refs
+    blocks = [own], [next_to], [middle], [last]
     aux, orb = lax.axis_index("aux"), lax.axis_index("orb")
-    form_pairs(LATE_PAIRS, blocks, grams)
+    form_pairs(LATE_PAIRS, blocks, grams, before)
     for k in range(len(LATE_PAIRS)):
         for chip in (0, 1):
             row = 2 * (aux ^ chip)
@@ -321,14 +327,22 @@
 
 def late_pairs(blocks):
     shape, grams = quarters(LATE_PAIRS)
+    own, next_to, middle, last = blocks
+    begun = local_call(
+        begin_kernel,
+        "begin_pairs",
+        [like(grams.shape, jnp.float32)],
+        GROUPS,
+        pair_flops(LATE_PAIRS, blocks) // CHUNKS,
+    )(own[0], middle[0], next_to[0], last[0])
     return local_call(
         late_kernel,
         "late_pairs",
         [like(shape, jnp.float32)] * 2,
-        GROUPS * CHUNKS,
-        pair_flops(LATE_PAIRS, blocks),
+        GROUPS + 1,
+        pair_flops(LATE_PAIRS, blocks) // CHUNKS,
         [grams],
-    )(*blocks[0], *blocks[2], *blocks[1], *blocks[3])
+    )(own[1], middle[1], next_to[1], last[1], *begun)
 
 
 def spread_kernel(factor, place, near0, far0, got0, near1, got1, far1, out, sums, rows, sems):

time: 68.6 us -> 68.4 us (level)
  transfers between devices with their start and end apart: 15 -> 15, of which waited for: 11 -> 11; matrix products, arithmetic and copies ran while one was open for 0% -> 0% of each run, Pallas kernels for 5% -> 6%
where the time goes in v13:
time: 68.4 us; the launch traced here: 68.3 us
  waiting for transfers between devices  42.4 us (62%)
  starting transfers between devices  19.2 us (28%)
  Pallas kernels  6.46 us (9%)
    ppermute x6, waiting for transfers between devices, fetch(): return [lax.ppermute(piece, 'ao', swap) for piece in blocks[s]]  29.5 us
    ppermute x6, starting transfers between devices, fetch(): return [lax.ppermute(piece, 'ao', swap) for piece in blocks[s]]  7.62 us
    ppermute x2, starting transfers between devices, six_pair_body(): inner = [lax.ppermute(part, 'ao', INSIDE) for part in (parts[0], mine)]  5.84 us
    ppermute x2, waiting for transfers between devices, six_pair_body(): inner = [lax.ppermute(part, 'ao', INSIDE) for part in (parts[0], mine)]  4.61 us
    ppermute x2, waiting for transfers between devices, six_pair_body(): outer = [lax.ppermute(part, 'ao', OUTSIDE) for part in parts]  3.8 us
    ppermute x1, waiting for transfers between devices, six_pair_body(): far1 = lax.ppermute((near1[1] + got1[1]).astype(jnp.bfloat16), 'aux', SWAP)  3.34 us
    ppermute x1, starting transfers between devices, six_pair_body(): swapped = lax.ppermute(inner[1], 'aux', SWAP)  1.56 us
    ppermute x1, starting transfers between devices, six_pair_body(): far0 = lax.ppermute(across0, 'aux', SWAP)  1.55 us
  transfers between devices with their start and end apart: 15, of which 11 were waited for; matrix products, arithmetic and copies ran while one was open for 0% of the time, Pallas kernels for 6%

profile of v13, /device:TPU:8, one launch (start us, length us, event | category | flops | bytes accessed | tf_op | source)
XLA Modules:
  0.0 68.3 jit_solution(4199802447196751720)
XLA Ops:
  0.0 1.1 %cut.1 = (bf16[512,256]{1,0:T(8,128)(2,1)S(1)}, bf16[512,256]{1,0:T(8,128)(2,1)S(1)}, bf16[512,128]{1,0:T(8,128)(2,1)S(1)}) custom-call(bf16[512,512]{1,0:T(8,128)(2,1)} %coeffs.1), custom_call_target="tpu_custom_call" | custom-call | flops 4294967296 | tf_op jit(solution)/shard_map/cut/pallas_call | solution.py:134
  1.2 3.5 %collective-permute-start.2 = (bf16[512,256]{1,0:T(8,128)(2,1)S(1)}, bf16[512,256]{1,0:T(8,128)(2,1)S(1)}, u32[]{:S(2)}, u32[]{:S(2)}) collective-permute-start(bf16[512,256]{1,0:T(8,128)(2,1)S(1)} %get-tuple-element.24.own), channel_id=1, source_target_pairs={{4,8},{8,4},{5,9},{9,5},{6,10},{10,6},{7,11},{11,7},{20,24},{24,20... | collective-permute-start | bytes 786440 | tf_op jit(solution)/shard_map/ppermute | solution.py:398
  4.7 2.4 %collective-permute-start = (bf16[512,128]{1,0:T(8,128)(2,1)S(1)}, bf16[512,128]{1,0:T(8,128)(2,1)S(1)}, u32[]{:S(2)}, u32[]{:S(2)}) collective-permute-start(bf16[512,128]{1,0:T(8,128)(2,1)S(1)} %get-tuple-element.23), channel_id=1, source_target_pairs={{4,8},{8,4},{5,9},{9,5},{6,10},{10,6},{7,11},{11,7},{20,24},{24,20... | collective-permute-start | bytes 393224 | tf_op jit(solution)/shard_map/ppermute | solution.py:398
  7.6 4.6 %collective-permute-done.2.inner = bf16[512,256]{1,0:T(8,128)(2,1)S(1)} collective-permute-done((bf16[512,256]{1,0:T(8,128)(2,1)S(1)}, bf16[512,256]{1,0:T(8,128)(2,1)S(1)}, u32[]{:S(2)}, u32[]{:S(2)}) %collective-permute-start.2) | collective-permute-done | bytes 262176 | tf_op jit(solution)/shard_map/ppermute | solution.py:398
  12.2 1.7 %collective-permute-done.1.outer = bf16[512,256]{1,0:T(8,128)(2,1)S(1)} collective-permute-done((bf16[512,256]{1,0:T(8,128)(2,1)S(1)}, bf16[512,256]{1,0:T(8,128)(2,1)S(1)}, u32[]{:S(2)}, u32[]{:S(2)}) %collective-permute-start.1) | collective-permute-done | bytes 262176 | tf_op jit(solution)/shard_map/ppermute | solution.py:399
  14.0 0.9 %transform.2 = (bf16[2,256,256]{2,1,0:T(8,128)(2,1)S(1)}, bf16[2,256,256]{2,1,0:T(8,128)(2,1)S(1)}, bf16[2,256,256]{2,1,0:T(8,128)(2,1)S(1)}, bf16[2,256,256]{2,1,0:T(8,128)(2,1)S(1)}) custom-call(s32[8,256]{1,0:T(8,128)S(1)} %tables.1.wants, bf16[2,512,1280]{2,1,0:T(8,128)(2,1)S(1)} %copy-done, bf16[512,256]{1,0:T(8,128)(2,1)S(1)} %get-tuple-element.24.own, ...), custom_call_target="tpu_custom_call" | custom-call | flops 671088640 | bytes 2097152 | tf_op jit(solution)/shard_map/transform/pallas_call | solution.py:219
  14.9 1.6 %collective-permute-start.4 = (bf16[512,128]{1,0:T(8,128)(2,1)S(1)}, bf16[512,128]{1,0:T(8,128)(2,1)S(1)}, u32[]{:S(2)}, u32[]{:S(2)}) collective-permute-start(bf16[512,128]{1,0:T(8,128)(2,1)S(1)} %collective-permute-done.inner), channel_id=1, source_target_pairs={{0,2},{2,0},{1,3},{3,1},{4,6},{6,4},{5,7},{7,5},{8,10},{10,8},{9,1... | collective-permute-start | bytes 393224 | tf_op jit(solution)/shard_map/ppermute | solution.py:405
  16.5 1.8 %collective-permute-start.7 = (bf16[2,256,256]{2,1,0:T(8,128)(2,1)S(1)}, bf16[2,256,256]{2,1,0:T(8,128)(2,1)S(1)}, u32[]{:S(2)}, u32[]{:S(2)}) collective-permute-start(bf16[2,256,256]{2,1,0:T(8,128)(2,1)S(1)} %get-tuple-element.32), channel_id=1, source_target_pairs={{0,4},{4,0},{8,12},{12,8},{1,5},{5,1},{9,13},{13,9},{2,6},{6,2},{1... | collective-permute-start | bytes 786440 | tf_op jit(solution)/shard_map/ppermute | solution.py:414
  18.3 2.1 %collective-permute-done.3.outer = bf16[512,256]{1,0:T(8,128)(2,1)S(1)} collective-permute-done((bf16[512,256]{1,0:T(8,128)(2,1)S(1)}, bf16[512,256]{1,0:T(8,128)(2,1)S(1)}, u32[]{:S(2)}, u32[]{:S(2)}) %collective-permute-start.3) | collective-permute-done | bytes 262176 | tf_op jit(solution)/shard_map/ppermute | solution.py:399
  20.4 0.9 %transform.3 = (bf16[2,256,256]{2,1,0:T(8,128)(2,1)S(1)}, bf16[2,256,256]{2,1,0:T(8,128)(2,1)S(1)}, bf16[2,256,256]{2,1,0:T(8,128)(2,1)S(1)}, bf16[2,256,256]{2,1,0:T(8,128)(2,1)S(1)}) custom-call(s32[8,256]{1,0:T(8,128)S(1)} %tables.1.wants, bf16[2,512,1280]{2,1,0:T(8,128)(2,1)S(1)} %copy-done, bf16[512,256]{1,0:T(8,128)(2,1)S(1)} %get-tuple-element.27.own, ...), custom_call_target="tpu_custom_call" | custom-call | flops 671088640 | bytes 2097152 | tf_op jit(solution)/shard_map/transform/pallas_call | solution.py:207
  21.3 3.2 %collective-permute-start.6 = (bf16[2,256,256]{2,1,0:T(8,128)(2,1)S(1)}, bf16[2,256,256]{2,1,0:T(8,128)(2,1)S(1)}, u32[]{:S(2)}, u32[]{:S(2)}) collective-permute-start(bf16[2,256,256]{2,1,0:T(8,128)(2,1)S(1)} %get-tuple-element.31), channel_id=1, source_target_pairs={{0,8},{4,12},{8,0},{12,4},{1,9},{5,13},{9,1},{13,5},{2,10},{6,14},... | collective-permute-start | bytes 786440 | tf_op jit(solution)/shard_map/ppermute | solution.py:414
  24.6 0.8 %collective-permute-start.12 = (bf16[2,256,256]{2,1,0:T(8,128)(2,1)S(1)}, bf16[2,256,256]{2,1,0:T(8,128)(2,1)S(1)}, u32[]{:S(2)}, u32[]{:S(2)}) collective-permute-start(bf16[2,256,256]{2,1,0:T(8,128)(2,1)S(1)} %get-tuple-element.38), channel_id=1, source_target_pairs={{0,12},{4,8},{8,4},{12,0},{1,13},{5,9},{9,5},{13,1},{2,14},{6,10},... | collective-permute-start | bytes 786440 | tf_op jit(solution)/shard_map/ppermute | solution.py:414
  25.6 1.7 %collective-permute-start.11 = (bf16[2,256,256]{2,1,0:T(8,128)(2,1)S(1)}, bf16[2,256,256]{2,1,0:T(8,128)(2,1)S(1)}, u32[]{:S(2)}, u32[]{:S(2)}) collective-permute-start(bf16[2,256,256]{2,1,0:T(8,128)(2,1)S(1)} %get-tuple-element.37), channel_id=1, source_target_pairs={{0,12},{4,8},{8,4},{12,0},{1,13},{5,9},{9,5},{13,1},{2,14},{6,10},... | collective-permute-start | bytes 786440 | tf_op jit(solution)/shard_map/ppermute | solution.py:414
  27.3 4.3 %collective-permute-done.7.refs_4_.next_to = bf16[2,256,256]{2,1,0:T(8,128)(2,1)S(1)} collective-permute-done((bf16[2,256,256]{2,1,0:T(8,128)(2,1)S(1)}, bf16[2,256,256]{2,1,0:T(8,128)(2,1)S(1)}, u32[]{:S(2)}, u32[]{:S(2)}) %collective-permute-start.7) | collective-permute-done | bytes 262176 | tf_op jit(solution)/shard_map/ppermute | solution.py:414
  31.6 5.3 %collective-permute-done.6.refs_3_.middle = bf16[2,256,256]{2,1,0:T(8,128)(2,1)S(1)} collective-permute-done((bf16[2,256,256]{2,1,0:T(8,128)(2,1)S(1)}, bf16[2,256,256]{2,1,0:T(8,128)(2,1)S(1)}, u32[]{:S(2)}, u32[]{:S(2)}) %collective-permute-start.6) | collective-permute-done | bytes 262176 | tf_op jit(solution)/shard_map/ppermute | solution.py:414
  36.9 5.2 %collective-permute-done.8.refs_5_.next_to = bf16[2,256,256]{2,1,0:T(8,128)(2,1)S(1)} collective-permute-done((bf16[2,256,256]{2,1,0:T(8,128)(2,1)S(1)}, bf16[2,256,256]{2,1,0:T(8,128)(2,1)S(1)}, u32[]{:S(2)}, u32[]{:S(2)}) %collective-permute-start.8) | collective-permute-done | bytes 262176 | tf_op jit(solution)/shard_map/ppermute | solution.py:414
  42.1 1.0 %early_pairs.1 = (f32[2,3,64,256]{3,2,1,0:T(8,128)S(1)}, bf16[2,3,64,256]{3,2,1,0:T(8,128)(2,1)S(1)}, s32[16,256]{1,0:T(8,128)S(1)}) custom-call(s32[1,4]{1,0:T(1,128)S(1)} %bitcast.9, s32[2,64]{1,0:T(2,128)S(1)} %bitcast.8, bf16[2,256,256]{2,1,0:T(8,128)(2,1)S(1)} %get-tuple-element.26.refs_0_.own, bf16[2,256,256]{2,1,0:T(8,128)(2,1)S(1)} %get-tuple-element.29.refs_1_.own, ...), custom_call_target="tpu_custom_call" | custom-call | flops 402653184 | bytes 1212416 | tf_op jit(solution)/shard_map/early_pairs/pallas_call | solution.py:314
  43.1 1.6 %collective-permute-start.9 = (bf16[2,3,64,256]{3,2,1,0:T(8,128)(2,1)S(1)}, bf16[2,3,64,256]{3,2,1,0:T(8,128)(2,1)S(1)}, u32[]{:S(2)}, u32[]{:S(2)}) collective-permute-start(bf16[2,3,64,256]{3,2,1,0:T(8,128)(2,1)S(1)} %get-tuple-element.36), channel_id=1, source_target_pairs={{0,2},{2,0},{1,3},{3,1},{4,6},{6,4},{5,7},{7,5},{8,10},{10,8},{9,1... | collective-permute-start | bytes 589832 | tf_op jit(solution)/shard_map/ppermute | solution.py:419
  44.7 11.2 %collective-permute-done.12.last = bf16[2,256,256]{2,1,0:T(8,128)(2,1)S(1)} collective-permute-done((bf16[2,256,256]{2,1,0:T(8,128)(2,1)S(1)}, bf16[2,256,256]{2,1,0:T(8,128)(2,1)S(1)}, u32[]{:S(2)}, u32[]{:S(2)}) %collective-permute-start.12) | collective-permute-done | bytes 262176 | tf_op jit(solution)/shard_map/ppermute | solution.py:414
  56.5 3.3 %collective-permute-done.11.last = bf16[2,256,256]{2,1,0:T(8,128)(2,1)S(1)} collective-permute-done((bf16[2,256,256]{2,1,0:T(8,128)(2,1)S(1)}, bf16[2,256,256]{2,1,0:T(8,128)(2,1)S(1)}, u32[]{:S(2)}, u32[]{:S(2)}) %collective-permute-start.11) | collective-permute-done | bytes 262176 | tf_op jit(solution)/shard_map/ppermute | solution.py:414
  61.1 1.1 %collective-permute-done.13.got1 = f32[2,3,64,256]{3,2,1,0:T(8,128)S(1)} collective-permute-done((f32[2,3,64,256]{3,2,1,0:T(8,128)S(1)}, f32[2,3,64,256]{3,2,1,0:T(8,128)S(1)}, u32[]{:S(2)}, u32[]{:S(2)}) %collective-permute-start.13) | collective-permute-done | bytes 393248 | tf_op jit(solution)/shard_map/ppermute | solution.py:422
  62.2 1.6 %collective-permute-start.14 = (bf16[3,64,256]{2,1,0:T(8,128)(2,1)S(1)}, bf16[3,64,256]{2,1,0:T(8,128)(2,1)S(1)}, u32[]{:S(2)}, u32[]{:S(2)}) collective-permute-start(bf16[3,64,256]{2,1,0:T(8,128)(2,1)S(1)} %fusion.1), channel_id=1, source_target_pairs={{0,2},{2,0},{1,3},{3,1},{4,6},{6,4},{5,7},{7,5},{8,10},{10,8},{9,1... | collective-permute-start | bytes 294920 | tf_op jit(solution)/shard_map/ppermute | solution.py:423
  63.8 3.3 %collective-permute-done.14.far1 = bf16[3,64,256]{2,1,0:T(8,128)(2,1)S(1)} collective-permute-done((bf16[3,64,256]{2,1,0:T(8,128)(2,1)S(1)}, bf16[3,64,256]{2,1,0:T(8,128)(2,1)S(1)}, u32[]{:S(2)}, u32[]{:S(2)}) %collective-permute-start.14) | collective-permute-done | bytes 98336 | tf_op jit(solution)/shard_map/ppermute | solution.py:423
  67.1 1.2 %spread.1 = f32[64,16,256]{2,1,0:T(8,128)} custom-call(s32[16,256]{1,0:T(8,128)S(1)} %get-tuple-element.34.place, f32[2,3,64,256]{3,2,1,0:T(8,128)S(1)} %get-tuple-element.35.near0, bf16[2,3,64,256]{3,2,1,0:T(8,128)(2,1)S(1)} %collective-permute-done.9.far0, f32[3,64,256]{2,1,0:T(8,128)S(1)} %collective-permute-done.10.got0, ...), custom_call_target="tpu_custom_call" | custom-call | flops 1572864 | bytes 2097152 | tf_op jit(solution)/shard_map/spread/pallas_call | solution.py:377
  (24 shorter events, 2.9 us)
Async XLA Ops:
  0.0 7.5 %copy-start.3 = (s32[8]{0:T(128)S(1)}, s32[8]{0:T(128)}, u32[]{:S(2)}) copy-start(s32[8]{0:T(128)} %param.9) | copy-start | bytes 100
  0.0 7.5 %copy-start.1 = (s32[64,2]{0,1:T(2,128)S(1)}, s32[64,2]{0,1:T(2,128)}, u32[]{:S(2)}) copy-start(s32[64,2]{0,1:T(2,128)} %param.7) | copy-start | bytes 1540
  1.2 11.1 %collective-permute-start.2 = (bf16[512,256]{1,0:T(8,128)(2,1)S(1)}, bf16[512,256]{1,0:T(8,128)(2,1)S(1)}, u32[]{:S(2)}, u32[]{:S(2)}) collective-permute-start(bf16[512,256]{1,0:T(8,128)(2,1)S(1)} %get-tuple-element.24.own), channel_id=1, source_target_pairs={{4,8},{8,4},{5,9},{9,5},{6,10},{10,6},{7,11},{11,7},{20,24},{24,20... | collective-permute-start | bytes 786440 | tf_op jit(solution)/shard_map/ppermute | solution.py:398
  4.7 9.3 %collective-permute-start.1 = (bf16[512,256]{1,0:T(8,128)(2,1)S(1)}, bf16[512,256]{1,0:T(8,128)(2,1)S(1)}, u32[]{:S(2)}, u32[]{:S(2)}) collective-permute-start(bf16[512,256]{1,0:T(8,128)(2,1)S(1)} %get-tuple-element.24.own), channel_id=1, source_target_pairs={{0,4},{4,0},{8,12},{12,8},{1,5},{5,1},{9,13},{13,9},{2,6},{6,2},{1... | collective-permute-start | bytes 786440 | tf_op jit(solution)/shard_map/ppermute | solution.py:399
  4.7 10.2 %collective-permute-start = (bf16[512,128]{1,0:T(8,128)(2,1)S(1)}, bf16[512,128]{1,0:T(8,128)(2,1)S(1)}, u32[]{:S(2)}, u32[]{:S(2)}) collective-permute-start(bf16[512,128]{1,0:T(8,128)(2,1)S(1)} %get-tuple-element.23), channel_id=1, source_target_pairs={{4,8},{8,4},{5,9},{9,5},{6,10},{10,6},{7,11},{11,7},{20,24},{24,20... | collective-permute-start | bytes 393224 | tf_op jit(solution)/shard_map/ppermute | solution.py:398
  7.1 13.3 %collective-permute-start.3 = (bf16[512,256]{1,0:T(8,128)(2,1)S(1)}, bf16[512,256]{1,0:T(8,128)(2,1)S(1)}, u32[]{:S(2)}, u32[]{:S(2)}) collective-permute-start(bf16[512,256]{1,0:T(8,128)(2,1)S(1)} %get-tuple-element.27.own), channel_id=1, source_target_pairs={{0,4},{4,0},{8,12},{12,8},{1,5},{5,1},{9,13},{13,9},{2,6},{6,2},{1... | collective-permute-start | bytes 786440 | tf_op jit(solution)/shard_map/ppermute | solution.py:399
  7.5 6.5 %copy-start = (bf16[2,512,1280]{2,1,0:T(8,128)(2,1)S(1)}, bf16[2,512,1280]{2,1,0:T(8,128)(2,1)}, u32[]{:S(2)}) copy-start(bf16[2,512,1280]{2,1,0:T(8,128)(2,1)} %integrals.3) | copy-start | bytes 7864324
  7.6 34.5 %copy-start.2 = (s32[4]{0:T(128)S(1)}, s32[4]{0:T(128)}, u32[]{:S(2)}) copy-start(s32[4]{0:T(128)} %param.8) | copy-start | bytes 52
  14.8 10.8 %collective-permute-start.5 = (bf16[2,256,256]{2,1,0:T(8,128)(2,1)S(1)}, bf16[2,256,256]{2,1,0:T(8,128)(2,1)S(1)}, u32[]{:S(2)}, u32[]{:S(2)}) collective-permute-start(bf16[2,256,256]{2,1,0:T(8,128)(2,1)S(1)} %get-tuple-element.30), channel_id=1, source_target_pairs={{0,8},{4,12},{8,0},{12,4},{1,9},{5,13},{9,1},{13,5},{2,10},{6,14},... | collective-permute-start | bytes 786440 | tf_op jit(solution)/shard_map/ppermute | solution.py:414
  14.9 5.5 %collective-permute-start.4 = (bf16[512,128]{1,0:T(8,128)(2,1)S(1)}, bf16[512,128]{1,0:T(8,128)(2,1)S(1)}, u32[]{:S(2)}, u32[]{:S(2)}) collective-permute-start(bf16[512,128]{1,0:T(8,128)(2,1)S(1)} %collective-permute-done.inner), channel_id=1, source_target_pairs={{0,2},{2,0},{1,3},{3,1},{4,6},{6,4},{5,7},{7,5},{8,10},{10,8},{9,1... | collective-permute-start | bytes 393224 | tf_op jit(solution)/shard_map/ppermute | solution.py:405
  16.5 15.2 %collective-permute-start.7 = (bf16[2,256,256]{2,1,0:T(8,128)(2,1)S(1)}, bf16[2,256,256]{2,1,0:T(8,128)(2,1)S(1)}, u32[]{:S(2)}, u32[]{:S(2)}) collective-permute-start(bf16[2,256,256]{2,1,0:T(8,128)(2,1)S(1)} %get-tuple-element.32), channel_id=1, source_target_pairs={{0,4},{4,0},{8,12},{12,8},{1,5},{5,1},{9,13},{13,9},{2,6},{6,2},{1... | collective-permute-start | bytes 786440 | tf_op jit(solution)/shard_map/ppermute | solution.py:414
  21.3 15.6 %collective-permute-start.6 = (bf16[2,256,256]{2,1,0:T(8,128)(2,1)S(1)}, bf16[2,256,256]{2,1,0:T(8,128)(2,1)S(1)}, u32[]{:S(2)}, u32[]{:S(2)}) collective-permute-start(bf16[2,256,256]{2,1,0:T(8,128)(2,1)S(1)} %get-tuple-element.31), channel_id=1, source_target_pairs={{0,8},{4,12},{8,0},{12,4},{1,9},{5,13},{9,1},{13,5},{2,10},{6,14},... | collective-permute-start | bytes 786440 | tf_op jit(solution)/shard_map/ppermute | solution.py:414
  24.6 17.6 %collective-permute-start.8 = (bf16[2,256,256]{2,1,0:T(8,128)(2,1)S(1)}, bf16[2,256,256]{2,1,0:T(8,128)(2,1)S(1)}, u32[]{:S(2)}, u32[]{:S(2)}) collective-permute-start(bf16[2,256,256]{2,1,0:T(8,128)(2,1)S(1)} %get-tuple-element.33), channel_id=1, source_target_pairs={{0,4},{4,0},{8,12},{12,8},{1,5},{5,1},{9,13},{13,9},{2,6},{6,2},{1... | collective-permute-start | bytes 786440 | tf_op jit(solution)/shard_map/ppermute | solution.py:414
  24.6 31.3 %collective-permute-start.12 = (bf16[2,256,256]{2,1,0:T(8,128)(2,1)S(1)}, bf16[2,256,256]{2,1,0:T(8,128)(2,1)S(1)}, u32[]{:S(2)}, u32[]{:S(2)}) collective-permute-start(bf16[2,256,256]{2,1,0:T(8,128)(2,1)S(1)} %get-tuple-element.38), channel_id=1, source_target_pairs={{0,12},{4,8},{8,4},{12,0},{1,13},{5,9},{9,5},{13,1},{2,14},{6,10},... | collective-permute-start | bytes 786440 | tf_op jit(solution)/shard_map/ppermute | solution.py:414
  25.6 34.1 %collective-permute-start.11 = (bf16[2,256,256]{2,1,0:T(8,128)(2,1)S(1)}, bf16[2,256,256]{2,1,0:T(8,128)(2,1)S(1)}, u32[]{:S(2)}, u32[]{:S(2)}) collective-permute-start(bf16[2,256,256]{2,1,0:T(8,128)(2,1)S(1)} %get-tuple-element.37), channel_id=1, source_target_pairs={{0,12},{4,8},{8,4},{12,0},{1,13},{5,9},{9,5},{13,1},{2,14},{6,10},... | collective-permute-start | bytes 786440 | tf_op jit(solution)/shard_map/ppermute | solution.py:414
  43.1 17.4 %collective-permute-start.9 = (bf16[2,3,64,256]{3,2,1,0:T(8,128)(2,1)S(1)}, bf16[2,3,64,256]{3,2,1,0:T(8,128)(2,1)S(1)}, u32[]{:S(2)}, u32[]{:S(2)}) collective-permute-start(bf16[2,3,64,256]{3,2,1,0:T(8,128)(2,1)S(1)} %get-tuple-element.36), channel_id=1, source_target_pairs={{0,2},{2,0},{1,3},{3,1},{4,6},{6,4},{5,7},{7,5},{8,10},{10,8},{9,1... | collective-permute-start | bytes 589832 | tf_op jit(solution)/shard_map/ppermute | solution.py:419
  60.4 1.8 %collective-permute-start.13 = (f32[2,3,64,256]{3,2,1,0:T(8,128)S(1)}, f32[2,3,64,256]{3,2,1,0:T(8,128)S(1)}, u32[]{:S(2)}, u32[]{:S(2)}) collective-permute-start(f32[2,3,64,256]{3,2,1,0:T(8,128)S(1)} %get-tuple-element.40), channel_id=1, source_target_pairs={{0,1},{1,0},{2,3},{3,2},{4,5},{5,4},{6,7},{7,6},{8,9},{9,8},{10,11... | collective-permute-start | bytes 1179656 | tf_op jit(solution)/shard_map/ppermute | solution.py:422
  60.5 3.3 %collective-permute-start.10 = (f32[3,64,256]{2,1,0:T(8,128)S(1)}, f32[3,64,256]{2,1,0:T(8,128)S(1)}, u32[]{:S(2)}, u32[]{:S(2)}) collective-permute-start(f32[3,64,256]{2,1,0:T(8,128)S(1)} %add_bitcast_fusion), channel_id=1, source_target_pairs={{0,1},{1,0},{2,3},{3,2},{4,5},{5,4},{6,7},{7,6},{8,9},{9,8},{10,11... | collective-permute-start | bytes 589832 | tf_op jit(solution)/shard_map/ppermute | solution.py:424
  62.2 4.9 %collective-permute-start.14 = (bf16[3,64,256]{2,1,0:T(8,128)(2,1)S(1)}, bf16[3,64,256]{2,1,0:T(8,128)(2,1)S(1)}, u32[]{:S(2)}, u32[]{:S(2)}) collective-permute-start(bf16[3,64,256]{2,1,0:T(8,128)(2,1)S(1)} %fusion.1), channel_id=1, source_target_pairs={{0,2},{2,0},{1,3},{3,1},{4,6},{6,4},{5,7},{7,5},{8,10},{10,8},{9,1... | collective-permute-start | bytes 294920 | tf_op jit(solution)/shard_map/ppermute | solution.py:423

commit v14 on v9

--- a/solution.py
+++ b/solution.py
@@ -79,8 +79,9 @@
 
 
 EARLY_PAIRS = ((0, 1), (0, 2), (1, 2))
-LATE_PAIRS = ((0, 3),), ((1, 3), (2, 3))
-ALL_PAIRS = EARLY_PAIRS + LATE_PAIRS[0] + LATE_PAIRS[1]
+LATE_PAIRS = ((0, 3), (1, 3), (2, 3))
+LATE_GROUPS = 2, 1
+ALL_PAIRS = EARLY_PAIRS + LATE_PAIRS
 GROUPS = 4
 SWAP = [(0, 1), (1, 0)]
 OUTSIDE = [(0, 1), (1, 0), (2, 3), (3, 2)]
@@ -202,7 +203,7 @@
     )(wants, integrals, own, outer, inner)
 
 
-def form_pairs(pairs, blocks, grams):
+def form_pairs(pairs, blocks, grams, before=None):
     here = lax.axis_index("ao")
     slices = [[(ref, p) for ref in block for p in range(ref.shape[0])] for block in blocks]
 
@@ -215,6 +216,10 @@
             total = part if total is None else total + part
         return total.reshape(grams.shape[1:])
 
+    def formed(k, left, right):
+        gram = product(left, right)
+        return gram if before is None else gram + before[k]
+
     for bit in (0, 1):
         mine = [(k, a, b) for k, (a, b) in enumerate(pairs) if (a ^ b) >> 1 == bit]
         upper = (here >> bit) & 1
@@ -222,12 +227,12 @@
         @pl.when(upper == 0)
         def _(mine=mine):
             for k, a, b in mine:
-                grams[k] = product(a, b)
+                grams[k] = formed(k, a, b)
 
         @pl.when(upper == 1)
         def _(mine=mine):
             for k, a, b in mine:
-                grams[k] = product(b, a)
+                grams[k] = formed(k, b, a)
 
 
 def early_kernel(live, table, *refs):
@@ -257,18 +262,23 @@
             far[core, k] = grams[k, 2 * (1 - aux) + (orb ^ core)].astype(jnp.bfloat16)
 
 
-def late_kernel(pairs, *refs):
-    used = GROUPS * CHUNKS
-    own, middle, next_to, last = [refs[i : i + CHUNKS] for i in range(0, used, CHUNKS)]
-    blocks = own, next_to, middle, last
-    keep, give, grams = refs[used:]
+def begin_kernel(own, middle, next_to, last, grams):
+    form_pairs(LATE_PAIRS, ([own], [next_to], [middle], [last]), grams)
+
+
+def late_kernel(own, middle, next_to, last, before, *refs):
+    *shares, grams = refs
+    blocks = [own], [next_to], [middle], [last]
     aux, orb = lax.axis_index("aux"), lax.axis_index("orb")
-    form_pairs(pairs, blocks, grams)
-    for k in range(len(pairs)):
-        for chip in (0, 1):
-            row = 2 * (aux ^ chip)
-            keep[chip, k] = grams[k, row + orb]
-            give[chip, k] = grams[k, row + 1 - orb]
+    form_pairs(LATE_PAIRS, blocks, grams, before)
+    done = 0
+    for keep, give in zip(shares[::2], shares[1::2]):
+        for k in range(keep.shape[1]):
+            for chip in (0, 1):
+                row = 2 * (aux ^ chip)
+                keep[chip, k] = grams[done + k, row + orb]
+                give[chip, k] = grams[done + k, row + 1 - orb]
+        done += keep.shape[1]
 
 
 def pair_flops(pairs, blocks):
@@ -296,16 +306,24 @@
     )(live.reshape(1, -1), table, *blocks[0], *blocks[2], *blocks[1])
 
 
-def late_pairs(pairs, blocks):
-    shape, grams = quarters(pairs)
-    return local_call(
-        functools.partial(late_kernel, pairs),
+def late_pairs(blocks):
+    shape, grams = quarters(LATE_PAIRS)
+    own, next_to, middle, last = blocks
+    begun = local_call(
+        begin_kernel,
+        "begin_pairs",
+        [like(grams.shape, jnp.float32)],
+        GROUPS,
+        16 * pair_flops(LATE_PAIRS, blocks),
+    )(own[0], middle[0], next_to[0], last[0])
+    return local_call(
+        late_kernel,
         "late_pairs",
-        [like(shape, jnp.float32)] * 2,
-        GROUPS * CHUNKS,
-        pair_flops(pairs, blocks),
+        [like((2, n, *shape[2:]), jnp.float32) for n in LATE_GROUPS for _ in range(2)],
+        GROUPS + 1,
+        16 * pair_flops(LATE_PAIRS, blocks),
         [grams],
-    )(*blocks[0], *blocks[2], *blocks[1], *blocks[3])
+    )(own[1], middle[1], next_to[1], last[1], *begun)
 
 
 def spread_kernel(factor, place, near, far, got, *refs):
@@ -390,8 +408,9 @@
     near0, across0, place = early_pairs(pair_count, table, got)
     far0 = lax.ppermute(across0, "aux", SWAP)
     got.append(fetch(3))
+    shares = late_pairs(got)
     late = []
-    for near1, give1 in [late_pairs(pairs, got) for pairs in LATE_PAIRS]:
+    for near1, give1 in zip(shares[::2], shares[1::2]):
         got1 = lax.ppermute(give1, "orb", SWAP)
         far1 = lax.ppermute((near1[1] + got1[1]).astype(jnp.bfloat16), "aux", SWAP)
         late += [near1, got1, far1]

time: 70.2 us -> 73 us (1.040)
  the two profiles are of different devices: /device:TPU:8 before, /device:TPU:0 now
where the time goes in v14:
time: 73 us; the launch traced here: 72.8 us
  waiting for transfers between devices  41.2 us (56%)
  starting transfers between devices  23.2 us (32%)
  Pallas kernels  5.29 us (7%)
  local copies, waits for them, and re-layouts  2.87 us (4%)
    ppermute x6, waiting for transfers between devices, fetch(): return [lax.ppermute(piece, 'ao', swap) for piece in blocks[s]]  28.7 us
    ppermute x6, starting transfers between devices, fetch(): return [lax.ppermute(piece, 'ao', swap) for piece in blocks[s]]  8.09 us
    ppermute x2, starting transfers between devices, six_pair_body(): outer = [lax.ppermute(part, 'ao', OUTSIDE) for part in parts]  7.81 us
    ppermute x2, waiting for transfers between devices, six_pair_body(): outer = [lax.ppermute(part, 'ao', OUTSIDE) for part in parts]  4.63 us
    ppermute x2, waiting for transfers between devices, six_pair_body(): far1 = lax.ppermute((near1[1] + got1[1]).astype(jnp.bfloat16), 'aux', SWAP)  3.4 us
    ppermute x1, waiting for transfers between devices, six_pair_body(): far0 = lax.ppermute(across0, 'aux', SWAP)  2.93 us
    ppermute x2, starting transfers between devices, six_pair_body(): far1 = lax.ppermute((near1[1] + got1[1]).astype(jnp.bfloat16), 'aux', SWAP)  2.16 us
    ppermute x1, starting transfers between devices, six_pair_body(): far0 = lax.ppermute(across0, 'aux', SWAP)  1.57 us
  transfers between devices with their start and end apart: 17, of which 9 were waited for; matrix products, arithmetic and copies ran while one was open for 3% of the time, Pallas kernels for 6%

profile of v14, /device:TPU:0, one launch (start us, length us, event | category | flops | bytes accessed | tf_op | source)
XLA Modules:
  0.0 72.8 jit_solution(2582950555009793021)
XLA Ops:
  0.0 1.0 %slice.24.own = bf16[512,256]{1,0:T(8,128)(2,1)S(1)} slice(bf16[512,512]{1,0:T(8,128)(2,1)} %param.6), slice={[0:512], [0:256]} | slice | bytes 524288 | tf_op jit(solution)/shard_map/slice | solution.py:384
  1.8 6.0 %collective-permute-start.1 = (bf16[512,256]{1,0:T(8,128)(2,1)S(1)}, bf16[512,256]{1,0:T(8,128)(2,1)S(1)}, u32[]{:S(2)}, u32[]{:S(2)}) collective-permute-start(bf16[512,256]{1,0:T(8,128)(2,1)S(1)} %slice.24.own), channel_id=1, source_target_pairs={{0,4},{4,0},{8,12},{12,8},{1,5},{5,1},{9,13},{13,9},{2,6},{6,2},{1... | collective-permute-start | bytes 786440 | tf_op jit(solution)/shard_map/ppermute | solution.py:389
  7.9 0.9 %constant_dynamic-slice_fusion = bf16[512,128]{1,0:T(8,128)(2,1)S(1)} fusion(bf16[512,512]{1,0:T(8,128)(2,1)} %param.6, s32[]{:T(128)S(6)} %select_n.3), kind=kLoop, calls=%fused_computation.7 | loop fusion | bytes 262148 | tf_op jit(solution)/shard_map/dynamic_slice | solution.py:387
  9.4 1.0 %slice.25.own = bf16[512,256]{1,0:T(8,128)(2,1)S(1)} slice(bf16[512,512]{1,0:T(8,128)(2,1)} %param.6), slice={[0:512], [256:512]} | slice | bytes 524288 | tf_op jit(solution)/shard_map/slice | solution.py:386
  10.4 1.8 %collective-permute-start.3 = (bf16[512,256]{1,0:T(8,128)(2,1)S(1)}, bf16[512,256]{1,0:T(8,128)(2,1)S(1)}, u32[]{:S(2)}, u32[]{:S(2)}) collective-permute-start(bf16[512,256]{1,0:T(8,128)(2,1)S(1)} %slice.25.own), channel_id=1, source_target_pairs={{0,4},{4,0},{8,12},{12,8},{1,5},{5,1},{9,13},{13,9},{2,6},{6,2},{1... | collective-permute-start | bytes 786440 | tf_op jit(solution)/shard_map/ppermute | solution.py:389
  12.4 2.7 %collective-permute-done.1.outer = bf16[512,256]{1,0:T(8,128)(2,1)S(1)} collective-permute-done((bf16[512,256]{1,0:T(8,128)(2,1)S(1)}, bf16[512,256]{1,0:T(8,128)(2,1)S(1)}, u32[]{:S(2)}, u32[]{:S(2)}) %collective-permute-start.1) | collective-permute-done | bytes 262176 | tf_op jit(solution)/shard_map/ppermute | solution.py:389
  15.9 1.4 %collective-permute-start.5 = (bf16[2,256,256]{2,1,0:T(8,128)(2,1)S(1)}, bf16[2,256,256]{2,1,0:T(8,128)(2,1)S(1)}, u32[]{:S(2)}, u32[]{:S(2)}) collective-permute-start(bf16[2,256,256]{2,1,0:T(8,128)(2,1)S(1)} %get-tuple-element.30), channel_id=1, source_target_pairs={{0,8},{4,12},{8,0},{12,4},{1,9},{5,13},{9,1},{13,5},{2,10},{6,14},... | collective-permute-start | bytes 786440 | tf_op jit(solution)/shard_map/ppermute | solution.py:404
  18.1 2.3 %collective-permute-start.12 = (bf16[2,256,256]{2,1,0:T(8,128)(2,1)S(1)}, bf16[2,256,256]{2,1,0:T(8,128)(2,1)S(1)}, u32[]{:S(2)}, u32[]{:S(2)}) collective-permute-start(bf16[2,256,256]{2,1,0:T(8,128)(2,1)S(1)} %get-tuple-element.38), channel_id=1, source_target_pairs={{0,12},{4,8},{8,4},{12,0},{1,13},{5,9},{9,5},{13,1},{2,14},{6,10},... | collective-permute-start | bytes 786440 | tf_op jit(solution)/shard_map/ppermute | solution.py:404
  20.4 1.5 %collective-permute-start.4 = (bf16[512,128]{1,0:T(8,128)(2,1)S(1)}, bf16[512,128]{1,0:T(8,128)(2,1)S(1)}, u32[]{:S(2)}, u32[]{:S(2)}) collective-permute-start(bf16[512,128]{1,0:T(8,128)(2,1)S(1)} %collective-permute-done.inner), channel_id=1, source_target_pairs={{0,2},{2,0},{1,3},{3,1},{4,6},{6,4},{5,7},{7,5},{8,10},{10,8},{9,1... | collective-permute-start | bytes 393224 | tf_op jit(solution)/shard_map/ppermute | solution.py:395
  21.9 2.0 %collective-permute-done.3.outer = bf16[512,256]{1,0:T(8,128)(2,1)S(1)} collective-permute-done((bf16[512,256]{1,0:T(8,128)(2,1)S(1)}, bf16[512,256]{1,0:T(8,128)(2,1)S(1)}, u32[]{:S(2)}, u32[]{:S(2)}) %collective-permute-start.3) | collective-permute-done | bytes 262176 | tf_op jit(solution)/shard_map/ppermute | solution.py:389
  23.8 1.5 %collective-permute-done.4.swapped = bf16[512,128]{1,0:T(8,128)(2,1)S(1)} collective-permute-done((bf16[512,128]{1,0:T(8,128)(2,1)S(1)}, bf16[512,128]{1,0:T(8,128)(2,1)S(1)}, u32[]{:S(2)}, u32[]{:S(2)}) %collective-permute-start.4) | collective-permute-done | bytes 131104 | tf_op jit(solution)/shard_map/ppermute | solution.py:395
  25.3 0.9 %transform.3 = (bf16[2,256,256]{2,1,0:T(8,128)(2,1)S(1)}, bf16[2,256,256]{2,1,0:T(8,128)(2,1)S(1)}, bf16[2,256,256]{2,1,0:T(8,128)(2,1)S(1)}, bf16[2,256,256]{2,1,0:T(8,128)(2,1)S(1)}) custom-call(s32[8,256]{1,0:T(8,128)S(1)} %tables.1.wants, bf16[2,512,1280]{2,1,0:T(8,128)(2,1)S(1)} %copy-done, bf16[512,256]{1,0:T(8,128)(2,1)S(1)} %slice.25.own, ...), custom_call_target="tpu_custom_call" | custom-call | flops 671088640 | bytes 2097152 | tf_op jit(solution)/shard_map/transform/pallas_call | solution.py:185
  26.9 1.5 %collective-permute-start.8 = (bf16[2,256,256]{2,1,0:T(8,128)(2,1)S(1)}, bf16[2,256,256]{2,1,0:T(8,128)(2,1)S(1)}, u32[]{:S(2)}, u32[]{:S(2)}) collective-permute-start(bf16[2,256,256]{2,1,0:T(8,128)(2,1)S(1)} %get-tuple-element.33), channel_id=1, source_target_pairs={{0,4},{4,0},{8,12},{12,8},{1,5},{5,1},{9,13},{13,9},{2,6},{6,2},{1... | collective-permute-start | bytes 786440 | tf_op jit(solution)/shard_map/ppermute | solution.py:404
  28.4 3.4 %collective-permute-done.5.refs_2_.middle = bf16[2,256,256]{2,1,0:T(8,128)(2,1)S(1)} collective-permute-done((bf16[2,256,256]{2,1,0:T(8,128)(2,1)S(1)}, bf16[2,256,256]{2,1,0:T(8,128)(2,1)S(1)}, u32[]{:S(2)}, u32[]{:S(2)}) %collective-permute-start.5) | collective-permute-done | bytes 262176 | tf_op jit(solution)/shard_map/ppermute | solution.py:404
  31.8 1.4 %collective-permute-start.11 = (bf16[2,256,256]{2,1,0:T(8,128)(2,1)S(1)}, bf16[2,256,256]{2,1,0:T(8,128)(2,1)S(1)}, u32[]{:S(2)}, u32[]{:S(2)}) collective-permute-start(bf16[2,256,256]{2,1,0:T(8,128)(2,1)S(1)} %get-tuple-element.37), channel_id=1, source_target_pairs={{0,12},{4,8},{8,4},{12,0},{1,13},{5,9},{9,5},{13,1},{2,14},{6,10},... | collective-permute-start | bytes 786440 | tf_op jit(solution)/shard_map/ppermute | solution.py:404
  33.2 3.1 %collective-permute-done.7.refs_4_.next_to = bf16[2,256,256]{2,1,0:T(8,128)(2,1)S(1)} collective-permute-done((bf16[2,256,256]{2,1,0:T(8,128)(2,1)S(1)}, bf16[2,256,256]{2,1,0:T(8,128)(2,1)S(1)}, u32[]{:S(2)}, u32[]{:S(2)}) %collective-permute-start.7) | collective-permute-done | bytes 262176 | tf_op jit(solution)/shard_map/ppermute | solution.py:404
  36.4 2.6 %collective-permute-done.12.last = bf16[2,256,256]{2,1,0:T(8,128)(2,1)S(1)} collective-permute-done((bf16[2,256,256]{2,1,0:T(8,128)(2,1)S(1)}, bf16[2,256,256]{2,1,0:T(8,128)(2,1)S(1)}, u32[]{:S(2)}, u32[]{:S(2)}) %collective-permute-start.12) | collective-permute-done | bytes 262176 | tf_op jit(solution)/shard_map/ppermute | solution.py:404
  39.6 19.6 %collective-permute-done.6.refs_3_.middle = bf16[2,256,256]{2,1,0:T(8,128)(2,1)S(1)} collective-permute-done((bf16[2,256,256]{2,1,0:T(8,128)(2,1)S(1)}, bf16[2,256,256]{2,1,0:T(8,128)(2,1)S(1)}, u32[]{:S(2)}, u32[]{:S(2)}) %collective-permute-start.6) | collective-permute-done | bytes 262176 | tf_op jit(solution)/shard_map/ppermute | solution.py:404
  59.2 1.0 %early_pairs.1 = (f32[2,3,64,256]{3,2,1,0:T(8,128)S(1)}, bf16[2,3,64,256]{3,2,1,0:T(8,128)(2,1)S(1)}, s32[16,256]{1,0:T(8,128)S(1)}) custom-call(s32[1,4]{1,0:T(1,128)S(1)} %bitcast.11, s32[2,64]{1,0:T(2,128)S(1)} %bitcast.10, bf16[2,256,256]{2,1,0:T(8,128)(2,1)S(1)} %get-tuple-element.27.refs_0_.own, ...), custom_call_target="tpu_custom_call" | custom-call | flops 402653184 | bytes 1212416 | tf_op jit(solution)/shard_map/early_pairs/pallas_call | solution.py:295
  60.2 1.6 %collective-permute-start.9 = (bf16[2,3,64,256]{3,2,1,0:T(8,128)(2,1)S(1)}, bf16[2,3,64,256]{3,2,1,0:T(8,128)(2,1)S(1)}, u32[]{:S(2)}, u32[]{:S(2)}) collective-permute-start(bf16[2,3,64,256]{3,2,1,0:T(8,128)(2,1)S(1)} %get-tuple-element.36), channel_id=1, source_target_pairs={{0,2},{2,0},{1,3},{3,1},{4,6},{6,4},{5,7},{7,5},{8,10},{10,8},{9,1... | collective-permute-start | bytes 589832 | tf_op jit(solution)/shard_map/ppermute | solution.py:409
  63.0 2.9 %collective-permute-done.9.far = bf16[2,3,64,256]{3,2,1,0:T(8,128)(2,1)S(1)} collective-permute-done((bf16[2,3,64,256]{3,2,1,0:T(8,128)(2,1)S(1)}, bf16[2,3,64,256]{3,2,1,0:T(8,128)(2,1)S(1)}, u32[]{:S(2)}, u32[]{:S(2)}) %collective-permute-start.9) | collective-permute-done | bytes 196640 | tf_op jit(solution)/shard_map/ppermute | solution.py:409
  66.1 1.6 %collective-permute-start.14 = (bf16[2,64,256]{2,1,0:T(8,128)(2,1)S(1)}, bf16[2,64,256]{2,1,0:T(8,128)(2,1)S(1)}, u32[]{:S(2)}, u32[]{:S(2)}) collective-permute-start(bf16[2,64,256]{2,1,0:T(8,128)(2,1)S(1)} %fusion.1), channel_id=1, source_target_pairs={{0,2},{2,0},{1,3},{3,1},{4,6},{6,4},{5,7},{7,5},{8,10},{10,8},{9,1... | collective-permute-start | bytes 196616 | tf_op jit(solution)/shard_map/ppermute | solution.py:415
  68.2 3.4 %collective-permute-done.16.refs_5_ = bf16[1,64,256]{2,1,0:T(8,128)(2,1)S(1)} collective-permute-done((bf16[1,64,256]{2,1,0:T(8,128)(2,1)S(1)}, bf16[1,64,256]{2,1,0:T(8,128)(2,1)S(1)}, u32[]{:S(2)}, u32[]{:S(2)}) %collective-permute-start.16) | collective-permute-done | bytes 32800 | tf_op jit(solution)/shard_map/ppermute | solution.py:415
  71.6 1.1 %spread.1 = f32[64,16,256]{2,1,0:T(8,128)} custom-call(s32[16,256]{1,0:T(8,128)S(1)} %get-tuple-element.34.place, f32[2,3,64,256]{3,2,1,0:T(8,128)S(1)} %get-tuple-element.35.near, bf16[2,3,64,256]{3,2,1,0:T(8,128)(2,1)S(1)} %collective-permute-done.9.far, f32[3,64,256]{2,1,0:T(8,128)S(1)} %collective-permute-done.10.got, ...), custom_call_target="tpu_custom_call" | custom-call | flops 1572864 | bytes 2097152 | tf_op jit(solution)/shard_map/spread/pallas_call | solution.py:363
  (32 shorter events, 6.4 us)
Async XLA Ops:
  1.0 11.2 %copy-start.1 = (s32[64,2]{0,1:T(2,128)S(1)}, s32[64,2]{0,1:T(2,128)}, u32[]{:S(2)}) copy-start(s32[64,2]{0,1:T(2,128)} %param.7) | copy-start | bytes 1540
  1.0 11.2 %copy-start.3 = (s32[8]{0:T(128)S(1)}, s32[8]{0:T(128)}, u32[]{:S(2)}) copy-start(s32[8]{0:T(128)} %param.9) | copy-start | bytes 100
  1.0 14.0 %copy-start = (bf16[2,512,1280]{2,1,0:T(8,128)(2,1)S(1)}, bf16[2,512,1280]{2,1,0:T(8,128)(2,1)}, u32[]{:S(2)}) copy-start(bf16[2,512,1280]{2,1,0:T(8,128)(2,1)} %integrals.3) | copy-start | bytes 7864324
  1.0 11.4 %collective-permute-start.2 = (bf16[512,256]{1,0:T(8,128)(2,1)S(1)}, bf16[512,256]{1,0:T(8,128)(2,1)S(1)}, u32[]{:S(2)}, u32[]{:S(2)}) collective-permute-start(bf16[512,256]{1,0:T(8,128)(2,1)S(1)} %slice.24.own), channel_id=1, source_target_pairs={{4,8},{8,4},{5,9},{9,5},{6,10},{10,6},{7,11},{11,7},{20,24},{24,20... | collective-permute-start | bytes 786440 | tf_op jit(solution)/shard_map/ppermute | solution.py:388
  1.8 13.2 %collective-permute-start.1 = (bf16[512,256]{1,0:T(8,128)(2,1)S(1)}, bf16[512,256]{1,0:T(8,128)(2,1)S(1)}, u32[]{:S(2)}, u32[]{:S(2)}) collective-permute-start(bf16[512,256]{1,0:T(8,128)(2,1)S(1)} %slice.24.own), channel_id=1, source_target_pairs={{0,4},{4,0},{8,12},{12,8},{1,5},{5,1},{9,13},{13,9},{2,6},{6,2},{1... | collective-permute-start | bytes 786440 | tf_op jit(solution)/shard_map/ppermute | solution.py:389
  8.8 11.6 %collective-permute-start = (bf16[512,128]{1,0:T(8,128)(2,1)S(1)}, bf16[512,128]{1,0:T(8,128)(2,1)S(1)}, u32[]{:S(2)}, u32[]{:S(2)}) collective-permute-start(bf16[512,128]{1,0:T(8,128)(2,1)S(1)} %constant_dynamic-slice_fusion), channel_id=1, source_target_pairs={{4,8},{8,4},{5,9},{9,5},{6,10},{10,6},{7,11},{11,7},{20,24},{24,20... | collective-permute-start | bytes 393224 | tf_op jit(solution)/shard_map/ppermute | solution.py:388
  10.4 13.4 %collective-permute-start.3 = (bf16[512,256]{1,0:T(8,128)(2,1)S(1)}, bf16[512,256]{1,0:T(8,128)(2,1)S(1)}, u32[]{:S(2)}, u32[]{:S(2)}) collective-permute-start(bf16[512,256]{1,0:T(8,128)(2,1)S(1)} %slice.25.own), channel_id=1, source_target_pairs={{0,4},{4,0},{8,12},{12,8},{1,5},{5,1},{9,13},{13,9},{2,6},{6,2},{1... | collective-permute-start | bytes 786440 | tf_op jit(solution)/shard_map/ppermute | solution.py:389
  15.9 15.9 %collective-permute-start.5 = (bf16[2,256,256]{2,1,0:T(8,128)(2,1)S(1)}, bf16[2,256,256]{2,1,0:T(8,128)(2,1)S(1)}, u32[]{:S(2)}, u32[]{:S(2)}) collective-permute-start(bf16[2,256,256]{2,1,0:T(8,128)(2,1)S(1)} %get-tuple-element.30), channel_id=1, source_target_pairs={{0,8},{4,12},{8,0},{12,4},{1,9},{5,13},{9,1},{13,5},{2,10},{6,14},... | collective-permute-start | bytes 786440 | tf_op jit(solution)/shard_map/ppermute | solution.py:404
  17.3 19.0 %collective-permute-start.7 = (bf16[2,256,256]{2,1,0:T(8,128)(2,1)S(1)}, bf16[2,256,256]{2,1,0:T(8,128)(2,1)S(1)}, u32[]{:S(2)}, u32[]{:S(2)}) collective-permute-start(bf16[2,256,256]{2,1,0:T(8,128)(2,1)S(1)} %get-tuple-element.32), channel_id=1, source_target_pairs={{0,4},{4,0},{8,12},{12,8},{1,5},{5,1},{9,13},{13,9},{2,6},{6,2},{1... | collective-permute-start | bytes 786440 | tf_op jit(solution)/shard_map/ppermute | solution.py:404
  18.1 20.9 %collective-permute-start.12 = (bf16[2,256,256]{2,1,0:T(8,128)(2,1)S(1)}, bf16[2,256,256]{2,1,0:T(8,128)(2,1)S(1)}, u32[]{:S(2)}, u32[]{:S(2)}) collective-permute-start(bf16[2,256,256]{2,1,0:T(8,128)(2,1)S(1)} %get-tuple-element.38), channel_id=1, source_target_pairs={{0,12},{4,8},{8,4},{12,0},{1,13},{5,9},{9,5},{13,1},{2,14},{6,10},... | collective-permute-start | bytes 786440 | tf_op jit(solution)/shard_map/ppermute | solution.py:404
  20.4 5.0 %collective-permute-start.4 = (bf16[512,128]{1,0:T(8,128)(2,1)S(1)}, bf16[512,128]{1,0:T(8,128)(2,1)S(1)}, u32[]{:S(2)}, u32[]{:S(2)}) collective-permute-start(bf16[512,128]{1,0:T(8,128)(2,1)S(1)} %collective-permute-done.inner), channel_id=1, source_target_pairs={{0,2},{2,0},{1,3},{3,1},{4,6},{6,4},{5,7},{7,5},{8,10},{10,8},{9,1... | collective-permute-start | bytes 393224 | tf_op jit(solution)/shard_map/ppermute | solution.py:395
  26.3 32.9 %collective-permute-start.6 = (bf16[2,256,256]{2,1,0:T(8,128)(2,1)S(1)}, bf16[2,256,256]{2,1,0:T(8,128)(2,1)S(1)}, u32[]{:S(2)}, u32[]{:S(2)}) collective-permute-start(bf16[2,256,256]{2,1,0:T(8,128)(2,1)S(1)} %get-tuple-element.31), channel_id=1, source_target_pairs={{0,8},{4,12},{8,0},{12,4},{1,9},{5,13},{9,1},{13,5},{2,10},{6,14},... | collective-permute-start | bytes 786440 | tf_op jit(solution)/shard_map/ppermute | solution.py:404
  26.9 32.3 %collective-permute-start.8 = (bf16[2,256,256]{2,1,0:T(8,128)(2,1)S(1)}, bf16[2,256,256]{2,1,0:T(8,128)(2,1)S(1)}, u32[]{:S(2)}, u32[]{:S(2)}) collective-permute-start(bf16[2,256,256]{2,1,0:T(8,128)(2,1)S(1)} %get-tuple-element.33), channel_id=1, source_target_pairs={{0,4},{4,0},{8,12},{12,8},{1,5},{5,1},{9,13},{13,9},{2,6},{6,2},{1... | collective-permute-start | bytes 786440 | tf_op jit(solution)/shard_map/ppermute | solution.py:404
  31.8 27.4 %copy-start.2 = (s32[4]{0:T(128)S(1)}, s32[4]{0:T(128)}, u32[]{:S(2)}) copy-start(s32[4]{0:T(128)} %param.8) | copy-start | bytes 52
  31.8 30.0 %collective-permute-start.11 = (bf16[2,256,256]{2,1,0:T(8,128)(2,1)S(1)}, bf16[2,256,256]{2,1,0:T(8,128)(2,1)S(1)}, u32[]{:S(2)}, u32[]{:S(2)}) collective-permute-start(bf16[2,256,256]{2,1,0:T(8,128)(2,1)S(1)} %get-tuple-element.37), channel_id=1, source_target_pairs={{0,12},{4,8},{8,4},{12,0},{1,13},{5,9},{9,5},{13,1},{2,14},{6,10},... | collective-permute-start | bytes 786440 | tf_op jit(solution)/shard_map/ppermute | solution.py:404
  60.2 5.7 %collective-permute-start.9 = (bf16[2,3,64,256]{3,2,1,0:T(8,128)(2,1)S(1)}, bf16[2,3,64,256]{3,2,1,0:T(8,128)(2,1)S(1)}, u32[]{:S(2)}, u32[]{:S(2)}) collective-permute-start(bf16[2,3,64,256]{3,2,1,0:T(8,128)(2,1)S(1)} %get-tuple-element.36), channel_id=1, source_target_pairs={{0,2},{2,0},{1,3},{3,1},{4,6},{6,4},{5,7},{7,5},{8,10},{10,8},{9,1... | collective-permute-start | bytes 589832 | tf_op jit(solution)/shard_map/ppermute | solution.py:409
  62.4 3.6 %collective-permute-start.13 = (f32[2,2,64,256]{3,2,1,0:T(8,128)S(1)}, f32[2,2,64,256]{3,2,1,0:T(8,128)S(1)}, u32[]{:S(2)}, u32[]{:S(2)}) collective-permute-start(f32[2,2,64,256]{3,2,1,0:T(8,128)S(1)} %get-tuple-element.40), channel_id=1, source_target_pairs={{0,1},{1,0},{2,3},{3,2},{4,5},{5,4},{6,7},{7,6},{8,9},{9,8},{10,11... | collective-permute-start | bytes 786440 | tf_op jit(solution)/shard_map/ppermute | solution.py:414
  62.5 5.1 %collective-permute-start.15 = (f32[2,1,64,256]{3,2,1,0:T(8,128)S(1)}, f32[2,1,64,256]{3,2,1,0:T(8,128)S(1)}, u32[]{:S(2)}, u32[]{:S(2)}) collective-permute-start(f32[2,1,64,256]{3,2,1,0:T(8,128)S(1)} %get-tuple-element.42), channel_id=1, source_target_pairs={{0,1},{1,0},{2,3},{3,2},{4,5},{5,4},{6,7},{7,6},{8,9},{9,8},{10,11... | collective-permute-start | bytes 393224 | tf_op jit(solution)/shard_map/ppermute | solution.py:414
  65.9 5.7 %collective-permute-start.10 = (f32[3,64,256]{2,1,0:T(8,128)S(1)}, f32[3,64,256]{2,1,0:T(8,128)S(1)}, u32[]{:S(2)}, u32[]{:S(2)}) collective-permute-start(f32[3,64,256]{2,1,0:T(8,128)S(1)} %add_bitcast_fusion), channel_id=1, source_target_pairs={{0,1},{1,0},{2,3},{3,2},{4,5},{5,4},{6,7},{7,6},{8,9},{9,8},{10,11... | collective-permute-start | bytes 589832 | tf_op jit(solution)/shard_map/ppermute | solution.py:417
  66.1 5.6 %collective-permute-start.14 = (bf16[2,64,256]{2,1,0:T(8,128)(2,1)S(1)}, bf16[2,64,256]{2,1,0:T(8,128)(2,1)S(1)}, u32[]{:S(2)}, u32[]{:S(2)}) collective-permute-start(bf16[2,64,256]{2,1,0:T(8,128)(2,1)S(1)} %fusion.1), channel_id=1, source_target_pairs={{0,2},{2,0},{1,3},{3,1},{4,6},{6,4},{5,7},{7,5},{8,10},{10,8},{9,1... | collective-permute-start | bytes 196616 | tf_op jit(solution)/shard_map/ppermute | solution.py:415
  67.6 4.0 %collective-permute-start.16 = (bf16[1,64,256]{2,1,0:T(8,128)(2,1)S(1)}, bf16[1,64,256]{2,1,0:T(8,128)(2,1)S(1)}, u32[]{:S(2)}, u32[]{:S(2)}) collective-permute-start(bf16[1,64,256]{2,1,0:T(8,128)(2,1)S(1)} %fusion.3), channel_id=1, source_target_pairs={{0,2},{2,0},{1,3},{3,1},{4,6},{6,4},{5,7},{7,5},{8,10},{10,8},{9,1... | collective-permute-start | bytes 98312 | tf_op jit(solution)/shard_map/ppermute | solution.py:415

commit v15 on v14

--- a/solution.py
+++ b/solution.py
@@ -21,6 +21,7 @@
 SPREAD_STEPS = 4
 VMEM_LIMIT = 40 * 1024 * 1024
 LEAD_FLOPS = 1 << 32
+LATE_WEIGHT = 8
 
 
 def with_halo(cells, sides, width):
@@ -314,14 +315,14 @@
         "begin_pairs",
         [like(grams.shape, jnp.float32)],
         GROUPS,
-        16 * pair_flops(LATE_PAIRS, blocks),
+        pair_flops(LATE_PAIRS, blocks) // CHUNKS,
     )(own[0], middle[0], next_to[0], last[0])
     return local_call(
         late_kernel,
         "late_pairs",
         [like((2, n, *shape[2:]), jnp.float32) for n in LATE_GROUPS for _ in range(2)],
         GROUPS + 1,
-        16 * pair_flops(LATE_PAIRS, blocks),
+        LATE_WEIGHT * pair_flops(LATE_PAIRS, blocks) // CHUNKS,
         [grams],
     )(own[1], middle[1], next_to[1], last[1], *begun)
 

time: 73 us -> 69 us (0.945)
  the two profiles are of different devices: /device:TPU:0 before, /device:TPU:8 now
where the time goes in v15:
time: 69 us; the launch traced here: 68.8 us
  waiting for transfers between devices  40.8 us (59%)
  starting transfers between devices  19.6 us (28%)
  Pallas kernels  5.31 us (8%)
  local copies, waits for them, and re-layouts  2.88 us (4%)
    ppermute x6, waiting for transfers between devices, fetch(): return [lax.ppermute(piece, 'ao', swap) for piece in blocks[s]]  29.5 us
    ppermute x6, starting transfers between devices, fetch(): return [lax.ppermute(piece, 'ao', swap) for piece in blocks[s]]  7.09 us
    ppermute x2, starting transfers between devices, six_pair_body(): inner = [lax.ppermute(part, 'ao', INSIDE) for part in (parts[0], mine)]  6.11 us
    ppermute x2, waiting for transfers between devices, six_pair_body(): outer = [lax.ppermute(part, 'ao', OUTSIDE) for part in parts]  4.39 us
    ppermute x2, waiting for transfers between devices, six_pair_body(): far1 = lax.ppermute((near1[1] + got1[1]).astype(jnp.bfloat16), 'aux', SWAP)  3.38 us
    ppermute x2, waiting for transfers between devices, six_pair_body(): inner = [lax.ppermute(part, 'ao', INSIDE) for part in (parts[0], mine)]  2.71 us
    ppermute x2, starting transfers between devices, six_pair_body(): far1 = lax.ppermute((near1[1] + got1[1]).astype(jnp.bfloat16), 'aux', SWAP)  2.16 us
    ppermute x1, starting transfers between devices, six_pair_body(): swapped = lax.ppermute(inner[1], 'aux', SWAP)  1.56 us
  transfers between devices with their start and end apart: 17, of which 11 were waited for; matrix products, arithmetic and copies ran while one was open for 3% of the time, Pallas kernels for 6%

profile of v15, /device:TPU:8, one launch (start us, length us, event | category | flops | bytes accessed | tf_op | source)
XLA Modules:
  0.0 68.8 jit_solution(14688017103246254855)
XLA Ops:
  0.0 1.0 %slice.24.own = bf16[512,256]{1,0:T(8,128)(2,1)S(1)} slice(bf16[512,512]{1,0:T(8,128)(2,1)} %param.6), slice={[0:512], [0:256]} | slice | bytes 524288 | tf_op jit(solution)/shard_map/slice | solution.py:385
  1.0 3.7 %collective-permute-start.2 = (bf16[512,256]{1,0:T(8,128)(2,1)S(1)}, bf16[512,256]{1,0:T(8,128)(2,1)S(1)}, u32[]{:S(2)}, u32[]{:S(2)}) collective-permute-start(bf16[512,256]{1,0:T(8,128)(2,1)S(1)} %slice.24.own), channel_id=1, source_target_pairs={{4,8},{8,4},{5,9},{9,5},{6,10},{10,6},{7,11},{11,7},{20,24},{24,20... | collective-permute-start | bytes 786440 | tf_op jit(solution)/shard_map/ppermute | solution.py:389
  4.9 0.9 %constant_dynamic-slice_fusion = bf16[512,128]{1,0:T(8,128)(2,1)S(1)} fusion(bf16[512,512]{1,0:T(8,128)(2,1)} %param.6, s32[]{:T(128)S(6)} %select_n.3), kind=kLoop, calls=%fused_computation.7 | loop fusion | bytes 262148 | tf_op jit(solution)/shard_map/dynamic_slice | solution.py:388
  5.8 2.4 %collective-permute-start = (bf16[512,128]{1,0:T(8,128)(2,1)S(1)}, bf16[512,128]{1,0:T(8,128)(2,1)S(1)}, u32[]{:S(2)}, u32[]{:S(2)}) collective-permute-start(bf16[512,128]{1,0:T(8,128)(2,1)S(1)} %constant_dynamic-slice_fusion), channel_id=1, source_target_pairs={{4,8},{8,4},{5,9},{9,5},{6,10},{10,6},{7,11},{11,7},{20,24},{24,20... | collective-permute-start | bytes 393224 | tf_op jit(solution)/shard_map/ppermute | solution.py:389
  8.1 1.0 %slice.25.own = bf16[512,256]{1,0:T(8,128)(2,1)S(1)} slice(bf16[512,512]{1,0:T(8,128)(2,1)} %param.6), slice={[0:512], [256:512]} | slice | bytes 524288 | tf_op jit(solution)/shard_map/slice | solution.py:387
  9.7 2.7 %collective-permute-done.2.inner = bf16[512,256]{1,0:T(8,128)(2,1)S(1)} collective-permute-done((bf16[512,256]{1,0:T(8,128)(2,1)S(1)}, bf16[512,256]{1,0:T(8,128)(2,1)S(1)}, u32[]{:S(2)}, u32[]{:S(2)}) %collective-permute-start.2) | collective-permute-done | bytes 262176 | tf_op jit(solution)/shard_map/ppermute | solution.py:389
  12.4 1.7 %collective-permute-done.1.outer = bf16[512,256]{1,0:T(8,128)(2,1)S(1)} collective-permute-done((bf16[512,256]{1,0:T(8,128)(2,1)S(1)}, bf16[512,256]{1,0:T(8,128)(2,1)S(1)}, u32[]{:S(2)}, u32[]{:S(2)}) %collective-permute-start.1) | collective-permute-done | bytes 262176 | tf_op jit(solution)/shard_map/ppermute | solution.py:390
  15.0 1.6 %collective-permute-start.4 = (bf16[512,128]{1,0:T(8,128)(2,1)S(1)}, bf16[512,128]{1,0:T(8,128)(2,1)S(1)}, u32[]{:S(2)}, u32[]{:S(2)}) collective-permute-start(bf16[512,128]{1,0:T(8,128)(2,1)S(1)} %collective-permute-done.inner), channel_id=1, source_target_pairs={{0,2},{2,0},{1,3},{3,1},{4,6},{6,4},{5,7},{7,5},{8,10},{10,8},{9,1... | collective-permute-start | bytes 393224 | tf_op jit(solution)/shard_map/ppermute | solution.py:396
  16.6 1.3 %collective-permute-start.7 = (bf16[2,256,256]{2,1,0:T(8,128)(2,1)S(1)}, bf16[2,256,256]{2,1,0:T(8,128)(2,1)S(1)}, u32[]{:S(2)}, u32[]{:S(2)}) collective-permute-start(bf16[2,256,256]{2,1,0:T(8,128)(2,1)S(1)} %get-tuple-element.32), channel_id=1, source_target_pairs={{0,4},{4,0},{8,12},{12,8},{1,5},{5,1},{9,13},{13,9},{2,6},{6,2},{1... | collective-permute-start | bytes 786440 | tf_op jit(solution)/shard_map/ppermute | solution.py:405
  17.8 2.7 %collective-permute-done.3.outer = bf16[512,256]{1,0:T(8,128)(2,1)S(1)} collective-permute-done((bf16[512,256]{1,0:T(8,128)(2,1)S(1)}, bf16[512,256]{1,0:T(8,128)(2,1)S(1)}, u32[]{:S(2)}, u32[]{:S(2)}) %collective-permute-start.3) | collective-permute-done | bytes 262176 | tf_op jit(solution)/shard_map/ppermute | solution.py:390
  20.5 0.9 %transform.3 = (bf16[2,256,256]{2,1,0:T(8,128)(2,1)S(1)}, bf16[2,256,256]{2,1,0:T(8,128)(2,1)S(1)}, bf16[2,256,256]{2,1,0:T(8,128)(2,1)S(1)}, bf16[2,256,256]{2,1,0:T(8,128)(2,1)S(1)}) custom-call(s32[8,256]{1,0:T(8,128)S(1)} %tables.1.wants, bf16[2,512,1280]{2,1,0:T(8,128)(2,1)S(1)} %copy-done, bf16[512,256]{1,0:T(8,128)(2,1)S(1)} %slice.25.own, ...), custom_call_target="tpu_custom_call" | custom-call | flops 671088640 | bytes 2097152 | tf_op jit(solution)/shard_map/transform/pallas_call | solution.py:186
  21.5 3.1 %collective-permute-start.6 = (bf16[2,256,256]{2,1,0:T(8,128)(2,1)S(1)}, bf16[2,256,256]{2,1,0:T(8,128)(2,1)S(1)}, u32[]{:S(2)}, u32[]{:S(2)}) collective-permute-start(bf16[2,256,256]{2,1,0:T(8,128)(2,1)S(1)} %get-tuple-element.31), channel_id=1, source_target_pairs={{0,8},{4,12},{8,0},{12,4},{1,9},{5,13},{9,1},{13,5},{2,10},{6,14},... | collective-permute-start | bytes 786440 | tf_op jit(solution)/shard_map/ppermute | solution.py:405
  24.6 0.9 %collective-permute-start.12 = (bf16[2,256,256]{2,1,0:T(8,128)(2,1)S(1)}, bf16[2,256,256]{2,1,0:T(8,128)(2,1)S(1)}, u32[]{:S(2)}, u32[]{:S(2)}) collective-permute-start(bf16[2,256,256]{2,1,0:T(8,128)(2,1)S(1)} %get-tuple-element.38), channel_id=1, source_target_pairs={{0,12},{4,8},{8,4},{12,0},{1,13},{5,9},{9,5},{13,1},{2,14},{6,10},... | collective-permute-start | bytes 786440 | tf_op jit(solution)/shard_map/ppermute | solution.py:405
  25.6 1.7 %collective-permute-start.11 = (bf16[2,256,256]{2,1,0:T(8,128)(2,1)S(1)}, bf16[2,256,256]{2,1,0:T(8,128)(2,1)S(1)}, u32[]{:S(2)}, u32[]{:S(2)}) collective-permute-start(bf16[2,256,256]{2,1,0:T(8,128)(2,1)S(1)} %get-tuple-element.37), channel_id=1, source_target_pairs={{0,12},{4,8},{8,4},{12,0},{1,13},{5,9},{9,5},{13,1},{2,14},{6,10},... | collective-permute-start | bytes 786440 | tf_op jit(solution)/shard_map/ppermute | solution.py:405
  27.4 4.4 %collective-permute-done.7.refs_4_.next_to = bf16[2,256,256]{2,1,0:T(8,128)(2,1)S(1)} collective-permute-done((bf16[2,256,256]{2,1,0:T(8,128)(2,1)S(1)}, bf16[2,256,256]{2,1,0:T(8,128)(2,1)S(1)}, u32[]{:S(2)}, u32[]{:S(2)}) %collective-permute-start.7) | collective-permute-done | bytes 262176 | tf_op jit(solution)/shard_map/ppermute | solution.py:405
  31.7 5.2 %collective-permute-done.6.refs_3_.middle = bf16[2,256,256]{2,1,0:T(8,128)(2,1)S(1)} collective-permute-done((bf16[2,256,256]{2,1,0:T(8,128)(2,1)S(1)}, bf16[2,256,256]{2,1,0:T(8,128)(2,1)S(1)}, u32[]{:S(2)}, u32[]{:S(2)}) %collective-permute-start.6) | collective-permute-done | bytes 262176 | tf_op jit(solution)/shard_map/ppermute | solution.py:405
  37.0 5.3 %collective-permute-done.8.refs_5_.next_to = bf16[2,256,256]{2,1,0:T(8,128)(2,1)S(1)} collective-permute-done((bf16[2,256,256]{2,1,0:T(8,128)(2,1)S(1)}, bf16[2,256,256]{2,1,0:T(8,128)(2,1)S(1)}, u32[]{:S(2)}, u32[]{:S(2)}) %collective-permute-start.8) | collective-permute-done | bytes 262176 | tf_op jit(solution)/shard_map/ppermute | solution.py:405
  42.2 1.0 %early_pairs.1 = (f32[2,3,64,256]{3,2,1,0:T(8,128)S(1)}, bf16[2,3,64,256]{3,2,1,0:T(8,128)(2,1)S(1)}, s32[16,256]{1,0:T(8,128)S(1)}) custom-call(s32[1,4]{1,0:T(1,128)S(1)} %bitcast.11, s32[2,64]{1,0:T(2,128)S(1)} %bitcast.10, bf16[2,256,256]{2,1,0:T(8,128)(2,1)S(1)} %get-tuple-element.27.refs_0_.own, ...), custom_call_target="tpu_custom_call" | custom-call | flops 402653184 | bytes 1212416 | tf_op jit(solution)/shard_map/early_pairs/pallas_call | solution.py:296
  43.2 1.6 %collective-permute-start.9 = (bf16[2,3,64,256]{3,2,1,0:T(8,128)(2,1)S(1)}, bf16[2,3,64,256]{3,2,1,0:T(8,128)(2,1)S(1)}, u32[]{:S(2)}, u32[]{:S(2)}) collective-permute-start(bf16[2,3,64,256]{3,2,1,0:T(8,128)(2,1)S(1)} %get-tuple-element.36), channel_id=1, source_target_pairs={{0,2},{2,0},{1,3},{3,1},{4,6},{6,4},{5,7},{7,5},{8,10},{10,8},{9,1... | collective-permute-start | bytes 589832 | tf_op jit(solution)/shard_map/ppermute | solution.py:410
  44.8 11.1 %collective-permute-done.12.last = bf16[2,256,256]{2,1,0:T(8,128)(2,1)S(1)} collective-permute-done((bf16[2,256,256]{2,1,0:T(8,128)(2,1)S(1)}, bf16[2,256,256]{2,1,0:T(8,128)(2,1)S(1)}, u32[]{:S(2)}, u32[]{:S(2)}) %collective-permute-start.12) | collective-permute-done | bytes 262176 | tf_op jit(solution)/shard_map/ppermute | solution.py:405
  56.5 3.3 %collective-permute-done.11.last = bf16[2,256,256]{2,1,0:T(8,128)(2,1)S(1)} collective-permute-done((bf16[2,256,256]{2,1,0:T(8,128)(2,1)S(1)}, bf16[2,256,256]{2,1,0:T(8,128)(2,1)S(1)}, u32[]{:S(2)}, u32[]{:S(2)}) %collective-permute-start.11) | collective-permute-done | bytes 262176 | tf_op jit(solution)/shard_map/ppermute | solution.py:405
  62.1 1.6 %collective-permute-start.14 = (bf16[2,64,256]{2,1,0:T(8,128)(2,1)S(1)}, bf16[2,64,256]{2,1,0:T(8,128)(2,1)S(1)}, u32[]{:S(2)}, u32[]{:S(2)}) collective-permute-start(bf16[2,64,256]{2,1,0:T(8,128)(2,1)S(1)} %fusion.1), channel_id=1, source_target_pairs={{0,2},{2,0},{1,3},{3,1},{4,6},{6,4},{5,7},{7,5},{8,10},{10,8},{9,1... | collective-permute-start | bytes 196616 | tf_op jit(solution)/shard_map/ppermute | solution.py:416
  64.3 3.4 %collective-permute-done.16.refs_5_ = bf16[1,64,256]{2,1,0:T(8,128)(2,1)S(1)} collective-permute-done((bf16[1,64,256]{2,1,0:T(8,128)(2,1)S(1)}, bf16[1,64,256]{2,1,0:T(8,128)(2,1)S(1)}, u32[]{:S(2)}, u32[]{:S(2)}) %collective-permute-start.16) | collective-permute-done | bytes 32800 | tf_op jit(solution)/shard_map/ppermute | solution.py:416
  67.7 1.1 %spread.1 = f32[64,16,256]{2,1,0:T(8,128)} custom-call(s32[16,256]{1,0:T(8,128)S(1)} %get-tuple-element.34.place, f32[2,3,64,256]{3,2,1,0:T(8,128)S(1)} %get-tuple-element.35.near, bf16[2,3,64,256]{3,2,1,0:T(8,128)(2,1)S(1)} %collective-permute-done.9.far, f32[3,64,256]{2,1,0:T(8,128)S(1)} %collective-permute-done.10.got, ...), custom_call_target="tpu_custom_call" | custom-call | flops 1572864 | bytes 2097152 | tf_op jit(solution)/shard_map/spread/pallas_call | solution.py:364
  (32 shorter events, 5.2 us)
Async XLA Ops:
  1.0 8.5 %copy-start.1 = (s32[64,2]{0,1:T(2,128)S(1)}, s32[64,2]{0,1:T(2,128)}, u32[]{:S(2)}) copy-start(s32[64,2]{0,1:T(2,128)} %param.7) | copy-start | bytes 1540
  1.0 8.5 %copy-start.3 = (s32[8]{0:T(128)S(1)}, s32[8]{0:T(128)}, u32[]{:S(2)}) copy-start(s32[8]{0:T(128)} %param.9) | copy-start | bytes 100
  1.0 13.1 %copy-start = (bf16[2,512,1280]{2,1,0:T(8,128)(2,1)S(1)}, bf16[2,512,1280]{2,1,0:T(8,128)(2,1)}, u32[]{:S(2)}) copy-start(bf16[2,512,1280]{2,1,0:T(8,128)(2,1)} %integrals.3) | copy-start | bytes 7864324
  1.0 11.3 %collective-permute-start.2 = (bf16[512,256]{1,0:T(8,128)(2,1)S(1)}, bf16[512,256]{1,0:T(8,128)(2,1)S(1)}, u32[]{:S(2)}, u32[]{:S(2)}) collective-permute-start(bf16[512,256]{1,0:T(8,128)(2,1)S(1)} %slice.24.own), channel_id=1, source_target_pairs={{4,8},{8,4},{5,9},{9,5},{6,10},{10,6},{7,11},{11,7},{20,24},{24,20... | collective-permute-start | bytes 786440 | tf_op jit(solution)/shard_map/ppermute | solution.py:389
  4.8 9.3 %collective-permute-start.1 = (bf16[512,256]{1,0:T(8,128)(2,1)S(1)}, bf16[512,256]{1,0:T(8,128)(2,1)S(1)}, u32[]{:S(2)}, u32[]{:S(2)}) collective-permute-start(bf16[512,256]{1,0:T(8,128)(2,1)S(1)} %slice.24.own), channel_id=1, source_target_pairs={{0,4},{4,0},{8,12},{12,8},{1,5},{5,1},{9,13},{13,9},{2,6},{6,2},{1... | collective-permute-start | bytes 786440 | tf_op jit(solution)/shard_map/ppermute | solution.py:390
  5.8 9.2 %collective-permute-start = (bf16[512,128]{1,0:T(8,128)(2,1)S(1)}, bf16[512,128]{1,0:T(8,128)(2,1)S(1)}, u32[]{:S(2)}, u32[]{:S(2)}) collective-permute-start(bf16[512,128]{1,0:T(8,128)(2,1)S(1)} %constant_dynamic-slice_fusion), channel_id=1, source_target_pairs={{4,8},{8,4},{5,9},{9,5},{6,10},{10,6},{7,11},{11,7},{20,24},{24,20... | collective-permute-start | bytes 393224 | tf_op jit(solution)/shard_map/ppermute | solution.py:389
  9.1 11.4 %collective-permute-start.3 = (bf16[512,256]{1,0:T(8,128)(2,1)S(1)}, bf16[512,256]{1,0:T(8,128)(2,1)S(1)}, u32[]{:S(2)}, u32[]{:S(2)}) collective-permute-start(bf16[512,256]{1,0:T(8,128)(2,1)S(1)} %slice.25.own), channel_id=1, source_target_pairs={{0,4},{4,0},{8,12},{12,8},{1,5},{5,1},{9,13},{13,9},{2,6},{6,2},{1... | collective-permute-start | bytes 786440 | tf_op jit(solution)/shard_map/ppermute | solution.py:390
  9.6 32.6 %copy-start.2 = (s32[4]{0:T(128)S(1)}, s32[4]{0:T(128)}, u32[]{:S(2)}) copy-start(s32[4]{0:T(128)} %param.8) | copy-start | bytes 52
  14.9 10.7 %collective-permute-start.5 = (bf16[2,256,256]{2,1,0:T(8,128)(2,1)S(1)}, bf16[2,256,256]{2,1,0:T(8,128)(2,1)S(1)}, u32[]{:S(2)}, u32[]{:S(2)}) collective-permute-start(bf16[2,256,256]{2,1,0:T(8,128)(2,1)S(1)} %get-tuple-element.30), channel_id=1, source_target_pairs={{0,8},{4,12},{8,0},{12,4},{1,9},{5,13},{9,1},{13,5},{2,10},{6,14},... | collective-permute-start | bytes 786440 | tf_op jit(solution)/shard_map/ppermute | solution.py:405
  15.0 5.5 %collective-permute-start.4 = (bf16[512,128]{1,0:T(8,128)(2,1)S(1)}, bf16[512,128]{1,0:T(8,128)(2,1)S(1)}, u32[]{:S(2)}, u32[]{:S(2)}) collective-permute-start(bf16[512,128]{1,0:T(8,128)(2,1)S(1)} %collective-permute-done.inner), channel_id=1, source_target_pairs={{0,2},{2,0},{1,3},{3,1},{4,6},{6,4},{5,7},{7,5},{8,10},{10,8},{9,1... | collective-permute-start | bytes 393224 | tf_op jit(solution)/shard_map/ppermute | solution.py:396
  16.6 15.2 %collective-permute-start.7 = (bf16[2,256,256]{2,1,0:T(8,128)(2,1)S(1)}, bf16[2,256,256]{2,1,0:T(8,128)(2,1)S(1)}, u32[]{:S(2)}, u32[]{:S(2)}) collective-permute-start(bf16[2,256,256]{2,1,0:T(8,128)(2,1)S(1)} %get-tuple-element.32), channel_id=1, source_target_pairs={{0,4},{4,0},{8,12},{12,8},{1,5},{5,1},{9,13},{13,9},{2,6},{6,2},{1... | collective-permute-start | bytes 786440 | tf_op jit(solution)/shard_map/ppermute | solution.py:405
  21.5 15.5 %collective-permute-start.6 = (bf16[2,256,256]{2,1,0:T(8,128)(2,1)S(1)}, bf16[2,256,256]{2,1,0:T(8,128)(2,1)S(1)}, u32[]{:S(2)}, u32[]{:S(2)}) collective-permute-start(bf16[2,256,256]{2,1,0:T(8,128)(2,1)S(1)} %get-tuple-element.31), channel_id=1, source_target_pairs={{0,8},{4,12},{8,0},{12,4},{1,9},{5,13},{9,1},{13,5},{2,10},{6,14},... | collective-permute-start | bytes 786440 | tf_op jit(solution)/shard_map/ppermute | solution.py:405
  24.6 17.6 %collective-permute-start.8 = (bf16[2,256,256]{2,1,0:T(8,128)(2,1)S(1)}, bf16[2,256,256]{2,1,0:T(8,128)(2,1)S(1)}, u32[]{:S(2)}, u32[]{:S(2)}) collective-permute-start(bf16[2,256,256]{2,1,0:T(8,128)(2,1)S(1)} %get-tuple-element.33), channel_id=1, source_target_pairs={{0,4},{4,0},{8,12},{12,8},{1,5},{5,1},{9,13},{13,9},{2,6},{6,2},{1... | collective-permute-start | bytes 786440 | tf_op jit(solution)/shard_map/ppermute | solution.py:405
  24.6 31.3 %collective-permute-start.12 = (bf16[2,256,256]{2,1,0:T(8,128)(2,1)S(1)}, bf16[2,256,256]{2,1,0:T(8,128)(2,1)S(1)}, u32[]{:S(2)}, u32[]{:S(2)}) collective-permute-start(bf16[2,256,256]{2,1,0:T(8,128)(2,1)S(1)} %get-tuple-element.38), channel_id=1, source_target_pairs={{0,12},{4,8},{8,4},{12,0},{1,13},{5,9},{9,5},{13,1},{2,14},{6,10},... | collective-permute-start | bytes 786440 | tf_op jit(solution)/shard_map/ppermute | solution.py:405
  25.6 34.2 %collective-permute-start.11 = (bf16[2,256,256]{2,1,0:T(8,128)(2,1)S(1)}, bf16[2,256,256]{2,1,0:T(8,128)(2,1)S(1)}, u32[]{:S(2)}, u32[]{:S(2)}) collective-permute-start(bf16[2,256,256]{2,1,0:T(8,128)(2,1)S(1)} %get-tuple-element.37), channel_id=1, source_target_pairs={{0,12},{4,8},{8,4},{12,0},{1,13},{5,9},{9,5},{13,1},{2,14},{6,10},... | collective-permute-start | bytes 786440 | tf_op jit(solution)/shard_map/ppermute | solution.py:405
  43.2 17.8 %collective-permute-start.9 = (bf16[2,3,64,256]{3,2,1,0:T(8,128)(2,1)S(1)}, bf16[2,3,64,256]{3,2,1,0:T(8,128)(2,1)S(1)}, u32[]{:S(2)}, u32[]{:S(2)}) collective-permute-start(bf16[2,3,64,256]{3,2,1,0:T(8,128)(2,1)S(1)} %get-tuple-element.36), channel_id=1, source_target_pairs={{0,2},{2,0},{1,3},{3,1},{4,6},{6,4},{5,7},{7,5},{8,10},{10,8},{9,1... | collective-permute-start | bytes 589832 | tf_op jit(solution)/shard_map/ppermute | solution.py:410
  60.5 1.6 %collective-permute-start.13 = (f32[2,2,64,256]{3,2,1,0:T(8,128)S(1)}, f32[2,2,64,256]{3,2,1,0:T(8,128)S(1)}, u32[]{:S(2)}, u32[]{:S(2)}) collective-permute-start(f32[2,2,64,256]{3,2,1,0:T(8,128)S(1)} %get-tuple-element.40), channel_id=1, source_target_pairs={{0,1},{1,0},{2,3},{3,2},{4,5},{5,4},{6,7},{7,6},{8,9},{9,8},{10,11... | collective-permute-start | bytes 786440 | tf_op jit(solution)/shard_map/ppermute | solution.py:415
  60.6 3.1 %collective-permute-start.15 = (f32[2,1,64,256]{3,2,1,0:T(8,128)S(1)}, f32[2,1,64,256]{3,2,1,0:T(8,128)S(1)}, u32[]{:S(2)}, u32[]{:S(2)}) collective-permute-start(f32[2,1,64,256]{3,2,1,0:T(8,128)S(1)} %get-tuple-element.42), channel_id=1, source_target_pairs={{0,1},{1,0},{2,3},{3,2},{4,5},{5,4},{6,7},{7,6},{8,9},{9,8},{10,11... | collective-permute-start | bytes 393224 | tf_op jit(solution)/shard_map/ppermute | solution.py:415
  61.1 6.6 %collective-permute-start.10 = (f32[3,64,256]{2,1,0:T(8,128)S(1)}, f32[3,64,256]{2,1,0:T(8,128)S(1)}, u32[]{:S(2)}, u32[]{:S(2)}) collective-permute-start(f32[3,64,256]{2,1,0:T(8,128)S(1)} %add_bitcast_fusion), channel_id=1, source_target_pairs={{0,1},{1,0},{2,3},{3,2},{4,5},{5,4},{6,7},{7,6},{8,9},{9,8},{10,11... | collective-permute-start | bytes 589832 | tf_op jit(solution)/shard_map/ppermute | solution.py:418
  62.1 5.6 %collective-permute-start.14 = (bf16[2,64,256]{2,1,0:T(8,128)(2,1)S(1)}, bf16[2,64,256]{2,1,0:T(8,128)(2,1)S(1)}, u32[]{:S(2)}, u32[]{:S(2)}) collective-permute-start(bf16[2,64,256]{2,1,0:T(8,128)(2,1)S(1)} %fusion.1), channel_id=1, source_target_pairs={{0,2},{2,0},{1,3},{3,1},{4,6},{6,4},{5,7},{7,5},{8,10},{10,8},{9,1... | collective-permute-start | bytes 196616 | tf_op jit(solution)/shard_map/ppermute | solution.py:416
  63.7 4.0 %collective-permute-start.16 = (bf16[1,64,256]{2,1,0:T(8,128)(2,1)S(1)}, bf16[1,64,256]{2,1,0:T(8,128)(2,1)S(1)}, u32[]{:S(2)}, u32[]{:S(2)}) collective-permute-start(bf16[1,64,256]{2,1,0:T(8,128)(2,1)S(1)} %fusion.3), channel_id=1, source_target_pairs={{0,2},{2,0},{1,3},{3,1},{4,6},{6,4},{5,7},{7,5},{8,10},{10,8},{9,1... | collective-permute-start | bytes 98312 | tf_op jit(solution)/shard_map/ppermute | solution.py:416

commit v16 on v13

--- a/solution.py
+++ b/solution.py
@@ -21,6 +21,7 @@
 SPREAD_STEPS = 4
 VMEM_LIMIT = 40 * 1024 * 1024
 LEAD_FLOPS = 1 << 32
+LATE_WEIGHT = 10
 CUT_LIMIT = 53 * 1024 * 1024 + 256 * 1024
 
 
@@ -297,7 +298,7 @@
         for chip in (0, 1):
             row = 2 * (aux ^ chip)
             keep[chip, k] = grams[k, row + orb]
-            give[chip, k] = grams[k, row + 1 - orb]
+            give[chip, k] = grams[k, row + 1 - orb].astype(jnp.bfloat16)
 
 
 def pair_flops(pairs, blocks):
@@ -338,9 +339,9 @@
     return local_call(
         late_kernel,
         "late_pairs",
-        [like(shape, jnp.float32)] * 2,
+        [like(shape, jnp.float32), like(shape, jnp.bfloat16)],
         GROUPS + 1,
-        pair_flops(LATE_PAIRS, blocks) // CHUNKS,
+        LATE_WEIGHT * pair_flops(LATE_PAIRS, blocks) // CHUNKS,
         [grams],
     )(own[1], middle[1], next_to[1], last[1], *begun)
 
@@ -348,7 +349,7 @@
 def spread_kernel(factor, place, near0, far0, got0, near1, got1, far1, out, sums, rows, sems):
     early = near0.shape[1]
     sums[:early] = (near0[0] + far0[0].astype(jnp.float32) + got0[...]) * factor
-    sums[early:] = (near1[0] + got1[0] + far1[...].astype(jnp.float32)) * factor
+    sums[early:] = (near1[0] + got1[0].astype(jnp.float32) + far1[...].astype(jnp.float32)) * factor
     total, slots, width = out.shape
     masks = [place[...] == k for k in range(sums.shape[0])]
 
@@ -420,7 +421,7 @@
     got.append(fetch(3))
     near1, give1 = late_pairs(got)
     got1 = lax.ppermute(give1, "orb", SWAP)
-    far1 = lax.ppermute((near1[1] + got1[1]).astype(jnp.bfloat16), "aux", SWAP)
+    far1 = lax.ppermute((near1[1] + got1[1].astype(jnp.float32)).astype(jnp.bfloat16), "aux", SWAP)
     got0 = lax.ppermute(near0[1] + far0[1].astype(jnp.float32), "orb", SWAP)
     factor = 1.0 / math.sqrt(total_aux * ORBS)
     return spread(factor, place, near0, far0, got0, near1, got1, far1)

time: 68.4 us -> 68.2 us (level)
  no operation moved by 1% of the time
where the time goes in v16:
time: 68.2 us; the launch traced here: 68 us
  waiting for transfers between devices  42.1 us (62%)
  starting transfers between devices  19.2 us (28%)
  Pallas kernels  6.46 us (9%)
    ppermute x6, waiting for transfers between devices, fetch(): return [lax.ppermute(piece, 'ao', swap) for piece in blocks[s]]  29.5 us
    ppermute x6, starting transfers between devices, fetch(): return [lax.ppermute(piece, 'ao', swap) for piece in blocks[s]]  7.62 us
    ppermute x2, starting transfers between devices, six_pair_body(): inner = [lax.ppermute(part, 'ao', INSIDE) for part in (parts[0], mine)]  5.84 us
    ppermute x2, waiting for transfers between devices, six_pair_body(): inner = [lax.ppermute(part, 'ao', INSIDE) for part in (parts[0], mine)]  4.61 us
    ppermute x2, waiting for transfers between devices, six_pair_body(): outer = [lax.ppermute(part, 'ao', OUTSIDE) for part in parts]  3.8 us
    ppermute x1, waiting for transfers between devices, six_pair_body(): lax.ppermute((near1[1] + got1[1].astype(jnp.float32)).astype(jnp.bfloat16...  3.35 us
    ppermute x1, starting transfers between devices, six_pair_body(): swapped = lax.ppermute(inner[1], 'aux', SWAP)  1.56 us
    ppermute x1, starting transfers between devices, six_pair_body(): far0 = lax.ppermute(across0, 'aux', SWAP)  1.55 us
  transfers between devices with their start and end apart: 15, of which 11 were waited for; matrix products, arithmetic and copies ran while one was open for 0% of the time, Pallas kernels for 6%

profile of v16, /device:TPU:8, one launch (start us, length us, event | category | flops | bytes accessed | tf_op | source)
XLA Modules:
  0.0 68.0 jit_solution(4925378145051470424)
XLA Ops:
  0.0 1.1 %cut.1 = (bf16[512,256]{1,0:T(8,128)(2,1)S(1)}, bf16[512,256]{1,0:T(8,128)(2,1)S(1)}, bf16[512,128]{1,0:T(8,128)(2,1)S(1)}) custom-call(bf16[512,512]{1,0:T(8,128)(2,1)} %coeffs.1), custom_call_target="tpu_custom_call" | custom-call | flops 4294967296 | tf_op jit(solution)/shard_map/cut/pallas_call | solution.py:135
  1.2 3.5 %collective-permute-start.2 = (bf16[512,256]{1,0:T(8,128)(2,1)S(1)}, bf16[512,256]{1,0:T(8,128)(2,1)S(1)}, u32[]{:S(2)}, u32[]{:S(2)}) collective-permute-start(bf16[512,256]{1,0:T(8,128)(2,1)S(1)} %get-tuple-element.24.own), channel_id=1, source_target_pairs={{4,8},{8,4},{5,9},{9,5},{6,10},{10,6},{7,11},{11,7},{20,24},{24,20... | collective-permute-start | bytes 786440 | tf_op jit(solution)/shard_map/ppermute | solution.py:399
  4.7 2.4 %collective-permute-start = (bf16[512,128]{1,0:T(8,128)(2,1)S(1)}, bf16[512,128]{1,0:T(8,128)(2,1)S(1)}, u32[]{:S(2)}, u32[]{:S(2)}) collective-permute-start(bf16[512,128]{1,0:T(8,128)(2,1)S(1)} %get-tuple-element.23), channel_id=1, source_target_pairs={{4,8},{8,4},{5,9},{9,5},{6,10},{10,6},{7,11},{11,7},{20,24},{24,20... | collective-permute-start | bytes 393224 | tf_op jit(solution)/shard_map/ppermute | solution.py:399
  7.6 4.6 %collective-permute-done.2.inner = bf16[512,256]{1,0:T(8,128)(2,1)S(1)} collective-permute-done((bf16[512,256]{1,0:T(8,128)(2,1)S(1)}, bf16[512,256]{1,0:T(8,128)(2,1)S(1)}, u32[]{:S(2)}, u32[]{:S(2)}) %collective-permute-start.2) | collective-permute-done | bytes 262176 | tf_op jit(solution)/shard_map/ppermute | solution.py:399
  12.2 1.7 %collective-permute-done.1.outer = bf16[512,256]{1,0:T(8,128)(2,1)S(1)} collective-permute-done((bf16[512,256]{1,0:T(8,128)(2,1)S(1)}, bf16[512,256]{1,0:T(8,128)(2,1)S(1)}, u32[]{:S(2)}, u32[]{:S(2)}) %collective-permute-start.1) | collective-permute-done | bytes 262176 | tf_op jit(solution)/shard_map/ppermute | solution.py:400
  14.0 0.9 %transform.2 = (bf16[2,256,256]{2,1,0:T(8,128)(2,1)S(1)}, bf16[2,256,256]{2,1,0:T(8,128)(2,1)S(1)}, bf16[2,256,256]{2,1,0:T(8,128)(2,1)S(1)}, bf16[2,256,256]{2,1,0:T(8,128)(2,1)S(1)}) custom-call(s32[8,256]{1,0:T(8,128)S(1)} %tables.1.wants, bf16[2,512,1280]{2,1,0:T(8,128)(2,1)S(1)} %copy-done, bf16[512,256]{1,0:T(8,128)(2,1)S(1)} %get-tuple-element.24.own, ...), custom_call_target="tpu_custom_call" | custom-call | flops 671088640 | bytes 2097152 | tf_op jit(solution)/shard_map/transform/pallas_call | solution.py:220
  14.9 1.6 %collective-permute-start.4 = (bf16[512,128]{1,0:T(8,128)(2,1)S(1)}, bf16[512,128]{1,0:T(8,128)(2,1)S(1)}, u32[]{:S(2)}, u32[]{:S(2)}) collective-permute-start(bf16[512,128]{1,0:T(8,128)(2,1)S(1)} %collective-permute-done.inner), channel_id=1, source_target_pairs={{0,2},{2,0},{1,3},{3,1},{4,6},{6,4},{5,7},{7,5},{8,10},{10,8},{9,1... | collective-permute-start | bytes 393224 | tf_op jit(solution)/shard_map/ppermute | solution.py:406
  16.5 1.8 %collective-permute-start.7 = (bf16[2,256,256]{2,1,0:T(8,128)(2,1)S(1)}, bf16[2,256,256]{2,1,0:T(8,128)(2,1)S(1)}, u32[]{:S(2)}, u32[]{:S(2)}) collective-permute-start(bf16[2,256,256]{2,1,0:T(8,128)(2,1)S(1)} %get-tuple-element.32), channel_id=1, source_target_pairs={{0,4},{4,0},{8,12},{12,8},{1,5},{5,1},{9,13},{13,9},{2,6},{6,2},{1... | collective-permute-start | bytes 786440 | tf_op jit(solution)/shard_map/ppermute | solution.py:415
  18.3 2.1 %collective-permute-done.3.outer = bf16[512,256]{1,0:T(8,128)(2,1)S(1)} collective-permute-done((bf16[512,256]{1,0:T(8,128)(2,1)S(1)}, bf16[512,256]{1,0:T(8,128)(2,1)S(1)}, u32[]{:S(2)}, u32[]{:S(2)}) %collective-permute-start.3) | collective-permute-done | bytes 262176 | tf_op jit(solution)/shard_map/ppermute | solution.py:400
  20.4 0.9 %transform.3 = (bf16[2,256,256]{2,1,0:T(8,128)(2,1)S(1)}, bf16[2,256,256]{2,1,0:T(8,128)(2,1)S(1)}, bf16[2,256,256]{2,1,0:T(8,128)(2,1)S(1)}, bf16[2,256,256]{2,1,0:T(8,128)(2,1)S(1)}) custom-call(s32[8,256]{1,0:T(8,128)S(1)} %tables.1.wants, bf16[2,512,1280]{2,1,0:T(8,128)(2,1)S(1)} %copy-done, bf16[512,256]{1,0:T(8,128)(2,1)S(1)} %get-tuple-element.27.own, ...), custom_call_target="tpu_custom_call" | custom-call | flops 671088640 | bytes 2097152 | tf_op jit(solution)/shard_map/transform/pallas_call | solution.py:208
  21.3 3.2 %collective-permute-start.6 = (bf16[2,256,256]{2,1,0:T(8,128)(2,1)S(1)}, bf16[2,256,256]{2,1,0:T(8,128)(2,1)S(1)}, u32[]{:S(2)}, u32[]{:S(2)}) collective-permute-start(bf16[2,256,256]{2,1,0:T(8,128)(2,1)S(1)} %get-tuple-element.31), channel_id=1, source_target_pairs={{0,8},{4,12},{8,0},{12,4},{1,9},{5,13},{9,1},{13,5},{2,10},{6,14},... | collective-permute-start | bytes 786440 | tf_op jit(solution)/shard_map/ppermute | solution.py:415
  24.6 0.8 %collective-permute-start.12 = (bf16[2,256,256]{2,1,0:T(8,128)(2,1)S(1)}, bf16[2,256,256]{2,1,0:T(8,128)(2,1)S(1)}, u32[]{:S(2)}, u32[]{:S(2)}) collective-permute-start(bf16[2,256,256]{2,1,0:T(8,128)(2,1)S(1)} %get-tuple-element.38), channel_id=1, source_target_pairs={{0,12},{4,8},{8,4},{12,0},{1,13},{5,9},{9,5},{13,1},{2,14},{6,10},... | collective-permute-start | bytes 786440 | tf_op jit(solution)/shard_map/ppermute | solution.py:415
  25.6 1.7 %collective-permute-start.11 = (bf16[2,256,256]{2,1,0:T(8,128)(2,1)S(1)}, bf16[2,256,256]{2,1,0:T(8,128)(2,1)S(1)}, u32[]{:S(2)}, u32[]{:S(2)}) collective-permute-start(bf16[2,256,256]{2,1,0:T(8,128)(2,1)S(1)} %get-tuple-element.37), channel_id=1, source_target_pairs={{0,12},{4,8},{8,4},{12,0},{1,13},{5,9},{9,5},{13,1},{2,14},{6,10},... | collective-permute-start | bytes 786440 | tf_op jit(solution)/shard_map/ppermute | solution.py:415
  27.3 4.3 %collective-permute-done.7.refs_4_.next_to = bf16[2,256,256]{2,1,0:T(8,128)(2,1)S(1)} collective-permute-done((bf16[2,256,256]{2,1,0:T(8,128)(2,1)S(1)}, bf16[2,256,256]{2,1,0:T(8,128)(2,1)S(1)}, u32[]{:S(2)}, u32[]{:S(2)}) %collective-permute-start.7) | collective-permute-done | bytes 262176 | tf_op jit(solution)/shard_map/ppermute | solution.py:415
  31.6 5.3 %collective-permute-done.6.refs_3_.middle = bf16[2,256,256]{2,1,0:T(8,128)(2,1)S(1)} collective-permute-done((bf16[2,256,256]{2,1,0:T(8,128)(2,1)S(1)}, bf16[2,256,256]{2,1,0:T(8,128)(2,1)S(1)}, u32[]{:S(2)}, u32[]{:S(2)}) %collective-permute-start.6) | collective-permute-done | bytes 262176 | tf_op jit(solution)/shard_map/ppermute | solution.py:415
  36.9 5.2 %collective-permute-done.8.refs_5_.next_to = bf16[2,256,256]{2,1,0:T(8,128)(2,1)S(1)} collective-permute-done((bf16[2,256,256]{2,1,0:T(8,128)(2,1)S(1)}, bf16[2,256,256]{2,1,0:T(8,128)(2,1)S(1)}, u32[]{:S(2)}, u32[]{:S(2)}) %collective-permute-start.8) | collective-permute-done | bytes 262176 | tf_op jit(solution)/shard_map/ppermute | solution.py:415
  42.1 1.0 %early_pairs.1 = (f32[2,3,64,256]{3,2,1,0:T(8,128)S(1)}, bf16[2,3,64,256]{3,2,1,0:T(8,128)(2,1)S(1)}, s32[16,256]{1,0:T(8,128)S(1)}) custom-call(s32[1,4]{1,0:T(1,128)S(1)} %bitcast.9, s32[2,64]{1,0:T(2,128)S(1)} %bitcast.8, bf16[2,256,256]{2,1,0:T(8,128)(2,1)S(1)} %get-tuple-element.26.refs_0_.own, bf16[2,256,256]{2,1,0:T(8,128)(2,1)S(1)} %get-tuple-element.29.refs_1_.own, ...), custom_call_target="tpu_custom_call" | custom-call | flops 402653184 | bytes 1212416 | tf_op jit(solution)/shard_map/early_pairs/pallas_call | solution.py:315
  43.1 1.6 %collective-permute-start.9 = (bf16[2,3,64,256]{3,2,1,0:T(8,128)(2,1)S(1)}, bf16[2,3,64,256]{3,2,1,0:T(8,128)(2,1)S(1)}, u32[]{:S(2)}, u32[]{:S(2)}) collective-permute-start(bf16[2,3,64,256]{3,2,1,0:T(8,128)(2,1)S(1)} %get-tuple-element.36), channel_id=1, source_target_pairs={{0,2},{2,0},{1,3},{3,1},{4,6},{6,4},{5,7},{7,5},{8,10},{10,8},{9,1... | collective-permute-start | bytes 589832 | tf_op jit(solution)/shard_map/ppermute | solution.py:420
  44.7 11.2 %collective-permute-done.12.last = bf16[2,256,256]{2,1,0:T(8,128)(2,1)S(1)} collective-permute-done((bf16[2,256,256]{2,1,0:T(8,128)(2,1)S(1)}, bf16[2,256,256]{2,1,0:T(8,128)(2,1)S(1)}, u32[]{:S(2)}, u32[]{:S(2)}) %collective-permute-start.12) | collective-permute-done | bytes 262176 | tf_op jit(solution)/shard_map/ppermute | solution.py:415
  56.5 3.3 %collective-permute-done.11.last = bf16[2,256,256]{2,1,0:T(8,128)(2,1)S(1)} collective-permute-done((bf16[2,256,256]{2,1,0:T(8,128)(2,1)S(1)}, bf16[2,256,256]{2,1,0:T(8,128)(2,1)S(1)}, u32[]{:S(2)}, u32[]{:S(2)}) %collective-permute-start.11) | collective-permute-done | bytes 262176 | tf_op jit(solution)/shard_map/ppermute | solution.py:415
  61.1 0.8 %collective-permute-done.13.got1 = bf16[2,3,64,256]{3,2,1,0:T(8,128)(2,1)S(1)} collective-permute-done((bf16[2,3,64,256]{3,2,1,0:T(8,128)(2,1)S(1)}, bf16[2,3,64,256]{3,2,1,0:T(8,128)(2,1)S(1)}, u32[]{:S(2)}, u32[]{:S(2)}) %collective-permute-start.13) | collective-permute-done | bytes 196640 | tf_op jit(solution)/shard_map/ppermute | solution.py:423
  61.9 1.6 %collective-permute-start.14 = (bf16[3,64,256]{2,1,0:T(8,128)(2,1)S(1)}, bf16[3,64,256]{2,1,0:T(8,128)(2,1)S(1)}, u32[]{:S(2)}, u32[]{:S(2)}) collective-permute-start(bf16[3,64,256]{2,1,0:T(8,128)(2,1)S(1)} %fusion), channel_id=1, source_target_pairs={{0,2},{2,0},{1,3},{3,1},{4,6},{6,4},{5,7},{7,5},{8,10},{10,8},{9,1... | collective-permute-start | bytes 294920 | tf_op jit(solution)/shard_map/ppermute | solution.py:424
  63.5 3.4 %collective-permute-done.14.far1 = bf16[3,64,256]{2,1,0:T(8,128)(2,1)S(1)} collective-permute-done((bf16[3,64,256]{2,1,0:T(8,128)(2,1)S(1)}, bf16[3,64,256]{2,1,0:T(8,128)(2,1)S(1)}, u32[]{:S(2)}, u32[]{:S(2)}) %collective-permute-start.14) | collective-permute-done | bytes 98336 | tf_op jit(solution)/shard_map/ppermute | solution.py:424
  66.8 1.2 %spread.1 = f32[64,16,256]{2,1,0:T(8,128)} custom-call(s32[16,256]{1,0:T(8,128)S(1)} %get-tuple-element.34.place, f32[2,3,64,256]{3,2,1,0:T(8,128)S(1)} %get-tuple-element.35.near0, bf16[2,3,64,256]{3,2,1,0:T(8,128)(2,1)S(1)} %collective-permute-done.9.far0, f32[3,64,256]{2,1,0:T(8,128)S(1)} %collective-permute-done.10.got0, ...), custom_call_target="tpu_custom_call" | custom-call | flops 1572864 | bytes 2097152 | tf_op jit(solution)/shard_map/spread/pallas_call | solution.py:378
  (24 shorter events, 2.9 us)
Async XLA Ops:
  0.0 7.5 %copy-start.3 = (s32[8]{0:T(128)S(1)}, s32[8]{0:T(128)}, u32[]{:S(2)}) copy-start(s32[8]{0:T(128)} %param.9) | copy-start | bytes 100
  0.0 7.5 %copy-start.1 = (s32[64,2]{0,1:T(2,128)S(1)}, s32[64,2]{0,1:T(2,128)}, u32[]{:S(2)}) copy-start(s32[64,2]{0,1:T(2,128)} %param.7) | copy-start | bytes 1540
  1.2 11.1 %collective-permute-start.2 = (bf16[512,256]{1,0:T(8,128)(2,1)S(1)}, bf16[512,256]{1,0:T(8,128)(2,1)S(1)}, u32[]{:S(2)}, u32[]{:S(2)}) collective-permute-start(bf16[512,256]{1,0:T(8,128)(2,1)S(1)} %get-tuple-element.24.own), channel_id=1, source_target_pairs={{4,8},{8,4},{5,9},{9,5},{6,10},{10,6},{7,11},{11,7},{20,24},{24,20... | collective-permute-start | bytes 786440 | tf_op jit(solution)/shard_map/ppermute | solution.py:399
  4.7 9.3 %collective-permute-start.1 = (bf16[512,256]{1,0:T(8,128)(2,1)S(1)}, bf16[512,256]{1,0:T(8,128)(2,1)S(1)}, u32[]{:S(2)}, u32[]{:S(2)}) collective-permute-start(bf16[512,256]{1,0:T(8,128)(2,1)S(1)} %get-tuple-element.24.own), channel_id=1, source_target_pairs={{0,4},{4,0},{8,12},{12,8},{1,5},{5,1},{9,13},{13,9},{2,6},{6,2},{1... | collective-permute-start | bytes 786440 | tf_op jit(solution)/shard_map/ppermute | solution.py:400
  4.7 10.2 %collective-permute-start = (bf16[512,128]{1,0:T(8,128)(2,1)S(1)}, bf16[512,128]{1,0:T(8,128)(2,1)S(1)}, u32[]{:S(2)}, u32[]{:S(2)}) collective-permute-start(bf16[512,128]{1,0:T(8,128)(2,1)S(1)} %get-tuple-element.23), channel_id=1, source_target_pairs={{4,8},{8,4},{5,9},{9,5},{6,10},{10,6},{7,11},{11,7},{20,24},{24,20... | collective-permute-start | bytes 393224 | tf_op jit(solution)/shard_map/ppermute | solution.py:399
  7.1 13.3 %collective-permute-start.3 = (bf16[512,256]{1,0:T(8,128)(2,1)S(1)}, bf16[512,256]{1,0:T(8,128)(2,1)S(1)}, u32[]{:S(2)}, u32[]{:S(2)}) collective-permute-start(bf16[512,256]{1,0:T(8,128)(2,1)S(1)} %get-tuple-element.27.own), channel_id=1, source_target_pairs={{0,4},{4,0},{8,12},{12,8},{1,5},{5,1},{9,13},{13,9},{2,6},{6,2},{1... | collective-permute-start | bytes 786440 | tf_op jit(solution)/shard_map/ppermute | solution.py:400
  7.5 6.5 %copy-start = (bf16[2,512,1280]{2,1,0:T(8,128)(2,1)S(1)}, bf16[2,512,1280]{2,1,0:T(8,128)(2,1)}, u32[]{:S(2)}) copy-start(bf16[2,512,1280]{2,1,0:T(8,128)(2,1)} %integrals.3) | copy-start | bytes 7864324
  7.6 34.5 %copy-start.2 = (s32[4]{0:T(128)S(1)}, s32[4]{0:T(128)}, u32[]{:S(2)}) copy-start(s32[4]{0:T(128)} %param.8) | copy-start | bytes 52
  14.8 10.8 %collective-permute-start.5 = (bf16[2,256,256]{2,1,0:T(8,128)(2,1)S(1)}, bf16[2,256,256]{2,1,0:T(8,128)(2,1)S(1)}, u32[]{:S(2)}, u32[]{:S(2)}) collective-permute-start(bf16[2,256,256]{2,1,0:T(8,128)(2,1)S(1)} %get-tuple-element.30), channel_id=1, source_target_pairs={{0,8},{4,12},{8,0},{12,4},{1,9},{5,13},{9,1},{13,5},{2,10},{6,14},... | collective-permute-start | bytes 786440 | tf_op jit(solution)/shard_map/ppermute | solution.py:415
  14.9 5.5 %collective-permute-start.4 = (bf16[512,128]{1,0:T(8,128)(2,1)S(1)}, bf16[512,128]{1,0:T(8,128)(2,1)S(1)}, u32[]{:S(2)}, u32[]{:S(2)}) collective-permute-start(bf16[512,128]{1,0:T(8,128)(2,1)S(1)} %collective-permute-done.inner), channel_id=1, source_target_pairs={{0,2},{2,0},{1,3},{3,1},{4,6},{6,4},{5,7},{7,5},{8,10},{10,8},{9,1... | collective-permute-start | bytes 393224 | tf_op jit(solution)/shard_map/ppermute | solution.py:406
  16.5 15.2 %collective-permute-start.7 = (bf16[2,256,256]{2,1,0:T(8,128)(2,1)S(1)}, bf16[2,256,256]{2,1,0:T(8,128)(2,1)S(1)}, u32[]{:S(2)}, u32[]{:S(2)}) collective-permute-start(bf16[2,256,256]{2,1,0:T(8,128)(2,1)S(1)} %get-tuple-element.32), channel_id=1, source_target_pairs={{0,4},{4,0},{8,12},{12,8},{1,5},{5,1},{9,13},{13,9},{2,6},{6,2},{1... | collective-permute-start | bytes 786440 | tf_op jit(solution)/shard_map/ppermute | solution.py:415
  21.3 15.6 %collective-permute-start.6 = (bf16[2,256,256]{2,1,0:T(8,128)(2,1)S(1)}, bf16[2,256,256]{2,1,0:T(8,128)(2,1)S(1)}, u32[]{:S(2)}, u32[]{:S(2)}) collective-permute-start(bf16[2,256,256]{2,1,0:T(8,128)(2,1)S(1)} %get-tuple-element.31), channel_id=1, source_target_pairs={{0,8},{4,12},{8,0},{12,4},{1,9},{5,13},{9,1},{13,5},{2,10},{6,14},... | collective-permute-start | bytes 786440 | tf_op jit(solution)/shard_map/ppermute | solution.py:415
  24.6 17.6 %collective-permute-start.8 = (bf16[2,256,256]{2,1,0:T(8,128)(2,1)S(1)}, bf16[2,256,256]{2,1,0:T(8,128)(2,1)S(1)}, u32[]{:S(2)}, u32[]{:S(2)}) collective-permute-start(bf16[2,256,256]{2,1,0:T(8,128)(2,1)S(1)} %get-tuple-element.33), channel_id=1, source_target_pairs={{0,4},{4,0},{8,12},{12,8},{1,5},{5,1},{9,13},{13,9},{2,6},{6,2},{1... | collective-permute-start | bytes 786440 | tf_op jit(solution)/shard_map/ppermute | solution.py:415
  24.6 31.3 %collective-permute-start.12 = (bf16[2,256,256]{2,1,0:T(8,128)(2,1)S(1)}, bf16[2,256,256]{2,1,0:T(8,128)(2,1)S(1)}, u32[]{:S(2)}, u32[]{:S(2)}) collective-permute-start(bf16[2,256,256]{2,1,0:T(8,128)(2,1)S(1)} %get-tuple-element.38), channel_id=1, source_target_pairs={{0,12},{4,8},{8,4},{12,0},{1,13},{5,9},{9,5},{13,1},{2,14},{6,10},... | collective-permute-start | bytes 786440 | tf_op jit(solution)/shard_map/ppermute | solution.py:415
  25.6 34.1 %collective-permute-start.11 = (bf16[2,256,256]{2,1,0:T(8,128)(2,1)S(1)}, bf16[2,256,256]{2,1,0:T(8,128)(2,1)S(1)}, u32[]{:S(2)}, u32[]{:S(2)}) collective-permute-start(bf16[2,256,256]{2,1,0:T(8,128)(2,1)S(1)} %get-tuple-element.37), channel_id=1, source_target_pairs={{0,12},{4,8},{8,4},{12,0},{1,13},{5,9},{9,5},{13,1},{2,14},{6,10},... | collective-permute-start | bytes 786440 | tf_op jit(solution)/shard_map/ppermute | solution.py:415
  43.1 17.4 %collective-permute-start.9 = (bf16[2,3,64,256]{3,2,1,0:T(8,128)(2,1)S(1)}, bf16[2,3,64,256]{3,2,1,0:T(8,128)(2,1)S(1)}, u32[]{:S(2)}, u32[]{:S(2)}) collective-permute-start(bf16[2,3,64,256]{3,2,1,0:T(8,128)(2,1)S(1)} %get-tuple-element.36), channel_id=1, source_target_pairs={{0,2},{2,0},{1,3},{3,1},{4,6},{6,4},{5,7},{7,5},{8,10},{10,8},{9,1... | collective-permute-start | bytes 589832 | tf_op jit(solution)/shard_map/ppermute | solution.py:420
  60.4 1.5 %collective-permute-start.13 = (bf16[2,3,64,256]{3,2,1,0:T(8,128)(2,1)S(1)}, bf16[2,3,64,256]{3,2,1,0:T(8,128)(2,1)S(1)}, u32[]{:S(2)}, u32[]{:S(2)}) collective-permute-start(bf16[2,3,64,256]{3,2,1,0:T(8,128)(2,1)S(1)} %get-tuple-element.40), channel_id=1, source_target_pairs={{0,1},{1,0},{2,3},{3,2},{4,5},{5,4},{6,7},{7,6},{8,9},{9,8},{10,11... | collective-permute-start | bytes 589832 | tf_op jit(solution)/shard_map/ppermute | solution.py:423
  60.5 6.3 %collective-permute-start.10 = (f32[3,64,256]{2,1,0:T(8,128)S(1)}, f32[3,64,256]{2,1,0:T(8,128)S(1)}, u32[]{:S(2)}, u32[]{:S(2)}) collective-permute-start(f32[3,64,256]{2,1,0:T(8,128)S(1)} %add_bitcast_fusion), channel_id=1, source_target_pairs={{0,1},{1,0},{2,3},{3,2},{4,5},{5,4},{6,7},{7,6},{8,9},{9,8},{10,11... | collective-permute-start | bytes 589832 | tf_op jit(solution)/shard_map/ppermute | solution.py:425
  61.9 4.9 %collective-permute-start.14 = (bf16[3,64,256]{2,1,0:T(8,128)(2,1)S(1)}, bf16[3,64,256]{2,1,0:T(8,128)(2,1)S(1)}, u32[]{:S(2)}, u32[]{:S(2)}) collective-permute-start(bf16[3,64,256]{2,1,0:T(8,128)(2,1)S(1)} %fusion), channel_id=1, source_target_pairs={{0,2},{2,0},{1,3},{3,1},{4,6},{6,4},{5,7},{7,5},{8,10},{10,8},{9,1... | collective-permute-start | bytes 294920 | tf_op jit(solution)/shard_map/ppermute | solution.py:424

commit v17 on v7

--- a/solution.py
+++ b/solution.py
@@ -202,7 +202,7 @@
     )(wants, integrals, own, outer, inner)
 
 
-def form_pairs(pairs, blocks, grams):
+def form_pairs(pairs, blocks, grams, before=None):
     here = lax.axis_index("ao")
     slices = [[(ref, p) for ref in block for p in range(ref.shape[0])] for block in blocks]
 
@@ -215,6 +215,10 @@
             total = part if total is None else total + part
         return total.reshape(grams.shape[1:])
 
+    def formed(k, left, right):
+        gram = product(left, right)
+        return gram if before is None else gram + before[k]
+
     for bit in (0, 1):
         mine = [(k, a, b) for k, (a, b) in enumerate(pairs) if (a ^ b) >> 1 == bit]
         upper = (here >> bit) & 1
@@ -222,12 +226,12 @@
         @pl.when(upper == 0)
         def _(mine=mine):
             for k, a, b in mine:
-                grams[k] = product(a, b)
+                grams[k] = formed(k, a, b)
 
         @pl.when(upper == 1)
         def _(mine=mine):
             for k, a, b in mine:
-                grams[k] = product(b, a)
+                grams[k] = formed(k, b, a)
 
 
 def early_kernel(live, table, *refs):
@@ -257,13 +261,15 @@
             far[core, k] = grams[k, 2 * (1 - aux) + (orb ^ core)].astype(jnp.bfloat16)
 
 
-def late_kernel(*refs):
-    used = GROUPS * CHUNKS
-    own, middle, next_to, last = [refs[i : i + CHUNKS] for i in range(0, used, CHUNKS)]
-    blocks = own, next_to, middle, last
-    keep, give, grams = refs[used:]
+def begin_kernel(own, middle, next_to, last, grams):
+    form_pairs(LATE_PAIRS, ([own], [next_to], [middle], [last]), grams)
+
+
+def late_kernel(own, middle, next_to, last, before, *refs):
+    keep, give, grams = refs
+    blocks = [own], [next_to], [middle], [last]
     aux, orb = lax.axis_index("aux"), lax.axis_index("orb")
-    form_pairs(LATE_PAIRS, blocks, grams)
+    form_pairs(LATE_PAIRS, blocks, grams, before)
     for k in range(len(LATE_PAIRS)):
         for chip in (0, 1):
             row = 2 * (aux ^ chip)
@@ -298,14 +304,22 @@
 
 def late_pairs(blocks):
     shape, grams = quarters(LATE_PAIRS)
+    own, next_to, middle, last = blocks
+    begun = local_call(
+        begin_kernel,
+        "begin_pairs",
+        [like(grams.shape, jnp.float32)],
+        GROUPS,
+        pair_flops(LATE_PAIRS, blocks) // CHUNKS,
+    )(own[0], middle[0], next_to[0], last[0])
     return local_call(
         late_kernel,
         "late_pairs",
         [like(shape, jnp.float32)] * 2,
-        GROUPS * CHUNKS,
-        pair_flops(LATE_PAIRS, blocks),
+        GROUPS + 1,
+        pair_flops(LATE_PAIRS, blocks) // CHUNKS,
         [grams],
-    )(*blocks[0], *blocks[2], *blocks[1], *blocks[3])
+    )(own[1], middle[1], next_to[1], last[1], *begun)
 
 
 def spread_kernel(factor, place, near0, far0, got0, near1, got1, far1, out, sums, rows, sems):

time: 68.8 us -> 68.6 us (level)
  no operation moved by 1% of the time
where the time goes in v17:
time: 68.6 us; the launch traced here: 68.4 us
  waiting for transfers between devices  41 us (60%)
  starting transfers between devices  18.9 us (28%)
  Pallas kernels  5.32 us (8%)
  local copies, waits for them, and re-layouts  2.88 us (4%)
    ppermute x6, waiting for transfers between devices, fetch(): return [lax.ppermute(piece, 'ao', swap) for piece in blocks[s]]  29.5 us
    ppermute x6, starting transfers between devices, fetch(): return [lax.ppermute(piece, 'ao', swap) for piece in blocks[s]]  7.09 us
    ppermute x2, starting transfers between devices, six_pair_body(): inner = [lax.ppermute(part, 'ao', INSIDE) for part in (parts[0], mine)]  6.11 us
    ppermute x2, waiting for transfers between devices, six_pair_body(): outer = [lax.ppermute(part, 'ao', OUTSIDE) for part in parts]  4.39 us
    ppermute x1, waiting for transfers between devices, six_pair_body(): far1 = lax.ppermute((near1[1] + got1[1]).astype(jnp.bfloat16), 'aux', SWAP)  3.34 us
    ppermute x2, waiting for transfers between devices, six_pair_body(): inner = [lax.ppermute(part, 'ao', INSIDE) for part in (parts[0], mine)]  2.71 us
    ppermute x1, starting transfers between devices, six_pair_body(): swapped = lax.ppermute(inner[1], 'aux', SWAP)  1.56 us
    ppermute x1, starting transfers between devices, six_pair_body(): far0 = lax.ppermute(across0, 'aux', SWAP)  1.55 us
  transfers between devices with their start and end apart: 15, of which 11 were waited for; matrix products, arithmetic and copies ran while one was open for 3% of the time, Pallas kernels for 6%

profile of v17, /device:TPU:8, one launch (start us, length us, event | category | flops | bytes accessed | tf_op | source)
XLA Modules:
  0.0 68.4 jit_solution(8787539595062583103)
XLA Ops:
  0.0 1.0 %slice.18.own = bf16[512,256]{1,0:T(8,128)(2,1)S(1)} slice(bf16[512,512]{1,0:T(8,128)(2,1)} %param.6), slice={[0:512], [0:256]} | slice | bytes 524288 | tf_op jit(solution)/shard_map/slice | solution.py:375
  1.0 3.7 %collective-permute-start.2 = (bf16[512,256]{1,0:T(8,128)(2,1)S(1)}, bf16[512,256]{1,0:T(8,128)(2,1)S(1)}, u32[]{:S(2)}, u32[]{:S(2)}) collective-permute-start(bf16[512,256]{1,0:T(8,128)(2,1)S(1)} %slice.18.own), channel_id=1, source_target_pairs={{4,8},{8,4},{5,9},{9,5},{6,10},{10,6},{7,11},{11,7},{20,24},{24,20... | collective-permute-start | bytes 786440 | tf_op jit(solution)/shard_map/ppermute | solution.py:379
  4.9 0.9 %constant_dynamic-slice_fusion = bf16[512,128]{1,0:T(8,128)(2,1)S(1)} fusion(bf16[512,512]{1,0:T(8,128)(2,1)} %param.6, s32[]{:T(128)S(6)} %select_n.3), kind=kLoop, calls=%fused_computation.4 | loop fusion | bytes 262148 | tf_op jit(solution)/shard_map/dynamic_slice | solution.py:378
  5.8 2.4 %collective-permute-start = (bf16[512,128]{1,0:T(8,128)(2,1)S(1)}, bf16[512,128]{1,0:T(8,128)(2,1)S(1)}, u32[]{:S(2)}, u32[]{:S(2)}) collective-permute-start(bf16[512,128]{1,0:T(8,128)(2,1)S(1)} %constant_dynamic-slice_fusion), channel_id=1, source_target_pairs={{4,8},{8,4},{5,9},{9,5},{6,10},{10,6},{7,11},{11,7},{20,24},{24,20... | collective-permute-start | bytes 393224 | tf_op jit(solution)/shard_map/ppermute | solution.py:379
  8.1 1.0 %slice.19.own = bf16[512,256]{1,0:T(8,128)(2,1)S(1)} slice(bf16[512,512]{1,0:T(8,128)(2,1)} %param.6), slice={[0:512], [256:512]} | slice | bytes 524288 | tf_op jit(solution)/shard_map/slice | solution.py:377
  9.7 2.7 %collective-permute-done.2.inner = bf16[512,256]{1,0:T(8,128)(2,1)S(1)} collective-permute-done((bf16[512,256]{1,0:T(8,128)(2,1)S(1)}, bf16[512,256]{1,0:T(8,128)(2,1)S(1)}, u32[]{:S(2)}, u32[]{:S(2)}) %collective-permute-start.2) | collective-permute-done | bytes 262176 | tf_op jit(solution)/shard_map/ppermute | solution.py:379
  12.4 1.7 %collective-permute-done.1.outer = bf16[512,256]{1,0:T(8,128)(2,1)S(1)} collective-permute-done((bf16[512,256]{1,0:T(8,128)(2,1)S(1)}, bf16[512,256]{1,0:T(8,128)(2,1)S(1)}, u32[]{:S(2)}, u32[]{:S(2)}) %collective-permute-start.1) | collective-permute-done | bytes 262176 | tf_op jit(solution)/shard_map/ppermute | solution.py:380
  15.0 1.6 %collective-permute-start.4 = (bf16[512,128]{1,0:T(8,128)(2,1)S(1)}, bf16[512,128]{1,0:T(8,128)(2,1)S(1)}, u32[]{:S(2)}, u32[]{:S(2)}) collective-permute-start(bf16[512,128]{1,0:T(8,128)(2,1)S(1)} %collective-permute-done.inner), channel_id=1, source_target_pairs={{0,2},{2,0},{1,3},{3,1},{4,6},{6,4},{5,7},{7,5},{8,10},{10,8},{9,1... | collective-permute-start | bytes 393224 | tf_op jit(solution)/shard_map/ppermute | solution.py:386
  16.6 1.3 %collective-permute-start.7 = (bf16[2,256,256]{2,1,0:T(8,128)(2,1)S(1)}, bf16[2,256,256]{2,1,0:T(8,128)(2,1)S(1)}, u32[]{:S(2)}, u32[]{:S(2)}) collective-permute-start(bf16[2,256,256]{2,1,0:T(8,128)(2,1)S(1)} %get-tuple-element.30), channel_id=1, source_target_pairs={{0,4},{4,0},{8,12},{12,8},{1,5},{5,1},{9,13},{13,9},{2,6},{6,2},{1... | collective-permute-start | bytes 786440 | tf_op jit(solution)/shard_map/ppermute | solution.py:395
  17.8 2.7 %collective-permute-done.3.outer = bf16[512,256]{1,0:T(8,128)(2,1)S(1)} collective-permute-done((bf16[512,256]{1,0:T(8,128)(2,1)S(1)}, bf16[512,256]{1,0:T(8,128)(2,1)S(1)}, u32[]{:S(2)}, u32[]{:S(2)}) %collective-permute-start.3) | collective-permute-done | bytes 262176 | tf_op jit(solution)/shard_map/ppermute | solution.py:380
  20.5 0.9 %transform.3 = (bf16[2,256,256]{2,1,0:T(8,128)(2,1)S(1)}, bf16[2,256,256]{2,1,0:T(8,128)(2,1)S(1)}, bf16[2,256,256]{2,1,0:T(8,128)(2,1)S(1)}, bf16[2,256,256]{2,1,0:T(8,128)(2,1)S(1)}) custom-call(s32[8,256]{1,0:T(8,128)S(1)} %tables.1.wants, bf16[2,512,1280]{2,1,0:T(8,128)(2,1)S(1)} %copy-done, bf16[512,256]{1,0:T(8,128)(2,1)S(1)} %slice.19.own, ...), custom_call_target="tpu_custom_call" | custom-call | flops 671088640 | bytes 2097152 | tf_op jit(solution)/shard_map/transform/pallas_call | solution.py:184
  21.5 3.1 %collective-permute-start.6 = (bf16[2,256,256]{2,1,0:T(8,128)(2,1)S(1)}, bf16[2,256,256]{2,1,0:T(8,128)(2,1)S(1)}, u32[]{:S(2)}, u32[]{:S(2)}) collective-permute-start(bf16[2,256,256]{2,1,0:T(8,128)(2,1)S(1)} %get-tuple-element.29), channel_id=1, source_target_pairs={{0,8},{4,12},{8,0},{12,4},{1,9},{5,13},{9,1},{13,5},{2,10},{6,14},... | collective-permute-start | bytes 786440 | tf_op jit(solution)/shard_map/ppermute | solution.py:395
  25.6 1.7 %collective-permute-start.11 = (bf16[2,256,256]{2,1,0:T(8,128)(2,1)S(1)}, bf16[2,256,256]{2,1,0:T(8,128)(2,1)S(1)}, u32[]{:S(2)}, u32[]{:S(2)}) collective-permute-start(bf16[2,256,256]{2,1,0:T(8,128)(2,1)S(1)} %get-tuple-element.35), channel_id=1, source_target_pairs={{0,12},{4,8},{8,4},{12,0},{1,13},{5,9},{9,5},{13,1},{2,14},{6,10},... | collective-permute-start | bytes 786440 | tf_op jit(solution)/shard_map/ppermute | solution.py:395
  27.4 4.4 %collective-permute-done.7.refs_4_.next_to = bf16[2,256,256]{2,1,0:T(8,128)(2,1)S(1)} collective-permute-done((bf16[2,256,256]{2,1,0:T(8,128)(2,1)S(1)}, bf16[2,256,256]{2,1,0:T(8,128)(2,1)S(1)}, u32[]{:S(2)}, u32[]{:S(2)}) %collective-permute-start.7) | collective-permute-done | bytes 262176 | tf_op jit(solution)/shard_map/ppermute | solution.py:395
  31.7 5.2 %collective-permute-done.6.refs_3_.middle = bf16[2,256,256]{2,1,0:T(8,128)(2,1)S(1)} collective-permute-done((bf16[2,256,256]{2,1,0:T(8,128)(2,1)S(1)}, bf16[2,256,256]{2,1,0:T(8,128)(2,1)S(1)}, u32[]{:S(2)}, u32[]{:S(2)}) %collective-permute-start.6) | collective-permute-done | bytes 262176 | tf_op jit(solution)/shard_map/ppermute | solution.py:395
  37.0 5.3 %collective-permute-done.8.refs_5_.next_to = bf16[2,256,256]{2,1,0:T(8,128)(2,1)S(1)} collective-permute-done((bf16[2,256,256]{2,1,0:T(8,128)(2,1)S(1)}, bf16[2,256,256]{2,1,0:T(8,128)(2,1)S(1)}, u32[]{:S(2)}, u32[]{:S(2)}) %collective-permute-start.8) | collective-permute-done | bytes 262176 | tf_op jit(solution)/shard_map/ppermute | solution.py:395
  42.2 1.0 %early_pairs.1 = (f32[2,3,64,256]{3,2,1,0:T(8,128)S(1)}, bf16[2,3,64,256]{3,2,1,0:T(8,128)(2,1)S(1)}, s32[16,256]{1,0:T(8,128)S(1)}) custom-call(s32[1,4]{1,0:T(1,128)S(1)} %bitcast.9, s32[2,64]{1,0:T(2,128)S(1)} %bitcast.8, bf16[2,256,256]{2,1,0:T(8,128)(2,1)S(1)} %get-tuple-element.25.refs_0_.own, bf16[2,256,256]{2,1,0:T(8,128)(2,1)S(1)} %get-tuple-element.27.refs_1_.own, ...), custom_call_target="tpu_custom_call" | custom-call | flops 402653184 | bytes 1212416 | tf_op jit(solution)/shard_map/early_pairs/pallas_call | solution.py:291
  43.2 1.6 %collective-permute-start.9 = (bf16[2,3,64,256]{3,2,1,0:T(8,128)(2,1)S(1)}, bf16[2,3,64,256]{3,2,1,0:T(8,128)(2,1)S(1)}, u32[]{:S(2)}, u32[]{:S(2)}) collective-permute-start(bf16[2,3,64,256]{3,2,1,0:T(8,128)(2,1)S(1)} %get-tuple-element.34), channel_id=1, source_target_pairs={{0,2},{2,0},{1,3},{3,1},{4,6},{6,4},{5,7},{7,5},{8,10},{10,8},{9,1... | collective-permute-start | bytes 589832 | tf_op jit(solution)/shard_map/ppermute | solution.py:400
  44.8 11.1 %collective-permute-done.12.last = bf16[2,256,256]{2,1,0:T(8,128)(2,1)S(1)} collective-permute-done((bf16[2,256,256]{2,1,0:T(8,128)(2,1)S(1)}, bf16[2,256,256]{2,1,0:T(8,128)(2,1)S(1)}, u32[]{:S(2)}, u32[]{:S(2)}) %collective-permute-start.12) | collective-permute-done | bytes 262176 | tf_op jit(solution)/shard_map/ppermute | solution.py:395
  56.5 3.3 %collective-permute-done.11.last = bf16[2,256,256]{2,1,0:T(8,128)(2,1)S(1)} collective-permute-done((bf16[2,256,256]{2,1,0:T(8,128)(2,1)S(1)}, bf16[2,256,256]{2,1,0:T(8,128)(2,1)S(1)}, u32[]{:S(2)}, u32[]{:S(2)}) %collective-permute-start.11) | collective-permute-done | bytes 262176 | tf_op jit(solution)/shard_map/ppermute | solution.py:395
  61.2 1.1 %collective-permute-done.13.got1 = f32[2,3,64,256]{3,2,1,0:T(8,128)S(1)} collective-permute-done((f32[2,3,64,256]{3,2,1,0:T(8,128)S(1)}, f32[2,3,64,256]{3,2,1,0:T(8,128)S(1)}, u32[]{:S(2)}, u32[]{:S(2)}) %collective-permute-start.13) | collective-permute-done | bytes 393248 | tf_op jit(solution)/shard_map/ppermute | solution.py:403
  62.3 1.6 %collective-permute-start.14 = (bf16[3,64,256]{2,1,0:T(8,128)(2,1)S(1)}, bf16[3,64,256]{2,1,0:T(8,128)(2,1)S(1)}, u32[]{:S(2)}, u32[]{:S(2)}) collective-permute-start(bf16[3,64,256]{2,1,0:T(8,128)(2,1)S(1)} %fusion.1), channel_id=1, source_target_pairs={{0,2},{2,0},{1,3},{3,1},{4,6},{6,4},{5,7},{7,5},{8,10},{10,8},{9,1... | collective-permute-start | bytes 294920 | tf_op jit(solution)/shard_map/ppermute | solution.py:404
  63.9 3.3 %collective-permute-done.14.far1 = bf16[3,64,256]{2,1,0:T(8,128)(2,1)S(1)} collective-permute-done((bf16[3,64,256]{2,1,0:T(8,128)(2,1)S(1)}, bf16[3,64,256]{2,1,0:T(8,128)(2,1)S(1)}, u32[]{:S(2)}, u32[]{:S(2)}) %collective-permute-start.14) | collective-permute-done | bytes 98336 | tf_op jit(solution)/shard_map/ppermute | solution.py:404
  67.2 1.2 %spread.1 = f32[64,16,256]{2,1,0:T(8,128)} custom-call(s32[16,256]{1,0:T(8,128)S(1)} %get-tuple-element.32.place, f32[2,3,64,256]{3,2,1,0:T(8,128)S(1)} %get-tuple-element.33.near0, bf16[2,3,64,256]{3,2,1,0:T(8,128)(2,1)S(1)} %collective-permute-done.9.far0, f32[3,64,256]{2,1,0:T(8,128)S(1)} %collective-permute-done.10.got0, ...), custom_call_target="tpu_custom_call" | custom-call | flops 1572864 | bytes 2097152 | tf_op jit(solution)/shard_map/spread/pallas_call | solution.py:354
  (27 shorter events, 4.5 us)
Async XLA Ops:
  1.0 8.5 %copy-start.1 = (s32[64,2]{0,1:T(2,128)S(1)}, s32[64,2]{0,1:T(2,128)}, u32[]{:S(2)}) copy-start(s32[64,2]{0,1:T(2,128)} %param.7) | copy-start | bytes 1540
  1.0 8.5 %copy-start.3 = (s32[8]{0:T(128)S(1)}, s32[8]{0:T(128)}, u32[]{:S(2)}) copy-start(s32[8]{0:T(128)} %param.9) | copy-start | bytes 100
  1.0 13.1 %copy-start = (bf16[2,512,1280]{2,1,0:T(8,128)(2,1)S(1)}, bf16[2,512,1280]{2,1,0:T(8,128)(2,1)}, u32[]{:S(2)}) copy-start(bf16[2,512,1280]{2,1,0:T(8,128)(2,1)} %integrals.3) | copy-start | bytes 7864324
  1.0 11.3 %collective-permute-start.2 = (bf16[512,256]{1,0:T(8,128)(2,1)S(1)}, bf16[512,256]{1,0:T(8,128)(2,1)S(1)}, u32[]{:S(2)}, u32[]{:S(2)}) collective-permute-start(bf16[512,256]{1,0:T(8,128)(2,1)S(1)} %slice.18.own), channel_id=1, source_target_pairs={{4,8},{8,4},{5,9},{9,5},{6,10},{10,6},{7,11},{11,7},{20,24},{24,20... | collective-permute-start | bytes 786440 | tf_op jit(solution)/shard_map/ppermute | solution.py:379
  4.8 9.3 %collective-permute-start.1 = (bf16[512,256]{1,0:T(8,128)(2,1)S(1)}, bf16[512,256]{1,0:T(8,128)(2,1)S(1)}, u32[]{:S(2)}, u32[]{:S(2)}) collective-permute-start(bf16[512,256]{1,0:T(8,128)(2,1)S(1)} %slice.18.own), channel_id=1, source_target_pairs={{0,4},{4,0},{8,12},{12,8},{1,5},{5,1},{9,13},{13,9},{2,6},{6,2},{1... | collective-permute-start | bytes 786440 | tf_op jit(solution)/shard_map/ppermute | solution.py:380
  5.8 9.2 %collective-permute-start = (bf16[512,128]{1,0:T(8,128)(2,1)S(1)}, bf16[512,128]{1,0:T(8,128)(2,1)S(1)}, u32[]{:S(2)}, u32[]{:S(2)}) collective-permute-start(bf16[512,128]{1,0:T(8,128)(2,1)S(1)} %constant_dynamic-slice_fusion), channel_id=1, source_target_pairs={{4,8},{8,4},{5,9},{9,5},{6,10},{10,6},{7,11},{11,7},{20,24},{24,20... | collective-permute-start | bytes 393224 | tf_op jit(solution)/shard_map/ppermute | solution.py:379
  9.1 11.4 %collective-permute-start.3 = (bf16[512,256]{1,0:T(8,128)(2,1)S(1)}, bf16[512,256]{1,0:T(8,128)(2,1)S(1)}, u32[]{:S(2)}, u32[]{:S(2)}) collective-permute-start(bf16[512,256]{1,0:T(8,128)(2,1)S(1)} %slice.19.own), channel_id=1, source_target_pairs={{0,4},{4,0},{8,12},{12,8},{1,5},{5,1},{9,13},{13,9},{2,6},{6,2},{1... | collective-permute-start | bytes 786440 | tf_op jit(solution)/shard_map/ppermute | solution.py:380
  9.6 32.6 %copy-start.2 = (s32[4]{0:T(128)S(1)}, s32[4]{0:T(128)}, u32[]{:S(2)}) copy-start(s32[4]{0:T(128)} %param.8) | copy-start | bytes 52
  14.9 10.7 %collective-permute-start.5 = (bf16[2,256,256]{2,1,0:T(8,128)(2,1)S(1)}, bf16[2,256,256]{2,1,0:T(8,128)(2,1)S(1)}, u32[]{:S(2)}, u32[]{:S(2)}) collective-permute-start(bf16[2,256,256]{2,1,0:T(8,128)(2,1)S(1)} %get-tuple-element.28), channel_id=1, source_target_pairs={{0,8},{4,12},{8,0},{12,4},{1,9},{5,13},{9,1},{13,5},{2,10},{6,14},... | collective-permute-start | bytes 786440 | tf_op jit(solution)/shard_map/ppermute | solution.py:395
  15.0 5.5 %collective-permute-start.4 = (bf16[512,128]{1,0:T(8,128)(2,1)S(1)}, bf16[512,128]{1,0:T(8,128)(2,1)S(1)}, u32[]{:S(2)}, u32[]{:S(2)}) collective-permute-start(bf16[512,128]{1,0:T(8,128)(2,1)S(1)} %collective-permute-done.inner), channel_id=1, source_target_pairs={{0,2},{2,0},{1,3},{3,1},{4,6},{6,4},{5,7},{7,5},{8,10},{10,8},{9,1... | collective-permute-start | bytes 393224 | tf_op jit(solution)/shard_map/ppermute | solution.py:386
  16.6 15.2 %collective-permute-start.7 = (bf16[2,256,256]{2,1,0:T(8,128)(2,1)S(1)}, bf16[2,256,256]{2,1,0:T(8,128)(2,1)S(1)}, u32[]{:S(2)}, u32[]{:S(2)}) collective-permute-start(bf16[2,256,256]{2,1,0:T(8,128)(2,1)S(1)} %get-tuple-element.30), channel_id=1, source_target_pairs={{0,4},{4,0},{8,12},{12,8},{1,5},{5,1},{9,13},{13,9},{2,6},{6,2},{1... | collective-permute-start | bytes 786440 | tf_op jit(solution)/shard_map/ppermute | solution.py:395
  21.5 15.5 %collective-permute-start.6 = (bf16[2,256,256]{2,1,0:T(8,128)(2,1)S(1)}, bf16[2,256,256]{2,1,0:T(8,128)(2,1)S(1)}, u32[]{:S(2)}, u32[]{:S(2)}) collective-permute-start(bf16[2,256,256]{2,1,0:T(8,128)(2,1)S(1)} %get-tuple-element.29), channel_id=1, source_target_pairs={{0,8},{4,12},{8,0},{12,4},{1,9},{5,13},{9,1},{13,5},{2,10},{6,14},... | collective-permute-start | bytes 786440 | tf_op jit(solution)/shard_map/ppermute | solution.py:395
  24.6 17.6 %collective-permute-start.8 = (bf16[2,256,256]{2,1,0:T(8,128)(2,1)S(1)}, bf16[2,256,256]{2,1,0:T(8,128)(2,1)S(1)}, u32[]{:S(2)}, u32[]{:S(2)}) collective-permute-start(bf16[2,256,256]{2,1,0:T(8,128)(2,1)S(1)} %get-tuple-element.31), channel_id=1, source_target_pairs={{0,4},{4,0},{8,12},{12,8},{1,5},{5,1},{9,13},{13,9},{2,6},{6,2},{1... | collective-permute-start | bytes 786440 | tf_op jit(solution)/shard_map/ppermute | solution.py:395
  24.6 31.3 %collective-permute-start.12 = (bf16[2,256,256]{2,1,0:T(8,128)(2,1)S(1)}, bf16[2,256,256]{2,1,0:T(8,128)(2,1)S(1)}, u32[]{:S(2)}, u32[]{:S(2)}) collective-permute-start(bf16[2,256,256]{2,1,0:T(8,128)(2,1)S(1)} %get-tuple-element.36), channel_id=1, source_target_pairs={{0,12},{4,8},{8,4},{12,0},{1,13},{5,9},{9,5},{13,1},{2,14},{6,10},... | collective-permute-start | bytes 786440 | tf_op jit(solution)/shard_map/ppermute | solution.py:395
  25.6 34.2 %collective-permute-start.11 = (bf16[2,256,256]{2,1,0:T(8,128)(2,1)S(1)}, bf16[2,256,256]{2,1,0:T(8,128)(2,1)S(1)}, u32[]{:S(2)}, u32[]{:S(2)}) collective-permute-start(bf16[2,256,256]{2,1,0:T(8,128)(2,1)S(1)} %get-tuple-element.35), channel_id=1, source_target_pairs={{0,12},{4,8},{8,4},{12,0},{1,13},{5,9},{9,5},{13,1},{2,14},{6,10},... | collective-permute-start | bytes 786440 | tf_op jit(solution)/shard_map/ppermute | solution.py:395
  43.2 17.3 %collective-permute-start.9 = (bf16[2,3,64,256]{3,2,1,0:T(8,128)(2,1)S(1)}, bf16[2,3,64,256]{3,2,1,0:T(8,128)(2,1)S(1)}, u32[]{:S(2)}, u32[]{:S(2)}) collective-permute-start(bf16[2,3,64,256]{3,2,1,0:T(8,128)(2,1)S(1)} %get-tuple-element.34), channel_id=1, source_target_pairs={{0,2},{2,0},{1,3},{3,1},{4,6},{6,4},{5,7},{7,5},{8,10},{10,8},{9,1... | collective-permute-start | bytes 589832 | tf_op jit(solution)/shard_map/ppermute | solution.py:400
  60.5 1.8 %collective-permute-start.13 = (f32[2,3,64,256]{3,2,1,0:T(8,128)S(1)}, f32[2,3,64,256]{3,2,1,0:T(8,128)S(1)}, u32[]{:S(2)}, u32[]{:S(2)}) collective-permute-start(f32[2,3,64,256]{3,2,1,0:T(8,128)S(1)} %get-tuple-element.38), channel_id=1, source_target_pairs={{0,1},{1,0},{2,3},{3,2},{4,5},{5,4},{6,7},{7,6},{8,9},{9,8},{10,11... | collective-permute-start | bytes 1179656 | tf_op jit(solution)/shard_map/ppermute | solution.py:403
  60.6 3.3 %collective-permute-start.10 = (f32[3,64,256]{2,1,0:T(8,128)S(1)}, f32[3,64,256]{2,1,0:T(8,128)S(1)}, u32[]{:S(2)}, u32[]{:S(2)}) collective-permute-start(f32[3,64,256]{2,1,0:T(8,128)S(1)} %add_bitcast_fusion), channel_id=1, source_target_pairs={{0,1},{1,0},{2,3},{3,2},{4,5},{5,4},{6,7},{7,6},{8,9},{9,8},{10,11... | collective-permute-start | bytes 589832 | tf_op jit(solution)/shard_map/ppermute | solution.py:405
  62.3 4.9 %collective-permute-start.14 = (bf16[3,64,256]{2,1,0:T(8,128)(2,1)S(1)}, bf16[3,64,256]{2,1,0:T(8,128)(2,1)S(1)}, u32[]{:S(2)}, u32[]{:S(2)}) collective-permute-start(bf16[3,64,256]{2,1,0:T(8,128)(2,1)S(1)} %fusion.1), channel_id=1, source_target_pairs={{0,2},{2,0},{1,3},{3,1},{4,6},{6,4},{5,7},{7,5},{8,10},{10,8},{9,1... | collective-permute-start | bytes 294920 | tf_op jit(solution)/shard_map/ppermute | solution.py:404

commit v18 on v13

--- a/solution.py
+++ b/solution.py
@@ -113,34 +113,39 @@
     return jnp.dot(a, b, preferred_element_type=jnp.float32)
 
 
-def cut_kernel(coeffs, direct, shared, mine, sems):
-    width, half = direct.shape[1], mine.shape[1]
-    start = pl.multiple_of(width + lax.axis_index("aux") * half, half)
-    copies = [
-        pltpu.make_async_copy(coeffs.at[:, columns], out, sems.at[i])
-        for i, (columns, out) in enumerate(
-            ((pl.ds(0, width), direct), (pl.ds(start, half), mine), (pl.ds(width, width), shared))
-        )
-    ]
-    for copy in copies:
-        copy.start()
-    for copy in copies:
-        copy.wait()
+def cut_kernel(coeffs, direct, sem):
+    copy = pltpu.make_async_copy(coeffs.at[:, pl.ds(0, direct.shape[1])], direct, sem)
+    copy.start()
+    copy.wait()
 
 
 def cut(coeffs):
     rows, columns = coeffs.shape
-    width = columns // CHUNKS
     return pl.pallas_call(
         cut_kernel,
-        out_shape=[like((rows, n), coeffs.dtype) for n in (width, width, width // 2)],
+        out_shape=like((rows, columns // CHUNKS), coeffs.dtype),
         in_specs=[IN_HBM],
-        out_specs=[IN_VMEM] * 3,
-        scratch_shapes=[pltpu.SemaphoreType.DMA((3,))],
+        out_specs=IN_VMEM,
+        scratch_shapes=[pltpu.SemaphoreType.DMA],
         compiler_params=pltpu.CompilerParams(vmem_limit_bytes=CUT_LIMIT),
         cost_estimate=pl.CostEstimate(flops=LEAD_FLOPS, bytes_accessed=0, transcendentals=0),
         name="cut",
     )(coeffs)
+
+
+def rest_kernel(coeffs, first, shared, mine):
+    width, half = shared.shape[1], mine.shape[1]
+    shared[...] = coeffs[:, width:]
+    start = pl.multiple_of(width + lax.axis_index("aux") * half, half)
+    mine[...] = coeffs[:, pl.ds(start, half)]
+
+
+def cut_rest(coeffs, first):
+    rows, columns = coeffs.shape
+    width = columns // CHUNKS
+    return local_call(
+        rest_kernel, "cut_rest", [like((rows, n), coeffs.dtype) for n in (width, width // 2)], 2, LEAD_FLOPS
+    )(coeffs, first)
 
 
 def scalar_at(values, index):
@@ -394,7 +399,9 @@
     total_aux = integrals.shape[0] * lax.axis_size("aux")
     table = pair_blocks.T
 
-    *parts, mine = cut(coeffs)
+    direct = cut(coeffs)
+    shared, mine = cut_rest(coeffs, direct)
+    parts = [direct, shared]
     inner = [lax.ppermute(part, "ao", INSIDE) for part in (parts[0], mine)]
     outer = [lax.ppermute(part, "ao", OUTSIDE) for part in parts]
     wants = tables(orbital_count, table, width)

time: 68.4 us -> 68.3 us (level)
  no operation moved by 1% of the time
where the time goes in v18:
time: 68.3 us; the launch traced here: 68.2 us
  waiting for transfers between devices  42.3 us (62%)
  starting transfers between devices  19.2 us (28%)
  Pallas kernels  6.38 us (9%)
    ppermute x6, waiting for transfers between devices, fetch(): return [lax.ppermute(piece, 'ao', swap) for piece in blocks[s]]  29.5 us
    ppermute x6, starting transfers between devices, fetch(): return [lax.ppermute(piece, 'ao', swap) for piece in blocks[s]]  7.62 us
    ppermute x2, starting transfers between devices, six_pair_body(): inner = [lax.ppermute(part, 'ao', INSIDE) for part in (parts[0], mine)]  5.84 us
    ppermute x2, waiting for transfers between devices, six_pair_body(): inner = [lax.ppermute(part, 'ao', INSIDE) for part in (parts[0], mine)]  4.55 us
    ppermute x2, waiting for transfers between devices, six_pair_body(): outer = [lax.ppermute(part, 'ao', OUTSIDE) for part in parts]  3.8 us
    ppermute x1, waiting for transfers between devices, six_pair_body(): far1 = lax.ppermute((near1[1] + got1[1]).astype(jnp.bfloat16), 'aux', SWAP)  3.34 us
    ppermute x1, starting transfers between devices, six_pair_body(): far0 = lax.ppermute(across0, 'aux', SWAP)  1.56 us
    ppermute x1, starting transfers between devices, six_pair_body(): far1 = lax.ppermute((near1[1] + got1[1]).astype(jnp.bfloat16), 'aux', SWAP)  1.56 us
  transfers between devices with their start and end apart: 15, of which 11 were waited for; matrix products, arithmetic and copies ran while one was open for 0% of the time, Pallas kernels for 6%

profile of v18, /device:TPU:8, one launch (start us, length us, event | category | flops | bytes accessed | tf_op | source)
XLA Modules:
  0.0 68.2 jit_solution(8856889473961078553)
XLA Ops:
  0.0 1.0 %cut.1.first.own = bf16[512,256]{1,0:T(8,128)(2,1)S(1)} custom-call(bf16[512,512]{1,0:T(8,128)(2,1)} %coeffs.3), custom_call_target="tpu_custom_call" | custom-call | flops 4294967296 | tf_op jit(solution)/shard_map/cut/pallas_call | solution.py:124
  1.1 3.5 %collective-permute-start.2 = (bf16[512,256]{1,0:T(8,128)(2,1)S(1)}, bf16[512,256]{1,0:T(8,128)(2,1)S(1)}, u32[]{:S(2)}, u32[]{:S(2)}) collective-permute-start(bf16[512,256]{1,0:T(8,128)(2,1)S(1)} %cut.1.first.own), channel_id=1, source_target_pairs={{4,8},{8,4},{5,9},{9,5},{6,10},{10,6},{7,11},{11,7},{20,24},{24,20... | collective-permute-start | bytes 786440 | tf_op jit(solution)/shard_map/ppermute | solution.py:405
  4.7 2.4 %collective-permute-start = (bf16[512,128]{1,0:T(8,128)(2,1)S(1)}, bf16[512,128]{1,0:T(8,128)(2,1)S(1)}, u32[]{:S(2)}, u32[]{:S(2)}) collective-permute-start(bf16[512,128]{1,0:T(8,128)(2,1)S(1)} %get-tuple-element.22), channel_id=1, source_target_pairs={{4,8},{8,4},{5,9},{9,5},{6,10},{10,6},{7,11},{11,7},{20,24},{24,20... | collective-permute-start | bytes 393224 | tf_op jit(solution)/shard_map/ppermute | solution.py:405
  7.6 4.6 %collective-permute-done.2.inner = bf16[512,256]{1,0:T(8,128)(2,1)S(1)} collective-permute-done((bf16[512,256]{1,0:T(8,128)(2,1)S(1)}, bf16[512,256]{1,0:T(8,128)(2,1)S(1)}, u32[]{:S(2)}, u32[]{:S(2)}) %collective-permute-start.2) | collective-permute-done | bytes 262176 | tf_op jit(solution)/shard_map/ppermute | solution.py:405
  12.2 1.7 %collective-permute-done.1.outer = bf16[512,256]{1,0:T(8,128)(2,1)S(1)} collective-permute-done((bf16[512,256]{1,0:T(8,128)(2,1)S(1)}, bf16[512,256]{1,0:T(8,128)(2,1)S(1)}, u32[]{:S(2)}, u32[]{:S(2)}) %collective-permute-start.1) | collective-permute-done | bytes 262176 | tf_op jit(solution)/shard_map/ppermute | solution.py:406
  13.9 0.9 %transform.2 = (bf16[2,256,256]{2,1,0:T(8,128)(2,1)S(1)}, bf16[2,256,256]{2,1,0:T(8,128)(2,1)S(1)}, bf16[2,256,256]{2,1,0:T(8,128)(2,1)S(1)}, bf16[2,256,256]{2,1,0:T(8,128)(2,1)S(1)}) custom-call(s32[8,256]{1,0:T(8,128)S(1)} %tables.1.wants, bf16[2,512,1280]{2,1,0:T(8,128)(2,1)S(1)} %copy-done, bf16[512,256]{1,0:T(8,128)(2,1)S(1)} %cut.1.first.own, ...), custom_call_target="tpu_custom_call" | custom-call | flops 671088640 | bytes 2097152 | tf_op jit(solution)/shard_map/transform/pallas_call | solution.py:224
  14.8 1.6 %collective-permute-start.4 = (bf16[512,128]{1,0:T(8,128)(2,1)S(1)}, bf16[512,128]{1,0:T(8,128)(2,1)S(1)}, u32[]{:S(2)}, u32[]{:S(2)}) collective-permute-start(bf16[512,128]{1,0:T(8,128)(2,1)S(1)} %collective-permute-done.inner), channel_id=1, source_target_pairs={{0,2},{2,0},{1,3},{3,1},{4,6},{6,4},{5,7},{7,5},{8,10},{10,8},{9,1... | collective-permute-start | bytes 393224 | tf_op jit(solution)/shard_map/ppermute | solution.py:412
  16.4 1.8 %collective-permute-start.7 = (bf16[2,256,256]{2,1,0:T(8,128)(2,1)S(1)}, bf16[2,256,256]{2,1,0:T(8,128)(2,1)S(1)}, u32[]{:S(2)}, u32[]{:S(2)}) collective-permute-start(bf16[2,256,256]{2,1,0:T(8,128)(2,1)S(1)} %get-tuple-element.30), channel_id=1, source_target_pairs={{0,4},{4,0},{8,12},{12,8},{1,5},{5,1},{9,13},{13,9},{2,6},{6,2},{1... | collective-permute-start | bytes 786440 | tf_op jit(solution)/shard_map/ppermute | solution.py:421
  18.2 2.1 %collective-permute-done.3.outer = bf16[512,256]{1,0:T(8,128)(2,1)S(1)} collective-permute-done((bf16[512,256]{1,0:T(8,128)(2,1)S(1)}, bf16[512,256]{1,0:T(8,128)(2,1)S(1)}, u32[]{:S(2)}, u32[]{:S(2)}) %collective-permute-start.3) | collective-permute-done | bytes 262176 | tf_op jit(solution)/shard_map/ppermute | solution.py:406
  20.3 0.9 %transform.3 = (bf16[2,256,256]{2,1,0:T(8,128)(2,1)S(1)}, bf16[2,256,256]{2,1,0:T(8,128)(2,1)S(1)}, bf16[2,256,256]{2,1,0:T(8,128)(2,1)S(1)}, bf16[2,256,256]{2,1,0:T(8,128)(2,1)S(1)}) custom-call(s32[8,256]{1,0:T(8,128)S(1)} %tables.1.wants, bf16[2,512,1280]{2,1,0:T(8,128)(2,1)S(1)} %copy-done, bf16[512,256]{1,0:T(8,128)(2,1)S(1)} %get-tuple-element.25.own, ...), custom_call_target="tpu_custom_call" | custom-call | flops 671088640 | bytes 2097152 | tf_op jit(solution)/shard_map/transform/pallas_call | solution.py:212
  21.2 3.2 %collective-permute-start.6 = (bf16[2,256,256]{2,1,0:T(8,128)(2,1)S(1)}, bf16[2,256,256]{2,1,0:T(8,128)(2,1)S(1)}, u32[]{:S(2)}, u32[]{:S(2)}) collective-permute-start(bf16[2,256,256]{2,1,0:T(8,128)(2,1)S(1)} %get-tuple-element.29), channel_id=1, source_target_pairs={{0,8},{4,12},{8,0},{12,4},{1,9},{5,13},{9,1},{13,5},{2,10},{6,14},... | collective-permute-start | bytes 786440 | tf_op jit(solution)/shard_map/ppermute | solution.py:421
  24.5 0.8 %collective-permute-start.12 = (bf16[2,256,256]{2,1,0:T(8,128)(2,1)S(1)}, bf16[2,256,256]{2,1,0:T(8,128)(2,1)S(1)}, u32[]{:S(2)}, u32[]{:S(2)}) collective-permute-start(bf16[2,256,256]{2,1,0:T(8,128)(2,1)S(1)} %get-tuple-element.36), channel_id=1, source_target_pairs={{0,12},{4,8},{8,4},{12,0},{1,13},{5,9},{9,5},{13,1},{2,14},{6,10},... | collective-permute-start | bytes 786440 | tf_op jit(solution)/shard_map/ppermute | solution.py:421
  25.5 1.7 %collective-permute-start.11 = (bf16[2,256,256]{2,1,0:T(8,128)(2,1)S(1)}, bf16[2,256,256]{2,1,0:T(8,128)(2,1)S(1)}, u32[]{:S(2)}, u32[]{:S(2)}) collective-permute-start(bf16[2,256,256]{2,1,0:T(8,128)(2,1)S(1)} %get-tuple-element.35), channel_id=1, source_target_pairs={{0,12},{4,8},{8,4},{12,0},{1,13},{5,9},{9,5},{13,1},{2,14},{6,10},... | collective-permute-start | bytes 786440 | tf_op jit(solution)/shard_map/ppermute | solution.py:421
  27.2 4.3 %collective-permute-done.7.refs_4_.next_to = bf16[2,256,256]{2,1,0:T(8,128)(2,1)S(1)} collective-permute-done((bf16[2,256,256]{2,1,0:T(8,128)(2,1)S(1)}, bf16[2,256,256]{2,1,0:T(8,128)(2,1)S(1)}, u32[]{:S(2)}, u32[]{:S(2)}) %collective-permute-start.7) | collective-permute-done | bytes 262176 | tf_op jit(solution)/shard_map/ppermute | solution.py:421
  31.5 5.3 %collective-permute-done.6.refs_3_.middle = bf16[2,256,256]{2,1,0:T(8,128)(2,1)S(1)} collective-permute-done((bf16[2,256,256]{2,1,0:T(8,128)(2,1)S(1)}, bf16[2,256,256]{2,1,0:T(8,128)(2,1)S(1)}, u32[]{:S(2)}, u32[]{:S(2)}) %collective-permute-start.6) | collective-permute-done | bytes 262176 | tf_op jit(solution)/shard_map/ppermute | solution.py:421
  36.9 5.2 %collective-permute-done.8.refs_5_.next_to = bf16[2,256,256]{2,1,0:T(8,128)(2,1)S(1)} collective-permute-done((bf16[2,256,256]{2,1,0:T(8,128)(2,1)S(1)}, bf16[2,256,256]{2,1,0:T(8,128)(2,1)S(1)}, u32[]{:S(2)}, u32[]{:S(2)}) %collective-permute-start.8) | collective-permute-done | bytes 262176 | tf_op jit(solution)/shard_map/ppermute | solution.py:421
  42.0 1.0 %early_pairs.1 = (f32[2,3,64,256]{3,2,1,0:T(8,128)S(1)}, bf16[2,3,64,256]{3,2,1,0:T(8,128)(2,1)S(1)}, s32[16,256]{1,0:T(8,128)S(1)}) custom-call(s32[1,4]{1,0:T(1,128)S(1)} %bitcast.9, s32[2,64]{1,0:T(2,128)S(1)} %bitcast.8, bf16[2,256,256]{2,1,0:T(8,128)(2,1)S(1)} %get-tuple-element.24.refs_0_.own, bf16[2,256,256]{2,1,0:T(8,128)(2,1)S(1)} %get-tuple-element.27.refs_1_.own, ...), custom_call_target="tpu_custom_call" | custom-call | flops 402653184 | bytes 1212416 | tf_op jit(solution)/shard_map/early_pairs/pallas_call | solution.py:319
  43.0 1.6 %collective-permute-start.9 = (bf16[2,3,64,256]{3,2,1,0:T(8,128)(2,1)S(1)}, bf16[2,3,64,256]{3,2,1,0:T(8,128)(2,1)S(1)}, u32[]{:S(2)}, u32[]{:S(2)}) collective-permute-start(bf16[2,3,64,256]{3,2,1,0:T(8,128)(2,1)S(1)} %get-tuple-element.34), channel_id=1, source_target_pairs={{0,2},{2,0},{1,3},{3,1},{4,6},{6,4},{5,7},{7,5},{8,10},{10,8},{9,1... | collective-permute-start | bytes 589832 | tf_op jit(solution)/shard_map/ppermute | solution.py:426
  44.6 11.2 %collective-permute-done.12.last = bf16[2,256,256]{2,1,0:T(8,128)(2,1)S(1)} collective-permute-done((bf16[2,256,256]{2,1,0:T(8,128)(2,1)S(1)}, bf16[2,256,256]{2,1,0:T(8,128)(2,1)S(1)}, u32[]{:S(2)}, u32[]{:S(2)}) %collective-permute-start.12) | collective-permute-done | bytes 262176 | tf_op jit(solution)/shard_map/ppermute | solution.py:421
  56.4 3.3 %collective-permute-done.11.last = bf16[2,256,256]{2,1,0:T(8,128)(2,1)S(1)} collective-permute-done((bf16[2,256,256]{2,1,0:T(8,128)(2,1)S(1)}, bf16[2,256,256]{2,1,0:T(8,128)(2,1)S(1)}, u32[]{:S(2)}, u32[]{:S(2)}) %collective-permute-start.11) | collective-permute-done | bytes 262176 | tf_op jit(solution)/shard_map/ppermute | solution.py:421
  61.0 1.1 %collective-permute-done.13.got1 = f32[2,3,64,256]{3,2,1,0:T(8,128)S(1)} collective-permute-done((f32[2,3,64,256]{3,2,1,0:T(8,128)S(1)}, f32[2,3,64,256]{3,2,1,0:T(8,128)S(1)}, u32[]{:S(2)}, u32[]{:S(2)}) %collective-permute-start.13) | collective-permute-done | bytes 393248 | tf_op jit(solution)/shard_map/ppermute | solution.py:429
  62.1 1.6 %collective-permute-start.14 = (bf16[3,64,256]{2,1,0:T(8,128)(2,1)S(1)}, bf16[3,64,256]{2,1,0:T(8,128)(2,1)S(1)}, u32[]{:S(2)}, u32[]{:S(2)}) collective-permute-start(bf16[3,64,256]{2,1,0:T(8,128)(2,1)S(1)} %fusion.1), channel_id=1, source_target_pairs={{0,2},{2,0},{1,3},{3,1},{4,6},{6,4},{5,7},{7,5},{8,10},{10,8},{9,1... | collective-permute-start | bytes 294920 | tf_op jit(solution)/shard_map/ppermute | solution.py:430
  63.7 3.3 %collective-permute-done.14.far1 = bf16[3,64,256]{2,1,0:T(8,128)(2,1)S(1)} collective-permute-done((bf16[3,64,256]{2,1,0:T(8,128)(2,1)S(1)}, bf16[3,64,256]{2,1,0:T(8,128)(2,1)S(1)}, u32[]{:S(2)}, u32[]{:S(2)}) %collective-permute-start.14) | collective-permute-done | bytes 98336 | tf_op jit(solution)/shard_map/ppermute | solution.py:430
  67.0 1.2 %spread.1 = f32[64,16,256]{2,1,0:T(8,128)} custom-call(s32[16,256]{1,0:T(8,128)S(1)} %get-tuple-element.32.place, f32[2,3,64,256]{3,2,1,0:T(8,128)S(1)} %get-tuple-element.33.near0, bf16[2,3,64,256]{3,2,1,0:T(8,128)(2,1)S(1)} %collective-permute-done.9.far0, f32[3,64,256]{2,1,0:T(8,128)S(1)} %collective-permute-done.10.got0, ...), custom_call_target="tpu_custom_call" | custom-call | flops 1572864 | bytes 2097152 | tf_op jit(solution)/shard_map/spread/pallas_call | solution.py:382
  (27 shorter events, 2.9 us)
Async XLA Ops:
  0.0 4.6 %copy-start.3 = (bf16[512,512]{1,0:T(8,128)(2,1)S(1)}, bf16[512,512]{1,0:T(8,128)(2,1)}, u32[]{:S(2)}) copy-start(bf16[512,512]{1,0:T(8,128)(2,1)} %coeffs.3) | copy-start | bytes 1572868
  1.0 6.4 %copy-start.1 = (s32[64,2]{0,1:T(2,128)S(1)}, s32[64,2]{0,1:T(2,128)}, u32[]{:S(2)}) copy-start(s32[64,2]{0,1:T(2,128)} %param.7) | copy-start | bytes 1540
  1.1 6.4 %copy-start.4 = (s32[8]{0:T(128)S(1)}, s32[8]{0:T(128)}, u32[]{:S(2)}) copy-start(s32[8]{0:T(128)} %param.9) | copy-start | bytes 100
  1.1 11.1 %collective-permute-start.2 = (bf16[512,256]{1,0:T(8,128)(2,1)S(1)}, bf16[512,256]{1,0:T(8,128)(2,1)S(1)}, u32[]{:S(2)}, u32[]{:S(2)}) collective-permute-start(bf16[512,256]{1,0:T(8,128)(2,1)S(1)} %cut.1.first.own), channel_id=1, source_target_pairs={{4,8},{8,4},{5,9},{9,5},{6,10},{10,6},{7,11},{11,7},{20,24},{24,20... | collective-permute-start | bytes 786440 | tf_op jit(solution)/shard_map/ppermute | solution.py:405
  4.6 9.3 %collective-permute-start.1 = (bf16[512,256]{1,0:T(8,128)(2,1)S(1)}, bf16[512,256]{1,0:T(8,128)(2,1)S(1)}, u32[]{:S(2)}, u32[]{:S(2)}) collective-permute-start(bf16[512,256]{1,0:T(8,128)(2,1)S(1)} %cut.1.first.own), channel_id=1, source_target_pairs={{0,4},{4,0},{8,12},{12,8},{1,5},{5,1},{9,13},{13,9},{2,6},{6,2},{1... | collective-permute-start | bytes 786440 | tf_op jit(solution)/shard_map/ppermute | solution.py:406
  4.7 10.1 %collective-permute-start = (bf16[512,128]{1,0:T(8,128)(2,1)S(1)}, bf16[512,128]{1,0:T(8,128)(2,1)S(1)}, u32[]{:S(2)}, u32[]{:S(2)}) collective-permute-start(bf16[512,128]{1,0:T(8,128)(2,1)S(1)} %get-tuple-element.22), channel_id=1, source_target_pairs={{4,8},{8,4},{5,9},{9,5},{6,10},{10,6},{7,11},{11,7},{20,24},{24,20... | collective-permute-start | bytes 393224 | tf_op jit(solution)/shard_map/ppermute | solution.py:405
  7.1 13.2 %collective-permute-start.3 = (bf16[512,256]{1,0:T(8,128)(2,1)S(1)}, bf16[512,256]{1,0:T(8,128)(2,1)S(1)}, u32[]{:S(2)}, u32[]{:S(2)}) collective-permute-start(bf16[512,256]{1,0:T(8,128)(2,1)S(1)} %get-tuple-element.25.own), channel_id=1, source_target_pairs={{0,4},{4,0},{8,12},{12,8},{1,5},{5,1},{9,13},{13,9},{2,6},{6,2},{1... | collective-permute-start | bytes 786440 | tf_op jit(solution)/shard_map/ppermute | solution.py:406
  7.4 6.4 %copy-start = (bf16[2,512,1280]{2,1,0:T(8,128)(2,1)S(1)}, bf16[2,512,1280]{2,1,0:T(8,128)(2,1)}, u32[]{:S(2)}) copy-start(bf16[2,512,1280]{2,1,0:T(8,128)(2,1)} %integrals.3) | copy-start | bytes 7864324
  7.6 34.4 %copy-start.2 = (s32[4]{0:T(128)S(1)}, s32[4]{0:T(128)}, u32[]{:S(2)}) copy-start(s32[4]{0:T(128)} %param.8) | copy-start | bytes 52
  14.7 10.8 %collective-permute-start.5 = (bf16[2,256,256]{2,1,0:T(8,128)(2,1)S(1)}, bf16[2,256,256]{2,1,0:T(8,128)(2,1)S(1)}, u32[]{:S(2)}, u32[]{:S(2)}) collective-permute-start(bf16[2,256,256]{2,1,0:T(8,128)(2,1)S(1)} %get-tuple-element.28), channel_id=1, source_target_pairs={{0,8},{4,12},{8,0},{12,4},{1,9},{5,13},{9,1},{13,5},{2,10},{6,14},... | collective-permute-start | bytes 786440 | tf_op jit(solution)/shard_map/ppermute | solution.py:421
  14.8 5.5 %collective-permute-start.4 = (bf16[512,128]{1,0:T(8,128)(2,1)S(1)}, bf16[512,128]{1,0:T(8,128)(2,1)S(1)}, u32[]{:S(2)}, u32[]{:S(2)}) collective-permute-start(bf16[512,128]{1,0:T(8,128)(2,1)S(1)} %collective-permute-done.inner), channel_id=1, source_target_pairs={{0,2},{2,0},{1,3},{3,1},{4,6},{6,4},{5,7},{7,5},{8,10},{10,8},{9,1... | collective-permute-start | bytes 393224 | tf_op jit(solution)/shard_map/ppermute | solution.py:412
  16.4 15.2 %collective-permute-start.7 = (bf16[2,256,256]{2,1,0:T(8,128)(2,1)S(1)}, bf16[2,256,256]{2,1,0:T(8,128)(2,1)S(1)}, u32[]{:S(2)}, u32[]{:S(2)}) collective-permute-start(bf16[2,256,256]{2,1,0:T(8,128)(2,1)S(1)} %get-tuple-element.30), channel_id=1, source_target_pairs={{0,4},{4,0},{8,12},{12,8},{1,5},{5,1},{9,13},{13,9},{2,6},{6,2},{1... | collective-permute-start | bytes 786440 | tf_op jit(solution)/shard_map/ppermute | solution.py:421
  21.2 15.6 %collective-permute-start.6 = (bf16[2,256,256]{2,1,0:T(8,128)(2,1)S(1)}, bf16[2,256,256]{2,1,0:T(8,128)(2,1)S(1)}, u32[]{:S(2)}, u32[]{:S(2)}) collective-permute-start(bf16[2,256,256]{2,1,0:T(8,128)(2,1)S(1)} %get-tuple-element.29), channel_id=1, source_target_pairs={{0,8},{4,12},{8,0},{12,4},{1,9},{5,13},{9,1},{13,5},{2,10},{6,14},... | collective-permute-start | bytes 786440 | tf_op jit(solution)/shard_map/ppermute | solution.py:421
  24.5 17.6 %collective-permute-start.8 = (bf16[2,256,256]{2,1,0:T(8,128)(2,1)S(1)}, bf16[2,256,256]{2,1,0:T(8,128)(2,1)S(1)}, u32[]{:S(2)}, u32[]{:S(2)}) collective-permute-start(bf16[2,256,256]{2,1,0:T(8,128)(2,1)S(1)} %get-tuple-element.31), channel_id=1, source_target_pairs={{0,4},{4,0},{8,12},{12,8},{1,5},{5,1},{9,13},{13,9},{2,6},{6,2},{1... | collective-permute-start | bytes 786440 | tf_op jit(solution)/shard_map/ppermute | solution.py:421
  24.5 31.3 %collective-permute-start.12 = (bf16[2,256,256]{2,1,0:T(8,128)(2,1)S(1)}, bf16[2,256,256]{2,1,0:T(8,128)(2,1)S(1)}, u32[]{:S(2)}, u32[]{:S(2)}) collective-permute-start(bf16[2,256,256]{2,1,0:T(8,128)(2,1)S(1)} %get-tuple-element.36), channel_id=1, source_target_pairs={{0,12},{4,8},{8,4},{12,0},{1,13},{5,9},{9,5},{13,1},{2,14},{6,10},... | collective-permute-start | bytes 786440 | tf_op jit(solution)/shard_map/ppermute | solution.py:421
  25.5 34.1 %collective-permute-start.11 = (bf16[2,256,256]{2,1,0:T(8,128)(2,1)S(1)}, bf16[2,256,256]{2,1,0:T(8,128)(2,1)S(1)}, u32[]{:S(2)}, u32[]{:S(2)}) collective-permute-start(bf16[2,256,256]{2,1,0:T(8,128)(2,1)S(1)} %get-tuple-element.35), channel_id=1, source_target_pairs={{0,12},{4,8},{8,4},{12,0},{1,13},{5,9},{9,5},{13,1},{2,14},{6,10},... | collective-permute-start | bytes 786440 | tf_op jit(solution)/shard_map/ppermute | solution.py:421
  43.0 17.4 %collective-permute-start.9 = (bf16[2,3,64,256]{3,2,1,0:T(8,128)(2,1)S(1)}, bf16[2,3,64,256]{3,2,1,0:T(8,128)(2,1)S(1)}, u32[]{:S(2)}, u32[]{:S(2)}) collective-permute-start(bf16[2,3,64,256]{3,2,1,0:T(8,128)(2,1)S(1)} %get-tuple-element.34), channel_id=1, source_target_pairs={{0,2},{2,0},{1,3},{3,1},{4,6},{6,4},{5,7},{7,5},{8,10},{10,8},{9,1... | collective-permute-start | bytes 589832 | tf_op jit(solution)/shard_map/ppermute | solution.py:426
  60.3 1.8 %collective-permute-start.13 = (f32[2,3,64,256]{3,2,1,0:T(8,128)S(1)}, f32[2,3,64,256]{3,2,1,0:T(8,128)S(1)}, u32[]{:S(2)}, u32[]{:S(2)}) collective-permute-start(f32[2,3,64,256]{3,2,1,0:T(8,128)S(1)} %get-tuple-element.38), channel_id=1, source_target_pairs={{0,1},{1,0},{2,3},{3,2},{4,5},{5,4},{6,7},{7,6},{8,9},{9,8},{10,11... | collective-permute-start | bytes 1179656 | tf_op jit(solution)/shard_map/ppermute | solution.py:429
  60.4 3.3 %collective-permute-start.10 = (f32[3,64,256]{2,1,0:T(8,128)S(1)}, f32[3,64,256]{2,1,0:T(8,128)S(1)}, u32[]{:S(2)}, u32[]{:S(2)}) collective-permute-start(f32[3,64,256]{2,1,0:T(8,128)S(1)} %add_bitcast_fusion), channel_id=1, source_target_pairs={{0,1},{1,0},{2,3},{3,2},{4,5},{5,4},{6,7},{7,6},{8,9},{9,8},{10,11... | collective-permute-start | bytes 589832 | tf_op jit(solution)/shard_map/ppermute | solution.py:431
  62.1 4.9 %collective-permute-start.14 = (bf16[3,64,256]{2,1,0:T(8,128)(2,1)S(1)}, bf16[3,64,256]{2,1,0:T(8,128)(2,1)S(1)}, u32[]{:S(2)}, u32[]{:S(2)}) collective-permute-start(bf16[3,64,256]{2,1,0:T(8,128)(2,1)S(1)} %fusion.1), channel_id=1, source_target_pairs={{0,2},{2,0},{1,3},{3,1},{4,6},{6,4},{5,7},{7,5},{8,10},{10,8},{9,1... | collective-permute-start | bytes 294920 | tf_op jit(solution)/shard_map/ppermute | solution.py:430

commit v19 on v18

--- a/solution.py
+++ b/solution.py
@@ -21,6 +21,7 @@
 SPREAD_STEPS = 4
 VMEM_LIMIT = 40 * 1024 * 1024
 LEAD_FLOPS = 1 << 32
+LATE_WEIGHT = 10
 CUT_LIMIT = 53 * 1024 * 1024 + 256 * 1024
 
 
@@ -302,7 +303,7 @@
         for chip in (0, 1):
             row = 2 * (aux ^ chip)
             keep[chip, k] = grams[k, row + orb]
-            give[chip, k] = grams[k, row + 1 - orb]
+            give[chip, k] = grams[k, row + 1 - orb].astype(jnp.bfloat16)
 
 
 def pair_flops(pairs, blocks):
@@ -343,9 +344,9 @@
     return local_call(
         late_kernel,
         "late_pairs",
-        [like(shape, jnp.float32)] * 2,
+        [like(shape, jnp.float32), like(shape, jnp.bfloat16)],
         GROUPS + 1,
-        pair_flops(LATE_PAIRS, blocks) // CHUNKS,
+        LATE_WEIGHT * pair_flops(LATE_PAIRS, blocks) // CHUNKS,
         [grams],
     )(own[1], middle[1], next_to[1], last[1], *begun)
 
@@ -353,7 +354,7 @@
 def spread_kernel(factor, place, near0, far0, got0, near1, got1, far1, out, sums, rows, sems):
     early = near0.shape[1]
     sums[:early] = (near0[0] + far0[0].astype(jnp.float32) + got0[...]) * factor
-    sums[early:] = (near1[0] + got1[0] + far1[...].astype(jnp.float32)) * factor
+    sums[early:] = (near1[0] + got1[0].astype(jnp.float32) + far1[...].astype(jnp.float32)) * factor
     total, slots, width = out.shape
     masks = [place[...] == k for k in range(sums.shape[0])]
 
@@ -427,7 +428,7 @@
     got.append(fetch(3))
     near1, give1 = late_pairs(got)
     got1 = lax.ppermute(give1, "orb", SWAP)
-    far1 = lax.ppermute((near1[1] + got1[1]).astype(jnp.bfloat16), "aux", SWAP)
+    far1 = lax.ppermute((near1[1] + got1[1].astype(jnp.float32)).astype(jnp.bfloat16), "aux", SWAP)
     got0 = lax.ppermute(near0[1] + far0[1].astype(jnp.float32), "orb", SWAP)
     factor = 1.0 / math.sqrt(total_aux * ORBS)
     return spread(factor, place, near0, far0, got0, near1, got1, far1)

time: 68.3 us -> 68.1 us (level)
  no operation moved by 1% of the time
where the time goes in v19:
time: 68.1 us; the launch traced here: 67.9 us
  waiting for transfers between devices  42.1 us (62%)
  starting transfers between devices  19.2 us (28%)
  Pallas kernels  6.38 us (9%)
    ppermute x6, waiting for transfers between devices, fetch(): return [lax.ppermute(piece, 'ao', swap) for piece in blocks[s]]  29.5 us
    ppermute x6, starting transfers between devices, fetch(): return [lax.ppermute(piece, 'ao', swap) for piece in blocks[s]]  7.62 us
    ppermute x2, starting transfers between devices, six_pair_body(): inner = [lax.ppermute(part, 'ao', INSIDE) for part in (parts[0], mine)]  5.84 us
    ppermute x2, waiting for transfers between devices, six_pair_body(): inner = [lax.ppermute(part, 'ao', INSIDE) for part in (parts[0], mine)]  4.55 us
    ppermute x2, waiting for transfers between devices, six_pair_body(): outer = [lax.ppermute(part, 'ao', OUTSIDE) for part in parts]  3.8 us
    ppermute x1, waiting for transfers between devices, six_pair_body(): lax.ppermute((near1[1] + got1[1].astype(jnp.float32)).astype(jnp.bfloat16...  3.34 us
    ppermute x1, starting transfers between devices, six_pair_body(): far0 = lax.ppermute(across0, 'aux', SWAP)  1.56 us
    ppermute x1, starting transfers between devices, six_pair_body(): lax.ppermute((near1[1] + got1[1].astype(jnp.float32)).astype(jnp.bfloat16...  1.56 us
  transfers between devices with their start and end apart: 15, of which 11 were waited for; matrix products, arithmetic and copies ran while one was open for 0% of the time, Pallas kernels for 6%

profile of v19, /device:TPU:8, one launch (start us, length us, event | category | flops | bytes accessed | tf_op | source)
XLA Modules:
  0.0 67.9 jit_solution(2186581041928483692)
XLA Ops:
  0.0 1.0 %cut.1.first.own = bf16[512,256]{1,0:T(8,128)(2,1)S(1)} custom-call(bf16[512,512]{1,0:T(8,128)(2,1)} %coeffs.3), custom_call_target="tpu_custom_call" | custom-call | flops 4294967296 | tf_op jit(solution)/shard_map/cut/pallas_call | solution.py:125
  1.1 3.5 %collective-permute-start.2 = (bf16[512,256]{1,0:T(8,128)(2,1)S(1)}, bf16[512,256]{1,0:T(8,128)(2,1)S(1)}, u32[]{:S(2)}, u32[]{:S(2)}) collective-permute-start(bf16[512,256]{1,0:T(8,128)(2,1)S(1)} %cut.1.first.own), channel_id=1, source_target_pairs={{4,8},{8,4},{5,9},{9,5},{6,10},{10,6},{7,11},{11,7},{20,24},{24,20... | collective-permute-start | bytes 786440 | tf_op jit(solution)/shard_map/ppermute | solution.py:406
  4.7 2.4 %collective-permute-start = (bf16[512,128]{1,0:T(8,128)(2,1)S(1)}, bf16[512,128]{1,0:T(8,128)(2,1)S(1)}, u32[]{:S(2)}, u32[]{:S(2)}) collective-permute-start(bf16[512,128]{1,0:T(8,128)(2,1)S(1)} %get-tuple-element.22), channel_id=1, source_target_pairs={{4,8},{8,4},{5,9},{9,5},{6,10},{10,6},{7,11},{11,7},{20,24},{24,20... | collective-permute-start | bytes 393224 | tf_op jit(solution)/shard_map/ppermute | solution.py:406
  7.6 4.6 %collective-permute-done.2.inner = bf16[512,256]{1,0:T(8,128)(2,1)S(1)} collective-permute-done((bf16[512,256]{1,0:T(8,128)(2,1)S(1)}, bf16[512,256]{1,0:T(8,128)(2,1)S(1)}, u32[]{:S(2)}, u32[]{:S(2)}) %collective-permute-start.2) | collective-permute-done | bytes 262176 | tf_op jit(solution)/shard_map/ppermute | solution.py:406
  12.2 1.7 %collective-permute-done.1.outer = bf16[512,256]{1,0:T(8,128)(2,1)S(1)} collective-permute-done((bf16[512,256]{1,0:T(8,128)(2,1)S(1)}, bf16[512,256]{1,0:T(8,128)(2,1)S(1)}, u32[]{:S(2)}, u32[]{:S(2)}) %collective-permute-start.1) | collective-permute-done | bytes 262176 | tf_op jit(solution)/shard_map/ppermute | solution.py:407
  13.9 0.9 %transform.2 = (bf16[2,256,256]{2,1,0:T(8,128)(2,1)S(1)}, bf16[2,256,256]{2,1,0:T(8,128)(2,1)S(1)}, bf16[2,256,256]{2,1,0:T(8,128)(2,1)S(1)}, bf16[2,256,256]{2,1,0:T(8,128)(2,1)S(1)}) custom-call(s32[8,256]{1,0:T(8,128)S(1)} %tables.1.wants, bf16[2,512,1280]{2,1,0:T(8,128)(2,1)S(1)} %copy-done, bf16[512,256]{1,0:T(8,128)(2,1)S(1)} %cut.1.first.own, ...), custom_call_target="tpu_custom_call" | custom-call | flops 671088640 | bytes 2097152 | tf_op jit(solution)/shard_map/transform/pallas_call | solution.py:225
  14.8 1.6 %collective-permute-start.4 = (bf16[512,128]{1,0:T(8,128)(2,1)S(1)}, bf16[512,128]{1,0:T(8,128)(2,1)S(1)}, u32[]{:S(2)}, u32[]{:S(2)}) collective-permute-start(bf16[512,128]{1,0:T(8,128)(2,1)S(1)} %collective-permute-done.inner), channel_id=1, source_target_pairs={{0,2},{2,0},{1,3},{3,1},{4,6},{6,4},{5,7},{7,5},{8,10},{10,8},{9,1... | collective-permute-start | bytes 393224 | tf_op jit(solution)/shard_map/ppermute | solution.py:413
  16.4 1.8 %collective-permute-start.7 = (bf16[2,256,256]{2,1,0:T(8,128)(2,1)S(1)}, bf16[2,256,256]{2,1,0:T(8,128)(2,1)S(1)}, u32[]{:S(2)}, u32[]{:S(2)}) collective-permute-start(bf16[2,256,256]{2,1,0:T(8,128)(2,1)S(1)} %get-tuple-element.30), channel_id=1, source_target_pairs={{0,4},{4,0},{8,12},{12,8},{1,5},{5,1},{9,13},{13,9},{2,6},{6,2},{1... | collective-permute-start | bytes 786440 | tf_op jit(solution)/shard_map/ppermute | solution.py:422
  18.2 2.1 %collective-permute-done.3.outer = bf16[512,256]{1,0:T(8,128)(2,1)S(1)} collective-permute-done((bf16[512,256]{1,0:T(8,128)(2,1)S(1)}, bf16[512,256]{1,0:T(8,128)(2,1)S(1)}, u32[]{:S(2)}, u32[]{:S(2)}) %collective-permute-start.3) | collective-permute-done | bytes 262176 | tf_op jit(solution)/shard_map/ppermute | solution.py:407
  20.3 0.9 %transform.3 = (bf16[2,256,256]{2,1,0:T(8,128)(2,1)S(1)}, bf16[2,256,256]{2,1,0:T(8,128)(2,1)S(1)}, bf16[2,256,256]{2,1,0:T(8,128)(2,1)S(1)}, bf16[2,256,256]{2,1,0:T(8,128)(2,1)S(1)}) custom-call(s32[8,256]{1,0:T(8,128)S(1)} %tables.1.wants, bf16[2,512,1280]{2,1,0:T(8,128)(2,1)S(1)} %copy-done, bf16[512,256]{1,0:T(8,128)(2,1)S(1)} %get-tuple-element.25.own, ...), custom_call_target="tpu_custom_call" | custom-call | flops 671088640 | bytes 2097152 | tf_op jit(solution)/shard_map/transform/pallas_call | solution.py:213
  21.2 3.2 %collective-permute-start.6 = (bf16[2,256,256]{2,1,0:T(8,128)(2,1)S(1)}, bf16[2,256,256]{2,1,0:T(8,128)(2,1)S(1)}, u32[]{:S(2)}, u32[]{:S(2)}) collective-permute-start(bf16[2,256,256]{2,1,0:T(8,128)(2,1)S(1)} %get-tuple-element.29), channel_id=1, source_target_pairs={{0,8},{4,12},{8,0},{12,4},{1,9},{5,13},{9,1},{13,5},{2,10},{6,14},... | collective-permute-start | bytes 786440 | tf_op jit(solution)/shard_map/ppermute | solution.py:422
  24.5 0.8 %collective-permute-start.12 = (bf16[2,256,256]{2,1,0:T(8,128)(2,1)S(1)}, bf16[2,256,256]{2,1,0:T(8,128)(2,1)S(1)}, u32[]{:S(2)}, u32[]{:S(2)}) collective-permute-start(bf16[2,256,256]{2,1,0:T(8,128)(2,1)S(1)} %get-tuple-element.36), channel_id=1, source_target_pairs={{0,12},{4,8},{8,4},{12,0},{1,13},{5,9},{9,5},{13,1},{2,14},{6,10},... | collective-permute-start | bytes 786440 | tf_op jit(solution)/shard_map/ppermute | solution.py:422
  25.5 1.7 %collective-permute-start.11 = (bf16[2,256,256]{2,1,0:T(8,128)(2,1)S(1)}, bf16[2,256,256]{2,1,0:T(8,128)(2,1)S(1)}, u32[]{:S(2)}, u32[]{:S(2)}) collective-permute-start(bf16[2,256,256]{2,1,0:T(8,128)(2,1)S(1)} %get-tuple-element.35), channel_id=1, source_target_pairs={{0,12},{4,8},{8,4},{12,0},{1,13},{5,9},{9,5},{13,1},{2,14},{6,10},... | collective-permute-start | bytes 786440 | tf_op jit(solution)/shard_map/ppermute | solution.py:422
  27.2 4.3 %collective-permute-done.7.refs_4_.next_to = bf16[2,256,256]{2,1,0:T(8,128)(2,1)S(1)} collective-permute-done((bf16[2,256,256]{2,1,0:T(8,128)(2,1)S(1)}, bf16[2,256,256]{2,1,0:T(8,128)(2,1)S(1)}, u32[]{:S(2)}, u32[]{:S(2)}) %collective-permute-start.7) | collective-permute-done | bytes 262176 | tf_op jit(solution)/shard_map/ppermute | solution.py:422
  31.5 5.3 %collective-permute-done.6.refs_3_.middle = bf16[2,256,256]{2,1,0:T(8,128)(2,1)S(1)} collective-permute-done((bf16[2,256,256]{2,1,0:T(8,128)(2,1)S(1)}, bf16[2,256,256]{2,1,0:T(8,128)(2,1)S(1)}, u32[]{:S(2)}, u32[]{:S(2)}) %collective-permute-start.6) | collective-permute-done | bytes 262176 | tf_op jit(solution)/shard_map/ppermute | solution.py:422
  36.9 5.2 %collective-permute-done.8.refs_5_.next_to = bf16[2,256,256]{2,1,0:T(8,128)(2,1)S(1)} collective-permute-done((bf16[2,256,256]{2,1,0:T(8,128)(2,1)S(1)}, bf16[2,256,256]{2,1,0:T(8,128)(2,1)S(1)}, u32[]{:S(2)}, u32[]{:S(2)}) %collective-permute-start.8) | collective-permute-done | bytes 262176 | tf_op jit(solution)/shard_map/ppermute | solution.py:422
  42.0 1.0 %early_pairs.1 = (f32[2,3,64,256]{3,2,1,0:T(8,128)S(1)}, bf16[2,3,64,256]{3,2,1,0:T(8,128)(2,1)S(1)}, s32[16,256]{1,0:T(8,128)S(1)}) custom-call(s32[1,4]{1,0:T(1,128)S(1)} %bitcast.9, s32[2,64]{1,0:T(2,128)S(1)} %bitcast.8, bf16[2,256,256]{2,1,0:T(8,128)(2,1)S(1)} %get-tuple-element.24.refs_0_.own, bf16[2,256,256]{2,1,0:T(8,128)(2,1)S(1)} %get-tuple-element.27.refs_1_.own, ...), custom_call_target="tpu_custom_call" | custom-call | flops 402653184 | bytes 1212416 | tf_op jit(solution)/shard_map/early_pairs/pallas_call | solution.py:320
  43.0 1.6 %collective-permute-start.9 = (bf16[2,3,64,256]{3,2,1,0:T(8,128)(2,1)S(1)}, bf16[2,3,64,256]{3,2,1,0:T(8,128)(2,1)S(1)}, u32[]{:S(2)}, u32[]{:S(2)}) collective-permute-start(bf16[2,3,64,256]{3,2,1,0:T(8,128)(2,1)S(1)} %get-tuple-element.34), channel_id=1, source_target_pairs={{0,2},{2,0},{1,3},{3,1},{4,6},{6,4},{5,7},{7,5},{8,10},{10,8},{9,1... | collective-permute-start | bytes 589832 | tf_op jit(solution)/shard_map/ppermute | solution.py:427
  44.6 11.2 %collective-permute-done.12.last = bf16[2,256,256]{2,1,0:T(8,128)(2,1)S(1)} collective-permute-done((bf16[2,256,256]{2,1,0:T(8,128)(2,1)S(1)}, bf16[2,256,256]{2,1,0:T(8,128)(2,1)S(1)}, u32[]{:S(2)}, u32[]{:S(2)}) %collective-permute-start.12) | collective-permute-done | bytes 262176 | tf_op jit(solution)/shard_map/ppermute | solution.py:422
  56.4 3.3 %collective-permute-done.11.last = bf16[2,256,256]{2,1,0:T(8,128)(2,1)S(1)} collective-permute-done((bf16[2,256,256]{2,1,0:T(8,128)(2,1)S(1)}, bf16[2,256,256]{2,1,0:T(8,128)(2,1)S(1)}, u32[]{:S(2)}, u32[]{:S(2)}) %collective-permute-start.11) | collective-permute-done | bytes 262176 | tf_op jit(solution)/shard_map/ppermute | solution.py:422
  61.0 0.8 %collective-permute-done.13.got1 = bf16[2,3,64,256]{3,2,1,0:T(8,128)(2,1)S(1)} collective-permute-done((bf16[2,3,64,256]{3,2,1,0:T(8,128)(2,1)S(1)}, bf16[2,3,64,256]{3,2,1,0:T(8,128)(2,1)S(1)}, u32[]{:S(2)}, u32[]{:S(2)}) %collective-permute-start.13) | collective-permute-done | bytes 196640 | tf_op jit(solution)/shard_map/ppermute | solution.py:430
  61.8 1.6 %collective-permute-start.14 = (bf16[3,64,256]{2,1,0:T(8,128)(2,1)S(1)}, bf16[3,64,256]{2,1,0:T(8,128)(2,1)S(1)}, u32[]{:S(2)}, u32[]{:S(2)}) collective-permute-start(bf16[3,64,256]{2,1,0:T(8,128)(2,1)S(1)} %fusion), channel_id=1, source_target_pairs={{0,2},{2,0},{1,3},{3,1},{4,6},{6,4},{5,7},{7,5},{8,10},{10,8},{9,1... | collective-permute-start | bytes 294920 | tf_op jit(solution)/shard_map/ppermute | solution.py:431
  63.4 3.3 %collective-permute-done.14.far1 = bf16[3,64,256]{2,1,0:T(8,128)(2,1)S(1)} collective-permute-done((bf16[3,64,256]{2,1,0:T(8,128)(2,1)S(1)}, bf16[3,64,256]{2,1,0:T(8,128)(2,1)S(1)}, u32[]{:S(2)}, u32[]{:S(2)}) %collective-permute-start.14) | collective-permute-done | bytes 98336 | tf_op jit(solution)/shard_map/ppermute | solution.py:431
  66.7 1.2 %spread.1 = f32[64,16,256]{2,1,0:T(8,128)} custom-call(s32[16,256]{1,0:T(8,128)S(1)} %get-tuple-element.32.place, f32[2,3,64,256]{3,2,1,0:T(8,128)S(1)} %get-tuple-element.33.near0, bf16[2,3,64,256]{3,2,1,0:T(8,128)(2,1)S(1)} %collective-permute-done.9.far0, f32[3,64,256]{2,1,0:T(8,128)S(1)} %collective-permute-done.10.got0, ...), custom_call_target="tpu_custom_call" | custom-call | flops 1572864 | bytes 2097152 | tf_op jit(solution)/shard_map/spread/pallas_call | solution.py:383
  (27 shorter events, 2.9 us)
Async XLA Ops:
  0.0 4.6 %copy-start.3 = (bf16[512,512]{1,0:T(8,128)(2,1)S(1)}, bf16[512,512]{1,0:T(8,128)(2,1)}, u32[]{:S(2)}) copy-start(bf16[512,512]{1,0:T(8,128)(2,1)} %coeffs.3) | copy-start | bytes 1572868
  1.0 6.4 %copy-start.1 = (s32[64,2]{0,1:T(2,128)S(1)}, s32[64,2]{0,1:T(2,128)}, u32[]{:S(2)}) copy-start(s32[64,2]{0,1:T(2,128)} %param.7) | copy-start | bytes 1540
  1.1 6.4 %copy-start.4 = (s32[8]{0:T(128)S(1)}, s32[8]{0:T(128)}, u32[]{:S(2)}) copy-start(s32[8]{0:T(128)} %param.9) | copy-start | bytes 100
  1.1 11.1 %collective-permute-start.2 = (bf16[512,256]{1,0:T(8,128)(2,1)S(1)}, bf16[512,256]{1,0:T(8,128)(2,1)S(1)}, u32[]{:S(2)}, u32[]{:S(2)}) collective-permute-start(bf16[512,256]{1,0:T(8,128)(2,1)S(1)} %cut.1.first.own), channel_id=1, source_target_pairs={{4,8},{8,4},{5,9},{9,5},{6,10},{10,6},{7,11},{11,7},{20,24},{24,20... | collective-permute-start | bytes 786440 | tf_op jit(solution)/shard_map/ppermute | solution.py:406
  4.6 9.3 %collective-permute-start.1 = (bf16[512,256]{1,0:T(8,128)(2,1)S(1)}, bf16[512,256]{1,0:T(8,128)(2,1)S(1)}, u32[]{:S(2)}, u32[]{:S(2)}) collective-permute-start(bf16[512,256]{1,0:T(8,128)(2,1)S(1)} %cut.1.first.own), channel_id=1, source_target_pairs={{0,4},{4,0},{8,12},{12,8},{1,5},{5,1},{9,13},{13,9},{2,6},{6,2},{1... | collective-permute-start | bytes 786440 | tf_op jit(solution)/shard_map/ppermute | solution.py:407
  4.7 10.1 %collective-permute-start = (bf16[512,128]{1,0:T(8,128)(2,1)S(1)}, bf16[512,128]{1,0:T(8,128)(2,1)S(1)}, u32[]{:S(2)}, u32[]{:S(2)}) collective-permute-start(bf16[512,128]{1,0:T(8,128)(2,1)S(1)} %get-tuple-element.22), channel_id=1, source_target_pairs={{4,8},{8,4},{5,9},{9,5},{6,10},{10,6},{7,11},{11,7},{20,24},{24,20... | collective-permute-start | bytes 393224 | tf_op jit(solution)/shard_map/ppermute | solution.py:406
  7.1 13.2 %collective-permute-start.3 = (bf16[512,256]{1,0:T(8,128)(2,1)S(1)}, bf16[512,256]{1,0:T(8,128)(2,1)S(1)}, u32[]{:S(2)}, u32[]{:S(2)}) collective-permute-start(bf16[512,256]{1,0:T(8,128)(2,1)S(1)} %get-tuple-element.25.own), channel_id=1, source_target_pairs={{0,4},{4,0},{8,12},{12,8},{1,5},{5,1},{9,13},{13,9},{2,6},{6,2},{1... | collective-permute-start | bytes 786440 | tf_op jit(solution)/shard_map/ppermute | solution.py:407
  7.4 6.4 %copy-start = (bf16[2,512,1280]{2,1,0:T(8,128)(2,1)S(1)}, bf16[2,512,1280]{2,1,0:T(8,128)(2,1)}, u32[]{:S(2)}) copy-start(bf16[2,512,1280]{2,1,0:T(8,128)(2,1)} %integrals.3) | copy-start | bytes 7864324
  7.6 34.4 %copy-start.2 = (s32[4]{0:T(128)S(1)}, s32[4]{0:T(128)}, u32[]{:S(2)}) copy-start(s32[4]{0:T(128)} %param.8) | copy-start | bytes 52
  14.7 10.8 %collective-permute-start.5 = (bf16[2,256,256]{2,1,0:T(8,128)(2,1)S(1)}, bf16[2,256,256]{2,1,0:T(8,128)(2,1)S(1)}, u32[]{:S(2)}, u32[]{:S(2)}) collective-permute-start(bf16[2,256,256]{2,1,0:T(8,128)(2,1)S(1)} %get-tuple-element.28), channel_id=1, source_target_pairs={{0,8},{4,12},{8,0},{12,4},{1,9},{5,13},{9,1},{13,5},{2,10},{6,14},... | collective-permute-start | bytes 786440 | tf_op jit(solution)/shard_map/ppermute | solution.py:422
  14.8 5.5 %collective-permute-start.4 = (bf16[512,128]{1,0:T(8,128)(2,1)S(1)}, bf16[512,128]{1,0:T(8,128)(2,1)S(1)}, u32[]{:S(2)}, u32[]{:S(2)}) collective-permute-start(bf16[512,128]{1,0:T(8,128)(2,1)S(1)} %collective-permute-done.inner), channel_id=1, source_target_pairs={{0,2},{2,0},{1,3},{3,1},{4,6},{6,4},{5,7},{7,5},{8,10},{10,8},{9,1... | collective-permute-start | bytes 393224 | tf_op jit(solution)/shard_map/ppermute | solution.py:413
  16.4 15.2 %collective-permute-start.7 = (bf16[2,256,256]{2,1,0:T(8,128)(2,1)S(1)}, bf16[2,256,256]{2,1,0:T(8,128)(2,1)S(1)}, u32[]{:S(2)}, u32[]{:S(2)}) collective-permute-start(bf16[2,256,256]{2,1,0:T(8,128)(2,1)S(1)} %get-tuple-element.30), channel_id=1, source_target_pairs={{0,4},{4,0},{8,12},{12,8},{1,5},{5,1},{9,13},{13,9},{2,6},{6,2},{1... | collective-permute-start | bytes 786440 | tf_op jit(solution)/shard_map/ppermute | solution.py:422
  21.2 15.6 %collective-permute-start.6 = (bf16[2,256,256]{2,1,0:T(8,128)(2,1)S(1)}, bf16[2,256,256]{2,1,0:T(8,128)(2,1)S(1)}, u32[]{:S(2)}, u32[]{:S(2)}) collective-permute-start(bf16[2,256,256]{2,1,0:T(8,128)(2,1)S(1)} %get-tuple-element.29), channel_id=1, source_target_pairs={{0,8},{4,12},{8,0},{12,4},{1,9},{5,13},{9,1},{13,5},{2,10},{6,14},... | collective-permute-start | bytes 786440 | tf_op jit(solution)/shard_map/ppermute | solution.py:422
  24.5 17.6 %collective-permute-start.8 = (bf16[2,256,256]{2,1,0:T(8,128)(2,1)S(1)}, bf16[2,256,256]{2,1,0:T(8,128)(2,1)S(1)}, u32[]{:S(2)}, u32[]{:S(2)}) collective-permute-start(bf16[2,256,256]{2,1,0:T(8,128)(2,1)S(1)} %get-tuple-element.31), channel_id=1, source_target_pairs={{0,4},{4,0},{8,12},{12,8},{1,5},{5,1},{9,13},{13,9},{2,6},{6,2},{1... | collective-permute-start | bytes 786440 | tf_op jit(solution)/shard_map/ppermute | solution.py:422
  24.5 31.3 %collective-permute-start.12 = (bf16[2,256,256]{2,1,0:T(8,128)(2,1)S(1)}, bf16[2,256,256]{2,1,0:T(8,128)(2,1)S(1)}, u32[]{:S(2)}, u32[]{:S(2)}) collective-permute-start(bf16[2,256,256]{2,1,0:T(8,128)(2,1)S(1)} %get-tuple-element.36), channel_id=1, source_target_pairs={{0,12},{4,8},{8,4},{12,0},{1,13},{5,9},{9,5},{13,1},{2,14},{6,10},... | collective-permute-start | bytes 786440 | tf_op jit(solution)/shard_map/ppermute | solution.py:422
  25.5 34.1 %collective-permute-start.11 = (bf16[2,256,256]{2,1,0:T(8,128)(2,1)S(1)}, bf16[2,256,256]{2,1,0:T(8,128)(2,1)S(1)}, u32[]{:S(2)}, u32[]{:S(2)}) collective-permute-start(bf16[2,256,256]{2,1,0:T(8,128)(2,1)S(1)} %get-tuple-element.35), channel_id=1, source_target_pairs={{0,12},{4,8},{8,4},{12,0},{1,13},{5,9},{9,5},{13,1},{2,14},{6,10},... | collective-permute-start | bytes 786440 | tf_op jit(solution)/shard_map/ppermute | solution.py:422
  43.0 17.4 %collective-permute-start.9 = (bf16[2,3,64,256]{3,2,1,0:T(8,128)(2,1)S(1)}, bf16[2,3,64,256]{3,2,1,0:T(8,128)(2,1)S(1)}, u32[]{:S(2)}, u32[]{:S(2)}) collective-permute-start(bf16[2,3,64,256]{3,2,1,0:T(8,128)(2,1)S(1)} %get-tuple-element.34), channel_id=1, source_target_pairs={{0,2},{2,0},{1,3},{3,1},{4,6},{6,4},{5,7},{7,5},{8,10},{10,8},{9,1... | collective-permute-start | bytes 589832 | tf_op jit(solution)/shard_map/ppermute | solution.py:427
  60.3 1.5 %collective-permute-start.13 = (bf16[2,3,64,256]{3,2,1,0:T(8,128)(2,1)S(1)}, bf16[2,3,64,256]{3,2,1,0:T(8,128)(2,1)S(1)}, u32[]{:S(2)}, u32[]{:S(2)}) collective-permute-start(bf16[2,3,64,256]{3,2,1,0:T(8,128)(2,1)S(1)} %get-tuple-element.38), channel_id=1, source_target_pairs={{0,1},{1,0},{2,3},{3,2},{4,5},{5,4},{6,7},{7,6},{8,9},{9,8},{10,11... | collective-permute-start | bytes 589832 | tf_op jit(solution)/shard_map/ppermute | solution.py:430
  60.4 6.3 %collective-permute-start.10 = (f32[3,64,256]{2,1,0:T(8,128)S(1)}, f32[3,64,256]{2,1,0:T(8,128)S(1)}, u32[]{:S(2)}, u32[]{:S(2)}) collective-permute-start(f32[3,64,256]{2,1,0:T(8,128)S(1)} %add_bitcast_fusion), channel_id=1, source_target_pairs={{0,1},{1,0},{2,3},{3,2},{4,5},{5,4},{6,7},{7,6},{8,9},{9,8},{10,11... | collective-permute-start | bytes 589832 | tf_op jit(solution)/shard_map/ppermute | solution.py:432
  61.8 4.9 %collective-permute-start.14 = (bf16[3,64,256]{2,1,0:T(8,128)(2,1)S(1)}, bf16[3,64,256]{2,1,0:T(8,128)(2,1)S(1)}, u32[]{:S(2)}, u32[]{:S(2)}) collective-permute-start(bf16[3,64,256]{2,1,0:T(8,128)(2,1)S(1)} %fusion), channel_id=1, source_target_pairs={{0,2},{2,0},{1,3},{3,1},{4,6},{6,4},{5,7},{7,5},{8,10},{10,8},{9,1... | collective-permute-start | bytes 294920 | tf_op jit(solution)/shard_map/ppermute | solution.py:431

commit v20 on v18

--- a/solution.py
+++ b/solution.py
@@ -21,6 +21,7 @@
 SPREAD_STEPS = 4
 VMEM_LIMIT = 40 * 1024 * 1024
 LEAD_FLOPS = 1 << 32
+CUT_COPIES = 4
 CUT_LIMIT = 53 * 1024 * 1024 + 256 * 1024
 
 
@@ -114,9 +115,17 @@
 
 
 def cut_kernel(coeffs, direct, sem):
-    copy = pltpu.make_async_copy(coeffs.at[:, pl.ds(0, direct.shape[1])], direct, sem)
-    copy.start()
-    copy.wait()
+    rows, width = direct.shape
+    step = rows // CUT_COPIES
+    copies = []
+    for i in range(CUT_COPIES):
+        part = pl.ds(i * step, step)
+        copies.append(
+            pltpu.make_async_copy(coeffs.at[part, pl.ds(0, width)], direct.at[part], sem.at[i])
+        )
+        copies[-1].start()
+    for copy in copies:
+        copy.wait()
 
 
 def cut(coeffs):
@@ -126,7 +135,7 @@
         out_shape=like((rows, columns // CHUNKS), coeffs.dtype),
         in_specs=[IN_HBM],
         out_specs=IN_VMEM,
-        scratch_shapes=[pltpu.SemaphoreType.DMA],
+        scratch_shapes=[pltpu.SemaphoreType.DMA((CUT_COPIES,))],
         compiler_params=pltpu.CompilerParams(vmem_limit_bytes=CUT_LIMIT),
         cost_estimate=pl.CostEstimate(flops=LEAD_FLOPS, bytes_accessed=0, transcendentals=0),
         name="cut",

time: 68.3 us -> 68.3 us (level)
  no operation moved by 1% of the time
where the time goes in v20:
time: 68.3 us; the launch traced here: 68.2 us
  waiting for transfers between devices  42.3 us (62%)
  starting transfers between devices  19.2 us (28%)
  Pallas kernels  6.38 us (9%)
    ppermute x6, waiting for transfers between devices, fetch(): return [lax.ppermute(piece, 'ao', swap) for piece in blocks[s]]  29.5 us
    ppermute x6, starting transfers between devices, fetch(): return [lax.ppermute(piece, 'ao', swap) for piece in blocks[s]]  7.62 us
    ppermute x2, starting transfers between devices, six_pair_body(): inner = [lax.ppermute(part, 'ao', INSIDE) for part in (parts[0], mine)]  5.84 us
    ppermute x2, waiting for transfers between devices, six_pair_body(): inner = [lax.ppermute(part, 'ao', INSIDE) for part in (parts[0], mine)]  4.55 us
    ppermute x2, waiting for transfers between devices, six_pair_body(): outer = [lax.ppermute(part, 'ao', OUTSIDE) for part in parts]  3.8 us
    ppermute x1, waiting for transfers between devices, six_pair_body(): far1 = lax.ppermute((near1[1] + got1[1]).astype(jnp.bfloat16), 'aux', SWAP)  3.34 us
    ppermute x1, starting transfers between devices, six_pair_body(): swapped = lax.ppermute(inner[1], 'aux', SWAP)  1.56 us
    ppermute x1, starting transfers between devices, six_pair_body(): far0 = lax.ppermute(across0, 'aux', SWAP)  1.55 us
  transfers between devices with their start and end apart: 15, of which 11 were waited for; matrix products, arithmetic and copies ran while one was open for 0% of the time, Pallas kernels for 6%

profile of v20, /device:TPU:8, one launch (start us, length us, event | category | flops | bytes accessed | tf_op | source)
XLA Modules:
  0.0 68.2 jit_solution(9038854743283064695)
XLA Ops:
  0.0 1.0 %cut.1.first.own = bf16[512,256]{1,0:T(8,128)(2,1)S(1)} custom-call(bf16[512,512]{1,0:T(8,128)(2,1)} %coeffs.3), custom_call_target="tpu_custom_call" | custom-call | flops 4294967296 | tf_op jit(solution)/shard_map/cut/pallas_call | solution.py:133
  1.1 3.5 %collective-permute-start.2 = (bf16[512,256]{1,0:T(8,128)(2,1)S(1)}, bf16[512,256]{1,0:T(8,128)(2,1)S(1)}, u32[]{:S(2)}, u32[]{:S(2)}) collective-permute-start(bf16[512,256]{1,0:T(8,128)(2,1)S(1)} %cut.1.first.own), channel_id=1, source_target_pairs={{4,8},{8,4},{5,9},{9,5},{6,10},{10,6},{7,11},{11,7},{20,24},{24,20... | collective-permute-start | bytes 786440 | tf_op jit(solution)/shard_map/ppermute | solution.py:414
  4.7 2.4 %collective-permute-start = (bf16[512,128]{1,0:T(8,128)(2,1)S(1)}, bf16[512,128]{1,0:T(8,128)(2,1)S(1)}, u32[]{:S(2)}, u32[]{:S(2)}) collective-permute-start(bf16[512,128]{1,0:T(8,128)(2,1)S(1)} %get-tuple-element.22), channel_id=1, source_target_pairs={{4,8},{8,4},{5,9},{9,5},{6,10},{10,6},{7,11},{11,7},{20,24},{24,20... | collective-permute-start | bytes 393224 | tf_op jit(solution)/shard_map/ppermute | solution.py:414
  7.6 4.6 %collective-permute-done.2.inner = bf16[512,256]{1,0:T(8,128)(2,1)S(1)} collective-permute-done((bf16[512,256]{1,0:T(8,128)(2,1)S(1)}, bf16[512,256]{1,0:T(8,128)(2,1)S(1)}, u32[]{:S(2)}, u32[]{:S(2)}) %collective-permute-start.2) | collective-permute-done | bytes 262176 | tf_op jit(solution)/shard_map/ppermute | solution.py:414
  12.1 1.7 %collective-permute-done.1.outer = bf16[512,256]{1,0:T(8,128)(2,1)S(1)} collective-permute-done((bf16[512,256]{1,0:T(8,128)(2,1)S(1)}, bf16[512,256]{1,0:T(8,128)(2,1)S(1)}, u32[]{:S(2)}, u32[]{:S(2)}) %collective-permute-start.1) | collective-permute-done | bytes 262176 | tf_op jit(solution)/shard_map/ppermute | solution.py:415
  13.9 0.9 %transform.2 = (bf16[2,256,256]{2,1,0:T(8,128)(2,1)S(1)}, bf16[2,256,256]{2,1,0:T(8,128)(2,1)S(1)}, bf16[2,256,256]{2,1,0:T(8,128)(2,1)S(1)}, bf16[2,256,256]{2,1,0:T(8,128)(2,1)S(1)}) custom-call(s32[8,256]{1,0:T(8,128)S(1)} %tables.1.wants, bf16[2,512,1280]{2,1,0:T(8,128)(2,1)S(1)} %copy-done, bf16[512,256]{1,0:T(8,128)(2,1)S(1)} %cut.1.first.own, ...), custom_call_target="tpu_custom_call" | custom-call | flops 671088640 | bytes 2097152 | tf_op jit(solution)/shard_map/transform/pallas_call | solution.py:233
  14.8 1.6 %collective-permute-start.4 = (bf16[512,128]{1,0:T(8,128)(2,1)S(1)}, bf16[512,128]{1,0:T(8,128)(2,1)S(1)}, u32[]{:S(2)}, u32[]{:S(2)}) collective-permute-start(bf16[512,128]{1,0:T(8,128)(2,1)S(1)} %collective-permute-done.inner), channel_id=1, source_target_pairs={{0,2},{2,0},{1,3},{3,1},{4,6},{6,4},{5,7},{7,5},{8,10},{10,8},{9,1... | collective-permute-start | bytes 393224 | tf_op jit(solution)/shard_map/ppermute | solution.py:421
  16.4 1.8 %collective-permute-start.7 = (bf16[2,256,256]{2,1,0:T(8,128)(2,1)S(1)}, bf16[2,256,256]{2,1,0:T(8,128)(2,1)S(1)}, u32[]{:S(2)}, u32[]{:S(2)}) collective-permute-start(bf16[2,256,256]{2,1,0:T(8,128)(2,1)S(1)} %get-tuple-element.30), channel_id=1, source_target_pairs={{0,4},{4,0},{8,12},{12,8},{1,5},{5,1},{9,13},{13,9},{2,6},{6,2},{1... | collective-permute-start | bytes 786440 | tf_op jit(solution)/shard_map/ppermute | solution.py:430
  18.2 2.1 %collective-permute-done.3.outer = bf16[512,256]{1,0:T(8,128)(2,1)S(1)} collective-permute-done((bf16[512,256]{1,0:T(8,128)(2,1)S(1)}, bf16[512,256]{1,0:T(8,128)(2,1)S(1)}, u32[]{:S(2)}, u32[]{:S(2)}) %collective-permute-start.3) | collective-permute-done | bytes 262176 | tf_op jit(solution)/shard_map/ppermute | solution.py:415
  20.3 0.9 %transform.3 = (bf16[2,256,256]{2,1,0:T(8,128)(2,1)S(1)}, bf16[2,256,256]{2,1,0:T(8,128)(2,1)S(1)}, bf16[2,256,256]{2,1,0:T(8,128)(2,1)S(1)}, bf16[2,256,256]{2,1,0:T(8,128)(2,1)S(1)}) custom-call(s32[8,256]{1,0:T(8,128)S(1)} %tables.1.wants, bf16[2,512,1280]{2,1,0:T(8,128)(2,1)S(1)} %copy-done, bf16[512,256]{1,0:T(8,128)(2,1)S(1)} %get-tuple-element.25.own, ...), custom_call_target="tpu_custom_call" | custom-call | flops 671088640 | bytes 2097152 | tf_op jit(solution)/shard_map/transform/pallas_call | solution.py:221
  21.2 3.2 %collective-permute-start.6 = (bf16[2,256,256]{2,1,0:T(8,128)(2,1)S(1)}, bf16[2,256,256]{2,1,0:T(8,128)(2,1)S(1)}, u32[]{:S(2)}, u32[]{:S(2)}) collective-permute-start(bf16[2,256,256]{2,1,0:T(8,128)(2,1)S(1)} %get-tuple-element.29), channel_id=1, source_target_pairs={{0,8},{4,12},{8,0},{12,4},{1,9},{5,13},{9,1},{13,5},{2,10},{6,14},... | collective-permute-start | bytes 786440 | tf_op jit(solution)/shard_map/ppermute | solution.py:430
  24.5 0.8 %collective-permute-start.12 = (bf16[2,256,256]{2,1,0:T(8,128)(2,1)S(1)}, bf16[2,256,256]{2,1,0:T(8,128)(2,1)S(1)}, u32[]{:S(2)}, u32[]{:S(2)}) collective-permute-start(bf16[2,256,256]{2,1,0:T(8,128)(2,1)S(1)} %get-tuple-element.36), channel_id=1, source_target_pairs={{0,12},{4,8},{8,4},{12,0},{1,13},{5,9},{9,5},{13,1},{2,14},{6,10},... | collective-permute-start | bytes 786440 | tf_op jit(solution)/shard_map/ppermute | solution.py:430
  25.5 1.7 %collective-permute-start.11 = (bf16[2,256,256]{2,1,0:T(8,128)(2,1)S(1)}, bf16[2,256,256]{2,1,0:T(8,128)(2,1)S(1)}, u32[]{:S(2)}, u32[]{:S(2)}) collective-permute-start(bf16[2,256,256]{2,1,0:T(8,128)(2,1)S(1)} %get-tuple-element.35), channel_id=1, source_target_pairs={{0,12},{4,8},{8,4},{12,0},{1,13},{5,9},{9,5},{13,1},{2,14},{6,10},... | collective-permute-start | bytes 786440 | tf_op jit(solution)/shard_map/ppermute | solution.py:430
  27.2 4.3 %collective-permute-done.7.refs_4_.next_to = bf16[2,256,256]{2,1,0:T(8,128)(2,1)S(1)} collective-permute-done((bf16[2,256,256]{2,1,0:T(8,128)(2,1)S(1)}, bf16[2,256,256]{2,1,0:T(8,128)(2,1)S(1)}, u32[]{:S(2)}, u32[]{:S(2)}) %collective-permute-start.7) | collective-permute-done | bytes 262176 | tf_op jit(solution)/shard_map/ppermute | solution.py:430
  31.5 5.3 %collective-permute-done.6.refs_3_.middle = bf16[2,256,256]{2,1,0:T(8,128)(2,1)S(1)} collective-permute-done((bf16[2,256,256]{2,1,0:T(8,128)(2,1)S(1)}, bf16[2,256,256]{2,1,0:T(8,128)(2,1)S(1)}, u32[]{:S(2)}, u32[]{:S(2)}) %collective-permute-start.6) | collective-permute-done | bytes 262176 | tf_op jit(solution)/shard_map/ppermute | solution.py:430
  36.8 5.2 %collective-permute-done.8.refs_5_.next_to = bf16[2,256,256]{2,1,0:T(8,128)(2,1)S(1)} collective-permute-done((bf16[2,256,256]{2,1,0:T(8,128)(2,1)S(1)}, bf16[2,256,256]{2,1,0:T(8,128)(2,1)S(1)}, u32[]{:S(2)}, u32[]{:S(2)}) %collective-permute-start.8) | collective-permute-done | bytes 262176 | tf_op jit(solution)/shard_map/ppermute | solution.py:430
  42.0 1.0 %early_pairs.1 = (f32[2,3,64,256]{3,2,1,0:T(8,128)S(1)}, bf16[2,3,64,256]{3,2,1,0:T(8,128)(2,1)S(1)}, s32[16,256]{1,0:T(8,128)S(1)}) custom-call(s32[1,4]{1,0:T(1,128)S(1)} %bitcast.9, s32[2,64]{1,0:T(2,128)S(1)} %bitcast.8, bf16[2,256,256]{2,1,0:T(8,128)(2,1)S(1)} %get-tuple-element.24.refs_0_.own, bf16[2,256,256]{2,1,0:T(8,128)(2,1)S(1)} %get-tuple-element.27.refs_1_.own, ...), custom_call_target="tpu_custom_call" | custom-call | flops 402653184 | bytes 1212416 | tf_op jit(solution)/shard_map/early_pairs/pallas_call | solution.py:328
  43.0 1.6 %collective-permute-start.9 = (bf16[2,3,64,256]{3,2,1,0:T(8,128)(2,1)S(1)}, bf16[2,3,64,256]{3,2,1,0:T(8,128)(2,1)S(1)}, u32[]{:S(2)}, u32[]{:S(2)}) collective-permute-start(bf16[2,3,64,256]{3,2,1,0:T(8,128)(2,1)S(1)} %get-tuple-element.34), channel_id=1, source_target_pairs={{0,2},{2,0},{1,3},{3,1},{4,6},{6,4},{5,7},{7,5},{8,10},{10,8},{9,1... | collective-permute-start | bytes 589832 | tf_op jit(solution)/shard_map/ppermute | solution.py:435
  44.6 11.2 %collective-permute-done.12.last = bf16[2,256,256]{2,1,0:T(8,128)(2,1)S(1)} collective-permute-done((bf16[2,256,256]{2,1,0:T(8,128)(2,1)S(1)}, bf16[2,256,256]{2,1,0:T(8,128)(2,1)S(1)}, u32[]{:S(2)}, u32[]{:S(2)}) %collective-permute-start.12) | collective-permute-done | bytes 262176 | tf_op jit(solution)/shard_map/ppermute | solution.py:430
  56.4 3.3 %collective-permute-done.11.last = bf16[2,256,256]{2,1,0:T(8,128)(2,1)S(1)} collective-permute-done((bf16[2,256,256]{2,1,0:T(8,128)(2,1)S(1)}, bf16[2,256,256]{2,1,0:T(8,128)(2,1)S(1)}, u32[]{:S(2)}, u32[]{:S(2)}) %collective-permute-start.11) | collective-permute-done | bytes 262176 | tf_op jit(solution)/shard_map/ppermute | solution.py:430
  61.0 1.1 %collective-permute-done.13.got1 = f32[2,3,64,256]{3,2,1,0:T(8,128)S(1)} collective-permute-done((f32[2,3,64,256]{3,2,1,0:T(8,128)S(1)}, f32[2,3,64,256]{3,2,1,0:T(8,128)S(1)}, u32[]{:S(2)}, u32[]{:S(2)}) %collective-permute-start.13) | collective-permute-done | bytes 393248 | tf_op jit(solution)/shard_map/ppermute | solution.py:438
  62.1 1.6 %collective-permute-start.14 = (bf16[3,64,256]{2,1,0:T(8,128)(2,1)S(1)}, bf16[3,64,256]{2,1,0:T(8,128)(2,1)S(1)}, u32[]{:S(2)}, u32[]{:S(2)}) collective-permute-start(bf16[3,64,256]{2,1,0:T(8,128)(2,1)S(1)} %fusion.1), channel_id=1, source_target_pairs={{0,2},{2,0},{1,3},{3,1},{4,6},{6,4},{5,7},{7,5},{8,10},{10,8},{9,1... | collective-permute-start | bytes 294920 | tf_op jit(solution)/shard_map/ppermute | solution.py:439
  63.7 3.3 %collective-permute-done.14.far1 = bf16[3,64,256]{2,1,0:T(8,128)(2,1)S(1)} collective-permute-done((bf16[3,64,256]{2,1,0:T(8,128)(2,1)S(1)}, bf16[3,64,256]{2,1,0:T(8,128)(2,1)S(1)}, u32[]{:S(2)}, u32[]{:S(2)}) %collective-permute-start.14) | collective-permute-done | bytes 98336 | tf_op jit(solution)/shard_map/ppermute | solution.py:439
  67.0 1.2 %spread.1 = f32[64,16,256]{2,1,0:T(8,128)} custom-call(s32[16,256]{1,0:T(8,128)S(1)} %get-tuple-element.32.place, f32[2,3,64,256]{3,2,1,0:T(8,128)S(1)} %get-tuple-element.33.near0, bf16[2,3,64,256]{3,2,1,0:T(8,128)(2,1)S(1)} %collective-permute-done.9.far0, f32[3,64,256]{2,1,0:T(8,128)S(1)} %collective-permute-done.10.got0, ...), custom_call_target="tpu_custom_call" | custom-call | flops 1572864 | bytes 2097152 | tf_op jit(solution)/shard_map/spread/pallas_call | solution.py:391
  (27 shorter events, 2.9 us)
Async XLA Ops:
  0.0 4.6 %copy-start.3 = (bf16[512,512]{1,0:T(8,128)(2,1)S(1)}, bf16[512,512]{1,0:T(8,128)(2,1)}, u32[]{:S(2)}) copy-start(bf16[512,512]{1,0:T(8,128)(2,1)} %coeffs.3) | copy-start | bytes 1572868
  1.0 6.4 %copy-start.1 = (s32[64,2]{0,1:T(2,128)S(1)}, s32[64,2]{0,1:T(2,128)}, u32[]{:S(2)}) copy-start(s32[64,2]{0,1:T(2,128)} %param.7) | copy-start | bytes 1540
  1.0 6.4 %copy-start.4 = (s32[8]{0:T(128)S(1)}, s32[8]{0:T(128)}, u32[]{:S(2)}) copy-start(s32[8]{0:T(128)} %param.9) | copy-start | bytes 100
  1.1 11.1 %collective-permute-start.2 = (bf16[512,256]{1,0:T(8,128)(2,1)S(1)}, bf16[512,256]{1,0:T(8,128)(2,1)S(1)}, u32[]{:S(2)}, u32[]{:S(2)}) collective-permute-start(bf16[512,256]{1,0:T(8,128)(2,1)S(1)} %cut.1.first.own), channel_id=1, source_target_pairs={{4,8},{8,4},{5,9},{9,5},{6,10},{10,6},{7,11},{11,7},{20,24},{24,20... | collective-permute-start | bytes 786440 | tf_op jit(solution)/shard_map/ppermute | solution.py:414
  4.6 9.3 %collective-permute-start.1 = (bf16[512,256]{1,0:T(8,128)(2,1)S(1)}, bf16[512,256]{1,0:T(8,128)(2,1)S(1)}, u32[]{:S(2)}, u32[]{:S(2)}) collective-permute-start(bf16[512,256]{1,0:T(8,128)(2,1)S(1)} %cut.1.first.own), channel_id=1, source_target_pairs={{0,4},{4,0},{8,12},{12,8},{1,5},{5,1},{9,13},{13,9},{2,6},{6,2},{1... | collective-permute-start | bytes 786440 | tf_op jit(solution)/shard_map/ppermute | solution.py:415
  4.7 10.1 %collective-permute-start = (bf16[512,128]{1,0:T(8,128)(2,1)S(1)}, bf16[512,128]{1,0:T(8,128)(2,1)S(1)}, u32[]{:S(2)}, u32[]{:S(2)}) collective-permute-start(bf16[512,128]{1,0:T(8,128)(2,1)S(1)} %get-tuple-element.22), channel_id=1, source_target_pairs={{4,8},{8,4},{5,9},{9,5},{6,10},{10,6},{7,11},{11,7},{20,24},{24,20... | collective-permute-start | bytes 393224 | tf_op jit(solution)/shard_map/ppermute | solution.py:414
  7.1 13.2 %collective-permute-start.3 = (bf16[512,256]{1,0:T(8,128)(2,1)S(1)}, bf16[512,256]{1,0:T(8,128)(2,1)S(1)}, u32[]{:S(2)}, u32[]{:S(2)}) collective-permute-start(bf16[512,256]{1,0:T(8,128)(2,1)S(1)} %get-tuple-element.25.own), channel_id=1, source_target_pairs={{0,4},{4,0},{8,12},{12,8},{1,5},{5,1},{9,13},{13,9},{2,6},{6,2},{1... | collective-permute-start | bytes 786440 | tf_op jit(solution)/shard_map/ppermute | solution.py:415
  7.4 6.4 %copy-start = (bf16[2,512,1280]{2,1,0:T(8,128)(2,1)S(1)}, bf16[2,512,1280]{2,1,0:T(8,128)(2,1)}, u32[]{:S(2)}) copy-start(bf16[2,512,1280]{2,1,0:T(8,128)(2,1)} %integrals.3) | copy-start | bytes 7864324
  7.6 34.4 %copy-start.2 = (s32[4]{0:T(128)S(1)}, s32[4]{0:T(128)}, u32[]{:S(2)}) copy-start(s32[4]{0:T(128)} %param.8) | copy-start | bytes 52
  14.7 10.8 %collective-permute-start.5 = (bf16[2,256,256]{2,1,0:T(8,128)(2,1)S(1)}, bf16[2,256,256]{2,1,0:T(8,128)(2,1)S(1)}, u32[]{:S(2)}, u32[]{:S(2)}) collective-permute-start(bf16[2,256,256]{2,1,0:T(8,128)(2,1)S(1)} %get-tuple-element.28), channel_id=1, source_target_pairs={{0,8},{4,12},{8,0},{12,4},{1,9},{5,13},{9,1},{13,5},{2,10},{6,14},... | collective-permute-start | bytes 786440 | tf_op jit(solution)/shard_map/ppermute | solution.py:430
  14.8 5.5 %collective-permute-start.4 = (bf16[512,128]{1,0:T(8,128)(2,1)S(1)}, bf16[512,128]{1,0:T(8,128)(2,1)S(1)}, u32[]{:S(2)}, u32[]{:S(2)}) collective-permute-start(bf16[512,128]{1,0:T(8,128)(2,1)S(1)} %collective-permute-done.inner), channel_id=1, source_target_pairs={{0,2},{2,0},{1,3},{3,1},{4,6},{6,4},{5,7},{7,5},{8,10},{10,8},{9,1... | collective-permute-start | bytes 393224 | tf_op jit(solution)/shard_map/ppermute | solution.py:421
  16.4 15.2 %collective-permute-start.7 = (bf16[2,256,256]{2,1,0:T(8,128)(2,1)S(1)}, bf16[2,256,256]{2,1,0:T(8,128)(2,1)S(1)}, u32[]{:S(2)}, u32[]{:S(2)}) collective-permute-start(bf16[2,256,256]{2,1,0:T(8,128)(2,1)S(1)} %get-tuple-element.30), channel_id=1, source_target_pairs={{0,4},{4,0},{8,12},{12,8},{1,5},{5,1},{9,13},{13,9},{2,6},{6,2},{1... | collective-permute-start | bytes 786440 | tf_op jit(solution)/shard_map/ppermute | solution.py:430
  21.2 15.6 %collective-permute-start.6 = (bf16[2,256,256]{2,1,0:T(8,128)(2,1)S(1)}, bf16[2,256,256]{2,1,0:T(8,128)(2,1)S(1)}, u32[]{:S(2)}, u32[]{:S(2)}) collective-permute-start(bf16[2,256,256]{2,1,0:T(8,128)(2,1)S(1)} %get-tuple-element.29), channel_id=1, source_target_pairs={{0,8},{4,12},{8,0},{12,4},{1,9},{5,13},{9,1},{13,5},{2,10},{6,14},... | collective-permute-start | bytes 786440 | tf_op jit(solution)/shard_map/ppermute | solution.py:430
  24.5 17.6 %collective-permute-start.8 = (bf16[2,256,256]{2,1,0:T(8,128)(2,1)S(1)}, bf16[2,256,256]{2,1,0:T(8,128)(2,1)S(1)}, u32[]{:S(2)}, u32[]{:S(2)}) collective-permute-start(bf16[2,256,256]{2,1,0:T(8,128)(2,1)S(1)} %get-tuple-element.31), channel_id=1, source_target_pairs={{0,4},{4,0},{8,12},{12,8},{1,5},{5,1},{9,13},{13,9},{2,6},{6,2},{1... | collective-permute-start | bytes 786440 | tf_op jit(solution)/shard_map/ppermute | solution.py:430
  24.5 31.3 %collective-permute-start.12 = (bf16[2,256,256]{2,1,0:T(8,128)(2,1)S(1)}, bf16[2,256,256]{2,1,0:T(8,128)(2,1)S(1)}, u32[]{:S(2)}, u32[]{:S(2)}) collective-permute-start(bf16[2,256,256]{2,1,0:T(8,128)(2,1)S(1)} %get-tuple-element.36), channel_id=1, source_target_pairs={{0,12},{4,8},{8,4},{12,0},{1,13},{5,9},{9,5},{13,1},{2,14},{6,10},... | collective-permute-start | bytes 786440 | tf_op jit(solution)/shard_map/ppermute | solution.py:430
  25.5 34.1 %collective-permute-start.11 = (bf16[2,256,256]{2,1,0:T(8,128)(2,1)S(1)}, bf16[2,256,256]{2,1,0:T(8,128)(2,1)S(1)}, u32[]{:S(2)}, u32[]{:S(2)}) collective-permute-start(bf16[2,256,256]{2,1,0:T(8,128)(2,1)S(1)} %get-tuple-element.35), channel_id=1, source_target_pairs={{0,12},{4,8},{8,4},{12,0},{1,13},{5,9},{9,5},{13,1},{2,14},{6,10},... | collective-permute-start | bytes 786440 | tf_op jit(solution)/shard_map/ppermute | solution.py:430
  43.0 17.4 %collective-permute-start.9 = (bf16[2,3,64,256]{3,2,1,0:T(8,128)(2,1)S(1)}, bf16[2,3,64,256]{3,2,1,0:T(8,128)(2,1)S(1)}, u32[]{:S(2)}, u32[]{:S(2)}) collective-permute-start(bf16[2,3,64,256]{3,2,1,0:T(8,128)(2,1)S(1)} %get-tuple-element.34), channel_id=1, source_target_pairs={{0,2},{2,0},{1,3},{3,1},{4,6},{6,4},{5,7},{7,5},{8,10},{10,8},{9,1... | collective-permute-start | bytes 589832 | tf_op jit(solution)/shard_map/ppermute | solution.py:435
  60.3 1.8 %collective-permute-start.13 = (f32[2,3,64,256]{3,2,1,0:T(8,128)S(1)}, f32[2,3,64,256]{3,2,1,0:T(8,128)S(1)}, u32[]{:S(2)}, u32[]{:S(2)}) collective-permute-start(f32[2,3,64,256]{3,2,1,0:T(8,128)S(1)} %get-tuple-element.38), channel_id=1, source_target_pairs={{0,1},{1,0},{2,3},{3,2},{4,5},{5,4},{6,7},{7,6},{8,9},{9,8},{10,11... | collective-permute-start | bytes 1179656 | tf_op jit(solution)/shard_map/ppermute | solution.py:438
  60.4 3.3 %collective-permute-start.10 = (f32[3,64,256]{2,1,0:T(8,128)S(1)}, f32[3,64,256]{2,1,0:T(8,128)S(1)}, u32[]{:S(2)}, u32[]{:S(2)}) collective-permute-start(f32[3,64,256]{2,1,0:T(8,128)S(1)} %add_bitcast_fusion), channel_id=1, source_target_pairs={{0,1},{1,0},{2,3},{3,2},{4,5},{5,4},{6,7},{7,6},{8,9},{9,8},{10,11... | collective-permute-start | bytes 589832 | tf_op jit(solution)/shard_map/ppermute | solution.py:440
  62.1 4.9 %collective-permute-start.14 = (bf16[3,64,256]{2,1,0:T(8,128)(2,1)S(1)}, bf16[3,64,256]{2,1,0:T(8,128)(2,1)S(1)}, u32[]{:S(2)}, u32[]{:S(2)}) collective-permute-start(bf16[3,64,256]{2,1,0:T(8,128)(2,1)S(1)} %fusion.1), channel_id=1, source_target_pairs={{0,2},{2,0},{1,3},{3,1},{4,6},{6,4},{5,7},{7,5},{8,10},{10,8},{9,1... | collective-permute-start | bytes 294920 | tf_op jit(solution)/shard_map/ppermute | solution.py:439

commit v21 on v20

--- a/solution.py
+++ b/solution.py
@@ -21,6 +21,7 @@
 SPREAD_STEPS = 4
 VMEM_LIMIT = 40 * 1024 * 1024
 LEAD_FLOPS = 1 << 32
+LATE_WEIGHT = 10
 CUT_COPIES = 4
 CUT_LIMIT = 53 * 1024 * 1024 + 256 * 1024
 
@@ -311,7 +312,7 @@
         for chip in (0, 1):
             row = 2 * (aux ^ chip)
             keep[chip, k] = grams[k, row + orb]
-            give[chip, k] = grams[k, row + 1 - orb]
+            give[chip, k] = grams[k, row + 1 - orb].astype(jnp.bfloat16)
 
 
 def pair_flops(pairs, blocks):
@@ -352,9 +353,9 @@
     return local_call(
         late_kernel,
         "late_pairs",
-        [like(shape, jnp.float32)] * 2,
+        [like(shape, jnp.float32), like(shape, jnp.bfloat16)],
         GROUPS + 1,
-        pair_flops(LATE_PAIRS, blocks) // CHUNKS,
+        LATE_WEIGHT * pair_flops(LATE_PAIRS, blocks) // CHUNKS,
         [grams],
     )(own[1], middle[1], next_to[1], last[1], *begun)
 
@@ -362,7 +363,7 @@
 def spread_kernel(factor, place, near0, far0, got0, near1, got1, far1, out, sums, rows, sems):
     early = near0.shape[1]
     sums[:early] = (near0[0] + far0[0].astype(jnp.float32) + got0[...]) * factor
-    sums[early:] = (near1[0] + got1[0] + far1[...].astype(jnp.float32)) * factor
+    sums[early:] = (near1[0] + got1[0].astype(jnp.float32) + far1[...].astype(jnp.float32)) * factor
     total, slots, width = out.shape
     masks = [place[...] == k for k in range(sums.shape[0])]
 
@@ -436,7 +437,7 @@
     got.append(fetch(3))
     near1, give1 = late_pairs(got)
     got1 = lax.ppermute(give1, "orb", SWAP)
-    far1 = lax.ppermute((near1[1] + got1[1]).astype(jnp.bfloat16), "aux", SWAP)
+    far1 = lax.ppermute((near1[1] + got1[1].astype(jnp.float32)).astype(jnp.bfloat16), "aux", SWAP)
     got0 = lax.ppermute(near0[1] + far0[1].astype(jnp.float32), "orb", SWAP)
     factor = 1.0 / math.sqrt(total_aux * ORBS)
     return spread(factor, place, near0, far0, got0, near1, got1, far1)

time: 68.3 us -> 68.1 us (level)
  no operation moved by 1% of the time
where the time goes in v21:
time: 68.1 us; the launch traced here: 67.9 us
  waiting for transfers between devices  42.1 us (62%)
  starting transfers between devices  19.2 us (28%)
  Pallas kernels  6.38 us (9%)
    ppermute x6, waiting for transfers between devices, fetch(): return [lax.ppermute(piece, 'ao', swap) for piece in blocks[s]]  29.5 us
    ppermute x6, starting transfers between devices, fetch(): return [lax.ppermute(piece, 'ao', swap) for piece in blocks[s]]  7.62 us
    ppermute x2, starting transfers between devices, six_pair_body(): inner = [lax.ppermute(part, 'ao', INSIDE) for part in (parts[0], mine)]  5.84 us
    ppermute x2, waiting for transfers between devices, six_pair_body(): inner = [lax.ppermute(part, 'ao', INSIDE) for part in (parts[0], mine)]  4.55 us
    ppermute x2, waiting for transfers between devices, six_pair_body(): outer = [lax.ppermute(part, 'ao', OUTSIDE) for part in parts]  3.8 us
    ppermute x1, waiting for transfers between devices, six_pair_body(): lax.ppermute((near1[1] + got1[1].astype(jnp.float32)).astype(jnp.bfloat16...  3.35 us
    ppermute x1, starting transfers between devices, six_pair_body(): swapped = lax.ppermute(inner[1], 'aux', SWAP)  1.56 us
    ppermute x1, starting transfers between devices, six_pair_body(): lax.ppermute((near1[1] + got1[1].astype(jnp.float32)).astype(jnp.bfloat16...  1.56 us
  transfers between devices with their start and end apart: 15, of which 11 were waited for; matrix products, arithmetic and copies ran while one was open for 0% of the time, Pallas kernels for 6%

profile of v21, /device:TPU:8, one launch (start us, length us, event | category | flops | bytes accessed | tf_op | source)
XLA Modules:
  0.0 67.9 jit_solution(2601604661913349491)
XLA Ops:
  0.0 1.0 %cut.1.first.own = bf16[512,256]{1,0:T(8,128)(2,1)S(1)} custom-call(bf16[512,512]{1,0:T(8,128)(2,1)} %coeffs.3), custom_call_target="tpu_custom_call" | custom-call | flops 4294967296 | tf_op jit(solution)/shard_map/cut/pallas_call | solution.py:134
  1.1 3.5 %collective-permute-start.2 = (bf16[512,256]{1,0:T(8,128)(2,1)S(1)}, bf16[512,256]{1,0:T(8,128)(2,1)S(1)}, u32[]{:S(2)}, u32[]{:S(2)}) collective-permute-start(bf16[512,256]{1,0:T(8,128)(2,1)S(1)} %cut.1.first.own), channel_id=1, source_target_pairs={{4,8},{8,4},{5,9},{9,5},{6,10},{10,6},{7,11},{11,7},{20,24},{24,20... | collective-permute-start | bytes 786440 | tf_op jit(solution)/shard_map/ppermute | solution.py:415
  4.7 2.4 %collective-permute-start = (bf16[512,128]{1,0:T(8,128)(2,1)S(1)}, bf16[512,128]{1,0:T(8,128)(2,1)S(1)}, u32[]{:S(2)}, u32[]{:S(2)}) collective-permute-start(bf16[512,128]{1,0:T(8,128)(2,1)S(1)} %get-tuple-element.22), channel_id=1, source_target_pairs={{4,8},{8,4},{5,9},{9,5},{6,10},{10,6},{7,11},{11,7},{20,24},{24,20... | collective-permute-start | bytes 393224 | tf_op jit(solution)/shard_map/ppermute | solution.py:415
  7.6 4.6 %collective-permute-done.2.inner = bf16[512,256]{1,0:T(8,128)(2,1)S(1)} collective-permute-done((bf16[512,256]{1,0:T(8,128)(2,1)S(1)}, bf16[512,256]{1,0:T(8,128)(2,1)S(1)}, u32[]{:S(2)}, u32[]{:S(2)}) %collective-permute-start.2) | collective-permute-done | bytes 262176 | tf_op jit(solution)/shard_map/ppermute | solution.py:415
  12.1 1.7 %collective-permute-done.1.outer = bf16[512,256]{1,0:T(8,128)(2,1)S(1)} collective-permute-done((bf16[512,256]{1,0:T(8,128)(2,1)S(1)}, bf16[512,256]{1,0:T(8,128)(2,1)S(1)}, u32[]{:S(2)}, u32[]{:S(2)}) %collective-permute-start.1) | collective-permute-done | bytes 262176 | tf_op jit(solution)/shard_map/ppermute | solution.py:416
  13.9 0.9 %transform.2 = (bf16[2,256,256]{2,1,0:T(8,128)(2,1)S(1)}, bf16[2,256,256]{2,1,0:T(8,128)(2,1)S(1)}, bf16[2,256,256]{2,1,0:T(8,128)(2,1)S(1)}, bf16[2,256,256]{2,1,0:T(8,128)(2,1)S(1)}) custom-call(s32[8,256]{1,0:T(8,128)S(1)} %tables.1.wants, bf16[2,512,1280]{2,1,0:T(8,128)(2,1)S(1)} %copy-done, bf16[512,256]{1,0:T(8,128)(2,1)S(1)} %cut.1.first.own, ...), custom_call_target="tpu_custom_call" | custom-call | flops 671088640 | bytes 2097152 | tf_op jit(solution)/shard_map/transform/pallas_call | solution.py:234
  14.8 1.6 %collective-permute-start.4 = (bf16[512,128]{1,0:T(8,128)(2,1)S(1)}, bf16[512,128]{1,0:T(8,128)(2,1)S(1)}, u32[]{:S(2)}, u32[]{:S(2)}) collective-permute-start(bf16[512,128]{1,0:T(8,128)(2,1)S(1)} %collective-permute-done.inner), channel_id=1, source_target_pairs={{0,2},{2,0},{1,3},{3,1},{4,6},{6,4},{5,7},{7,5},{8,10},{10,8},{9,1... | collective-permute-start | bytes 393224 | tf_op jit(solution)/shard_map/ppermute | solution.py:422
  16.4 1.8 %collective-permute-start.7 = (bf16[2,256,256]{2,1,0:T(8,128)(2,1)S(1)}, bf16[2,256,256]{2,1,0:T(8,128)(2,1)S(1)}, u32[]{:S(2)}, u32[]{:S(2)}) collective-permute-start(bf16[2,256,256]{2,1,0:T(8,128)(2,1)S(1)} %get-tuple-element.30), channel_id=1, source_target_pairs={{0,4},{4,0},{8,12},{12,8},{1,5},{5,1},{9,13},{13,9},{2,6},{6,2},{1... | collective-permute-start | bytes 786440 | tf_op jit(solution)/shard_map/ppermute | solution.py:431
  18.2 2.1 %collective-permute-done.3.outer = bf16[512,256]{1,0:T(8,128)(2,1)S(1)} collective-permute-done((bf16[512,256]{1,0:T(8,128)(2,1)S(1)}, bf16[512,256]{1,0:T(8,128)(2,1)S(1)}, u32[]{:S(2)}, u32[]{:S(2)}) %collective-permute-start.3) | collective-permute-done | bytes 262176 | tf_op jit(solution)/shard_map/ppermute | solution.py:416
  20.3 0.9 %transform.3 = (bf16[2,256,256]{2,1,0:T(8,128)(2,1)S(1)}, bf16[2,256,256]{2,1,0:T(8,128)(2,1)S(1)}, bf16[2,256,256]{2,1,0:T(8,128)(2,1)S(1)}, bf16[2,256,256]{2,1,0:T(8,128)(2,1)S(1)}) custom-call(s32[8,256]{1,0:T(8,128)S(1)} %tables.1.wants, bf16[2,512,1280]{2,1,0:T(8,128)(2,1)S(1)} %copy-done, bf16[512,256]{1,0:T(8,128)(2,1)S(1)} %get-tuple-element.25.own, ...), custom_call_target="tpu_custom_call" | custom-call | flops 671088640 | bytes 2097152 | tf_op jit(solution)/shard_map/transform/pallas_call | solution.py:222
  21.2 3.2 %collective-permute-start.6 = (bf16[2,256,256]{2,1,0:T(8,128)(2,1)S(1)}, bf16[2,256,256]{2,1,0:T(8,128)(2,1)S(1)}, u32[]{:S(2)}, u32[]{:S(2)}) collective-permute-start(bf16[2,256,256]{2,1,0:T(8,128)(2,1)S(1)} %get-tuple-element.29), channel_id=1, source_target_pairs={{0,8},{4,12},{8,0},{12,4},{1,9},{5,13},{9,1},{13,5},{2,10},{6,14},... | collective-permute-start | bytes 786440 | tf_op jit(solution)/shard_map/ppermute | solution.py:431
  24.5 0.8 %collective-permute-start.12 = (bf16[2,256,256]{2,1,0:T(8,128)(2,1)S(1)}, bf16[2,256,256]{2,1,0:T(8,128)(2,1)S(1)}, u32[]{:S(2)}, u32[]{:S(2)}) collective-permute-start(bf16[2,256,256]{2,1,0:T(8,128)(2,1)S(1)} %get-tuple-element.36), channel_id=1, source_target_pairs={{0,12},{4,8},{8,4},{12,0},{1,13},{5,9},{9,5},{13,1},{2,14},{6,10},... | collective-permute-start | bytes 786440 | tf_op jit(solution)/shard_map/ppermute | solution.py:431
  25.5 1.7 %collective-permute-start.11 = (bf16[2,256,256]{2,1,0:T(8,128)(2,1)S(1)}, bf16[2,256,256]{2,1,0:T(8,128)(2,1)S(1)}, u32[]{:S(2)}, u32[]{:S(2)}) collective-permute-start(bf16[2,256,256]{2,1,0:T(8,128)(2,1)S(1)} %get-tuple-element.35), channel_id=1, source_target_pairs={{0,12},{4,8},{8,4},{12,0},{1,13},{5,9},{9,5},{13,1},{2,14},{6,10},... | collective-permute-start | bytes 786440 | tf_op jit(solution)/shard_map/ppermute | solution.py:431
  27.2 4.3 %collective-permute-done.7.refs_4_.next_to = bf16[2,256,256]{2,1,0:T(8,128)(2,1)S(1)} collective-permute-done((bf16[2,256,256]{2,1,0:T(8,128)(2,1)S(1)}, bf16[2,256,256]{2,1,0:T(8,128)(2,1)S(1)}, u32[]{:S(2)}, u32[]{:S(2)}) %collective-permute-start.7) | collective-permute-done | bytes 262176 | tf_op jit(solution)/shard_map/ppermute | solution.py:431
  31.5 5.3 %collective-permute-done.6.refs_3_.middle = bf16[2,256,256]{2,1,0:T(8,128)(2,1)S(1)} collective-permute-done((bf16[2,256,256]{2,1,0:T(8,128)(2,1)S(1)}, bf16[2,256,256]{2,1,0:T(8,128)(2,1)S(1)}, u32[]{:S(2)}, u32[]{:S(2)}) %collective-permute-start.6) | collective-permute-done | bytes 262176 | tf_op jit(solution)/shard_map/ppermute | solution.py:431
  36.8 5.2 %collective-permute-done.8.refs_5_.next_to = bf16[2,256,256]{2,1,0:T(8,128)(2,1)S(1)} collective-permute-done((bf16[2,256,256]{2,1,0:T(8,128)(2,1)S(1)}, bf16[2,256,256]{2,1,0:T(8,128)(2,1)S(1)}, u32[]{:S(2)}, u32[]{:S(2)}) %collective-permute-start.8) | collective-permute-done | bytes 262176 | tf_op jit(solution)/shard_map/ppermute | solution.py:431
  42.0 1.0 %early_pairs.1 = (f32[2,3,64,256]{3,2,1,0:T(8,128)S(1)}, bf16[2,3,64,256]{3,2,1,0:T(8,128)(2,1)S(1)}, s32[16,256]{1,0:T(8,128)S(1)}) custom-call(s32[1,4]{1,0:T(1,128)S(1)} %bitcast.9, s32[2,64]{1,0:T(2,128)S(1)} %bitcast.8, bf16[2,256,256]{2,1,0:T(8,128)(2,1)S(1)} %get-tuple-element.24.refs_0_.own, bf16[2,256,256]{2,1,0:T(8,128)(2,1)S(1)} %get-tuple-element.27.refs_1_.own, ...), custom_call_target="tpu_custom_call" | custom-call | flops 402653184 | bytes 1212416 | tf_op jit(solution)/shard_map/early_pairs/pallas_call | solution.py:329
  43.0 1.6 %collective-permute-start.9 = (bf16[2,3,64,256]{3,2,1,0:T(8,128)(2,1)S(1)}, bf16[2,3,64,256]{3,2,1,0:T(8,128)(2,1)S(1)}, u32[]{:S(2)}, u32[]{:S(2)}) collective-permute-start(bf16[2,3,64,256]{3,2,1,0:T(8,128)(2,1)S(1)} %get-tuple-element.34), channel_id=1, source_target_pairs={{0,2},{2,0},{1,3},{3,1},{4,6},{6,4},{5,7},{7,5},{8,10},{10,8},{9,1... | collective-permute-start | bytes 589832 | tf_op jit(solution)/shard_map/ppermute | solution.py:436
  44.6 11.2 %collective-permute-done.12.last = bf16[2,256,256]{2,1,0:T(8,128)(2,1)S(1)} collective-permute-done((bf16[2,256,256]{2,1,0:T(8,128)(2,1)S(1)}, bf16[2,256,256]{2,1,0:T(8,128)(2,1)S(1)}, u32[]{:S(2)}, u32[]{:S(2)}) %collective-permute-start.12) | collective-permute-done | bytes 262176 | tf_op jit(solution)/shard_map/ppermute | solution.py:431
  56.4 3.3 %collective-permute-done.11.last = bf16[2,256,256]{2,1,0:T(8,128)(2,1)S(1)} collective-permute-done((bf16[2,256,256]{2,1,0:T(8,128)(2,1)S(1)}, bf16[2,256,256]{2,1,0:T(8,128)(2,1)S(1)}, u32[]{:S(2)}, u32[]{:S(2)}) %collective-permute-start.11) | collective-permute-done | bytes 262176 | tf_op jit(solution)/shard_map/ppermute | solution.py:431
  61.0 0.8 %collective-permute-done.13.got1 = bf16[2,3,64,256]{3,2,1,0:T(8,128)(2,1)S(1)} collective-permute-done((bf16[2,3,64,256]{3,2,1,0:T(8,128)(2,1)S(1)}, bf16[2,3,64,256]{3,2,1,0:T(8,128)(2,1)S(1)}, u32[]{:S(2)}, u32[]{:S(2)}) %collective-permute-start.13) | collective-permute-done | bytes 196640 | tf_op jit(solution)/shard_map/ppermute | solution.py:439
  61.8 1.6 %collective-permute-start.14 = (bf16[3,64,256]{2,1,0:T(8,128)(2,1)S(1)}, bf16[3,64,256]{2,1,0:T(8,128)(2,1)S(1)}, u32[]{:S(2)}, u32[]{:S(2)}) collective-permute-start(bf16[3,64,256]{2,1,0:T(8,128)(2,1)S(1)} %fusion), channel_id=1, source_target_pairs={{0,2},{2,0},{1,3},{3,1},{4,6},{6,4},{5,7},{7,5},{8,10},{10,8},{9,1... | collective-permute-start | bytes 294920 | tf_op jit(solution)/shard_map/ppermute | solution.py:440
  63.4 3.3 %collective-permute-done.14.far1 = bf16[3,64,256]{2,1,0:T(8,128)(2,1)S(1)} collective-permute-done((bf16[3,64,256]{2,1,0:T(8,128)(2,1)S(1)}, bf16[3,64,256]{2,1,0:T(8,128)(2,1)S(1)}, u32[]{:S(2)}, u32[]{:S(2)}) %collective-permute-start.14) | collective-permute-done | bytes 98336 | tf_op jit(solution)/shard_map/ppermute | solution.py:440
  66.7 1.2 %spread.1 = f32[64,16,256]{2,1,0:T(8,128)} custom-call(s32[16,256]{1,0:T(8,128)S(1)} %get-tuple-element.32.place, f32[2,3,64,256]{3,2,1,0:T(8,128)S(1)} %get-tuple-element.33.near0, bf16[2,3,64,256]{3,2,1,0:T(8,128)(2,1)S(1)} %collective-permute-done.9.far0, f32[3,64,256]{2,1,0:T(8,128)S(1)} %collective-permute-done.10.got0, ...), custom_call_target="tpu_custom_call" | custom-call | flops 1572864 | bytes 2097152 | tf_op jit(solution)/shard_map/spread/pallas_call | solution.py:392
  (27 shorter events, 2.9 us)
Async XLA Ops:
  0.0 4.6 %copy-start.3 = (bf16[512,512]{1,0:T(8,128)(2,1)S(1)}, bf16[512,512]{1,0:T(8,128)(2,1)}, u32[]{:S(2)}) copy-start(bf16[512,512]{1,0:T(8,128)(2,1)} %coeffs.3) | copy-start | bytes 1572868
  1.0 6.4 %copy-start.1 = (s32[64,2]{0,1:T(2,128)S(1)}, s32[64,2]{0,1:T(2,128)}, u32[]{:S(2)}) copy-start(s32[64,2]{0,1:T(2,128)} %param.7) | copy-start | bytes 1540
  1.0 6.4 %copy-start.4 = (s32[8]{0:T(128)S(1)}, s32[8]{0:T(128)}, u32[]{:S(2)}) copy-start(s32[8]{0:T(128)} %param.9) | copy-start | bytes 100
  1.1 11.1 %collective-permute-start.2 = (bf16[512,256]{1,0:T(8,128)(2,1)S(1)}, bf16[512,256]{1,0:T(8,128)(2,1)S(1)}, u32[]{:S(2)}, u32[]{:S(2)}) collective-permute-start(bf16[512,256]{1,0:T(8,128)(2,1)S(1)} %cut.1.first.own), channel_id=1, source_target_pairs={{4,8},{8,4},{5,9},{9,5},{6,10},{10,6},{7,11},{11,7},{20,24},{24,20... | collective-permute-start | bytes 786440 | tf_op jit(solution)/shard_map/ppermute | solution.py:415
  4.6 9.3 %collective-permute-start.1 = (bf16[512,256]{1,0:T(8,128)(2,1)S(1)}, bf16[512,256]{1,0:T(8,128)(2,1)S(1)}, u32[]{:S(2)}, u32[]{:S(2)}) collective-permute-start(bf16[512,256]{1,0:T(8,128)(2,1)S(1)} %cut.1.first.own), channel_id=1, source_target_pairs={{0,4},{4,0},{8,12},{12,8},{1,5},{5,1},{9,13},{13,9},{2,6},{6,2},{1... | collective-permute-start | bytes 786440 | tf_op jit(solution)/shard_map/ppermute | solution.py:416
  4.7 10.1 %collective-permute-start = (bf16[512,128]{1,0:T(8,128)(2,1)S(1)}, bf16[512,128]{1,0:T(8,128)(2,1)S(1)}, u32[]{:S(2)}, u32[]{:S(2)}) collective-permute-start(bf16[512,128]{1,0:T(8,128)(2,1)S(1)} %get-tuple-element.22), channel_id=1, source_target_pairs={{4,8},{8,4},{5,9},{9,5},{6,10},{10,6},{7,11},{11,7},{20,24},{24,20... | collective-permute-start | bytes 393224 | tf_op jit(solution)/shard_map/ppermute | solution.py:415
  7.1 13.2 %collective-permute-start.3 = (bf16[512,256]{1,0:T(8,128)(2,1)S(1)}, bf16[512,256]{1,0:T(8,128)(2,1)S(1)}, u32[]{:S(2)}, u32[]{:S(2)}) collective-permute-start(bf16[512,256]{1,0:T(8,128)(2,1)S(1)} %get-tuple-element.25.own), channel_id=1, source_target_pairs={{0,4},{4,0},{8,12},{12,8},{1,5},{5,1},{9,13},{13,9},{2,6},{6,2},{1... | collective-permute-start | bytes 786440 | tf_op jit(solution)/shard_map/ppermute | solution.py:416
  7.4 6.4 %copy-start = (bf16[2,512,1280]{2,1,0:T(8,128)(2,1)S(1)}, bf16[2,512,1280]{2,1,0:T(8,128)(2,1)}, u32[]{:S(2)}) copy-start(bf16[2,512,1280]{2,1,0:T(8,128)(2,1)} %integrals.3) | copy-start | bytes 7864324
  7.6 34.4 %copy-start.2 = (s32[4]{0:T(128)S(1)}, s32[4]{0:T(128)}, u32[]{:S(2)}) copy-start(s32[4]{0:T(128)} %param.8) | copy-start | bytes 52
  14.7 10.8 %collective-permute-start.5 = (bf16[2,256,256]{2,1,0:T(8,128)(2,1)S(1)}, bf16[2,256,256]{2,1,0:T(8,128)(2,1)S(1)}, u32[]{:S(2)}, u32[]{:S(2)}) collective-permute-start(bf16[2,256,256]{2,1,0:T(8,128)(2,1)S(1)} %get-tuple-element.28), channel_id=1, source_target_pairs={{0,8},{4,12},{8,0},{12,4},{1,9},{5,13},{9,1},{13,5},{2,10},{6,14},... | collective-permute-start | bytes 786440 | tf_op jit(solution)/shard_map/ppermute | solution.py:431
  14.8 5.5 %collective-permute-start.4 = (bf16[512,128]{1,0:T(8,128)(2,1)S(1)}, bf16[512,128]{1,0:T(8,128)(2,1)S(1)}, u32[]{:S(2)}, u32[]{:S(2)}) collective-permute-start(bf16[512,128]{1,0:T(8,128)(2,1)S(1)} %collective-permute-done.inner), channel_id=1, source_target_pairs={{0,2},{2,0},{1,3},{3,1},{4,6},{6,4},{5,7},{7,5},{8,10},{10,8},{9,1... | collective-permute-start | bytes 393224 | tf_op jit(solution)/shard_map/ppermute | solution.py:422
  16.4 15.2 %collective-permute-start.7 = (bf16[2,256,256]{2,1,0:T(8,128)(2,1)S(1)}, bf16[2,256,256]{2,1,0:T(8,128)(2,1)S(1)}, u32[]{:S(2)}, u32[]{:S(2)}) collective-permute-start(bf16[2,256,256]{2,1,0:T(8,128)(2,1)S(1)} %get-tuple-element.30), channel_id=1, source_target_pairs={{0,4},{4,0},{8,12},{12,8},{1,5},{5,1},{9,13},{13,9},{2,6},{6,2},{1... | collective-permute-start | bytes 786440 | tf_op jit(solution)/shard_map/ppermute | solution.py:431
  21.2 15.6 %collective-permute-start.6 = (bf16[2,256,256]{2,1,0:T(8,128)(2,1)S(1)}, bf16[2,256,256]{2,1,0:T(8,128)(2,1)S(1)}, u32[]{:S(2)}, u32[]{:S(2)}) collective-permute-start(bf16[2,256,256]{2,1,0:T(8,128)(2,1)S(1)} %get-tuple-element.29), channel_id=1, source_target_pairs={{0,8},{4,12},{8,0},{12,4},{1,9},{5,13},{9,1},{13,5},{2,10},{6,14},... | collective-permute-start | bytes 786440 | tf_op jit(solution)/shard_map/ppermute | solution.py:431
  24.5 17.6 %collective-permute-start.8 = (bf16[2,256,256]{2,1,0:T(8,128)(2,1)S(1)}, bf16[2,256,256]{2,1,0:T(8,128)(2,1)S(1)}, u32[]{:S(2)}, u32[]{:S(2)}) collective-permute-start(bf16[2,256,256]{2,1,0:T(8,128)(2,1)S(1)} %get-tuple-element.31), channel_id=1, source_target_pairs={{0,4},{4,0},{8,12},{12,8},{1,5},{5,1},{9,13},{13,9},{2,6},{6,2},{1... | collective-permute-start | bytes 786440 | tf_op jit(solution)/shard_map/ppermute | solution.py:431
  24.5 31.3 %collective-permute-start.12 = (bf16[2,256,256]{2,1,0:T(8,128)(2,1)S(1)}, bf16[2,256,256]{2,1,0:T(8,128)(2,1)S(1)}, u32[]{:S(2)}, u32[]{:S(2)}) collective-permute-start(bf16[2,256,256]{2,1,0:T(8,128)(2,1)S(1)} %get-tuple-element.36), channel_id=1, source_target_pairs={{0,12},{4,8},{8,4},{12,0},{1,13},{5,9},{9,5},{13,1},{2,14},{6,10},... | collective-permute-start | bytes 786440 | tf_op jit(solution)/shard_map/ppermute | solution.py:431
  25.5 34.1 %collective-permute-start.11 = (bf16[2,256,256]{2,1,0:T(8,128)(2,1)S(1)}, bf16[2,256,256]{2,1,0:T(8,128)(2,1)S(1)}, u32[]{:S(2)}, u32[]{:S(2)}) collective-permute-start(bf16[2,256,256]{2,1,0:T(8,128)(2,1)S(1)} %get-tuple-element.35), channel_id=1, source_target_pairs={{0,12},{4,8},{8,4},{12,0},{1,13},{5,9},{9,5},{13,1},{2,14},{6,10},... | collective-permute-start | bytes 786440 | tf_op jit(solution)/shard_map/ppermute | solution.py:431
  43.0 17.4 %collective-permute-start.9 = (bf16[2,3,64,256]{3,2,1,0:T(8,128)(2,1)S(1)}, bf16[2,3,64,256]{3,2,1,0:T(8,128)(2,1)S(1)}, u32[]{:S(2)}, u32[]{:S(2)}) collective-permute-start(bf16[2,3,64,256]{3,2,1,0:T(8,128)(2,1)S(1)} %get-tuple-element.34), channel_id=1, source_target_pairs={{0,2},{2,0},{1,3},{3,1},{4,6},{6,4},{5,7},{7,5},{8,10},{10,8},{9,1... | collective-permute-start | bytes 589832 | tf_op jit(solution)/shard_map/ppermute | solution.py:436
  60.3 1.5 %collective-permute-start.13 = (bf16[2,3,64,256]{3,2,1,0:T(8,128)(2,1)S(1)}, bf16[2,3,64,256]{3,2,1,0:T(8,128)(2,1)S(1)}, u32[]{:S(2)}, u32[]{:S(2)}) collective-permute-start(bf16[2,3,64,256]{3,2,1,0:T(8,128)(2,1)S(1)} %get-tuple-element.38), channel_id=1, source_target_pairs={{0,1},{1,0},{2,3},{3,2},{4,5},{5,4},{6,7},{7,6},{8,9},{9,8},{10,11... | collective-permute-start | bytes 589832 | tf_op jit(solution)/shard_map/ppermute | solution.py:439
  60.4 6.3 %collective-permute-start.10 = (f32[3,64,256]{2,1,0:T(8,128)S(1)}, f32[3,64,256]{2,1,0:T(8,128)S(1)}, u32[]{:S(2)}, u32[]{:S(2)}) collective-permute-start(f32[3,64,256]{2,1,0:T(8,128)S(1)} %add_bitcast_fusion), channel_id=1, source_target_pairs={{0,1},{1,0},{2,3},{3,2},{4,5},{5,4},{6,7},{7,6},{8,9},{9,8},{10,11... | collective-permute-start | bytes 589832 | tf_op jit(solution)/shard_map/ppermute | solution.py:441
  61.8 4.9 %collective-permute-start.14 = (bf16[3,64,256]{2,1,0:T(8,128)(2,1)S(1)}, bf16[3,64,256]{2,1,0:T(8,128)(2,1)S(1)}, u32[]{:S(2)}, u32[]{:S(2)}) collective-permute-start(bf16[3,64,256]{2,1,0:T(8,128)(2,1)S(1)} %fusion), channel_id=1, source_target_pairs={{0,2},{2,0},{1,3},{3,1},{4,6},{6,4},{5,7},{7,5},{8,10},{10,8},{9,1... | collective-permute-start | bytes 294920 | tf_op jit(solution)/shard_map/ppermute | solution.py:440
